TPU v7x, 32 devices: a whole 2x2x4 slice. The times are simulated.
32 devices in a mesh: dp: 8 (over z, x), tensor: 4 (over y, core).
Axes of the slice: x: 2, y: 2, z: 4, core: 2. Of those that a mesh axis runs over, the one named last changes fastest.
Arguments:
- images: bfloat16 [128, 256, 1764], P('tensor', 'dp'), may hold values from -6 to 6
- counts: int32 [16], P('dp'), may hold values from 2 to 16, as said below
- context: float32 [16, 100], P('dp'), may hold values from -6 to 6
- filter_two: bfloat16 [128, 128, 3, 3], P('tensor'), may hold values from -0.1875 to 0.1875
- gain_two: bfloat16 [128], P('tensor'), may hold values from 0.5 to 1.5
- shift_two: bfloat16 [128], P('tensor'), may hold values from -1.5 to 1.5
- filter_three: bfloat16 [128, 128, 3, 3], P('tensor'), may hold values from -0.1875 to 0.1875
- gain_three: bfloat16 [128], P('tensor'), may hold values from 0.5 to 1.5
- shift_three: bfloat16 [128], P('tensor'), may hold values from -1.5 to 1.5
- film_weight: bfloat16 [100, 2, 128], P(None, None, 'tensor'), may hold values from -0.1875 to 0.1875
- film_bias: bfloat16 [2, 128], P(None, 'tensor'), may hold values from -1 to 1
- cotangent: bfloat16 [128, 256, 100], P('tensor', 'dp'), may hold values from -6 to 6
Outputs:
- block_two: bfloat16 [128, 256, 441], P('tensor', 'dp')
- block_three: bfloat16 [128, 256, 100], P('tensor', 'dp')
- grad_images: float32 [128, 256, 1764], P('tensor', 'dp')
- grad_filter_two: float32 [128, 128, 3, 3], P('tensor')
- grad_gain_two: float32 [128], P('tensor')
- grad_shift_two: float32 [128], P('tensor')
- grad_filter_three: float32 [128, 128, 3, 3], P('tensor')
- grad_gain_three: float32 [128], P('tensor')
- grad_shift_three: float32 [128], P('tensor')
- grad_film_weight: float32 [100, 2, 128], P(None, None, 'tensor')
- grad_film_bias: float32 [2, 128], P(None, 'tensor')
- grad_context: float32 [16, 100], P('dp')
- levels: float32 [9], replicated
Inputs may be any that keep to these rules, and one draw needn't show every extreme that they name: `counts`: each task has 16 slots; some task in every draw has all 16 live.
All inputs are finite; a program needn't handle non-finite values.
Results may differ from a plain program's by a relative error of at most 0.0083.
Values may be sent and summed in bfloat16 or wider, within the bound.
No kernel may reach another device: no remote copies, remote signals or barrier semaphores. Data moves between devices by JAX's collectives and lax.ppermute only.
A program may use at most 320 MiB of HBM per device.

v0:
```python
import jax
import jax.numpy as jnp
from jax import lax
from jax.sharding import PartitionSpec as P

C = 128
MAP = 42
CAP = 16
HALF = 21
QUART = 10


EPSILON = 1e-05
PRECISE = lax.Precision.HIGHEST


def conv_apply(inputs, filters):
    return lax.conv_general_dilated(
        inputs,
        filters,
        (1, 1),
        ((1, 1), (1, 1)),
        dimension_numbers=("CNHW", "OIHW", "CNHW"),
        preferred_element_type=jnp.float32,
    )


def filter_grad(inputs, errors):
    padded = jnp.pad(inputs, ((0, 0), (0, 0), (1, 1), (1, 1)))
    summed = lax.conv_general_dilated(
        padded,
        errors,
        (1, 1),
        "VALID",
        dimension_numbers=("NCHW", "OIHW", "NCHW"),
        preferred_element_type=jnp.float32,
    )
    return jnp.transpose(summed, (1, 0, 2, 3))


def input_grad(errors, filters):
    return lax.conv_general_dilated(
        errors,
        filters[:, :, ::-1, ::-1],
        (1, 1),
        ((1, 1), (1, 1)),
        dimension_numbers=("CNHW", "IOHW", "CNHW"),
        preferred_element_type=jnp.float32,
    )


def pool_mean(values):
    channels, batch_size, height, breadth = values.shape
    half_h, half_w = (height // 2, breadth // 2)
    trimmed = values[:, :, : 2 * half_h, : 2 * half_w].reshape(
        channels, batch_size, half_h, 2, half_w, 2
    )
    return jnp.mean(trimmed, axis=(3, 5))


def expand(vector):
    return vector[:, None, None, None]


def normalize(conv_out, live_mask, mean_sum, spread_sum):
    weight = live_mask[None, :, None, None]
    cell_count = conv_out.shape[2] * conv_out.shape[3]
    totals, live_count = mean_sum((jnp.sum(conv_out * weight, axis=(1, 2, 3)), jnp.sum(live_mask)))
    extent = live_count * cell_count
    center = conv_out - expand(totals / extent)
    spread = spread_sum(jnp.sum(center * center * weight, axis=(1, 2, 3)))
    factor = lax.rsqrt(spread / extent + EPSILON)
    return (center * expand(factor), factor, extent, live_count)


def normalize_back(grad_pre, normed, gain_full, factor, extent, live_mask, back_sum):
    weight = live_mask[None, :, None, None]
    bias_sum, gain_sum = back_sum(
        (jnp.sum(grad_pre, axis=(1, 2, 3)), jnp.sum(grad_pre * normed, axis=(1, 2, 3)))
    )
    adjusted = grad_pre - expand(bias_sum / extent) - normed * expand(gain_sum / extent)
    return (adjusted * expand(gain_full * factor) * weight, gain_sum, bias_sum)


def run_blocks(
    inputs,
    cotangent,
    live_mask,
    onehot,
    context,
    params,
    widen,
    narrow,
    mean_sum,
    spread_sum,
    back_sum,
):
    f_two, f_three, g_two, s_two, g_three, s_three, film_w, film_b = params
    g_two = g_two.astype(jnp.float32)
    s_two = s_two.astype(jnp.float32)
    g_three = g_three.astype(jnp.float32)
    s_three = s_three.astype(jnp.float32)
    film_w = film_w.astype(jnp.float32)
    film_b = film_b.astype(jnp.float32)
    weight = live_mask[None, :, None, None]
    batch_size = inputs.shape[1]

    def squares(values):
        return jnp.sum(values * values * weight)

    full_in = widen(inputs).reshape(-1, batch_size, MAP, MAP)
    conv_two = conv_apply(full_in, f_two)
    normed_two, factor_two, extent_two, live_total = normalize(
        conv_two, live_mask, mean_sum, spread_sum
    )
    pre_two = expand(g_two) * normed_two + expand(s_two)
    active_two, gelu_back_two = jax.vjp(jax.nn.gelu, pre_two)
    pooled_two, pool_back_two = jax.vjp(pool_mean, active_two)
    hidden_two = pooled_two * weight
    hidden_low = hidden_two.astype(jnp.bfloat16)
    full_hidden = widen(hidden_low.reshape(hidden_low.shape[0], batch_size, HALF * HALF)).reshape(
        -1, batch_size, HALF, HALF
    )
    conv_three = conv_apply(full_hidden, f_three)
    normed_three, factor_three, extent_three, unused = normalize(
        conv_three, live_mask, mean_sum, spread_sum
    )
    pre_three = expand(g_three) * normed_three + expand(s_three)
    film_rows = jnp.einsum("tk,kjc->tjc", context, film_w, precision=PRECISE) + film_b[None]
    per_image = jnp.einsum("nt,tjc->jcn", onehot, film_rows, precision=PRECISE)
    scale_img = 1.0 + per_image[0][:, :, None, None]
    shift_img = per_image[1][:, :, None, None]
    filmed = scale_img * pre_three + shift_img
    active_three, gelu_back_three = jax.vjp(jax.nn.gelu, filmed)
    pooled_three, pool_back_three = jax.vjp(pool_mean, active_three)
    output_three = pooled_three * weight
    levels = jnp.stack(
        [
            squares(conv_two),
            squares(pre_two),
            squares(active_two),
            squares(hidden_two),
            squares(conv_three),
            squares(pre_three),
            squares(filmed),
            squares(active_three),
            squares(output_three),
        ]
    )
    target = cotangent.reshape(cotangent.shape[0], batch_size, QUART, QUART).astype(jnp.float32)
    (grad_active_three,) = pool_back_three(target * weight)
    (grad_filmed,) = gelu_back_three(grad_active_three)
    grad_shift_img = jnp.sum(grad_filmed, axis=(2, 3))
    grad_scale_img = jnp.sum(grad_filmed * pre_three, axis=(2, 3))
    grad_rows = jnp.einsum(
        "nt,jcn->tjc", onehot, jnp.stack([grad_scale_img, grad_shift_img]), precision=PRECISE
    )
    grad_film_w = jnp.einsum("tk,tjc->kjc", context, grad_rows, precision=PRECISE)
    grad_film_b = jnp.sum(grad_rows, axis=0)
    grad_context = jnp.einsum("tjc,kjc->tk", grad_rows, film_w, precision=PRECISE)
    grad_conv_three, grad_g_three, grad_s_three = normalize_back(
        grad_filmed * scale_img,
        normed_three,
        g_three,
        factor_three,
        extent_three,
        live_mask,
        back_sum,
    )
    errors_three = grad_conv_three.astype(jnp.bfloat16)
    grad_f_three = filter_grad(full_hidden, errors_three)
    grad_hidden = narrow(input_grad(errors_three, f_three))
    (grad_active_two,) = pool_back_two(grad_hidden * weight)
    (grad_pre_two,) = gelu_back_two(grad_active_two)
    grad_conv_two, grad_g_two, grad_s_two = normalize_back(
        grad_pre_two, normed_two, g_two, factor_two, extent_two, live_mask, back_sum
    )
    errors_two = grad_conv_two.astype(jnp.bfloat16)
    grad_f_two = filter_grad(full_in, errors_two)
    grad_input = narrow(input_grad(errors_two, f_two))
    return (
        hidden_low,
        output_three,
        grad_input,
        grad_f_two,
        grad_g_two,
        grad_s_two,
        grad_f_three,
        grad_g_three,
        grad_s_three,
        grad_film_w,
        grad_film_b,
        grad_context,
        levels,
        live_total,
    )


def local(
    images,
    counts,
    context,
    filter_two,
    gain_two,
    shift_two,
    filter_three,
    gain_three,
    shift_three,
    film_weight,
    film_bias,
    cotangent,
):
    local_in, local_cot = (images, cotangent)
    params = (
        filter_two,
        filter_three,
        gain_two,
        shift_two,
        gain_three,
        shift_three,
        film_weight,
        film_bias,
    )

    def widen(values):
        return lax.all_gather(values, "tensor", axis=0, tiled=True)

    def narrow(values):
        return lax.psum_scatter(values, "tensor", scatter_dimension=0, tiled=True)

    def mean_sum(parts):
        return lax.psum(parts, "dp")

    def spread_sum(parts):
        return lax.psum(parts, "dp")

    def back_sum(parts):
        return lax.psum(parts, "dp")

    slot_ids = jnp.arange(local_in.shape[1], dtype=jnp.int32)
    task_ids = slot_ids // CAP
    column = jnp.arange(counts.shape[0], dtype=jnp.int32)
    onehot = (task_ids[:, None] == column[None, :]).astype(jnp.float32)
    task_limit = jnp.sum(onehot * counts[None, :].astype(jnp.float32), axis=1)
    live_mask = ((slot_ids % CAP).astype(jnp.float32) < task_limit).astype(jnp.float32)
    results = run_blocks(
        local_in,
        local_cot,
        live_mask,
        onehot,
        context,
        params,
        widen,
        narrow,
        mean_sum,
        spread_sum,
        back_sum,
    )
    (
        hidden_low,
        output_three,
        grad_input,
        grad_f_two,
        grad_g_two,
        grad_s_two,
        grad_f_three,
        grad_g_three,
        grad_s_three,
        grad_film_w,
        grad_film_b,
        grad_ctx,
        levels,
        live_total,
    ) = results
    batch_size = local_in.shape[1]
    output_low = output_three.astype(jnp.bfloat16)
    block_two = hidden_low.reshape(hidden_low.shape[0], batch_size, HALF * HALF)
    block_three = output_low.reshape(output_low.shape[0], batch_size, QUART * QUART)
    grad_images = grad_input.reshape(grad_input.shape[0], batch_size, MAP * MAP)
    grad_f_two, grad_f_three, grad_film_w, grad_film_b = lax.psum(
        (grad_f_two, grad_f_three, grad_film_w, grad_film_b), "dp"
    )
    grad_context = lax.psum(grad_ctx, "tensor")
    level_sums = lax.psum(levels, ("dp", "tensor"))
    cell_areas = jnp.array([MAP * MAP] * 3 + [HALF * HALF] * 5 + [QUART * QUART], jnp.float32)
    root_mean = jnp.sqrt(level_sums / (live_total * C * cell_areas))
    return (
        block_two,
        block_three,
        grad_images,
        grad_f_two,
        grad_g_two,
        grad_s_two,
        grad_f_three,
        grad_g_three,
        grad_s_three,
        grad_film_w,
        grad_film_b,
        grad_context,
        root_mean,
    )


def solution(mesh):
    placed = (
        P("tensor", "dp", None),
        P("dp"),
        P("dp", None),
        P("tensor", None, None, None),
        P("tensor"),
        P("tensor"),
        P("tensor", None, None, None),
        P("tensor"),
        P("tensor"),
        P(None, None, "tensor"),
        P(None, "tensor"),
        P("tensor", "dp", None),
    )
    return jax.shard_map(
        local,
        mesh=mesh,
        in_specs=placed,
        out_specs=(
            P("tensor", "dp", None),
            P("tensor", "dp", None),
            P("tensor", "dp", None),
            P("tensor", None, None, None),
            P("tensor"),
            P("tensor"),
            P("tensor", None, None, None),
            P("tensor"),
            P("tensor"),
            P(None, None, "tensor"),
            P(None, "tensor"),
            P("dp", None),
            P(),
        ),
        check_vma=False,
    )
```

profile of v0, /device:TPU:0, one launch (start us, length us, event | category | flops | bytes accessed | tf_op | source)
XLA Modules:
  0.0 1444.5 jit_solution(16373436225417919134)
XLA Ops:
  10.7 95.7 %all-gather.3.cloned.1.call-done = bf16[128,32,1764]{2,1,0:T(8,128)(2,1)} async-done(((bf16[32,32,1764]{2,1,0:T(8,128)(2,1)}), bf16[128,32,1764]{2,1,0:T(8,128)(2,1)}) %all-gather.3.cloned.1.call-update) | async-done | bytes 14450704 | tf_op jit(solution)/shard_map/all_gather | solution.py:226
  106.3 21.7 %copy.54 = bf16[128,32,1764]{0,1,2:T(8,128)(2,1)} copy(bf16[128,32,1764]{2,1,0:T(8,128)(2,1)} %all-gather.3.cloned.1.call-done) | data formatting | bytes 28901376 | tf_op jit(solution)/shard_map/all_gather | solution.py:226
  128.1 39.4 %multiply_reduce_fusion.4 = (f32[32]{0:T(128)S(1)}, f32[32,32,42,42]{0,1,3,2:T(8,128)}) fusion(f32[32]{0:T(128)S(1)} %convert_element_type.62, bf16[128,32,42,42]{0,1,3,2:T(8,128)(2,1)} %bitcast.73, bf16[32,128,3,3]{1,0,3,2:T(8,128)(2,1)S(1)} %copy-done), kind=kOutput, calls=%fused_computation.16 | convolution fusion | flops 4034338816 | bytes 21750016 | tf_op jit(solution)/shard_map/conv_general_dilated | solution.py:18
  167.5 22.0 %all-reduce.3 = (f32[32]{0:T(128)S(1)}, f32[]{:T(128)}) all-reduce(f32[32]{0:T(128)S(1)} %get-tuple-element.100, f32[]{:T(128)} %convert_reduce_fusion), channel_id=1, replica_groups=mesh['dp'=8,'tensor'=4] {'dp'}, use_global_device_ids=true, to_apply=%region_2.3 | all-reduce | flops 33 | bytes 264 | tf_op jit(solution)/shard_map/psum | solution.py:232
  190.1 13.5 multiply_reduce_fusion.3
  203.6 17.4 %psum.110 = f32[32]{0:T(128)S(1)} all-reduce(f32[32]{0:T(128)S(1)} %multiply_reduce_fusion.3), channel_id=1, replica_groups=mesh['dp'=8,'tensor'=4] {'dp'}, use_global_device_ids=true, to_apply=%region_6.7 | all-reduce | flops 32 | bytes 256 | tf_op jit(solution)/shard_map/psum | solution.py:235
  221.0 26.6 %multiply_multiply_fusion.3 = f32[32,32,42,42]{0,1,3,2:T(8,128)} fusion(f32[32,32,42,42]{0,1,3,2:T(8,128)} %get-tuple-element.101, f32[32]{0:T(128)S(1)} %convert_element_type.63, f32[32]{0:T(128)S(1)} %get-tuple-element.91, f32[32]{0:T(128)S(1)} %broadcast_divide_fusion.5, f32[32]{0:T(128)S(1)} %convert_element_type.59), kind=kLoop, calls=%fused_computation.17 | loop fusion | flops 21676032 | bytes 14451200 | tf_op jit(solution)/shard_map/jvp()/mul | solution.py:117
  247.6 15.0 %reduce_sum.228 = f32[32,32,21,21]{0,1,3,2:T(8,128)} reduce(f32[32,32,21,2,21,2]{0,1,5,4,3,2:T(8,128)} %bitcast.66, f32[]{:T(128)} %constant.64.clone.1), dimensions={3,5}, to_apply=%region_7.8 | reduce | flops 1354752 | bytes 9031684 | tf_op jit(solution)/shard_map/jvp()/reduce_sum | solution.py:58
  274.4 27.7 %all-gather.5.cloned.1.call-done = bf16[128,32,441]{2,1,0:T(8,128)(2,1)} async-done(((bf16[32,32,441]{2,1,0:T(8,128)(2,1)}), bf16[128,32,441]{2,1,0:T(8,128)(2,1)}) %all-gather.5.cloned.1.call-update) | async-done | bytes 3612688 | tf_op jit(solution)/shard_map/all_gather | solution.py:226
  302.1 9.0 copy.57
  311.1 13.1 multiply_reduce_fusion.12
  324.2 33.9 %psum.111 = f32[32]{0:T(128)S(1)} all-reduce(f32[32]{0:T(128)S(1)} %get-tuple-element.102), channel_id=1, replica_groups=mesh['dp'=8,'tensor'=4] {'dp'}, use_global_device_ids=true, to_apply=%region_9.10 | all-reduce | flops 32 | bytes 256 | tf_op jit(solution)/shard_map/psum | solution.py:232
  363.3 17.1 %psum.112 = f32[32]{0:T(128)S(1)} all-reduce(f32[32]{0:T(128)S(1)} %multiply_reduce_fusion.11), channel_id=1, replica_groups=mesh['dp'=8,'tensor'=4] {'dp'}, use_global_device_ids=true, to_apply=%region_11.12 | all-reduce | flops 32 | bytes 256 | tf_op jit(solution)/shard_map/psum | solution.py:235
  383.1 17.5 %multiply_reduce_fusion.9 = (f32[32,32]{0,1:T(8,128)S(1)}, f32[32]{0:T(128)S(1)}, f32[]{:T(128)}, f32[32]{0:T(128)S(1)}, f32[]{:T(128)}, /*index=5*/f32[]{:T(128...) fusion(f32[32]{0:T(128)S(1)} %convert_element_type.67, ...), kind=kLoop, calls=%fused_computation.33 | loop fusion | flops 21673916 | bytes 8881172 | tf_op jit(solution)/shard_map/reduce_sum | solution.py:154
  400.6 19.1 %all-reduce.2 = (f32[32]{0:T(128)S(1)}, f32[32]{0:T(128)S(1)}) all-reduce(f32[32]{0:T(128)S(1)} %get-tuple-element.70, f32[32]{0:T(128)S(1)} %get-tuple-element.72), channel_id=1, replica_groups=mesh['dp'=8,'tensor'=4] {'dp'}, use_global_device_ids=true, to_apply=%region_16.17 | all-reduce | flops 64 | bytes 512 | tf_op jit(solution)/shard_map/psum | solution.py:238
  435.5 29.2 %copy.67 = f32[128,32,21,21]{1,3,2,0:T(8,128)} copy(f32[128,32,21,21]{0,1,3,2:T(8,128)} %fusion.35) | data formatting | bytes 14450688
  464.7 20.6 %reshape.120 = f32[128,14112]{1,0:T(8,128)} reshape(f32[128,21,21,32]{3,2,1,0:T(8,128)} %bitcast.64) | data formatting | bytes 14450688
  486.0 60.9 %reduce-scatter.7.cloned.1.call-done = f32[32,14112]{1,0:T(8,128)} async-done(((f32[128,14112]{1,0:T(8,128)}), f32[32,14112]{1,0:T(8,128)}) %reduce-scatter.7.cloned.1.call-update) | async-done | bytes 1806352
  566.0 10.0 broadcast_in_dim.5
  576.0 43.3 %fusion.6 = (f32[]{:T(128)}, f32[32]{0:T(128)S(1)}, f32[]{:T(128)}, f32[32]{0:T(128)S(1)}, f32[]{:T(128)}, /*index=5*/f32[32,32,42,42]{0,1,3,2:T(8,128)}) fusion(f32[32,32,42,42]{0,1,3,2:T(8,128)} %get-tuple-element.101, f32[32]{0:T(128)S(1)} %convert_element_type.63, f32[32]{0:T(128)S(1)} %get-tuple-element.91, f32[32]{0:T(128)S(1)} %broadcast_divide_fusion.5, ...), kind=kLoop, calls=%fused_computation.9 | loop fusion | flops 63221696 | bytes 21676940 | tf_op jit(solution)/shard_map/reduce_sum | solution.py:109
  619.3 38.5 %all-reduce.1 = (f32[32]{0:T(128)S(1)}, f32[32]{0:T(128)S(1)}, f32[100,2,32]{0,2,1:T(8,128)}, f32[2,32]{1,0:T(2,128)}) all-reduce(f32[32]{0:T(128)S(1)} %get-tuple-element.66, f32[32]{0:T(128)S(1)} %get-tuple-element.68, f32[100,2,32]{0,2,1:T(8,128)S(1)} %convolution_bitcast_fusion, ...), channel_id=1, replica_groups=mesh['dp'=8,'tensor'=4] {'dp'}, use_global_device_ids=true, to_apply=%region_21.22 | all-reduce | flops 6528 | bytes 52224 | tf_op jit(solution)/shard_map/psum | solution.py:238
  657.8 24.7 %multiply_convert_fusion = bf16[32,32,42,42]{0,1,3,2:T(8,128)(2,1)} fusion(f32[32,32,42,42]{0,1,3,2:T(8,128)} %get-tuple-element.89, f32[32,32,42,42]{0,1,3,2:T(8,128)} %get-tuple-element.101, f32[32]{0:T(128)S(1)} %get-tuple-element.90, f32[32]{0:T(128)S(1)} %get-tuple-element.106, f32[32]{0:T(128)S(1)} %get-tuple-element.107, f32[32]{0:T(128)S(1)} %get-tuple-element.91, ...), kind=kLoop, calls=%fused_computation.12 | loop fusion | flops 14450688 | bytes 18064128 | tf_op jit(solution)/shard_map/convert_element_type | solution.py:178
  682.5 25.7 %fusion.36 = f32[128,32,42,42]{0,1,3,2:T(8,128)} fusion(bf16[32,32,42,42]{0,1,3,2:T(8,128)(2,1)} %multiply_convert_fusion, bf16[32,128,3,3]{1,0,3,2:T(8,128)(2,1)S(1)} %copy-done), kind=kOutput, calls=%fused_computation.92 | convolution fusion | flops 4030726144 | bytes 32587776 | tf_op jit(solution)/shard_map/conv_general_dilated | solution.py:42
  708.2 68.1 %copy.62 = f32[128,32,42,42]{3,1,2,0:T(8,128)} copy(f32[128,32,42,42]{0,1,3,2:T(8,128)} %fusion.36) | data formatting | bytes 57802752 | tf_op jit(solution)/shard_map/conv_general_dilated | solution.py:42
  777.1 8.8 slice.14
  793.5 10.1 fusion.38
  803.6 24.6 %fusion.37 = f32[32,128,3,3]{1,0,3,2:T(8,128)} fusion(bf16[128,32,42,42]{0,1,3,2:T(8,128)(2,1)} %bitcast.74, bf16[32,32,42,42]{0,1,3,2:T(8,128)(2,1)} %multiply_convert_fusion), kind=kOutput, calls=%fused_computation.93 | convolution fusion | flops 4030726144 | bytes 18210816 | tf_op jit(solution)/shard_map/transpose | solution.py:38
  842.3 36.8 %psum.122 = f32[9]{0:T(128)S(1)} all-reduce(f32[9]{0:T(128)S(1)} %stack.51), channel_id=1, replica_groups=mesh['dp'=8,'tensor'=4] {'dp','tensor'}, use_global_device_ids=true, to_apply=%region_40.41 | all-reduce | flops 9 | bytes 72 | tf_op jit(solution)/shard_map/psum | solution.py:284
  879.7 480.2 %reduce-scatter.5.cloned.1.call-done = f32[32,32,42,42]{3,1,2,0:T(8,128)} async-done(((f32[128,32,42,42]{3,1,2,0:T(8,128)}), f32[32,32,42,42]{3,1,2,0:T(8,128)}) %reduce-scatter.5.cloned.1.call-update) | async-done | bytes 7225360 | tf_op jit(solution)/shard_map/reduce_scatter | solution.py:229
  1359.9 28.8 %copy.63 = f32[32,32,42,42]{3,2,1,0:T(8,128)} copy(f32[32,32,42,42]{3,1,2,0:T(8,128)} %reduce-scatter.5.cloned.1.call-done) | data formatting | bytes 14450688 | tf_op jit(solution)/shard_map/reduce_scatter | solution.py:229
  1388.6 19.0 %reshape.115 = f32[32,32,1764]{2,1,0:T(8,128)} reshape(f32[32,32,42,42]{3,2,1,0:T(8,128)} %copy.63) | data formatting | bytes 14450688 | tf_op jit(solution)/shard_map/reshape | solution.py:279
  1407.7 27.0 %all-reduce.7.cloned.1.call-done = (f32[32,128,3,3]{1,0,3,2:T(8,128)}, f32[32,128,3,3]{1,0,3,2:T(8,128)}) async-done(((f32[32,128,3,3]{1,0,3,2:T(8,128)}, f32[32,128,3,3]{1,0,3,2:T(8,128)}), (f32[32,128,3,3]{1,0,3,2:T(8,128)}, f32[32,128,3,3]{1,0,3,2:T(8,128)})) %all-reduce.7.cloned.1.call-update) | async-done | bytes 294928 | tf_op jit(solution)/shard_map/psum | solution.py:280
  (105 shorter events, 83.4 us)
Async XLA Ops:
  7.2 120.9 %copy-start = (bf16[32,128,3,3]{1,0,3,2:T(8,128)(2,1)S(1)}, bf16[32,128,3,3]{1,0,3,2:T(8,128)(2,1)}, u32[]{:S(2)}) copy-start(bf16[32,128,3,3]{1,0,3,2:T(8,128)(2,1)} %param.16) | copy-start | bytes 221188
  7.2 99.1 %all-gather.3.cloned.1.call-start = ((), (), s32[]{:S(2)}) async-start(), calls=%async_computation.2 | async-start | bytes 18350080 | tf_op jit(solution)/shard_map/all_gather | solution.py:226
  7.9 294.2 %all-gather.5.cloned.1.call-start = ((), (), s32[]{:S(2)}) async-start(), calls=%async_computation.3 | async-start | bytes 5242880 | tf_op jit(solution)/shard_map/all_gather | solution.py:226
  10.1 372.8 %copy-start.7 = (f32[32]{0:T(128)}, f32[32]{0:T(128)S(1)}, u32[]{:S(2)}) copy-start(f32[32]{0:T(128)S(1)} %get-tuple-element.96) | copy-start | bytes 388
  190.1 30.9 %copy-start.10 = (bf16[32]{0:T(256)(128)(2,1)S(1)}, bf16[32]{0:T(256)(128)(2,1)}, u32[]{:S(2)}) copy-start(bf16[32]{0:T(256)(128)(2,1)} %param.17) | copy-start | bytes 196
  262.6 7.1 copy-start.16
  262.6 7.2 copy-start.11
  262.6 7.2 copy-start.17
  262.6 7.2 copy-start.3
  262.6 7.2 copy-start.9
  262.6 7.8 copy-start.2
  269.7 277.2 %reduce-scatter.7.cloned.1.call-start = ((), (), s32[]{:S(2)}) async-start(), calls=%async_computation.5 | async-start | bytes 9093120
  270.4 40.7 %copy-start.15 = (bf16[32,128,3,3]{1,0,3,2:T(8,128)(2,1)S(1)}, bf16[32,128,3,3]{1,0,3,2:T(8,128)(2,1)}, u32[]{:S(2)}) copy-start(bf16[32,128,3,3]{1,0,3,2:T(8,128)(2,1)} %param.19) | copy-start | bytes 221188
  358.1 24.8 %slice-start = ((s8[7225344]{0:T(1024)(128)(4,1)}), s8[3031040]{0:T(1024)(128)(4,1)S(1)}, s32[]{:S(2)}) async-start(s8[7225344]{0:T(1024)(128)(4,1)} %bitcast.68), calls=%async_computation.7 | async-start | bytes 6062080
  380.4 2.7 slice-start.1
  419.7 6.4 copy-start.18
  419.7 6.4 copy-start.19
  426.2 1.8 copy-start.1
  485.3 874.6 %reduce-scatter.5.cloned.1.call-start = ((), (), s32[]{:S(2)}) async-start(), calls=%async_computation.4 | async-start | bytes 110100480 | tf_op jit(solution)/shard_map/reduce_scatter | solution.py:229
  485.7 76.2 %copy-start.5 = (f32[2,2,32]{2,0,1:T(2,128)}, f32[2,2,32]{2,0,1:T(2,128)S(1)}, u32[]{:S(2)}) copy-start(f32[2,2,32]{2,0,1:T(2,128)S(1)} %get-tuple-element.105) | copy-start | bytes 1540
  657.8 24.7 %copy-start.12 = (f32[32]{0:T(128)}, f32[32]{0:T(128)S(1)}, u32[]{:S(2)}) copy-start(f32[32]{0:T(128)S(1)} %get-tuple-element.112) | copy-start | bytes 388
  657.8 24.7 %copy-start.13 = (f32[32]{0:T(128)}, f32[32]{0:T(128)S(1)}, u32[]{:S(2)}) copy-start(f32[32]{0:T(128)S(1)} %get-tuple-element.113) | copy-start | bytes 388
  776.3 658.3 %all-reduce.7.cloned.1.call-start = ((), (), s32[]{:S(2)}) async-start(), calls=%async_computation.6 | async-start | bytes 589824 | tf_op jit(solution)/shard_map/psum | solution.py:280
  785.9 6.3 copy-start.8
  803.6 24.6 %copy-start.4 = (bf16[100,2,32]{0,2,1:T(8,128)(2,1)S(1)}, bf16[100,2,32]{0,2,1:T(8,128)(2,1)}, u32[]{:S(2)}) copy-start(bf16[100,2,32]{0,2,1:T(8,128)(2,1)} %param.22) | copy-start | bytes 38404
  803.6 24.6 %copy-start.6 = (f32[2,2,32]{2,0,1:T(2,128)S(1)}, f32[2,2,32]{2,0,1:T(2,128)}, u32[]{:S(2)}) copy-start(f32[2,2,32]{2,0,1:T(2,128)} %copy-done.5) | copy-start | bytes 1540
  803.6 75.5 %copy-start.14 = (f32[9]{0:T(128)S(1)}, f32[9]{0:T(128)}, u32[]{:S(2)}) copy-start(f32[9]{0:T(128)} %constant.76.clone) | copy-start | bytes 112
Sparse Core Ops, SparseCore 0:
  9.6 96.7 all-gather.2
  269.8 32.2 all-gather.4
  485.4 61.4 reduce-scatter.6
  776.4 583.4 reduce-scatter.4
  1363.6 70.9 all-reduce.6
where the time goes:
time: 1450 us; the launch traced here: 1440 us
  waiting for transfers between devices  692 us (48%)
  local copies, waits for them, and re-layouts  254 us (18%)
  blocking collectives  191 us (13%)
  other arithmetic  169 us (12%)
  matrix products  121 us (8%)
  between operations  16.3 us (1%)
    reduce_scatter x1, waiting for transfers between devices, narrow(): return lax.psum_scatter(values, 'tensor', scatter_dimension=0, tiled=True)  480 us
    all_gather x2, waiting for transfers between devices, widen(): return lax.all_gather(values, 'tensor', axis=0, tiled=True)  123 us
    unnamed x52, local copies, waits for them, and re-layouts  73 us
    conv_general_dilated x1, local copies, waits for them, and re-layouts, input_grad(): lax.conv_general_dilated(errors, filters[:, :, ::-1, ::-1], (1, 1), ((1,...  68.1 us
    unnamed x6, waiting for transfers between devices  61.6 us
    psum x2, blocking collectives, back_sum(): return lax.psum(parts, 'dp')  57.6 us
    psum x2, blocking collectives, mean_sum(): return lax.psum(parts, 'dp')  55.9 us
    conv_general_dilated x2, matrix products, conv_apply(): lax.conv_general_dilated(inputs, filters, (1, 1), ((1, 1), (1, 1)), dimen...  52.5 us
  transfers between devices with their start and end apart: 5, of which 5 were waited for; matrix products, arithmetic and copies ran while one was open for 8% of the time, Pallas kernels for 0%

commit v1 on v0

v1 whole, which is shorter than its diff:
```python
import functools

import jax
import jax.numpy as jnp
import numpy as np
from jax import lax
from jax.experimental import pallas as pl
from jax.experimental.pallas import tpu as pltpu
from jax.sharding import PartitionSpec as P

C = 128
MAP = 42
CAP = 16
HALF = 21
QUART = 10
CHUNK = 2
SENT = 4
VMEM_BYTES = 63 << 20

CELLS_TWO = MAP * MAP
CELLS_THREE = HALF * HALF
CELLS_OUT = QUART * QUART
LANES_TWO = 1792
LANES_THREE = 512
LANES_OUT = 128
EPSILON = 1e-05
PRECISE = lax.Precision.HIGHEST
F32 = jnp.float32
BF16 = jnp.bfloat16
ROOT = 0.7978845608028654
CUBIC = 0.044715


def lane_ids(width):
    return lax.broadcasted_iota(jnp.int32, (1, width), 1)


def as_columns(rows):
    return jnp.concatenate([rows] * (C // 8), axis=0).T


def column_tile(columns):
    ids = lax.broadcasted_iota(jnp.int32, (C, C), 1)
    tile = jnp.zeros((C, C), F32)
    for place, column in enumerate(columns):
        tile = jnp.where(ids == place, column, tile)
    return tile


def row_tile(rows, count=8):
    ids = lax.broadcasted_iota(jnp.int32, (count, C), 0)
    tile = jnp.zeros((count, C), F32)
    for place, row in enumerate(rows):
        tile = jnp.where(ids == place, row, tile)
    return tile


def row(tile_ref, place):
    return tile_ref[place : place + 1, :]


def column(tile_ref, place):
    return tile_ref[:, place : place + 1]


def merge_moments(state, weight, mean, spread, cells):
    count, middle, total = state
    added = weight * cells
    both = count + added
    away = mean - middle
    share = added / jnp.maximum(both, 1.0)
    return both, middle + away * share, total + weight * spread + away * away * count * share


def slice_norm(heard_ref):
    means, spreads, counts = heard_ref[:, 0, :], heard_ref[:, 1, :], heard_ref[:, 2, :]
    extent = jnp.sum(counts, axis=0, keepdims=True)
    middle = jnp.sum(counts * means, axis=0, keepdims=True) / extent
    away = means - middle
    variance = jnp.sum(spreads + counts * away * away, axis=0, keepdims=True) / extent
    return middle, lax.rsqrt(variance + EPSILON), variance, extent


def level_row(columns):
    return jnp.sum(column_tile(columns), axis=0, keepdims=True)


def spread_rows(tile, out_ref):
    out_ref[...] = jnp.broadcast_to(tile[None], out_ref.shape)


def stack_sideways(values, side, width, stack_ref):
    column = lane_ids(width) % side
    stack_ref[0:C] = jnp.where(column == 0, 0.0, pltpu.roll(values, 1, 1)).astype(BF16)
    stack_ref[C : 2 * C] = values.astype(BF16)
    stack_ref[2 * C : 3 * C] = jnp.where(column == side - 1, 0.0, pltpu.roll(values, width - 1, 1)).astype(BF16)


def stack_upright(values, side, width, stack_ref):
    ids = lane_ids(width)
    cells = side * side
    stack_ref[0:C] = jnp.where(ids >= side, pltpu.roll(values, side, 1), 0.0).astype(BF16)
    stack_ref[C : 2 * C] = values.astype(BF16)
    stack_ref[2 * C : 3 * C] = jnp.where(ids < cells - side, pltpu.roll(values, width - side, 1), 0.0).astype(BF16)


def conv_stacked(weights_ref, stack_ref, side, width):
    ids = lane_ids(width)
    cells = side * side
    parts = jnp.dot(weights_ref[...], stack_ref[...], preferred_element_type=F32)
    above = jnp.where(ids >= side, pltpu.roll(parts[:C], side, 1), 0.0)
    below = jnp.where(ids < cells - side, pltpu.roll(parts[2 * C :], width - side, 1), 0.0)
    return jnp.where(ids < cells, parts[C : 2 * C] + above + below, 0.0)


def moments(values, cells, width):
    mean = jnp.sum(values, axis=1, keepdims=True) * (1.0 / cells)
    centered = jnp.where(lane_ids(width) < cells, values - mean, 0.0)
    return mean, jnp.sum(centered * centered, axis=1, keepdims=True)


def gelu_tanh(values):
    return jnp.tanh(ROOT * values * (1.0 + CUBIC * values * values))


def gelu_slope(values, bend):
    inner = ROOT * (1.0 + 3.0 * CUBIC * values * values)
    return 0.5 * (1.0 + bend) + 0.5 * values * (1.0 - bend * bend) * inner


def halves(values):
    high = values.astype(BF16)
    return jnp.concatenate([high, (values - high.astype(F32)).astype(BF16)], axis=0)


def dot_halves(split, weights_ref):
    both = jnp.dot(split, weights_ref[...], preferred_element_type=F32)
    return both[:C] + both[C:]


def own_rows(me, partner, count):
    return pl.ds(pl.multiple_of((me ^ partner) * count, count), count)


def kernel_params():
    return pltpu.CompilerParams(vmem_limit_bytes=VMEM_BYTES, dimension_semantics=("arbitrary",))


def pack_kernel(group, images_each, skipped, me_ref, maps_ref, *piece_refs):
    piece_refs = piece_refs[skipped:]
    turned = jnp.swapaxes(maps_ref[...], 0, 1)
    per_device = len(piece_refs) // group
    step = images_each // per_device
    for lead in range(group):

        @pl.when(me_ref[0] % group == lead)
        def _():
            for other in range(group):
                for part in range(per_device):
                    first = (lead ^ other) * images_each + part * step
                    piece_refs[other * per_device + part][...] = turned[first : first + step]


def unpack_kernel(group, images_each, count, me_ref, *refs):
    out_ref = refs[-1]
    piece_refs = refs[:count]
    per_device = len(piece_refs) // group
    for lead in range(group):

        @pl.when(me_ref[0] % group == lead)
        def _():
            ordered = []
            for place in range(group):
                other = place ^ lead
                ordered += [piece_refs[other * per_device + part][...] for part in range(per_device)]
            joined = jnp.concatenate(ordered, axis=0)
            out_ref[...] = jnp.swapaxes(joined, 0, 1).astype(out_ref.dtype)


def first_conv_kernel(partners, part, final, me_ref, live_ref, weights_ref, *refs):
    piece_refs = refs[:partners]
    conv_ref, state_ref, maps, stack, state = refs[-5:]
    rows = C // partners
    step = pl.program_id(0)

    @pl.when(step == 0)
    def _():
        maps[...] = jnp.zeros_like(maps)
        state[...] = refs[partners][...] if part else jnp.zeros_like(state)

    for partner in range(partners):
        maps[own_rows(me_ref[0], partner, rows), 0:CELLS_TWO] = piece_refs[partner][0].astype(F32)
    stack_sideways(maps[...], MAP, LANES_TWO, stack)
    conv = conv_stacked(weights_ref, stack, MAP, LANES_TWO)
    conv_ref[0] = conv
    mean, spread = moments(conv, CELLS_TWO, LANES_TWO)
    live = live_ref[part * pl.num_programs(0) + step]
    merged = merge_moments([column(state, k) for k in range(3)], live, mean, spread, CELLS_TWO)
    state[...] = column_tile(merged)

    @pl.when(step == pl.num_programs(0) - 1)
    def _():
        if final:
            turned = state[...].T
            spread_rows(row_tile([turned[1:2], turned[2:3], turned[0:1]], SENT), state_ref)
        else:
            state_ref[...] = state[...]


def middle_kernel(
    partners, me_ref, live_ref, heard_ref, vectors_ref, pool_a_ref, pool_b_ref, weights_ref, conv_ref, *refs
):
    piece_refs = refs[:partners]
    hidden_ref, conv_three_ref, norm_ref, levels_ref, sums_ref, columns, state, stack = refs[partners:]
    rows = C // partners
    step = pl.program_id(0)

    @pl.when(step == 0)
    def _():
        middle, factor, variance, extent = slice_norm(heard_ref)
        norm_ref[...] = row_tile([middle, factor, variance, extent])
        columns[...] = as_columns(row_tile([middle, row(vectors_ref, 0) * factor, row(vectors_ref, 1)]))
        state[...] = jnp.zeros_like(state)

    live = live_ref[step]
    ids = lane_ids(LANES_TWO)
    pre = (conv_ref[0] - column(columns, 0)) * column(columns, 1) + column(columns, 2)
    active = 0.5 * pre * (1.0 + gelu_tanh(pre))
    active_squares = jnp.sum(jnp.where(ids < CELLS_TWO, active * active, 0.0), axis=1, keepdims=True)
    split = halves(active)
    hidden = live * jnp.concatenate(
        [dot_halves(split[:, :1152], pool_a_ref), dot_halves(split[:, 896:], pool_b_ref)], axis=1
    )
    hidden_squares = jnp.sum(hidden * hidden, axis=1, keepdims=True)
    hidden_low = hidden.astype(BF16)
    hidden_ref[0] = hidden_low
    for partner in range(partners):
        piece_refs[partner][0] = hidden_ref[0, own_rows(me_ref[0], partner, rows), 0:CELLS_THREE]
    stack_sideways(hidden_low.astype(F32), HALF, LANES_THREE, stack)
    conv = conv_stacked(weights_ref, stack, HALF, LANES_THREE)
    conv_three_ref[0] = conv
    mean, spread = moments(conv, CELLS_THREE, LANES_THREE)
    merged = merge_moments([column(state, k) for k in range(3)], live, mean, spread, CELLS_THREE)
    state[...] = column_tile(
        [*merged, column(state, 3) + live * active_squares, column(state, 4) + hidden_squares]
    )

    @pl.when(step == pl.num_programs(0) - 1)
    def _():
        turned = state[...].T
        spread_rows(row_tile([turned[k : k + 1] for k in (1, 2, 0)], SENT), sums_ref)
        levels_ref[...] = row_tile([level_row([column(state, 3), column(state, 4)])])


def top_kernel(
    partners, me_ref, live_ref, heard_ref, own_ref, before_ref, vectors_ref, pool_ref, spread_ref, conv_ref, *refs
):
    target_refs = refs[:partners]
    piece_refs = refs[partners : 2 * partners]
    grad_ref, norm_ref, levels_ref, sums_ref, columns, target, output, totals = refs[2 * partners :]
    rows = C // partners
    step = pl.program_id(0)

    @pl.when(step == 0)
    def _():
        middle, factor, variance, extent = slice_norm(heard_ref)
        norm_ref[...] = row_tile([middle, factor, variance, extent])
        columns[...] = as_columns(row_tile([middle, factor] + [row(vectors_ref, k) for k in (2, 3, 4, 5)]))
        target[...] = jnp.zeros_like(target)
        totals[...] = jnp.zeros_like(totals)

    live = live_ref[step]
    for partner in range(partners):
        target[own_rows(me_ref[0], partner, rows), 0:CELLS_OUT] = target_refs[partner][0].astype(F32)
    ids = lane_ids(LANES_THREE)
    normed = (conv_ref[0] - column(columns, 0)) * column(columns, 1)
    scale = column(columns, 4)
    filmed = scale * (normed * column(columns, 2) + column(columns, 3)) + column(columns, 5)
    bend = gelu_tanh(filmed)
    active = 0.5 * filmed * (1.0 + bend)
    active_squares = live * jnp.sum(jnp.where(ids < CELLS_THREE, active * active, 0.0), axis=1, keepdims=True)
    pooled = live * dot_halves(halves(active), pool_ref)
    pooled_squares = jnp.sum(pooled * pooled, axis=1, keepdims=True)
    output[...] = pooled
    for partner in range(partners):
        piece_refs[partner][0] = output[own_rows(me_ref[0], partner, rows), 0:CELLS_OUT].astype(BF16)
    grad_active = live * jnp.dot(target[...].astype(BF16), spread_ref[...], preferred_element_type=F32)
    grad_filmed = grad_active * gelu_slope(filmed, bend)
    grad_ref[0] = scale * grad_filmed
    totals[...] += column_tile(
        [
            jnp.sum(grad_filmed, axis=1, keepdims=True),
            jnp.sum(grad_filmed * normed, axis=1, keepdims=True),
            active_squares,
            pooled_squares,
        ]
    )

    @pl.when(step == pl.num_programs(0) - 1)
    def _():
        turned = totals[...].T
        shift_sum, scale_sum = turned[0:1], turned[1:2]
        film_scale = row(vectors_ref, 4)
        slope = film_scale * row(vectors_ref, 2) * row(norm_ref, 1)
        offset = film_scale * row(vectors_ref, 3) + row(vectors_ref, 5)
        extent = own_ref[0, 2:3, :]
        away = own_ref[0, 0:1, :] - row(norm_ref, 0)
        filmed_squares = (
            slope * slope * (own_ref[0, 1:2, :] + extent * away * away)
            + 2.0 * slope * offset * extent * away
            + extent * offset * offset
        )
        spread_rows(
            row_tile([shift_sum, scale_sum, film_scale * shift_sum, film_scale * scale_sum], SENT), sums_ref
        )
        nothing = jnp.zeros((C, 1), F32)
        others = level_row([nothing, nothing, nothing, column(totals, 2), column(totals, 3)])
        lanes = lane_ids(C)
        filmed_total = jnp.sum(filmed_squares, axis=1, keepdims=True)
        levels_ref[...] = before_ref[...] + row_tile([others + jnp.where(lanes == 2, filmed_total, 0.0)])


def back_kernel(
    live_ref,
    heard_ref,
    norm_three_ref,
    norm_two_ref,
    levels_ref,
    vectors_ref,
    weights_ref,
    unpool_a_ref,
    unpool_b_ref,
    grad_ref,
    conv_three_ref,
    hidden_ref,
    conv_two_ref,
    out_ref,
    sums_ref,
    filter_ref,
    columns_three,
    columns_two,
    totals,
    stack,
    upright,
):
    step = pl.program_id(0)

    @pl.when(step == 0)
    def _():
        sums = jnp.sum(heard_ref[...], axis=0)
        extent = row(norm_three_ref, 3)
        factor = row(norm_three_ref, 1)
        columns_three[...] = as_columns(
            row_tile(
                [
                    row(norm_three_ref, 0),
                    factor,
                    row(vectors_ref, 2) * factor,
                    sums[2:3] / extent,
                    sums[3:4] / extent,
                ]
            )
        )
        columns_two[...] = as_columns(
            row_tile([row(norm_two_ref, 0), row(norm_two_ref, 1), row(vectors_ref, 0), row(vectors_ref, 1)])
        )
        totals[...] = jnp.zeros_like(totals)
        filter_ref[...] = jnp.zeros_like(filter_ref)

    live = live_ref[step]
    normed = (conv_three_ref[0] - column(columns_three, 0)) * column(columns_three, 1)
    error = grad_ref[0] - column(columns_three, 3) - normed * column(columns_three, 4)
    error = jnp.where(lane_ids(LANES_THREE) < CELLS_THREE, live * error * column(columns_three, 2), 0.0)
    stack_sideways(error, HALF, LANES_THREE, stack)
    stack_upright(hidden_ref[0].astype(F32), HALF, LANES_THREE, upright)
    filter_ref[...] += lax.dot_general(
        stack[...], upright[...], (((1,), (1,)), ((), ())), preferred_element_type=F32
    )
    split = halves(conv_stacked(weights_ref, stack, HALF, LANES_THREE))
    grad_active = jnp.concatenate(
        [dot_halves(split[:, :256], unpool_a_ref), dot_halves(split[:, 128:], unpool_b_ref)], axis=1
    )
    normed_two = (conv_two_ref[0] - column(columns_two, 0)) * column(columns_two, 1)
    pre = normed_two * column(columns_two, 2) + column(columns_two, 3)
    grad_pre = live * grad_active * gelu_slope(pre, gelu_tanh(pre))
    out_ref[0] = grad_pre
    totals[...] += column_tile(
        [jnp.sum(grad_pre, axis=1, keepdims=True), jnp.sum(grad_pre * normed_two, axis=1, keepdims=True)]
    )

    @pl.when(step == pl.num_programs(0) - 1)
    def _():
        turned = totals[...].T
        spread_rows(row_tile([turned[0:1], turned[1:2], levels_ref[0:1, :]], SENT), sums_ref)


def last_kernel(
    partners, part, me_ref, live_ref, heard_ref, norm_ref, vectors_ref, weights_ref, grad_ref, conv_ref, *refs
):
    map_refs = refs[:partners]
    refs = refs[partners:]
    if part:
        before_ref, refs = refs[0], refs[1:]
    piece_refs = refs[:partners]
    filter_ref, columns, maps, output, stack, upright = refs[partners:]
    rows = C // partners
    step = pl.program_id(0)

    @pl.when(step == 0)
    def _():
        sums = jnp.sum(heard_ref[...], axis=0)
        factor, extent = row(norm_ref, 1), row(norm_ref, 3)
        columns[...] = as_columns(
            row_tile([row(norm_ref, 0), factor, row(vectors_ref, 0) * factor, sums[0:1] / extent, sums[1:2] / extent])
        )
        maps[...] = jnp.zeros_like(maps)
        filter_ref[...] = before_ref[...] if part else jnp.zeros_like(filter_ref)

    for partner in range(partners):
        maps[own_rows(me_ref[0], partner, rows), 0:CELLS_TWO] = map_refs[partner][0].astype(F32)
    live = live_ref[part * pl.num_programs(0) + step]
    normed = (conv_ref[0] - column(columns, 0)) * column(columns, 1)
    error = grad_ref[0] - column(columns, 3) - normed * column(columns, 4)
    error = jnp.where(lane_ids(LANES_TWO) < CELLS_TWO, live * error * column(columns, 2), 0.0)
    stack_sideways(error, MAP, LANES_TWO, stack)
    output[...] = conv_stacked(weights_ref, stack, MAP, LANES_TWO)
    for partner in range(partners):
        piece_refs[partner][0] = output[own_rows(me_ref[0], partner, rows), 0:CELLS_TWO].astype(BF16)
    stack_upright(maps[...], MAP, LANES_TWO, upright)
    filter_ref[...] += lax.dot_general(
        stack[...], upright[...], (((1,), (1,)), ((), ())), preferred_element_type=F32
    )


def pool_matrix(side, width, out_width):
    half = side // 2
    matrix = np.zeros((width, out_width), np.float32)
    for row in range(2 * half):
        for column in range(2 * half):
            matrix[row * side + column, (row // 2) * half + column // 2] = 0.25
    return matrix


def smem():
    return pl.BlockSpec(memory_space=pltpu.SMEM)


def whole(*shape):
    return pl.BlockSpec(shape, lambda n: (0,) * len(shape))


def each(*shape, first=0):
    return pl.BlockSpec((1, *shape), lambda n: (first + n,) + (0,) * len(shape))


def pack(maps, me, partners, images_each, chunk):
    rows, slots, cells = maps.shape
    group = CAP // images_each
    parts = images_each // chunk
    pieces = []
    earlier = []
    for block in reversed(range(partners // group)):
        result = pl.pallas_call(
            functools.partial(pack_kernel, group, images_each, len(earlier)),
            grid_spec=pltpu.PrefetchScalarGridSpec(
                num_scalar_prefetch=1,
                grid=(1,),
                in_specs=[
                    pl.BlockSpec((rows, CAP, cells), lambda n, me_ref, block=block: (0, (me_ref[0] // group) ^ block, 0))
                ]
                + [pl.BlockSpec(memory_space=pl.ANY)] * len(earlier),
                out_specs=[pl.BlockSpec((chunk, rows, cells), lambda n, me_ref: (0, 0, 0))] * (group * parts),
            ),
            out_shape=[jax.ShapeDtypeStruct((chunk, rows, cells), maps.dtype)] * (group * parts),
            compiler_params=kernel_params(),
            name="pack",
        )(me, maps, *earlier)
        earlier = result[:1]
        pieces = [result[other * parts : (other + 1) * parts] for other in range(group)] + pieces
    return pieces


def unpack(pieces, me, images_each, dtype, earlier=None):
    partners = len(pieces)
    group = CAP // images_each
    chunk, rows, cells = pieces[0][0].shape
    slots = partners * images_each
    out = None
    for block in range(partners // group):
        given = [piece for other in range(group) for piece in pieces[block * group + other]]
        specs = [pl.BlockSpec((chunk, rows, cells), lambda n, me_ref: (0, 0, 0))] * len(given)
        aliases = {}
        count = len(given)
        extra = [array for array in (out, earlier) if array is not None]
        if out is not None:
            aliases = {1 + count: 0}
        given = given + extra
        specs = specs + [pl.BlockSpec(memory_space=pl.ANY)] * len(extra)
        out = pl.pallas_call(
            functools.partial(unpack_kernel, group, images_each, count),
            grid_spec=pltpu.PrefetchScalarGridSpec(
                num_scalar_prefetch=1,
                grid=(1,),
                in_specs=specs,
                out_specs=pl.BlockSpec(
                    (rows, CAP, cells), lambda n, me_ref, block=block: (0, (me_ref[0] // group) ^ block, 0)
                ),
            ),
            out_shape=jax.ShapeDtypeStruct((rows, slots, cells), dtype),
            input_output_aliases=aliases,
            compiler_params=kernel_params(),
            name="unpack",
        )(me, *given)
    return out


def local(
    images,
    counts,
    context,
    filter_two,
    gain_two,
    shift_two,
    filter_three,
    gain_three,
    shift_three,
    film_weight,
    film_bias,
    cotangent,
    *,
    partners,
    columns,
):
    devices = partners * columns
    rows, slots = images.shape[:2]
    images_each = slots // partners
    group = CAP // images_each
    chunk = CHUNK
    parts = images_each // chunk
    position = lax.axis_index("tensor")
    me = jnp.reshape(position, (1,)).astype(jnp.int32)

    def swap(value, partner):
        if partner == 0:
            return value
        return lax.ppermute(value, "tensor", [(i, i ^ partner) for i in range(partners)])

    def share(copies):
        return lax.all_to_all(copies, ("dp", "tensor"), 0, 0)

    def gather(value):
        shape = value.shape
        bit, axis = partners // 2, 0
        while bit:
            other = swap(value, bit)
            low = jnp.stack([value, other], axis)
            high = jnp.stack([other, value], axis)
            value = jnp.where((position & bit) == 0, low, high)
            bit, axis = bit // 2, axis + 1
        return value.reshape(partners, *shape)

    def after(value, earlier):
        return value + (earlier[(0,) * earlier.ndim] * 0.0).astype(value.dtype)

    sent = pack(images, me, partners, images_each, chunk)
    order = [partner for partner in range(partners) if partner]
    order.sort(key=lambda partner: -partner)
    maps = [[None] * parts for _ in range(partners)]
    for part in range(parts):
        for partner in [*order, 0]:
            maps[partner][part] = swap(sent[partner][part], partner)

    begun = sent[partners - 1][0]
    filter_two, filter_three = after(filter_two, begun), after(filter_three, begun)
    film_bias, film_weight, cotangent = after(film_bias, begun), after(film_weight, begun), after(cotangent, begun)
    gain_two, shift_two = after(gain_two, begun), after(shift_two, begun)
    gain_three, shift_three = after(gain_three, begun), after(shift_three, begun)

    def spread_filter(own):
        full = gather(jnp.transpose(own, (2, 0, 3, 1)).reshape(3, rows, 3 * C))
        ahead = jnp.transpose(full, (1, 0, 2, 3)).reshape(3 * C, 3 * C)
        behind = jnp.transpose(ahead.reshape(3, C, 3, C)[::-1, :, ::-1], (0, 3, 2, 1)).reshape(3 * C, 3 * C)
        return ahead, behind

    ahead_two, behind_two = spread_filter(filter_two)
    ahead_three, behind_three = spread_filter(filter_three)
    entries = film_weight.shape[0]
    small = jnp.concatenate(
        [
            jnp.stack([gain_two, shift_two, gain_three, shift_three]),
            film_bias,
            film_weight.reshape(2 * entries, rows),
        ]
    )
    small = jnp.transpose(gather(small), (1, 0, 2)).reshape(-1, C).astype(F32)
    gain_three, shift_three = small[2], small[3]
    film_b = small[4:6]
    film_w = small[6:].reshape(entries, 2, C)

    turned = jnp.transpose(cotangent, (1, 0, 2))
    targets = [
        swap(lax.dynamic_slice_in_dim(turned, (position ^ partner) * images_each, images_each, 0), partner)
        for partner in range(partners)
    ]

    task = position // group
    slot = (position % group) * images_each + jnp.arange(images_each, dtype=jnp.int32)
    limit = lax.dynamic_index_in_dim(counts, task, 0, keepdims=False)
    live = (slot < limit).astype(F32)
    own_context = lax.dynamic_index_in_dim(context, task, 0, keepdims=False)
    film_own = jnp.einsum("e,ekc->kc", own_context, film_w, precision=PRECISE) + film_b
    vectors = jnp.concatenate([small[:4], 1.0 + film_own[:1], film_own[1:], jnp.zeros((2, C), F32)])
    all_context = jnp.broadcast_to(after(context, begun)[None], (columns, *context.shape))
    all_context = lax.all_to_all(all_context, "dp", 0, 0).reshape(-1, entries)

    conv_two = state = None
    for part in range(parts):
        given = [maps[partner][part] for partner in range(partners)]
        specs = [each(rows, CELLS_TWO)] * partners
        aliases = {}
        final = part == parts - 1
        if part:
            aliases = {4 + partners: 0}
            given = given + [state, conv_two]
            specs = specs + [whole(C, C), pl.BlockSpec(memory_space=pl.ANY)]
        conv_two, state = pl.pallas_call(
            functools.partial(first_conv_kernel, partners, part, final),
            grid=(chunk,),
            in_specs=[smem(), smem(), whole(3 * C, 3 * C), *specs],
            out_specs=[
                each(C, LANES_TWO, first=part * chunk),
                whole(devices, SENT, C) if final else whole(C, C),
            ],
            out_shape=[
                jax.ShapeDtypeStruct((images_each, C, LANES_TWO), F32),
                jax.ShapeDtypeStruct((devices, SENT, C) if final else (C, C), F32),
            ],
            scratch_shapes=[
                pltpu.VMEM((C, LANES_TWO), F32),
                pltpu.VMEM((3 * C, LANES_TWO), BF16),
                pltpu.VMEM((C, C), F32),
            ],
            input_output_aliases=aliases,
            compiler_params=kernel_params(),
            name="first_conv",
        )(me, live, ahead_two, *given)
    heard_two = share(state)

    pool = pool_matrix(MAP, LANES_TWO, LANES_THREE)
    pool_out = pool_matrix(HALF, LANES_THREE, LANES_OUT)
    *block_pieces, hidden, conv_three, norm_two, levels, sums_three = pl.pallas_call(
        functools.partial(middle_kernel, partners),
        grid=(images_each,),
        in_specs=[
            smem(),
            smem(),
            whole(devices, SENT, C),
            whole(8, C),
            whole(1152, 256),
            whole(896, 256),
            whole(3 * C, 3 * C),
            each(C, LANES_TWO),
        ],
        out_specs=[each(rows, CELLS_THREE)] * partners
        + [each(C, LANES_THREE), each(C, LANES_THREE), whole(8, C), whole(8, C), whole(devices, SENT, C)],
        out_shape=[jax.ShapeDtypeStruct((images_each, rows, CELLS_THREE), BF16)] * partners
        + [
            jax.ShapeDtypeStruct((images_each, C, LANES_THREE), BF16),
            jax.ShapeDtypeStruct((images_each, C, LANES_THREE), F32),
            jax.ShapeDtypeStruct((8, C), F32),
            jax.ShapeDtypeStruct((8, C), F32),
            jax.ShapeDtypeStruct((devices, SENT, C), F32),
        ],
        scratch_shapes=[
            pltpu.VMEM((C, C), F32),
            pltpu.VMEM((C, C), F32),
            pltpu.VMEM((3 * C, LANES_THREE), BF16),
        ],
        compiler_params=kernel_params(),
        name="middle",
    )(
        me,
        live,
        heard_two,
        vectors,
        jnp.asarray(pool[:1152, :256], BF16),
        jnp.asarray(pool[896:, 256:], BF16),
        ahead_three,
        conv_two,
    )
    heard_three = share(sums_three)

    *out_pieces, grad_three, norm_three, levels, sums_top = pl.pallas_call(
        functools.partial(top_kernel, partners),
        grid=(images_each,),
        in_specs=[
            smem(),
            smem(),
            whole(devices, SENT, C),
            whole(1, SENT, C),
            whole(8, C),
            whole(8, C),
            whole(LANES_THREE, LANES_OUT),
            whole(LANES_OUT, LANES_THREE),
            each(C, LANES_THREE),
            *[each(rows, CELLS_OUT)] * partners,
        ],
        out_specs=[each(rows, CELLS_OUT)] * partners
        + [each(C, LANES_THREE), whole(8, C), whole(8, C), whole(devices, SENT, C)],
        out_shape=[jax.ShapeDtypeStruct((images_each, rows, CELLS_OUT), BF16)] * partners
        + [
            jax.ShapeDtypeStruct((images_each, C, LANES_THREE), F32),
            jax.ShapeDtypeStruct((8, C), F32),
            jax.ShapeDtypeStruct((8, C), F32),
            jax.ShapeDtypeStruct((devices, SENT, C), F32),
        ],
        scratch_shapes=[
            pltpu.VMEM((C, C), F32),
            pltpu.VMEM((C, LANES_OUT), F32),
            pltpu.VMEM((C, LANES_OUT), F32),
            pltpu.VMEM((C, C), F32),
        ],
        compiler_params=kernel_params(),
        name="top",
    )(
        me,
        live,
        heard_three,
        sums_three,
        levels,
        vectors,
        jnp.asarray(pool_out, BF16),
        jnp.asarray(pool_out.T, BF16),
        conv_three,
        *targets,
    )
    heard_top = share(sums_top)

    grad_two, sums_two, filter_sum_three = pl.pallas_call(
        back_kernel,
        grid=(images_each,),
        in_specs=[
            smem(),
            whole(devices, SENT, C),
            whole(8, C),
            whole(8, C),
            whole(8, C),
            whole(8, C),
            whole(3 * C, 3 * C),
            whole(256, 896),
            whole(384, 896),
            each(C, LANES_THREE),
            each(C, LANES_THREE),
            each(C, LANES_THREE),
            each(C, LANES_TWO),
        ],
        out_specs=[each(C, LANES_TWO), whole(devices, SENT, C), whole(3 * C, 3 * C)],
        out_shape=[
            jax.ShapeDtypeStruct((images_each, C, LANES_TWO), F32),
            jax.ShapeDtypeStruct((devices, SENT, C), F32),
            jax.ShapeDtypeStruct((3 * C, 3 * C), F32),
        ],
        scratch_shapes=[
            pltpu.VMEM((C, C), F32),
            pltpu.VMEM((C, C), F32),
            pltpu.VMEM((C, C), F32),
            pltpu.VMEM((3 * C, LANES_THREE), BF16),
            pltpu.VMEM((3 * C, LANES_THREE), BF16),
        ],
        compiler_params=kernel_params(),
        name="back",
    )(
        live,
        heard_top,
        norm_three,
        norm_two,
        levels,
        vectors,
        behind_three,
        jnp.asarray(pool[:896, :256].T, BF16),
        jnp.asarray(pool[896:, 128:].T, BF16),
        grad_three,
        conv_three,
        hidden,
        conv_two,
    )
    heard_back = share(sums_two)

    returned = [[None] * parts for _ in range(partners)]
    filter_sum_two = None
    for part in range(parts):
        given = [maps[partner][part] for partner in range(partners)]
        specs = [each(rows, CELLS_TWO)] * partners
        if part:
            given = given + [filter_sum_two]
            specs = specs + [whole(3 * C, 3 * C)]
        *pieces, filter_sum_two = pl.pallas_call(
            functools.partial(last_kernel, partners, part),
            grid=(chunk,),
            in_specs=[
                smem(),
                smem(),
                whole(devices, SENT, C),
                whole(8, C),
                whole(8, C),
                whole(3 * C, 3 * C),
                each(C, LANES_TWO, first=part * chunk),
                each(C, LANES_TWO, first=part * chunk),
                *specs,
            ],
            out_specs=[each(rows, CELLS_TWO)] * partners + [whole(3 * C, 3 * C)],
            out_shape=[jax.ShapeDtypeStruct((chunk, rows, CELLS_TWO), BF16)] * partners
            + [jax.ShapeDtypeStruct((3 * C, 3 * C), F32)],
            scratch_shapes=[
                pltpu.VMEM((C, C), F32),
                pltpu.VMEM((C, LANES_TWO), F32),
                pltpu.VMEM((C, LANES_TWO), F32),
                pltpu.VMEM((3 * C, LANES_TWO), BF16),
                pltpu.VMEM((3 * C, LANES_TWO), BF16),
            ],
            compiler_params=kernel_params(),
            name="last",
        )(me, live, heard_back, norm_two, vectors, behind_two, grad_two, conv_two, *given)
        for partner in [*order, 0]:
            returned[partner][part] = swap(pieces[partner], partner)
    grad_images = unpack(returned, me, images_each, F32)

    ended = pieces[0]
    block_two = unpack([[swap(block_pieces[k], k)] for k in range(partners)], me, images_each, BF16, ended)
    block_three = unpack([[swap(out_pieces[k], k)] for k in range(partners)], me, images_each, BF16, ended)

    both = jnp.stack([filter_sum_two, after(filter_sum_three, ended)])
    strip = 6 * rows // columns
    split = jnp.transpose(both.reshape(2, 3, partners, rows, 3 * C), (2, 0, 1, 3, 4))
    split = jnp.transpose(split.reshape(partners, columns, strip, 3 * C), (1, 0, 2, 3))
    strips = jnp.sum(share(split.reshape(devices, strip, 3 * C)), axis=0)
    strips = lax.all_to_all(jnp.broadcast_to(strips[None], (columns, *strips.shape)), "dp", 0, 0)
    strips = strips.reshape(2, 3, rows, 3, C)
    grad_filters = jnp.transpose(jnp.stack([strips[:, 2], strips[:, 1], strips[:, 0]], 1), (0, 2, 4, 3, 1))

    def own(vector):
        return lax.dynamic_slice_in_dim(vector, position * rows, rows, vector.ndim - 1)

    tasks = devices // group
    heard_top, heard_back = after(heard_top, ended), after(heard_back, ended)
    norm_two, norm_three = after(norm_two, ended), after(norm_three, ended)
    by_task = jnp.sum(heard_top[:, :2].reshape(tasks, group, 2, C), axis=1)
    grad_film = jnp.stack([gain_three * by_task[:, 1] + shift_three * by_task[:, 0], by_task[:, 0]], axis=1)
    grad_film_own = own(grad_film)
    grad_film_w = jnp.einsum("te,tkc->ekc", all_context, grad_film_own, precision=PRECISE)
    grad_film_b = jnp.sum(grad_film_own, axis=0)
    here = lax.dynamic_slice_in_dim(grad_film, lax.axis_index("dp") * counts.shape[0], counts.shape[0], 0)
    grad_context = jnp.einsum("tkc,ekc->te", here, film_w, precision=PRECISE)

    def normed_squares(gain, shift, variance, factor):
        return jnp.mean(gain * gain * variance * factor * factor + shift * shift)

    live_total = norm_two[3, 0] / CELLS_TWO
    base = live_total * C
    levels = jnp.sum(heard_back[:, 2], axis=0)
    means = jnp.stack(
        [
            jnp.mean(norm_two[2] + norm_two[0] * norm_two[0]),
            normed_squares(small[0], small[1], norm_two[2], norm_two[1]),
            levels[0] / (base * CELLS_TWO),
            levels[1] / (base * CELLS_THREE),
            jnp.mean(norm_three[2] + norm_three[0] * norm_three[0]),
            normed_squares(gain_three, shift_three, norm_three[2], norm_three[1]),
            levels[2] / (base * CELLS_THREE),
            levels[3] / (base * CELLS_THREE),
            levels[4] / (base * CELLS_OUT),
        ]
    )
    norm_sums = own(jnp.concatenate([jnp.sum(heard_back, axis=0)[:2], jnp.sum(heard_top, axis=0)[2:4]]))
    return (
        block_two,
        block_three,
        grad_images,
        grad_filters[0],
        norm_sums[1],
        norm_sums[0],
        grad_filters[1],
        norm_sums[3],
        norm_sums[2],
        grad_film_w,
        grad_film_b,
        grad_context,
        jnp.sqrt(means),
    )


def solution(mesh):
    step = functools.partial(local, partners=mesh.shape["tensor"], columns=mesh.shape["dp"])
    placed = (
        P("tensor", "dp", None),
        P("dp"),
        P("dp", None),
        P("tensor", None, None, None),
        P("tensor"),
        P("tensor"),
        P("tensor", None, None, None),
        P("tensor"),
        P("tensor"),
        P(None, None, "tensor"),
        P(None, "tensor"),
        P("tensor", "dp", None),
    )
    return jax.shard_map(
        step,
        mesh=mesh,
        in_specs=placed,
        out_specs=(
            P("tensor", "dp", None),
            P("tensor", "dp", None),
            P("tensor", "dp", None),
            P("tensor", None, None, None),
            P("tensor"),
            P("tensor"),
            P("tensor", None, None, None),
            P("tensor"),
            P("tensor"),
            P(None, None, "tensor"),
            P(None, "tensor"),
            P("dp", None),
            P(),
        ),
        check_vma=False,
    )
```

time: 1450 us -> 298 us (0.21)
  waiting for transfers between devices: 692 us -> 68.8 us
  local copies, waits for them, and re-layouts: 254 us -> 25.6 us
  blocking collectives: 191 us -> 0 us
  other arithmetic: 169 us -> 11.6 us
  Pallas kernels: 0 us -> 122 us
  matrix products: 121 us -> 1.79 us
  starting transfers between devices: 0.37 us -> 55.1 us
    reduce_scatter x1 -> x0, waiting for transfers between devices: 480 us -> none  [narrow(): return lax.psum_scatter(values, 'tensor', scatter_dimension=0, tiled=True)]
    psum x8 -> x0, blocking collectives: 191 us -> none  [the longest x2 57.6 us: back_sum(): return lax.psum(parts, 'dp')]
    all_gather x2 -> x0, waiting for transfers between devices: 123 us -> none  [widen(): return lax.all_gather(values, 'tensor', axis=0, tiled=True)]
    pallas_call x0 -> x19, Pallas kernels: none -> 122 us  [the longest x4 29.6 us: local(): pl.pallas_call(functools.partial(last_kernel, partners, part), grid=(chun...]
    reduce_sum x9, other arithmetic: 102 us -> 2.78 us  [the longest x2 1.29 us: normed_squares(): return jnp.mean(gain * gain * variance * factor * factor + shift * shift)]
    conv_general_dilated x4 -> x0, matrix products: 85.7 us -> none  [the longest x2 52.5 us: conv_apply(): lax.conv_general_dilated(inputs, filters, (1, 1), ((1, 1), (1, 1)), dimen...]
    conv_general_dilated x1 -> x0, local copies, waits for them, and re-layouts: 68.1 us -> none  [input_grad(): lax.conv_general_dilated(errors, filters[:, :, ::-1, ::-1], (1, 1), ((1,...]
    unnamed x52 -> x108, local copies, waits for them, and re-layouts: 73 us -> 5.56 us
  transfers between devices with their start and end apart: 5 -> 46, of which waited for: 5 -> 13; matrix products, arithmetic and copies ran while one was open for 8% -> 10% of each run, Pallas kernels for 0% -> 14%
where the time goes in v1:
time: 298 us; the launch traced here: 296 us
  Pallas kernels  122 us (41%)
  waiting for transfers between devices  68.8 us (23%)
  starting transfers between devices  55.1 us (18%)
  local copies, waits for them, and re-layouts  25.6 us (9%)
  other arithmetic  11.6 us (4%)
  between operations  10.8 us (4%)
    all_to_all x5, waiting for transfers between devices, share(): return lax.all_to_all(copies, ('dp', 'tensor'), 0, 0)  35.3 us
    ppermute x39, waiting for transfers between devices, swap(): lax.ppermute(value, 'tensor', [(i, i ^ partner) for i in range(partners)])  33.6 us
    pallas_call x4, Pallas kernels, local(): pl.pallas_call(functools.partial(last_kernel, partners, part), grid=(chun...  29.6 us
    ppermute x39, starting transfers between devices, swap(): lax.ppermute(value, 'tensor', [(i, i ^ partner) for i in range(partners)])  27.3 us
    pallas_call x4, Pallas kernels, local(): pl.pallas_call(functools.partial(first_conv_kernel, partners, part, final...  22.3 us
    pallas_call x1, Pallas kernels, local(): pl.pallas_call(back_kernel, grid=(images_each,), in_specs=[smem(), whole(...  20.2 us
    pallas_call x1, Pallas kernels, local(): pl.pallas_call(functools.partial(middle_kernel, partners), grid=(images_e...  19.8 us
    all_to_all x5, starting transfers between devices, share(): return lax.all_to_all(copies, ('dp', 'tensor'), 0, 0)  18.2 us
  transfers between devices with their start and end apart: 46, of which 13 were waited for; matrix products, arithmetic and copies ran while one was open for 10% of the time, Pallas kernels for 14%

profile of v1, /device:TPU:0, one launch (start us, length us, event | category | flops | bytes accessed | tf_op | source)
XLA Modules:
  0.0 296.1 jit_solution(987038128015364501)
XLA Ops:
  0.7 3.4 %pack.2 = (bf16[2,32,1764]{2,1,0:T(8,128)(2,1)}, bf16[2,32,1764]{2,1,0:T(8,128)(2,1)}, bf16[2,32,1764]{2,1,0:T(8,128)(2,1)}, bf16[2,32,1764]{2,1,0:T(8,128)(2,1)...) custom-call(s32[1]{0:T(128)} %bitcast.me_ref, ...), custom_call_target="tpu_custom_call" | custom-call | tf_op jit(solution)/shard_map/pack/pallas_call | solution.py:463
  6.9 3.0 %collective-permute-start.14 = (bf16[206,32]{0,1:T(8,128)(2,1)S(1)}, bf16[206,32]{0,1:T(8,128)(2,1)S(1)}, u32[]{:S(2)}, u32[]{:S(2)}) collective-permute-start(bf16[206,32]{0,1:T(8,128)(2,1)S(1)} %concatenate.52), channel_id=1, source_target_pairs={{0,2},{1,3},{2,0},{3,1},{4,6},{5,7},{6,4},{7,5},{8,10},{9,11},{10,... | collective-permute-start | bytes 39560 | tf_op jit(solution)/shard_map/ppermute | solution.py:546
  19.3 3.3 %pack.3 = (bf16[2,32,1764]{2,1,0:T(8,128)(2,1)}, bf16[2,32,1764]{2,1,0:T(8,128)(2,1)}, bf16[2,32,1764]{2,1,0:T(8,128)(2,1)}, bf16[2,32,1764]{2,1,0:T(8,128)(2,1)...) custom-call(s32[1]{0:T(128)} %bitcast.me_ref, ...), custom_call_target="tpu_custom_call" | custom-call | tf_op jit(solution)/shard_map/pack/pallas_call | solution.py:463
  26.0 3.5 %collective-permute-done = bf16[3,32,384]{2,1,0:T(8,128)(2,1)} collective-permute-done((bf16[3,32,384]{2,1,0:T(8,128)(2,1)}, bf16[3,32,384]{2,1,0:T(8,128)(2,1)}, u32[]{:S(2)}, u32[]{:S(2)}) %collective-permute-start) | collective-permute-done | bytes 73760 | tf_op jit(solution)/shard_map/ppermute | solution.py:546
  36.1 12.4 %collective-permute-done.10.refs_3_ = bf16[2,32,1764]{2,1,0:T(8,128)(2,1)S(1)} collective-permute-done((bf16[2,32,1764]{2,1,0:T(8,128)(2,1)S(1)}, bf16[2,32,1764]{2,1,0:T(8,128)(2,1)S(1)}, u32[]{:S(2)}, u32[]{:S(2)}) %collective-permute-start.10) | collective-permute-done | bytes 225824 | tf_op jit(solution)/shard_map/ppermute | solution.py:546
  52.1 5.5 %first_conv.4 = (f32[8,128,1792]{2,1,0:T(8,128)}, f32[128,128]{1,0:T(8,128)}) custom-call(s32[1]{0:T(128)} %bitcast.me_ref, f32[8]{0:T(128)} %compare_convert_fusion.live_ref, bf16[384,384]{1,0:T(8,128)(2,1)} %bitcast.160, bf16[2,32,1764]{2,1,0:T(8,128)(2,1)} %get-tuple-element.91.refs_0_, bf16[2,32,1764]{2,1,0:T(8,128)(2,1)} %copy-done.9, ...), custom_call_target="tpu_custom_call" | custom-call | tf_op jit(solution)/shard_map/first_conv/pallas_call | solution.py:626
  57.6 5.6 %first_conv.5 = (f32[8,128,1792]{2,1,0:T(8,128)}, f32[128,128]{1,0:T(8,128)}) custom-call(s32[1]{0:T(128)} %bitcast.me_ref, f32[8]{0:T(128)} %compare_convert_fusion.live_ref, bf16[384,384]{1,0:T(8,128)(2,1)} %bitcast.161, bf16[2,32,1764]{2,1,0:T(8,128)(2,1)} %get-tuple-element.87.refs_0_, ...), custom_call_target="tpu_custom_call", output_to_operand_aliasing={{0}: (8, {})} | custom-call | tf_op jit(solution)/shard_map/first_conv/pallas_call | solution.py:626
  63.2 5.6 %first_conv.6 = (f32[8,128,1792]{2,1,0:T(8,128)}, f32[128,128]{1,0:T(8,128)}) custom-call(s32[1]{0:T(128)} %bitcast.me_ref, f32[8]{0:T(128)} %compare_convert_fusion.live_ref, bf16[384,384]{1,0:T(8,128)(2,1)} %bitcast.162, bf16[2,32,1764]{2,1,0:T(8,128)(2,1)} %get-tuple-element.83.refs_0_, ...), custom_call_target="tpu_custom_call", output_to_operand_aliasing={{0}: (8, {})} | custom-call | tf_op jit(solution)/shard_map/first_conv/pallas_call | solution.py:626
  68.8 5.7 %first_conv.7 = (f32[8,128,1792]{2,1,0:T(8,128)}, f32[32,4,128]{2,1,0:T(4,128)}) custom-call(s32[1]{0:T(128)} %bitcast.me_ref, f32[8]{0:T(128)} %compare_convert_fusion.live_ref, bf16[384,384]{1,0:T(8,128)(2,1)} %bitcast.163, bf16[2,32,1764]{2,1,0:T(8,128)(2,1)} %get-tuple-element.79.refs_0_, ...), custom_call_target="tpu_custom_call", output_to_operand_aliasing={{0}: (8, {})} | custom-call | tf_op jit(solution)/shard_map/first_conv/pallas_call | solution.py:626
  74.5 5.2 %all-to-all-start = ((f32[32,4,128]{2,1,0:T(4,128)}), f32[32,4,128]{2,1,0:T(4,128)S(1)}, u32[]{:S(2)}, u32[]{:S(2)}) async-start(f32[32,4,128]{2,1,0:T(4,128)} %get-tuple-element.99), calls=%async_computation | async-start | bytes 131072 | tf_op jit(solution)/shard_map/all_to_all | solution.py:549
  81.6 5.3 %all-to-all-done.heard_ref = f32[32,4,128]{2,1,0:T(4,128)S(1)} async-done(((f32[32,4,128]{2,1,0:T(4,128)}), f32[32,4,128]{2,1,0:T(4,128)S(1)}, u32[]{:S(2)}, u32[]{:S(2)}) %all-to-all-start) | async-done | bytes 65568 | tf_op jit(solution)/shard_map/all_to_all | solution.py:549
  87.5 19.8 %middle.1 = (bf16[8,32,441]{2,1,0:T(8,128)(2,1)}, bf16[8,32,441]{2,1,0:T(8,128)(2,1)}, bf16[8,32,441]{2,1,0:T(8,128)(2,1)}, bf16[8,32,441]{2,1,0:T(8,128)(2,1)},...) custom-call(s32[1]{0:T(128)} %bitcast.me_ref, ...), custom_call_target="tpu_custom_call" | custom-call | tf_op jit(solution)/shard_map/middle/pallas_call | solution.py:651
  107.3 2.7 all-to-all-start.1
  118.1 8.7 %top.1 = (bf16[8,32,100]{2,1,0:T(8,128)(2,1)}, bf16[8,32,100]{2,1,0:T(8,128)(2,1)}, bf16[8,32,100]{2,1,0:T(8,128)(2,1)}, bf16[8,32,100]{2,1,0:T(8,128)(2,1)}, f3...) custom-call(s32[1]{0:T(128)} %bitcast.me_ref, ...), custom_call_target="tpu_custom_call" | custom-call | tf_op jit(solution)/shard_map/top/pallas_call | solution.py:693
  126.8 4.9 %all-to-all-start.2 = ((f32[32,4,128]{2,1,0:T(4,128)}), f32[32,4,128]{2,1,0:T(4,128)S(1)}, u32[]{:S(2)}, u32[]{:S(2)}) async-start(f32[32,4,128]{2,1,0:T(4,128)} %get-tuple-element.108), calls=%async_computation.2 | async-start | bytes 131072 | tf_op jit(solution)/shard_map/all_to_all | solution.py:549
  134.7 4.5 %all-to-all-done.2.heard_ref = f32[32,4,128]{2,1,0:T(4,128)S(1)} async-done(((f32[32,4,128]{2,1,0:T(4,128)}), f32[32,4,128]{2,1,0:T(4,128)S(1)}, u32[]{:S(2)}, u32[]{:S(2)}) %all-to-all-start.2) | async-done | bytes 65568 | tf_op jit(solution)/shard_map/all_to_all | solution.py:549
  139.8 20.2 %back.1 = (f32[8,128,1792]{2,1,0:T(8,128)}, f32[32,4,128]{2,1,0:T(4,128)}, f32[384,384]{1,0:T(8,128)}) custom-call(f32[8]{0:T(128)} %compare_convert_fusion.live_ref, f32[32,4,128]{2,1,0:T(4,128)} %copy-done.10, f32[8,128]{1,0:T(8,128)} %get-tuple-element.109.norm_three_ref, f32[8,128]{1,0:T(8,128)} %get-tuple-element.110.norm_two_ref.norm_ref, ...), custom_call_target="tpu_custom_call" | custom-call | tf_op jit(solution)/shard_map/back/pallas_call | solution.py:739
  159.9 2.6 all-to-all-start.3
  165.5 4.5 %all-to-all-done.3.heard_ref = f32[32,4,128]{2,1,0:T(4,128)S(1)} async-done(((f32[32,4,128]{2,1,0:T(4,128)}), f32[32,4,128]{2,1,0:T(4,128)S(1)}, u32[]{:S(2)}, u32[]{:S(2)}) %all-to-all-start.3) | async-done | bytes 65568 | tf_op jit(solution)/shard_map/all_to_all | solution.py:549
  170.6 7.2 %last.4 = (bf16[2,32,1764]{2,1,0:T(8,128)(2,1)}, bf16[2,32,1764]{2,1,0:T(8,128)(2,1)}, bf16[2,32,1764]{2,1,0:T(8,128)(2,1)}, bf16[2,32,1764]{2,1,0:T(8,128)(2,1)}, f32[384,384]{1,0:T(8,128)}) custom-call(s32[1]{0:T(128)} %bitcast.me_ref, f32[8]{0:T(128)} %compare_convert_fusion.live_ref, f32[32,4,128]{2,1,0:T(4,128)} %copy-done.1, ...), custom_call_target="tpu_custom_call" | custom-call | tf_op jit(solution)/shard_map/last/pallas_call | solution.py:797
  177.8 7.5 %last.5 = (bf16[2,32,1764]{2,1,0:T(8,128)(2,1)}, bf16[2,32,1764]{2,1,0:T(8,128)(2,1)}, bf16[2,32,1764]{2,1,0:T(8,128)(2,1)}, bf16[2,32,1764]{2,1,0:T(8,128)(2,1)}, f32[384,384]{1,0:T(8,128)}) custom-call(s32[1]{0:T(128)} %bitcast.me_ref, f32[8]{0:T(128)} %compare_convert_fusion.live_ref, f32[32,4,128]{2,1,0:T(4,128)} %copy-done.1, ...), custom_call_target="tpu_custom_call" | custom-call | tf_op jit(solution)/shard_map/last/pallas_call | solution.py:797
  185.2 7.4 %last.6 = (bf16[2,32,1764]{2,1,0:T(8,128)(2,1)}, bf16[2,32,1764]{2,1,0:T(8,128)(2,1)}, bf16[2,32,1764]{2,1,0:T(8,128)(2,1)}, bf16[2,32,1764]{2,1,0:T(8,128)(2,1)}, f32[384,384]{1,0:T(8,128)}) custom-call(s32[1]{0:T(128)} %bitcast.me_ref, f32[8]{0:T(128)} %compare_convert_fusion.live_ref, f32[32,4,128]{2,1,0:T(4,128)} %copy-done.1, ...), custom_call_target="tpu_custom_call" | custom-call | tf_op jit(solution)/shard_map/last/pallas_call | solution.py:797
  192.7 7.5 %last.7 = (bf16[2,32,1764]{2,1,0:T(8,128)(2,1)}, bf16[2,32,1764]{2,1,0:T(8,128)(2,1)}, bf16[2,32,1764]{2,1,0:T(8,128)(2,1)}, bf16[2,32,1764]{2,1,0:T(8,128)(2,1)}, f32[384,384]{1,0:T(8,128)}) custom-call(s32[1]{0:T(128)} %bitcast.me_ref, f32[8]{0:T(128)} %compare_convert_fusion.live_ref, f32[32,4,128]{2,1,0:T(4,128)} %copy-done.1, ...), custom_call_target="tpu_custom_call" | custom-call | tf_op jit(solution)/shard_map/last/pallas_call | solution.py:797
  204.6 2.8 all-to-all-start.4
  215.8 20.6 %all-to-all-done.4 = f32[32,24,384]{2,1,0:T(8,128)S(1)} async-done(((f32[32,24,384]{2,1,0:T(8,128)}), f32[32,24,384]{2,1,0:T(8,128)S(1)}, u32[]{:S(2)}, u32[]{:S(2)}) %all-to-all-start.4) | async-done | bytes 1179680 | tf_op jit(solution)/shard_map/all_to_all | solution.py:549
  237.1 3.5 %all-to-all-start.6 = ((f32[8,2,100]{2,1,0:T(2,128)}), f32[8,2,100]{2,1,0:T(2,128)S(1)}, u32[]{:S(2)}, u32[]{:S(2)}) async-start(f32[8,2,100]{2,1,0:T(2,128)} %broadcast_in_dim.8), calls=%async_computation.6 | async-start | bytes 16384 | tf_op jit(solution)/shard_map/all_to_all | solution.py:614
  251.7 6.0 %all-to-all-start.5 = ((f32[8,24,384]{2,1,0:T(8,128)}), f32[8,24,384]{2,1,0:T(8,128)S(1)}, u32[]{:S(2)}, u32[]{:S(2)}) async-start(f32[8,24,384]{2,1,0:T(8,128)} %broadcast_in_dim.7), calls=%async_computation.5 | async-start | bytes 589824 | tf_op jit(solution)/shard_map/all_to_all | solution.py:837
  262.4 4.3 %collective-permute-done.29.refs_2_ = bf16[2,32,1764]{2,1,0:T(8,128)(2,1)} collective-permute-done((bf16[2,32,1764]{2,1,0:T(8,128)(2,1)}, bf16[2,32,1764]{2,1,0:T(8,128)(2,1)}, u32[]{:S(2)}, u32[]{:S(2)}) %collective-permute-start.29) | collective-permute-done | bytes 225824 | tf_op jit(solution)/shard_map/ppermute | solution.py:546
  278.3 4.0 %unpack.10.refs_8_ = f32[32,32,1764]{2,1,0:T(8,128)} custom-call(s32[1]{0:T(128)} %bitcast.me_ref, bf16[2,32,1764]{2,1,0:T(8,128)(2,1)} %get-tuple-element.132.refs_0_, bf16[2,32,1764]{2,1,0:T(8,128)(2,1)} %get-tuple-element.133.refs_1_, bf16[2,32,1764]{2,1,0:T(8,128)(2,1)} %get-tuple-element.134.refs_2_, ...), custom_call_target="tpu_custom_call" | custom-call | tf_op jit(solution)/shard_map/unpack/pallas_call | solution.py:499
  282.3 4.1 %collective-permute-done.27.refs_0_ = bf16[2,32,1764]{2,1,0:T(8,128)(2,1)} collective-permute-done((bf16[2,32,1764]{2,1,0:T(8,128)(2,1)}, bf16[2,32,1764]{2,1,0:T(8,128)(2,1)}, u32[]{:S(2)}, u32[]{:S(2)}) %collective-permute-start.27) | collective-permute-done | bytes 225824 | tf_op jit(solution)/shard_map/ppermute | solution.py:546
  286.4 4.0 %collective-permute-done.31.refs_4_ = bf16[2,32,1764]{2,1,0:T(8,128)(2,1)} collective-permute-done((bf16[2,32,1764]{2,1,0:T(8,128)(2,1)}, bf16[2,32,1764]{2,1,0:T(8,128)(2,1)}, u32[]{:S(2)}, u32[]{:S(2)}) %collective-permute-start.31) | collective-permute-done | bytes 225824 | tf_op jit(solution)/shard_map/ppermute | solution.py:546
  290.4 4.0 %unpack.11 = f32[32,32,1764]{2,1,0:T(8,128)} custom-call(s32[1]{0:T(128)} %bitcast.me_ref, bf16[2,32,1764]{2,1,0:T(8,128)(2,1)} %collective-permute-done.27.refs_0_, bf16[2,32,1764]{2,1,0:T(8,128)(2,1)} %collective-permute-done.28.refs_1_, bf16[2,32,1764]{2,1,0:T(8,128)(2,1)} %collective-permute-done.29.refs_2_, ...), custom_call_target="tpu_custom_call", output_to_operand_aliasing={{}: (9, {})} | custom-call | tf_op jit(solution)/shard_map/unpack/pallas_call | solution.py:499
  (286 shorter events, 76.3 us)
Async XLA Ops:
  6.9 15.8 %collective-permute-start.14 = (bf16[206,32]{0,1:T(8,128)(2,1)S(1)}, bf16[206,32]{0,1:T(8,128)(2,1)S(1)}, u32[]{:S(2)}, u32[]{:S(2)}) collective-permute-start(bf16[206,32]{0,1:T(8,128)(2,1)S(1)} %concatenate.52), channel_id=1, source_target_pairs={{0,2},{1,3},{2,0},{3,1},{4,6},{5,7},{6,4},{7,5},{8,10},{9,11},{10,... | collective-permute-start | bytes 39560 | tf_op jit(solution)/shard_map/ppermute | solution.py:546
  9.9 24.3 %collective-permute-start.6 = (bf16[2,32,1764]{2,1,0:T(8,128)(2,1)}, bf16[2,32,1764]{2,1,0:T(8,128)(2,1)S(1)}, u32[]{:S(2)}, u32[]{:S(2)}) collective-permute-start(bf16[2,32,1764]{2,1,0:T(8,128)(2,1)} %get-tuple-element.85), channel_id=1, source_target_pairs={{0,2},{1,3},{2,0},{3,1},{4,6},{5,7},{6,4},{7,5},{8,10},{9,11},{10,... | collective-permute-start | bytes 677384 | tf_op jit(solution)/shard_map/ppermute | solution.py:546
  10.0 24.3 %collective-permute-start.7 = (bf16[2,32,1764]{2,1,0:T(8,128)(2,1)}, bf16[2,32,1764]{2,1,0:T(8,128)(2,1)S(1)}, u32[]{:S(2)}, u32[]{:S(2)}) collective-permute-start(bf16[2,32,1764]{2,1,0:T(8,128)(2,1)} %get-tuple-element.86), channel_id=1, source_target_pairs={{0,3},{1,2},{2,1},{3,0},{4,7},{5,6},{6,5},{7,4},{8,11},{9,10},{10,... | collective-permute-start | bytes 677384 | tf_op jit(solution)/shard_map/ppermute | solution.py:546
  10.8 24.1 %collective-permute-start.9 = (bf16[2,32,1764]{2,1,0:T(8,128)(2,1)}, bf16[2,32,1764]{2,1,0:T(8,128)(2,1)}, u32[]{:S(2)}, u32[]{:S(2)}) collective-permute-start(bf16[2,32,1764]{2,1,0:T(8,128)(2,1)} %get-tuple-element.89), channel_id=1, source_target_pairs={{0,2},{1,3},{2,0},{3,1},{4,6},{5,7},{6,4},{7,5},{8,10},{9,11},{10,... | collective-permute-start | bytes 677384 | tf_op jit(solution)/shard_map/ppermute | solution.py:546
  12.7 16.9 %collective-permute-start = (bf16[3,32,384]{2,1,0:T(8,128)(2,1)}, bf16[3,32,384]{2,1,0:T(8,128)(2,1)}, u32[]{:S(2)}, u32[]{:S(2)}) collective-permute-start(bf16[3,32,384]{2,1,0:T(8,128)(2,1)} %bitcast.159), channel_id=1, source_target_pairs={{0,2},{1,3},{2,0},{3,1},{4,6},{5,7},{6,4},{7,5},{8,10},{9,11},{10,... | collective-permute-start | bytes 221192 | tf_op jit(solution)/shard_map/ppermute | solution.py:546
  31.3 17.7 %collective-permute-start.13 = (bf16[2,32,1764]{2,1,0:T(8,128)(2,1)S(1)}, bf16[2,32,1764]{2,1,0:T(8,128)(2,1)S(1)}, u32[]{:S(2)}, u32[]{:S(2)}) collective-permute-start(bf16[2,32,1764]{2,1,0:T(8,128)(2,1)S(1)} %copy-done.43), channel_id=1, source_target_pairs={{0,3},{1,2},{2,1},{3,0},{4,7},{5,6},{6,5},{7,4},{8,11},{9,10},{10,... | collective-permute-start | bytes 677384 | tf_op jit(solution)/shard_map/ppermute | solution.py:546
  32.7 17.6 %collective-permute-start.12 = (bf16[2,32,1764]{2,1,0:T(8,128)(2,1)S(1)}, bf16[2,32,1764]{2,1,0:T(8,128)(2,1)S(1)}, u32[]{:S(2)}, u32[]{:S(2)}) collective-permute-start(bf16[2,32,1764]{2,1,0:T(8,128)(2,1)S(1)} %copy-done.22), channel_id=1, source_target_pairs={{0,2},{1,3},{2,0},{3,1},{4,6},{5,7},{6,4},{7,5},{8,10},{9,11},{10,... | collective-permute-start | bytes 677384 | tf_op jit(solution)/shard_map/ppermute | solution.py:546
  34.2 14.3 %collective-permute-start.10 = (bf16[2,32,1764]{2,1,0:T(8,128)(2,1)S(1)}, bf16[2,32,1764]{2,1,0:T(8,128)(2,1)S(1)}, u32[]{:S(2)}, u32[]{:S(2)}) collective-permute-start(bf16[2,32,1764]{2,1,0:T(8,128)(2,1)S(1)} %copy-done.44), channel_id=1, source_target_pairs={{0,3},{1,2},{2,1},{3,0},{4,7},{5,6},{6,5},{7,4},{8,11},{9,10},{10,... | collective-permute-start | bytes 677384 | tf_op jit(solution)/shard_map/ppermute | solution.py:546
  34.3 16.3 %collective-permute-start.8 = (bf16[2,32,1764]{2,1,0:T(8,128)(2,1)S(1)}, bf16[2,32,1764]{2,1,0:T(8,128)(2,1)S(1)}, u32[]{:S(2)}, u32[]{:S(2)}) collective-permute-start(bf16[2,32,1764]{2,1,0:T(8,128)(2,1)S(1)} %copy-done.46), channel_id=1, source_target_pairs={{0,1},{1,0},{2,3},{3,2},{4,5},{5,4},{6,7},{7,6},{8,9},{9,8},{10,11... | collective-permute-start | bytes 677384 | tf_op jit(solution)/shard_map/ppermute | solution.py:546
  35.0 15.8 %collective-permute-start.11 = (bf16[2,32,1764]{2,1,0:T(8,128)(2,1)S(1)}, bf16[2,32,1764]{2,1,0:T(8,128)(2,1)S(1)}, u32[]{:S(2)}, u32[]{:S(2)}) collective-permute-start(bf16[2,32,1764]{2,1,0:T(8,128)(2,1)S(1)} %copy-done.45), channel_id=1, source_target_pairs={{0,1},{1,0},{2,3},{3,2},{4,5},{5,4},{6,7},{7,6},{8,9},{9,8},{10,11... | collective-permute-start | bytes 677384 | tf_op jit(solution)/shard_map/ppermute | solution.py:546
  48.5 20.3 %collective-permute-start.3 = (bf16[2,32,1764]{2,1,0:T(8,128)(2,1)}, bf16[2,32,1764]{2,1,0:T(8,128)(2,1)}, u32[]{:S(2)}, u32[]{:S(2)}) collective-permute-start(bf16[2,32,1764]{2,1,0:T(8,128)(2,1)} %get-tuple-element.81), channel_id=1, source_target_pairs={{0,2},{1,3},{2,0},{3,1},{4,6},{5,7},{6,4},{7,5},{8,10},{9,11},{10,... | collective-permute-start | bytes 677384 | tf_op jit(solution)/shard_map/ppermute | solution.py:546
  49.0 19.8 %collective-permute-start.4 = (bf16[2,32,1764]{2,1,0:T(8,128)(2,1)}, bf16[2,32,1764]{2,1,0:T(8,128)(2,1)}, u32[]{:S(2)}, u32[]{:S(2)}) collective-permute-start(bf16[2,32,1764]{2,1,0:T(8,128)(2,1)} %get-tuple-element.82), channel_id=1, source_target_pairs={{0,3},{1,2},{2,1},{3,0},{4,7},{5,6},{6,5},{7,4},{8,11},{9,10},{10,... | collective-permute-start | bytes 677384 | tf_op jit(solution)/shard_map/ppermute | solution.py:546
  50.3 18.5 %collective-permute-start.2 = (bf16[2,32,1764]{2,1,0:T(8,128)(2,1)}, bf16[2,32,1764]{2,1,0:T(8,128)(2,1)}, u32[]{:S(2)}, u32[]{:S(2)}) collective-permute-start(bf16[2,32,1764]{2,1,0:T(8,128)(2,1)} %get-tuple-element.80), channel_id=1, source_target_pairs={{0,1},{1,0},{2,3},{3,2},{4,5},{5,4},{6,7},{7,6},{8,9},{9,8},{10,11... | collective-permute-start | bytes 677384 | tf_op jit(solution)/shard_map/ppermute | solution.py:546
  50.6 12.6 %collective-permute-start.5 = (bf16[2,32,1764]{2,1,0:T(8,128)(2,1)}, bf16[2,32,1764]{2,1,0:T(8,128)(2,1)}, u32[]{:S(2)}, u32[]{:S(2)}) collective-permute-start(bf16[2,32,1764]{2,1,0:T(8,128)(2,1)} %get-tuple-element.84), channel_id=1, source_target_pairs={{0,1},{1,0},{2,3},{3,2},{4,5},{5,4},{6,7},{7,6},{8,9},{9,8},{10,11... | collective-permute-start | bytes 677384 | tf_op jit(solution)/shard_map/ppermute | solution.py:546
  50.8 28.9 %collective-permute-start.17 = (bf16[2,3,32,384]{3,2,1,0:T(8,128)(2,1)}, bf16[2,3,32,384]{3,2,1,0:T(8,128)(2,1)}, u32[]{:S(2)}, u32[]{:S(2)}) collective-permute-start(bf16[2,3,32,384]{3,2,1,0:T(8,128)(2,1)} %maximum_select_fusion.4), channel_id=1, source_target_pairs={{0,1},{1,0},{2,3},{3,2},{4,5},{5,4},{6,7},{7,6},{8,9},{9,8},{10,11... | collective-permute-start | bytes 442376 | tf_op jit(solution)/shard_map/ppermute | solution.py:546
  74.5 12.4 %all-to-all-start = ((f32[32,4,128]{2,1,0:T(4,128)}), f32[32,4,128]{2,1,0:T(4,128)S(1)}, u32[]{:S(2)}, u32[]{:S(2)}) async-start(f32[32,4,128]{2,1,0:T(4,128)} %get-tuple-element.99), calls=%async_computation | async-start | bytes 131072 | tf_op jit(solution)/shard_map/all_to_all | solution.py:549
  204.6 31.8 %all-to-all-start.4 = ((f32[32,24,384]{2,1,0:T(8,128)}), f32[32,24,384]{2,1,0:T(8,128)S(1)}, u32[]{:S(2)}, u32[]{:S(2)}) async-start(f32[32,24,384]{2,1,0:T(8,128)} %bitcast.50), calls=%async_computation.4 | async-start | bytes 2359296 | tf_op jit(solution)/shard_map/all_to_all | solution.py:549
  208.4 49.4 %collective-permute-start.18 = (bf16[8,32,441]{2,1,0:T(8,128)(2,1)S(1)}, bf16[8,32,441]{2,1,0:T(8,128)(2,1)S(1)}, u32[]{:S(2)}, u32[]{:S(2)}) collective-permute-start(bf16[8,32,441]{2,1,0:T(8,128)(2,1)S(1)} %copy-done.41), channel_id=1, source_target_pairs={{0,2},{1,3},{2,0},{3,1},{4,6},{5,7},{6,4},{7,5},{8,10},{9,11},{10,... | collective-permute-start | bytes 677384 | tf_op jit(solution)/shard_map/ppermute | solution.py:546
  210.1 47.8 %collective-permute-start.19 = (bf16[8,32,441]{2,1,0:T(8,128)(2,1)S(1)}, bf16[8,32,441]{2,1,0:T(8,128)(2,1)S(1)}, u32[]{:S(2)}, u32[]{:S(2)}) collective-permute-start(bf16[8,32,441]{2,1,0:T(8,128)(2,1)S(1)} %copy-done.40), channel_id=1, source_target_pairs={{0,3},{1,2},{2,1},{3,0},{4,7},{5,6},{6,5},{7,4},{8,11},{9,10},{10,... | collective-permute-start | bytes 677384 | tf_op jit(solution)/shard_map/ppermute | solution.py:546
  210.1 30.5 %collective-permute-start.24 = (bf16[8,32,100]{2,1,0:T(8,128)(2,1)S(1)}, bf16[8,32,100]{2,1,0:T(8,128)(2,1)S(1)}, u32[]{:S(2)}, u32[]{:S(2)}) collective-permute-start(bf16[8,32,100]{2,1,0:T(8,128)(2,1)S(1)} %copy-done.49), channel_id=1, source_target_pairs={{0,2},{1,3},{2,0},{3,1},{4,6},{5,7},{6,4},{7,5},{8,10},{9,11},{10,... | collective-permute-start | bytes 153608 | tf_op jit(solution)/shard_map/ppermute | solution.py:546
  211.6 29.1 %collective-permute-start.25 = (bf16[8,32,100]{2,1,0:T(8,128)(2,1)S(1)}, bf16[8,32,100]{2,1,0:T(8,128)(2,1)S(1)}, u32[]{:S(2)}, u32[]{:S(2)}) collective-permute-start(bf16[8,32,100]{2,1,0:T(8,128)(2,1)S(1)} %copy-done.48), channel_id=1, source_target_pairs={{0,3},{1,2},{2,1},{3,0},{4,7},{5,6},{6,5},{7,4},{8,11},{9,10},{10,... | collective-permute-start | bytes 153608 | tf_op jit(solution)/shard_map/ppermute | solution.py:546
  212.0 30.3 %collective-permute-start.26 = (bf16[8,32,100]{2,1,0:T(8,128)(2,1)S(1)}, bf16[8,32,100]{2,1,0:T(8,128)(2,1)S(1)}, u32[]{:S(2)}, u32[]{:S(2)}) collective-permute-start(bf16[8,32,100]{2,1,0:T(8,128)(2,1)S(1)} %copy-done.47), channel_id=1, source_target_pairs={{0,1},{1,0},{2,3},{3,2},{4,5},{5,4},{6,7},{7,6},{8,9},{9,8},{10,11... | collective-permute-start | bytes 153608 | tf_op jit(solution)/shard_map/ppermute | solution.py:546
  237.1 13.9 %all-to-all-start.6 = ((f32[8,2,100]{2,1,0:T(2,128)}), f32[8,2,100]{2,1,0:T(2,128)S(1)}, u32[]{:S(2)}, u32[]{:S(2)}) async-start(f32[8,2,100]{2,1,0:T(2,128)} %broadcast_in_dim.8), calls=%async_computation.6 | async-start | bytes 16384 | tf_op jit(solution)/shard_map/all_to_all | solution.py:614
  240.6 18.9 %collective-permute-start.20 = (bf16[8,32,441]{2,1,0:T(8,128)(2,1)S(1)}, bf16[8,32,441]{2,1,0:T(8,128)(2,1)}, u32[]{:S(2)}, u32[]{:S(2)}) collective-permute-start(bf16[8,32,441]{2,1,0:T(8,128)(2,1)S(1)} %copy-done.39), channel_id=1, source_target_pairs={{0,1},{1,0},{2,3},{3,2},{4,5},{5,4},{6,7},{7,6},{8,9},{9,8},{10,11... | collective-permute-start | bytes 677384 | tf_op jit(solution)/shard_map/ppermute | solution.py:546
  240.7 18.9 %collective-permute-start.30 = (bf16[2,32,1764]{2,1,0:T(8,128)(2,1)}, bf16[2,32,1764]{2,1,0:T(8,128)(2,1)}, u32[]{:S(2)}, u32[]{:S(2)}) collective-permute-start(bf16[2,32,1764]{2,1,0:T(8,128)(2,1)} %get-tuple-element.127), channel_id=1, source_target_pairs={{0,2},{1,3},{2,0},{3,1},{4,6},{5,7},{6,4},{7,5},{8,10},{9,11},{10,... | collective-permute-start | bytes 677384 | tf_op jit(solution)/shard_map/ppermute | solution.py:546
  242.2 17.7 %collective-permute-start.34 = (bf16[2,32,1764]{2,1,0:T(8,128)(2,1)}, bf16[2,32,1764]{2,1,0:T(8,128)(2,1)}, u32[]{:S(2)}, u32[]{:S(2)}) collective-permute-start(bf16[2,32,1764]{2,1,0:T(8,128)(2,1)} %get-tuple-element.131), channel_id=1, source_target_pairs={{0,3},{1,2},{2,1},{3,0},{4,7},{5,6},{6,5},{7,4},{8,11},{9,10},{10,... | collective-permute-start | bytes 677384 | tf_op jit(solution)/shard_map/ppermute | solution.py:546
  251.7 42.6 %all-to-all-start.5 = ((f32[8,24,384]{2,1,0:T(8,128)}), f32[8,24,384]{2,1,0:T(8,128)S(1)}, u32[]{:S(2)}, u32[]{:S(2)}) async-start(f32[8,24,384]{2,1,0:T(8,128)} %broadcast_in_dim.7), calls=%async_computation.5 | async-start | bytes 589824 | tf_op jit(solution)/shard_map/all_to_all | solution.py:837
  261.9 20.3 %collective-permute-start.33 = (bf16[2,32,1764]{2,1,0:T(8,128)(2,1)}, bf16[2,32,1764]{2,1,0:T(8,128)(2,1)}, u32[]{:S(2)}, u32[]{:S(2)}) collective-permute-start(bf16[2,32,1764]{2,1,0:T(8,128)(2,1)} %get-tuple-element.130), channel_id=1, source_target_pairs={{0,3},{1,2},{2,1},{3,0},{4,7},{5,6},{6,5},{7,4},{8,11},{9,10},{10,... | collective-permute-start | bytes 677384 | tf_op jit(solution)/shard_map/ppermute | solution.py:546
  266.7 15.6 %collective-permute-start.28 = (bf16[2,32,1764]{2,1,0:T(8,128)(2,1)}, bf16[2,32,1764]{2,1,0:T(8,128)(2,1)}, u32[]{:S(2)}, u32[]{:S(2)}) collective-permute-start(bf16[2,32,1764]{2,1,0:T(8,128)(2,1)} %get-tuple-element.125), channel_id=1, source_target_pairs={{0,2},{1,3},{2,0},{3,1},{4,6},{5,7},{6,4},{7,5},{8,10},{9,11},{10,... | collective-permute-start | bytes 677384 | tf_op jit(solution)/shard_map/ppermute | solution.py:546
  268.2 14.1 %collective-permute-start.32 = (bf16[2,32,1764]{2,1,0:T(8,128)(2,1)}, bf16[2,32,1764]{2,1,0:T(8,128)(2,1)}, u32[]{:S(2)}, u32[]{:S(2)}) collective-permute-start(bf16[2,32,1764]{2,1,0:T(8,128)(2,1)} %get-tuple-element.129), channel_id=1, source_target_pairs={{0,3},{1,2},{2,1},{3,0},{4,7},{5,6},{6,5},{7,4},{8,11},{9,10},{10,... | collective-permute-start | bytes 677384 | tf_op jit(solution)/shard_map/ppermute | solution.py:546
  268.2 18.2 %collective-permute-start.27 = (bf16[2,32,1764]{2,1,0:T(8,128)(2,1)}, bf16[2,32,1764]{2,1,0:T(8,128)(2,1)}, u32[]{:S(2)}, u32[]{:S(2)}) collective-permute-start(bf16[2,32,1764]{2,1,0:T(8,128)(2,1)} %get-tuple-element.124), channel_id=1, source_target_pairs={{0,2},{1,3},{2,0},{3,1},{4,6},{5,7},{6,4},{7,5},{8,10},{9,11},{10,... | collective-permute-start | bytes 677384 | tf_op jit(solution)/shard_map/ppermute | solution.py:546
  268.9 21.5 %collective-permute-start.31 = (bf16[2,32,1764]{2,1,0:T(8,128)(2,1)}, bf16[2,32,1764]{2,1,0:T(8,128)(2,1)}, u32[]{:S(2)}, u32[]{:S(2)}) collective-permute-start(bf16[2,32,1764]{2,1,0:T(8,128)(2,1)} %get-tuple-element.128), channel_id=1, source_target_pairs={{0,3},{1,2},{2,1},{3,0},{4,7},{5,6},{6,5},{7,4},{8,11},{9,10},{10,... | collective-permute-start | bytes 677384 | tf_op jit(solution)/shard_map/ppermute | solution.py:546
  (66 other events, 671.8 us)

commit v2 on v1

v2 whole, which is shorter than its diff:
```python
import functools

import jax
import jax.numpy as jnp
import numpy as np
from jax import lax
from jax.experimental import pallas as pl
from jax.experimental.pallas import tpu as pltpu
from jax.sharding import PartitionSpec as P

C = 128
MAP = 42
CAP = 16
HALF = 21
QUART = 10
SENT = 4
VMEM_BYTES = 63 << 20
WIDE = 256

CELLS_TWO = MAP * MAP
CELLS_THREE = HALF * HALF
CELLS_OUT = QUART * QUART
LANES_TWO = 1792
LANES_THREE = 512
LANES_OUT = 128
EPSILON = 1e-05
PRECISE = lax.Precision.HIGHEST
F32 = jnp.float32
BF16 = jnp.bfloat16
ROOT = 0.7978845608028654
CUBIC = 0.044715


def lane_ids(width):
    return lax.broadcasted_iota(jnp.int32, (1, width), 1)


def as_columns(rows):
    return jnp.concatenate([rows] * (C // 8), axis=0).T


def column_tile(columns):
    ids = lax.broadcasted_iota(jnp.int32, (C, C), 1)
    tile = jnp.zeros((C, C), F32)
    for place, column in enumerate(columns):
        tile = jnp.where(ids == place, column, tile)
    return tile


def row_tile(rows, count=8):
    ids = lax.broadcasted_iota(jnp.int32, (count, C), 0)
    tile = jnp.zeros((count, C), F32)
    for place, row in enumerate(rows):
        tile = jnp.where(ids == place, row, tile)
    return tile


def row(tile_ref, place):
    return tile_ref[place : place + 1, :]


def column(tile_ref, place):
    return tile_ref[:, place : place + 1]


def merge_moments(state, weight, mean, spread, cells):
    count, middle, total = state
    added = weight * cells
    both = count + added
    away = mean - middle
    share = added / jnp.maximum(both, 1.0)
    return both, middle + away * share, total + weight * spread + away * away * count * share


def slice_norm(heard_ref):
    means, spreads, counts = heard_ref[:, 0, :], heard_ref[:, 1, :], heard_ref[:, 2, :]
    extent = jnp.sum(counts, axis=0, keepdims=True)
    middle = jnp.sum(counts * means, axis=0, keepdims=True) / extent
    away = means - middle
    variance = jnp.sum(spreads + counts * away * away, axis=0, keepdims=True) / extent
    return middle, lax.rsqrt(variance + EPSILON), variance, extent


def level_row(columns):
    return jnp.sum(column_tile(columns), axis=0, keepdims=True)


def spread_rows(tile, out_ref):
    out_ref[...] = jnp.broadcast_to(tile[None], out_ref.shape)


def trim(values, first, last):
    tiles = cut(values, 128)
    ids = lane_ids(128)
    if first > 0:
        tiles[0] = jnp.where(ids >= first, tiles[0], jnp.zeros_like(tiles[0]))
    if last < values.shape[1]:
        tiles[-1] = jnp.where(ids < last - (values.shape[1] - 128), tiles[-1], jnp.zeros_like(tiles[-1]))
    return jnp.concatenate(tiles, axis=1)


def cut(values, wide):
    return [values[:, first : first + wide] for first in range(0, values.shape[1], wide)]


def shift_lanes(blocks, by):
    moved = [pltpu.roll(block, by % block.shape[1], 1) for block in blocks]
    nothing = jnp.zeros_like(moved[0][:, :128])
    ids = lane_ids(128)
    shifted = []
    for place, block in enumerate(moved):
        if by > 0:
            near = moved[place - 1][:, :128] if place else nothing
            edge = jnp.where(ids < by, near, block[:, :128])
            shifted.append(jnp.concatenate([edge, block[:, 128:]], axis=1) if block.shape[1] > 128 else edge)
        else:
            near = moved[place + 1][:, -128:] if place + 1 < len(moved) else nothing
            edge = jnp.where(ids >= 128 + by, near, block[:, -128:])
            shifted.append(jnp.concatenate([block[:, :-128], edge], axis=1) if block.shape[1] > 128 else edge)
    return shifted


def shift_column(blocks, by, side):
    shifted = []
    first = 0
    for block in shift_lanes(blocks, by):
        column = (lane_ids(block.shape[1]) + first) % side
        shifted.append(jnp.where(column == (0 if by > 0 else side - 1), jnp.zeros_like(block), block))
        first += block.shape[1]
    return shifted


def write(out_ref, blocks):
    first = 0
    for block in blocks:
        out_ref[:, first : first + block.shape[1]] = block
        first += block.shape[1]


def fill(stack_ref, tap, blocks):
    first = 0
    for block in blocks:
        stack_ref[tap * C : (tap + 1) * C, first : first + block.shape[1]] = block
        first += block.shape[1]


def stack_sideways(low, side, stack_ref):
    fill(stack_ref, 0, shift_column(low, 1, side))
    fill(stack_ref, 1, low)
    fill(stack_ref, 2, shift_column(low, -1, side))


def stack_upright(low, side, stack_ref):
    fill(stack_ref, 0, shift_lanes(low, -side))
    fill(stack_ref, 1, low)
    fill(stack_ref, 2, shift_lanes(low, side))


def conv_blocks(weights_ref, stack_ref):
    width = stack_ref.shape[1]
    parts = [
        jnp.dot(weights_ref[...], stack_ref[:, first : first + WIDE], preferred_element_type=F32)
        for first in range(0, width, WIDE)
    ]
    return [[part[tap * C : (tap + 1) * C] for part in parts] for tap in range(3)]


def conv_ahead(weights_ref, stack_ref, side):
    above, here, below = conv_blocks(weights_ref, stack_ref)
    total = [a + b + c for a, b, c in zip(shift_lanes(above, side), here, shift_lanes(below, -side))]
    total[-1] = trim(total[-1], 0, side * side - (stack_ref.shape[1] - total[-1].shape[1]))
    return total


def conv_behind(weights_ref, stack_ref, side):
    left, here, right = conv_blocks(weights_ref, stack_ref)
    return [a + b + c for a, b, c in zip(shift_column(left, -1, side), here, shift_column(right, 1, side))]


def across_cells(left_ref, right_ref):
    return lax.dot_general(left_ref[...], right_ref[...], (((1,), (1,)), ((), ())), preferred_element_type=F32)


def lane_sum(values):
    return jnp.sum(values, axis=1, keepdims=True)


def moments(blocks, cells):
    pivot = lane_sum(blocks[0]) * (1.0 / blocks[0].shape[1])
    total, squares = 0.0, 0.0
    for place, block in enumerate(blocks):
        away = block - pivot
        if place == len(blocks) - 1:
            away = trim(away, 0, cells - sum(b.shape[1] for b in blocks[:-1]))
        total = total + sum(cut(away, 128))
        squares = squares + sum(cut(away * away, 128))
    away = lane_sum(total) * (1.0 / cells)
    return pivot + away, lane_sum(squares) - cells * away * away


def gelu_gate(values):
    return 0.5 + 0.5 * jnp.tanh(values * (ROOT + (ROOT * CUBIC) * (values * values)))


def gelu_slope(values, gate):
    return gate * (1.0 + (1.0 - gate) * (values * (2.0 * ROOT + (6.0 * ROOT * CUBIC) * (values * values))))


def halves(values):
    high = values.astype(BF16)
    return jnp.concatenate([high, (values - high.astype(F32)).astype(BF16)], axis=0)


def dot_halves(split, weights_ref):
    both = jnp.dot(split, weights_ref[...], preferred_element_type=F32)
    return [both[first : first + C] + both[first + C : first + 2 * C] for first in range(0, both.shape[0], 2 * C)]


def own_rows(me, partner, count):
    return pl.ds(pl.multiple_of((me ^ partner) * count, count), count)


def kernel_params(axes=1):
    return pltpu.CompilerParams(vmem_limit_bytes=VMEM_BYTES, dimension_semantics=("arbitrary",) * axes)


def pack_kernel(images_each, group, wants, me_ref, maps_ref, *refs):
    piece_refs = refs[-len(wants) :]
    turned = jnp.swapaxes(maps_ref[...], 0, 1)
    for lead in range(group):

        @pl.when(me_ref[0] % group == lead)
        def _():
            for piece_ref, (partner, first, count) in zip(piece_refs, wants):
                start = (lead ^ (partner % group)) * images_each + first
                piece_ref[...] = turned[start : start + count]


def unpack_kernel(counts, me_ref, *refs):
    out_refs = refs[-len(counts) :]
    group = len(counts[0])
    for lead in range(group):

        @pl.when(me_ref[0] % group == lead)
        def _():
            start = 0
            for out_ref, parts in zip(out_refs, counts):
                ordered = []
                for slot in range(group):
                    place = start + sum(len(some) for some in parts[: slot ^ lead])
                    ordered += [refs[place + part][...] for part in range(len(parts[slot ^ lead]))]
                joined = jnp.concatenate(ordered, axis=0) if len(ordered) > 1 else ordered[0]
                out_ref[...] = jnp.swapaxes(joined, 0, 1).astype(out_ref.dtype)
                start += sum(len(some) for some in parts)


def bundle_kernel(filter_two_ref, filter_three_ref, film_ref, bias_ref, *refs):
    vector_refs, out_ref = refs[:4], refs[-1]
    rows = filter_two_ref.shape[2]
    out_ref[...] = jnp.zeros_like(out_ref)
    for place, filter_ref in enumerate((filter_two_ref, filter_three_ref)):
        for down in range(3):
            first = (3 * place + down) * rows
            for across in range(3):
                out_ref[first : first + rows, across * C : (across + 1) * C] = filter_ref[down, across]
    for kind in range(2):
        out_ref[6 * rows : 7 * rows, kind * C : kind * C + film_ref.shape[2]] = film_ref[kind]
    for place, vector_ref in enumerate(vector_refs):
        out_ref[7 * rows + place : 7 * rows + place + 1, 0:rows] = vector_ref[...]
    for kind in range(2):
        out_ref[7 * rows + 4 + kind : 7 * rows + 5 + kind, 0:rows] = bias_ref[kind : kind + 1]


def unbundle_kernel(partners, me_ref, task_ref, context_ref, *refs):
    piece_refs = refs[:partners]
    ahead_two_ref, behind_two_ref, ahead_three_ref, behind_three_ref, film_ref, vectors_ref = refs[partners:]
    rows = C // partners
    entries = film_ref.shape[2]
    lanes = jnp.zeros((8, C), F32)
    ids = lane_ids(C)
    for partner, piece_ref in enumerate(piece_refs):
        owner = me_ref[0] ^ partner
        for place, ahead_ref in enumerate((ahead_two_ref, ahead_three_ref)):
            for down in range(3):
                first = (3 * place + down) * rows
                ahead_ref[pl.ds(pl.multiple_of(down * C + owner * rows, rows), rows), :] = piece_ref[first : first + rows]
        for kind in range(2):
            film_ref[kind, own_rows(me_ref[0], partner, rows), :] = piece_ref[
                6 * rows : 7 * rows, kind * C : kind * C + entries
            ].astype(F32)
        own = jnp.where(ids < rows, piece_ref[7 * rows : 7 * rows + 16, 0:C].astype(F32)[:8], 0.0)
        lanes = lanes + pltpu.roll(own, owner * rows, 1)
    behind_two_ref[...] = ahead_two_ref[...].T
    behind_three_ref[...] = ahead_three_ref[...].T
    context = context_ref[pl.ds(task_ref[0], 1), :]
    told = [lane_sum(film_ref[kind] * context) for kind in range(2)]
    told = column_tile(told).T[:8]
    scale = 1.0 + told[0:1] + lanes[4:5]
    shift = told[1:2] + lanes[5:6]
    vectors_ref[...] = row_tile([lanes[0:1], lanes[1:2], lanes[2:3], lanes[3:4], scale, shift])


def assemble(maps, cells, me, piece_refs, index):
    rows = C // len(piece_refs)
    for partner, piece_ref in enumerate(piece_refs):
        maps[own_rows(me, partner, rows), 0:cells] = piece_ref[index]


def disperse(piece_refs, index, me, output, cells):
    rows = C // len(piece_refs)
    for partner, piece_ref in enumerate(piece_refs):
        piece_ref[index] = output[own_rows(me, partner, rows), 0:cells]


def first_conv_kernel(partners, first, final, me_ref, live_ref, told_ref, weights_ref, *refs):
    piece_refs = refs[:partners]
    conv_ref, maps_ref, state_ref, stack, state = refs[-5:]
    step = pl.program_id(0)
    count = conv_ref.shape[0]

    @pl.when(step == 0)
    def _():
        state[...] = refs[partners][...] if first else jnp.zeros_like(state)

    merged = [column(state, k) for k in range(3)]
    for image in range(count):
        maps_ref[image, :, CELLS_TWO // 128 * 128 :] = jnp.zeros((C, LANES_TWO - CELLS_TWO // 128 * 128), BF16)
        assemble(maps_ref.at[image], CELLS_TWO, me_ref[0], piece_refs, image)
        stack_sideways(cut(maps_ref[image], WIDE), MAP, stack.at[image])
        conv = conv_ahead(weights_ref, stack.at[image], MAP)
        write(conv_ref.at[image], conv)
        mean, spread = moments(conv, CELLS_TWO)
        live = live_ref[first + step * count + image]
        merged = merge_moments(merged, live, mean, spread, CELLS_TWO)
    state[...] = column_tile(merged)

    @pl.when(step == pl.num_programs(0) - 1)
    def _():
        if final:
            turned = state[...].T
            spread_rows(row_tile([turned[1:2], turned[2:3], turned[0:1], row(told_ref, 0)], SENT), state_ref)
        else:
            state_ref[...] = state[...]


def middle_kernel(
    partners, me_ref, live_ref, heard_ref, vectors_ref, pool_a_ref, pool_b_ref, weights_ref, conv_ref, *refs
):
    hidden_ref, conv_three_ref, norm_ref, levels_ref, sums_ref, columns, state, stack = refs[-8:]
    piece_refs = refs[-8 - partners : -8]
    step = pl.program_id(0)
    count = conv_ref.shape[0]

    @pl.when(step == 0)
    def _():
        middle, factor, variance, extent = slice_norm(heard_ref)
        norm_ref[...] = row_tile([middle, factor, variance, extent])
        columns[...] = as_columns(row_tile([middle, row(vectors_ref, 0) * factor, row(vectors_ref, 1)]))
        state[...] = jnp.zeros_like(state)

    merged = [column(state, k) for k in range(3)]
    active_squares, hidden_squares = column(state, 3), column(state, 4)
    for image in range(count):
        live = live_ref[step * count + image]
        pre = (conv_ref[image] - column(columns, 0)) * column(columns, 1) + column(columns, 2)
        active = pre * gelu_gate(pre)
        counted = trim(active, 0, CELLS_TWO)
        active_squares = active_squares + live * lane_sum(counted * counted)
        split = halves(active)
        (left,) = dot_halves(split[:, :1152], pool_a_ref)
        (right,) = dot_halves(split[:, 896:], pool_b_ref)
        hidden = live * jnp.concatenate([left, right], axis=1)
        hidden_squares = hidden_squares + lane_sum(hidden * hidden)
        hidden_low = hidden.astype(BF16)
        hidden_ref[image] = hidden_low
        disperse(piece_refs, image, me_ref[0], hidden_ref.at[image], CELLS_THREE)
        stack_sideways(cut(hidden_low, WIDE), HALF, stack.at[image])
        conv = conv_ahead(weights_ref, stack.at[image], HALF)
        write(conv_three_ref.at[image], conv)
        mean, spread = moments(conv, CELLS_THREE)
        merged = merge_moments(merged, live, mean, spread, CELLS_THREE)
    state[...] = column_tile([*merged, active_squares, hidden_squares])

    @pl.when(step == pl.num_programs(0) - 1)
    def _():
        turned = state[...].T
        spread_rows(row_tile([turned[k : k + 1] for k in (1, 2, 0)], SENT), sums_ref)
        levels_ref[...] = row_tile([level_row([column(state, 3), column(state, 4)])])


def top_kernel(
    partners, me_ref, live_ref, heard_ref, own_ref, before_ref, vectors_ref, pool_ref, spread_ref, conv_ref, *refs
):
    target_refs = refs[:partners]
    piece_refs = refs[partners : 2 * partners]
    grad_ref, norm_ref, levels_ref, sums_ref, columns, target, output, totals = refs[2 * partners :]
    step = pl.program_id(0)
    count = conv_ref.shape[0]

    @pl.when(step == 0)
    def _():
        middle, factor, variance, extent = slice_norm(heard_ref)
        norm_ref[...] = row_tile([middle, factor, variance, extent])
        columns[...] = as_columns(row_tile([middle, factor] + [row(vectors_ref, k) for k in (2, 3, 4, 5)]))
        target[...] = jnp.zeros_like(target)
        totals[...] = jnp.zeros_like(totals)

    scale = column(columns, 4)
    slope = scale * column(columns, 2)
    offset = scale * column(columns, 3) + column(columns, 5)
    sums = [jnp.zeros((C, 1), F32)] * 4
    for image in range(count):
        live = live_ref[step * count + image]
        assemble(target.at[image], CELLS_OUT, me_ref[0], target_refs, image)
        normed = (conv_ref[image] - column(columns, 0)) * column(columns, 1)
        filmed = slope * normed + offset
        gate = gelu_gate(filmed)
        active = filmed * gate
        counted = trim(active, 0, CELLS_THREE)
        (pooled,) = dot_halves(halves(active), pool_ref)
        pooled = live * pooled
        output[image] = pooled.astype(BF16)
        disperse(piece_refs, image, me_ref[0], output.at[image], CELLS_OUT)
        spread = jnp.dot(target[image], spread_ref[...], preferred_element_type=F32)
        grad_filmed = live * spread * gelu_slope(filmed, gate)
        grad_ref[image] = scale * grad_filmed
        parts = (
            lane_sum(grad_filmed),
            lane_sum(grad_filmed * normed),
            live * lane_sum(counted * counted),
            lane_sum(pooled * pooled),
        )
        sums = [total + part for total, part in zip(sums, parts)]
    totals[...] += column_tile(sums)

    @pl.when(step == pl.num_programs(0) - 1)
    def _():
        turned = totals[...].T
        shift_sum, scale_sum = turned[0:1], turned[1:2]
        film_scale = row(vectors_ref, 4)
        slope = film_scale * row(vectors_ref, 2) * row(norm_ref, 1)
        offset = film_scale * row(vectors_ref, 3) + row(vectors_ref, 5)
        extent = own_ref[0, 2:3, :]
        away = own_ref[0, 0:1, :] - row(norm_ref, 0)
        filmed_squares = (
            slope * slope * (own_ref[0, 1:2, :] + extent * away * away)
            + 2.0 * slope * offset * extent * away
            + extent * offset * offset
        )
        spread_rows(
            row_tile([shift_sum, scale_sum, film_scale * shift_sum, film_scale * scale_sum], SENT), sums_ref
        )
        nothing = jnp.zeros((C, 1), F32)
        others = level_row([nothing, nothing, nothing, column(totals, 2), column(totals, 3)])
        lanes = lane_ids(C)
        filmed_total = lane_sum(filmed_squares)
        levels_ref[...] = before_ref[...] + row_tile([others + jnp.where(lanes == 2, filmed_total, 0.0)])


def norm_back(live, columns, grad, away, cells):
    scaled = [live * column(columns, k) for k in (1, 2, 3)]
    error = grad.astype(F32) * scaled[0] - scaled[1] - away.astype(F32) * scaled[2]
    return trim(error, 0, cells).astype(BF16)


def norm_back_columns(norm_ref, gain, bias_sum, gain_sum):
    factor, extent = row(norm_ref, 1), row(norm_ref, 3)
    front = gain * factor
    return as_columns(
        row_tile([row(norm_ref, 0), front, front * bias_sum / extent, front * factor * gain_sum / extent])
    )


def back_kernel(
    live_ref,
    heard_ref,
    norm_three_ref,
    norm_two_ref,
    levels_ref,
    vectors_ref,
    weights_ref,
    unpool_a_ref,
    unpool_b_ref,
    grad_ref,
    conv_three_ref,
    hidden_ref,
    conv_two_ref,
    *refs,
):
    out_ref, away_ref, sums_ref, filter_ref, columns_three, columns_two, totals, product, stack, upright = refs[-10:]
    step = pl.program_id(0)
    count = conv_two_ref.shape[0]

    @pl.when(step == 0)
    def _():
        sums = jnp.sum(heard_ref[...], axis=0)
        columns_three[...] = norm_back_columns(norm_three_ref, row(vectors_ref, 2), sums[2:3], sums[3:4])
        columns_two[...] = as_columns(
            row_tile([row(norm_two_ref, 0), row(vectors_ref, 0) * row(norm_two_ref, 1), row(vectors_ref, 1)])
        )
        totals[...] = jnp.zeros_like(totals)
        product[...] = jnp.zeros_like(product)

    grad_sum, product_sum = column(totals, 0), column(totals, 1)
    for image in range(count):
        away = conv_three_ref[image] - column(columns_three, 0)
        error = norm_back(live_ref[step * count + image], columns_three, grad_ref[image], away, CELLS_THREE)
        stack_upright(cut(error, WIDE), HALF, upright.at[image])
        stack_sideways(cut(hidden_ref[image], WIDE), HALF, stack.at[image])
    split = jnp.concatenate(
        [
            halves(jnp.concatenate(conv_behind(weights_ref, upright.at[image], HALF), axis=1))
            for image in range(count)
        ],
        axis=0,
    )
    left = dot_halves(split[:, :256], unpool_a_ref)
    right = dot_halves(split[:, 128:], unpool_b_ref)
    for image in range(count):
        away = conv_two_ref[image] - column(columns_two, 0)
        pre = away * column(columns_two, 1) + column(columns_two, 2)
        grad_pre = jnp.concatenate([left[image], right[image]], axis=1) * gelu_slope(pre, gelu_gate(pre))
        out_ref[image] = grad_pre.astype(BF16)
        away_ref[image] = away.astype(BF16)
        grad_sum = grad_sum + lane_sum(grad_pre)
        product_sum = product_sum + lane_sum(grad_pre * away)
    product[...] += sum(across_cells(upright.at[image], stack.at[image]) for image in range(count))
    totals[...] = column_tile([grad_sum, product_sum])

    @pl.when(step == pl.num_programs(0) - 1)
    def _():
        split_filter(product, filter_ref)
        turned = totals[...].T
        normed_sum = turned[1:2] * row(norm_two_ref, 1)
        spread_rows(row_tile([turned[0:1], normed_sum, levels_ref[0:1, :]], SENT), sums_ref)


def split_filter(product, filter_ref):
    partners, _, rows, _ = filter_ref.shape
    for tap in range(3):
        for owner in range(partners):
            filter_ref[owner, tap] = product[tap * C + owner * rows : tap * C + (owner + 1) * rows].astype(BF16)


def last_columns(heard_ref, norm_ref, vectors_ref):
    sums = jnp.sum(heard_ref[...], axis=0)
    return norm_back_columns(norm_ref, row(vectors_ref, 0), sums[0:1], sums[1:2])


def last_kernel(
    partners,
    near,
    first,
    final,
    steps,
    me_ref,
    live_ref,
    heard_ref,
    norm_ref,
    vectors_ref,
    weights_ref,
    grad_ref,
    away_ref,
    maps_ref,
    *refs,
):
    far = partners - near
    before_ref, (filter_ref, product, columns, output, upright, stack) = refs[0], refs[-6:]
    piece_refs = refs[-6 - near - far * len(steps) : -6]
    step = pl.program_id(0)
    count = grad_ref.shape[0]

    @pl.when(step == 0)
    def _():
        columns[...] = last_columns(heard_ref, norm_ref, vectors_ref)
        product[...] = before_ref[...] if first else jnp.zeros_like(product)

    for image in range(count):
        live = live_ref[first + step * count + image]
        error = norm_back(live, columns, grad_ref[image], away_ref[image], CELLS_TWO)
        stack_upright(cut(error, WIDE), MAP, upright.at[image])
        write(output.at[image], [block.astype(BF16) for block in conv_behind(weights_ref, upright.at[image], MAP)])
        stack_sideways(cut(maps_ref[image], WIDE), MAP, stack.at[image])
        product[...] += across_cells(upright.at[image], stack.at[image])
    rows = C // partners
    start = 0
    for place, length in enumerate(steps):

        @pl.when((step >= start) & (step < start + length))
        def _():
            for image in range(count):
                for partner in range(partners):
                    piece_ref = piece_refs[partner if partner < near else near + place * far + partner - near]
                    piece_ref[image] = output[image, own_rows(me_ref[0], partner, rows), 0:CELLS_TWO]

        start += length

    @pl.when(step == pl.num_programs(0) - 1)
    def _():
        if final:
            split_filter(product, filter_ref)
        else:
            filter_ref[...] = product[...]


def strips_kernel(heard_ref, out_ref):
    out_ref[...] = jnp.broadcast_to(jnp.sum(heard_ref[...].astype(F32), axis=0)[None], out_ref.shape)


def one_hot(rows, columns, wanted):
    row_ids = lax.broadcasted_iota(jnp.int32, (rows, columns), 0)
    column_ids = lax.broadcasted_iota(jnp.int32, (rows, columns), 1)
    return jnp.where(wanted(row_ids, column_ids), 1.0, 0.0)


def exact_dot(left, right, contract=((1,), (0,))):
    return lax.dot_general(left, right, (contract, ((), ())), precision=PRECISE, preferred_element_type=F32)


def finish_kernel(
    partners,
    group,
    here_ref,
    me_ref,
    heard_two_ref,
    heard_top_ref,
    heard_back_ref,
    norm_two_ref,
    norm_three_ref,
    vectors_ref,
    film_ref,
    *refs,
):
    film_w_ref, film_b_ref, context_ref, sums_ref, levels_ref, product = refs[-6:]
    devices = heard_two_ref.shape[0]
    tasks = devices // group
    contexts = context_ref.shape[0]
    rows = C // partners
    entries = film_ref.shape[2]
    turn = (C - me_ref[0] * rows) % C

    def own_lanes(values):
        return pltpu.roll(values, turn, 1)[:, :rows]

    by_task = one_hot(tasks, devices, lambda t, d: d // group == t)
    of_task = one_hot(
        tasks, devices, lambda t, d: (d // partners == t // contexts) & (d % partners == t % contexts)
    )
    mine = one_hot(contexts, devices, lambda t, d: d // group == here_ref[0] * contexts + t)
    shift, normed = heard_top_ref[:, 0, :], heard_top_ref[:, 1, :]
    scale = row(vectors_ref, 2) * normed + row(vectors_ref, 3) * shift
    told = exact_dot(of_task, heard_two_ref[:, 3, :])
    total = jnp.zeros((contexts, entries), F32)
    for kind, grads in enumerate((scale, shift)):
        grads_by_task = exact_dot(by_task, grads)
        product[...] = exact_dot(grads_by_task, told, ((0,), (0,)))
        film_w_ref[kind] = product[pl.ds(pl.multiple_of(me_ref[0] * rows, rows), rows), :entries]
        film_b_ref[kind : kind + 1] = own_lanes(jnp.sum(grads_by_task, axis=0, keepdims=True))
        total = total + exact_dot(exact_dot(mine, grads), film_ref[kind])
    context_ref[...] = total

    back = jnp.sum(heard_back_ref[...], axis=0)
    top = jnp.sum(heard_top_ref[...], axis=0)
    sums_ref[...] = own_lanes(row_tile([back[1:2], back[0:1], top[3:4], top[2:3]]))

    live = norm_two_ref[3:4, 0:1] * (1.0 / CELLS_TWO)
    lanes = lane_ids(C)

    def mean_square(norm_ref, gain, shift):
        factor, variance = row(norm_ref, 1), row(norm_ref, 2)
        return jnp.sum(gain * gain * variance * factor * factor + shift * shift, axis=1, keepdims=True) * (1.0 / C)

    def mean_conv(norm_ref):
        middle = row(norm_ref, 0)
        return jnp.sum(row(norm_ref, 2) + middle * middle, axis=1, keepdims=True) * (1.0 / C)

    known = (
        mean_conv(norm_two_ref),
        mean_square(norm_two_ref, row(vectors_ref, 0), row(vectors_ref, 1)),
        back[2:3, 0:1] / (live * (C * CELLS_TWO)),
        back[2:3, 1:2] / (live * (C * CELLS_THREE)),
        mean_conv(norm_three_ref),
        mean_square(norm_three_ref, row(vectors_ref, 2), row(vectors_ref, 3)),
        back[2:3, 2:3] / (live * (C * CELLS_THREE)),
        back[2:3, 3:4] / (live * (C * CELLS_THREE)),
        back[2:3, 4:5] / (live * (C * CELLS_OUT)),
    )
    level = jnp.zeros((1, C), F32)
    for place, value in enumerate(known):
        level = jnp.where(lanes == place, value, level)
    levels_ref[...] = jnp.sqrt(level)


def pool_matrix(side, width, out_width):
    half = side // 2
    matrix = np.zeros((width, out_width), np.float32)
    for row in range(2 * half):
        for column in range(2 * half):
            matrix[row * side + column, (row // 2) * half + column // 2] = 0.25
    return matrix


def lasting(microseconds):
    return pl.CostEstimate(
        flops=int(microseconds * 1.1e9), bytes_accessed=int(microseconds * 3.5e6), transcendentals=0
    )


def smem():
    return pl.BlockSpec(memory_space=pltpu.SMEM)


def anywhere(count):
    return [pl.BlockSpec(memory_space=pl.ANY)] * count


def whole(*shape):
    return pl.BlockSpec(shape, lambda n: (0,) * len(shape))


def each(*shape, first=0, count=1):
    return pl.BlockSpec((count, *shape), lambda n: (first + n,) + (0,) * len(shape))


def pack(maps, me, images_each, wants, earlier=()):
    rows, slots, cells = maps.shape
    group = CAP // images_each
    halves = 2
    block = wants[0][0] // group
    return pl.pallas_call(
        functools.partial(pack_kernel, images_each, group, wants),
        grid_spec=pltpu.PrefetchScalarGridSpec(
            num_scalar_prefetch=1,
            grid=(halves,),
            in_specs=[
                pl.BlockSpec((rows // halves, CAP, cells), lambda n, me_ref: (n, (me_ref[0] // group) ^ block, 0)),
                *anywhere(len(earlier)),
            ],
            out_specs=[
                pl.BlockSpec((count, rows // halves, cells), lambda n, me_ref: (0, n, 0)) for _, _, count in wants
            ],
        ),
        out_shape=[jax.ShapeDtypeStruct((count, rows, cells), maps.dtype) for _, _, count in wants],
        compiler_params=kernel_params(),
        name="pack",
        cost_estimate=lasting(2.5),
    )(me, maps, *earlier)


def unpack(arrays, me, images_each, dtype, place, outs=(), earlier=()):
    partners = len(arrays[0])
    span = max(8, images_each) if dtype == F32 else 16
    group = span // images_each
    halves = 2
    given, specs, counts, shapes, out_specs = [], [], [], [], []
    for pieces in arrays:
        here = pieces[place * group : (place + 1) * group]
        counts.append(tuple(tuple(piece.shape[0] for piece in parts) for parts in here))
        rows, cells = here[0][0].shape[1:]
        for piece in (piece for parts in here for piece in parts):
            given.append(piece)
            specs.append(pl.BlockSpec((piece.shape[0], rows // halves, cells), lambda n, me_ref: (0, n, 0)))
        shapes.append(jax.ShapeDtypeStruct((rows, partners * images_each, cells), dtype))
        out_specs.append(
            pl.BlockSpec((rows // halves, span, cells), lambda n, me_ref: (n, (me_ref[0] // group) ^ place, 0))
        )
    aliases = {1 + len(given) + k: k for k in range(len(outs))}
    given += [*outs, *earlier]
    specs += anywhere(len(given) - len(specs))
    return pl.pallas_call(
        functools.partial(unpack_kernel, counts),
        grid_spec=pltpu.PrefetchScalarGridSpec(
            num_scalar_prefetch=1, grid=(halves,), in_specs=specs, out_specs=out_specs
        ),
        out_shape=shapes,
        input_output_aliases=aliases,
        compiler_params=kernel_params(),
        name="unpack",
        cost_estimate=lasting(2.0),
    )(me, *given)


def local(
    images,
    counts,
    context,
    filter_two,
    gain_two,
    shift_two,
    filter_three,
    gain_three,
    shift_three,
    film_weight,
    film_bias,
    cotangent,
    *,
    partners,
    columns,
):
    devices = partners * columns
    rows, slots = images.shape[:2]
    images_each = slots // partners
    group = CAP // images_each
    one = 1
    pair, some = min(images_each, 2), min(images_each, 4)
    position = lax.axis_index("tensor")
    me = jnp.reshape(position, (1,)).astype(jnp.int32)

    def swap(value, partner):
        if partner == 0:
            return value
        return lax.ppermute(value, "tensor", [(i, i ^ partner) for i in range(partners)])

    def share(copies):
        return lax.all_to_all(copies, ("dp", "tensor"), 0, 0)

    near = 2
    half, quarter = images_each // 2, images_each // 4
    sizes_in = (half, quarter, quarter) if quarter >= pair else (half, half)
    calls_out = ((pair,),) * (images_each // pair)
    starts_in = [sum(sizes_in[:part]) for part in range(len(sizes_in))]
    counts_of = [(images_each,) if partner < near else sizes_in for partner in range(partners)]
    far = [partner for partner in reversed(range(partners)) if partner >= near]
    maps = [[None] * len(counts_of[partner]) for partner in range(partners)]

    def send_in(some_parts, whole_near, earlier):
        for block in reversed(range(partners // group)):
            wants = [
                (partner, starts_in[part], sizes_in[part])
                for part in some_parts
                for partner in far
                if partner // group == block
            ]
            if block == 0 and whole_near:
                wants += [(partner, 0, images_each) for partner in range(near)]
            if wants:
                sent = pack(images, me, images_each, wants, earlier)
                for piece, (partner, first, _) in zip(sent, wants):
                    maps[partner][starts_in.index(first)] = swap(piece, partner)
                earlier = (*earlier, sent[0])
        return earlier

    first_sent = send_in((0,), True, ())
    entries = film_weight.shape[0]
    bundle = pl.pallas_call(
        bundle_kernel,
        in_specs=[pl.BlockSpec(memory_space=pltpu.VMEM)] * 8 + anywhere(1),
        out_shape=jax.ShapeDtypeStruct((7 * rows + 16, 3 * C), BF16),
        compiler_params=kernel_params(0),
        name="bundle",
        cost_estimate=lasting(1.0),
    )(
        jnp.transpose(filter_two, (2, 3, 0, 1)),
        jnp.transpose(filter_three, (2, 3, 0, 1)),
        jnp.transpose(film_weight, (1, 2, 0)),
        film_bias,
        *[vector[None] for vector in (gain_two, shift_two, gain_three, shift_three)],
        first_sent[0],
    )
    bundles = {0: bundle}
    bit = partners // 2
    while bit:
        bundles.update({partner | bit: swap(piece, bit) for partner, piece in bundles.items()})
        bit //= 2

    sent_in = {
        part: send_in((part,), False, (bundles[partners // 2] if part == 1 else maps[far[-1]][0],))
        for part in range(1, len(sizes_in))
    }

    task = position // group
    slot = (position % group) * images_each + jnp.arange(images_each, dtype=jnp.int32)
    limit = lax.dynamic_index_in_dim(counts, task, 0, keepdims=False)
    live = (slot < limit).astype(F32)
    ahead_two, behind_two, ahead_three, behind_three, film, vectors = pl.pallas_call(
        functools.partial(unbundle_kernel, partners),
        in_specs=[smem(), smem(), *[pl.BlockSpec(memory_space=pltpu.VMEM)] * (1 + partners)],
        out_shape=[jax.ShapeDtypeStruct((3 * C, 3 * C), BF16)] * 4
        + [jax.ShapeDtypeStruct((2, C, entries), F32), jax.ShapeDtypeStruct((8, C), F32)],
        compiler_params=kernel_params(0),
        name="unbundle",
        cost_estimate=lasting(2.0),
    )(me, jnp.reshape(task, (1,)).astype(jnp.int32), context, *[bundles[partner] for partner in range(partners)])

    told = lax.dynamic_index_in_dim(context, position % context.shape[0], 0)
    told = jnp.pad(told, ((0, 7), (0, C - entries)))

    conv_two = whole_maps = state = None
    for part, (first, count) in enumerate(zip(starts_in, sizes_in)):
        given = [maps[partner][0 if partner < near else part] for partner in range(partners)]
        specs = [
            each(rows, CELLS_TWO, first=first // pair if partner < near else 0, count=pair)
            for partner in range(partners)
        ]
        aliases = {}
        final = part == len(sizes_in) - 1
        if part:
            aliases = {5 + partners: 0, 6 + partners: 1}
            given = given + [state, conv_two, whole_maps]
            specs = specs + [whole(C, C), *anywhere(2)]
        waits = [] if final else [sent_in[part + 1][-1]]
        given = given + waits
        specs = specs + anywhere(len(waits))
        conv_two, whole_maps, state = pl.pallas_call(
            functools.partial(first_conv_kernel, partners, first, final),
            grid=(count // pair,),
            in_specs=[smem(), smem(), whole(8, C), whole(3 * C, 3 * C), *specs],
            out_specs=[
                each(C, LANES_TWO, first=first // pair, count=pair),
                each(C, LANES_TWO, first=first // pair, count=pair),
                whole(devices, SENT, C) if final else whole(C, C),
            ],
            out_shape=[
                jax.ShapeDtypeStruct((images_each, C, LANES_TWO), F32),
                jax.ShapeDtypeStruct((images_each, C, LANES_TWO), BF16),
                jax.ShapeDtypeStruct((devices, SENT, C) if final else (C, C), F32),
            ],
            scratch_shapes=[
                pltpu.VMEM((pair, 3 * C, LANES_TWO), BF16),
                pltpu.VMEM((C, C), F32),
            ],
            input_output_aliases=aliases,
            compiler_params=kernel_params(),
            name="first_conv",
            cost_estimate=lasting(2.3 * count),
        )(me, live, told, ahead_two, *given)
    heard_two = share(state)
    turned = jnp.transpose(cotangent, (1, 0, 2))
    targets = [
        swap(lax.dynamic_slice_in_dim(turned, (position ^ partner) * images_each, images_each, 0), partner)
        for partner in range(partners)
    ]

    pool = pool_matrix(MAP, LANES_TWO, LANES_THREE)
    pool_out = pool_matrix(HALF, LANES_THREE, LANES_OUT)
    *block_pieces, hidden, conv_three, norm_two, levels, sums_three = pl.pallas_call(
        functools.partial(middle_kernel, partners),
        grid=(images_each // pair,),
        in_specs=[
            smem(),
            smem(),
            whole(devices, SENT, C),
            whole(8, C),
            whole(1152, 256),
            whole(896, 256),
            whole(3 * C, 3 * C),
            each(C, LANES_TWO, count=pair),
        ],
        out_specs=[each(rows, CELLS_THREE, count=pair)] * partners
        + [each(C, LANES_THREE, count=pair), each(C, LANES_THREE, count=pair), whole(8, C), whole(8, C), whole(devices, SENT, C)],
        out_shape=[jax.ShapeDtypeStruct((images_each, rows, CELLS_THREE), BF16)] * partners
        + [
            jax.ShapeDtypeStruct((images_each, C, LANES_THREE), BF16),
            jax.ShapeDtypeStruct((images_each, C, LANES_THREE), F32),
            jax.ShapeDtypeStruct((8, C), F32),
            jax.ShapeDtypeStruct((8, C), F32),
            jax.ShapeDtypeStruct((devices, SENT, C), F32),
        ],
        scratch_shapes=[
            pltpu.VMEM((C, C), F32),
            pltpu.VMEM((C, C), F32),
            pltpu.VMEM((pair, 3 * C, LANES_THREE), BF16),
        ],
        compiler_params=kernel_params(),
        name="middle",
            cost_estimate=lasting(2.0 * images_each),
    )(
        me,
        live,
        heard_two,
        vectors,
        jnp.asarray(pool[:1152, :256], BF16),
        jnp.asarray(pool[896:, 256:], BF16),
        ahead_three,
        conv_two,
    )
    heard_three = share(sums_three)

    *out_pieces, grad_three, norm_three, levels, sums_top = pl.pallas_call(
        functools.partial(top_kernel, partners),
        grid=(images_each // some,),
        in_specs=[
            smem(),
            smem(),
            whole(devices, SENT, C),
            whole(1, SENT, C),
            whole(8, C),
            whole(8, C),
            whole(LANES_THREE, LANES_OUT),
            whole(LANES_OUT, LANES_THREE),
            each(C, LANES_THREE, count=some),
            *[each(rows, CELLS_OUT, count=some)] * partners,
        ],
        out_specs=[each(rows, CELLS_OUT, count=some)] * partners
        + [each(C, LANES_THREE, count=some), whole(8, C), whole(8, C), whole(devices, SENT, C)],
        out_shape=[jax.ShapeDtypeStruct((images_each, rows, CELLS_OUT), BF16)] * partners
        + [
            jax.ShapeDtypeStruct((images_each, C, LANES_THREE), F32),
            jax.ShapeDtypeStruct((8, C), F32),
            jax.ShapeDtypeStruct((8, C), F32),
            jax.ShapeDtypeStruct((devices, SENT, C), F32),
        ],
        scratch_shapes=[
            pltpu.VMEM((C, C), F32),
            pltpu.VMEM((some, C, LANES_OUT), BF16),
            pltpu.VMEM((some, C, LANES_OUT), BF16),
            pltpu.VMEM((C, C), F32),
        ],
        compiler_params=kernel_params(),
        name="top",
            cost_estimate=lasting(0.8 * images_each),
    )(
        me,
        live,
        heard_three,
        sums_three,
        levels,
        vectors,
        jnp.asarray(pool_out, BF16),
        jnp.asarray(pool_out.T, BF16),
        conv_three,
        *targets,
    )
    heard_top = share(sums_top)
    block_two = [[swap(block_pieces[k], k)] for k in range(partners)]
    out_pieces = [[swap(out_pieces[k], k)] for k in range(partners)]

    filter_shape = jax.ShapeDtypeStruct((partners, 2, 3, rows, 3 * C), BF16)

    def filter_spec(block):
        return pl.BlockSpec((partners, None, 3, rows, 3 * C), lambda n: (0, block, 0, 0, 0))

    grad_two, away_two, sums_two, filter_sums = pl.pallas_call(
        back_kernel,
        grid=(images_each // pair,),
        in_specs=[
            smem(),
            whole(devices, SENT, C),
            whole(8, C),
            whole(8, C),
            whole(8, C),
            whole(8, C),
            whole(3 * C, 3 * C),
            whole(256, 896),
            whole(384, 896),
            each(C, LANES_THREE, count=pair),
            each(C, LANES_THREE, count=pair),
            each(C, LANES_THREE, count=pair),
            each(C, LANES_TWO, count=pair),
        ],
        out_specs=[
            each(C, LANES_TWO, count=pair),
            each(C, LANES_TWO, count=pair),
            whole(devices, SENT, C),
            filter_spec(1),
        ],
        out_shape=[
            jax.ShapeDtypeStruct((images_each, C, LANES_TWO), BF16),
            jax.ShapeDtypeStruct((images_each, C, LANES_TWO), BF16),
            jax.ShapeDtypeStruct((devices, SENT, C), F32),
            filter_shape,
        ],
        scratch_shapes=[
            pltpu.VMEM((C, C), F32),
            pltpu.VMEM((C, C), F32),
            pltpu.VMEM((C, C), F32),
            pltpu.VMEM((3 * C, 3 * C), F32),
            pltpu.VMEM((pair, 3 * C, LANES_THREE), BF16),
            pltpu.VMEM((pair, 3 * C, LANES_THREE), BF16),
        ],
        compiler_params=kernel_params(),
        name="back",
            cost_estimate=lasting(2.0 * images_each),
    )(
        live,
        heard_top,
        norm_three,
        norm_two,
        levels,
        vectors,
        behind_three,
        jnp.asarray(pool[:896, :256].T, BF16),
        jnp.asarray(pool[896:, 128:].T, BF16),
        grad_three,
        conv_three,
        hidden,
        conv_two,
    )
    heard_back = share(sums_two)

    returned = [[] for partner in range(partners)]
    waits = [pieces[0] for pieces in (*block_two, *out_pieces)]
    kept = []
    product = vectors
    first = 0
    for part, sizes in enumerate(calls_out):
        count = sum(sizes)
        final = part == len(calls_out) - 1
        if part == 2:
            waits = waits + [returned[near][0]]
        if part == 3:
            waits = waits + [returned[near][1], *(returned[partner][0] for partner in far)]
        if final:
            waits = waits + [filter_sums]
        size = one
        steps = [some // size for some in sizes]
        first_steps = [sum(steps[:place]) for place in range(len(steps))]
        out_specs = [each(rows, CELLS_TWO, first=first // size, count=size)] * near
        out_shape = [jax.ShapeDtypeStruct((images_each, rows, CELLS_TWO), BF16)] * near
        for start, length in zip(first_steps, steps):
            out_specs += [
                pl.BlockSpec(
                    (size, rows, CELLS_TWO),
                    lambda n, start=start, length=length: (jnp.clip(n - start, 0, length - 1), 0, 0),
                )
            ] * len(far)
            out_shape += [jax.ShapeDtypeStruct((length * size, rows, CELLS_TWO), BF16)] * len(far)
        out_specs.append(filter_spec(0) if final else whole(3 * C, 3 * C))
        out_shape.append(filter_shape if final else jax.ShapeDtypeStruct((3 * C, 3 * C), F32))
        inputs = [me, live, heard_back, norm_two, vectors, behind_two, grad_two, away_two, whole_maps, product]
        aliases = {len(inputs) + len(waits) + k: k for k in range(len(kept))}
        if final:
            aliases[len(inputs) + len(waits) - 1] = len(out_shape) - 1
        *pieces, product = pl.pallas_call(
            functools.partial(last_kernel, partners, near, first, final, steps),
            grid=(count // size,),
            in_specs=[
                smem(),
                smem(),
                whole(devices, SENT, C),
                whole(8, C),
                whole(8, C),
                whole(3 * C, 3 * C),
                *[each(C, LANES_TWO, first=first // size, count=size)] * 3,
                whole(*product.shape),
                *anywhere(len(waits) + len(kept)),
            ],
            out_specs=out_specs,
            out_shape=out_shape,
            scratch_shapes=[
                pltpu.VMEM((3 * C, 3 * C), F32),
                pltpu.VMEM((C, C), F32),
                pltpu.VMEM((size, C, LANES_TWO), BF16),
                pltpu.VMEM((size, 3 * C, LANES_TWO), BF16),
                pltpu.VMEM((size, 3 * C, LANES_TWO), BF16),
            ],
            input_output_aliases=aliases,
            compiler_params=kernel_params(),
            name="last",
            cost_estimate=lasting(2.5 * count),
        )(*inputs, *waits, *kept)
        kept, waits, first = pieces[:near], [], first + count
        for place in range(len(sizes)):
            for partner in reversed(far):
                returned[partner].append(swap(pieces[near + place * len(far) + partner - near], partner))
    for partner in range(near):
        returned[partner].append(swap(kept[partner], partner))

    ahead = (returned[near][-2], *(returned[partner][-3:][0] for partner in far))
    spans = partners * images_each // max(8, images_each)
    near_spans = max(1, near * images_each // 8)
    grad_images = ()
    for place in [*range(near_spans), *range(near_spans, spans)]:
        grad_images = unpack(
            [returned], me, images_each, F32, place, grad_images, () if grad_images else ahead
        )
    (grad_images,) = grad_images

    blocks = ()
    for place in range(partners // group):
        waits = [kept[0], *(returned[partner][-2] for partner in far)]
        blocks = unpack([block_two, out_pieces], me, images_each, BF16, place, blocks, waits)
    block_two, block_three = blocks

    strip = 6 * rows // columns
    heard = lax.all_to_all(product.reshape(devices, strip, 3 * C), ("tensor", "dp"), 0, 0)
    strips = pl.pallas_call(
        strips_kernel,
        out_shape=jax.ShapeDtypeStruct((columns, strip, 3 * C), F32),
        compiler_params=kernel_params(0),
        name="strips",
        cost_estimate=lasting(1.5),
    )(heard)
    strips = lax.all_to_all(strips, "dp", 0, 0).reshape(2, 3, rows, 3, C)
    grad_filters = jnp.transpose(strips, (0, 2, 4, 1, 3))

    contexts = context.shape[0]
    grad_film_w, grad_film_b, grad_context, norm_sums, levels = pl.pallas_call(
        functools.partial(finish_kernel, partners, group),
        in_specs=[smem(), smem(), *[pl.BlockSpec(memory_space=pltpu.VMEM)] * 7, *anywhere(1)],
        out_shape=[
            jax.ShapeDtypeStruct((2, rows, entries), F32),
            jax.ShapeDtypeStruct((2, rows), F32),
            jax.ShapeDtypeStruct((contexts, entries), F32),
            jax.ShapeDtypeStruct((8, rows), F32),
            jax.ShapeDtypeStruct((1, C), F32),
        ],
        scratch_shapes=[pltpu.VMEM((C, C), F32)],
        compiler_params=kernel_params(0),
        name="finish",
        cost_estimate=lasting(2.0),
    )(
        jnp.reshape(lax.axis_index("dp"), (1,)).astype(jnp.int32),
        me,
        heard_two,
        heard_top,
        heard_back,
        norm_two,
        norm_three,
        vectors,
        film,
        kept[0],
    )
    return (
        block_two,
        block_three,
        grad_images,
        grad_filters[0],
        norm_sums[0],
        norm_sums[1],
        grad_filters[1],
        norm_sums[2],
        norm_sums[3],
        jnp.transpose(grad_film_w, (2, 0, 1)),
        grad_film_b,
        grad_context,
        levels[0, :9],
    )


def solution(mesh):
    step = functools.partial(local, partners=mesh.shape["tensor"], columns=mesh.shape["dp"])
    placed = (
        P("tensor", "dp", None),
        P("dp"),
        P("dp", None),
        P("tensor", None, None, None),
        P("tensor"),
        P("tensor"),
        P("tensor", None, None, None),
        P("tensor"),
        P("tensor"),
        P(None, None, "tensor"),
        P(None, "tensor"),
        P("tensor", "dp", None),
    )
    return jax.shard_map(
        step,
        mesh=mesh,
        in_specs=placed,
        out_specs=(
            P("tensor", "dp", None),
            P("tensor", "dp", None),
            P("tensor", "dp", None),
            P("tensor", None, None, None),
            P("tensor"),
            P("tensor"),
            P("tensor", None, None, None),
            P("tensor"),
            P("tensor"),
            P(None, None, "tensor"),
            P(None, "tensor"),
            P("dp", None),
            P(),
        ),
        check_vma=False,
    )
```

time: 298 us -> 220 us (0.74)
  waiting for transfers between devices: 68.8 us -> 39.9 us
  local copies, waits for them, and re-layouts: 25.6 us -> 12.8 us
  other arithmetic: 11.6 us -> 1.16 us
  between operations: 10.8 us -> 0.95 us
  Pallas kernels: 122 us -> 113 us
  starting transfers between devices: 55.1 us -> 51.8 us
    all_to_all x5 -> x4, waiting for transfers between devices: 35.3 us -> 14.1 us  [share(): return lax.all_to_all(copies, ('dp', 'tensor'), 0, 0)]
    ppermute x39 -> x28, waiting for transfers between devices: 33.6 us -> 24 us  [swap(): lax.ppermute(value, 'tensor', [(i, i ^ partner) for i in range(partners)])]
    pallas_call x1, Pallas kernels: 19.8 us -> 14 us  [local(): pl.pallas_call(functools.partial(middle_kernel, partners), grid=(images_e...]
    slice x15 -> x0, local copies, waits for them, and re-layouts: 4.06 us -> none  [the longest x2 2.38 us: after(): return value + (earlier[(0,) * earlier.ndim] * 0.0).astype(value.dtype)]
    select_n x9 -> x0, other arithmetic: 3.86 us -> none  [gather(): value = jnp.where(position & bit == 0, low, high)]
    rev x2 -> x0, local copies, waits for them, and re-layouts: 3.56 us -> none  [spread_filter(): ahead.reshape(3, C, 3, C)[::-1, :, ::-1]]
    transpose x7 -> x0, local copies, waits for them, and re-layouts: 3.35 us -> none  [the longest x2 1.59 us: spread_filter(): ahead = jnp.transpose(full, (1, 0, 2, 3)).reshape(3 * C, 3 * C)]
    unnamed x108 -> x54, local copies, waits for them, and re-layouts: 5.56 us -> 8.84 us
  transfers between devices with their start and end apart: 46 -> 34, of which waited for: 13 -> 13; matrix products, arithmetic and copies ran while one was open for 10% -> 3% of each run, Pallas kernels for 14% -> 35%
where the time goes in v2:
time: 220 us; the launch traced here: 219 us
  Pallas kernels  113 us (51%)
  starting transfers between devices  51.8 us (24%)
  waiting for transfers between devices  39.9 us (18%)
  local copies, waits for them, and re-layouts  12.8 us (6%)
    pallas_call x4, Pallas kernels, local(): pl.pallas_call(functools.partial(last_kernel, partners, near, first, fina...  27.2 us
    ppermute x28, starting transfers between devices, swap(): lax.ppermute(value, 'tensor', [(i, i ^ partner) for i in range(partners)])  24.3 us
    ppermute x28, waiting for transfers between devices, swap(): lax.ppermute(value, 'tensor', [(i, i ^ partner) for i in range(partners)])  24 us
    pallas_call x3, Pallas kernels, local(): pl.pallas_call(functools.partial(first_conv_kernel, partners, first, fina...  17.6 us
    pallas_call x1, Pallas kernels, local(): pl.pallas_call(back_kernel, grid=(images_each // pair,), in_specs=[smem()...  15.9 us
    all_to_all x4, starting transfers between devices, share(): return lax.all_to_all(copies, ('dp', 'tensor'), 0, 0)  15.7 us
    all_to_all x4, waiting for transfers between devices, share(): return lax.all_to_all(copies, ('dp', 'tensor'), 0, 0)  14.1 us
    pallas_call x1, Pallas kernels, local(): pl.pallas_call(functools.partial(middle_kernel, partners), grid=(images_e...  14 us
  transfers between devices with their start and end apart: 34, of which 13 were waited for; matrix products, arithmetic and copies ran while one was open for 3% of the time, Pallas kernels for 35%

profile of v2, /device:TPU:0, one launch (start us, length us, event | category | flops | bytes accessed | tf_op | source)
XLA Modules:
  0.0 219.3 jit_solution(5563585100276277832)
XLA Ops:
  0.6 2.5 %pack.4 = (bf16[4,32,1764]{2,1,0:T(8,128)(2,1)}, bf16[4,32,1764]{2,1,0:T(8,128)(2,1)}) custom-call(s32[1]{0:T(128)} %bitcast.me_ref, bf16[32,32,1764]{2,1,0:T(8,128)(2,1)} %maps_ref.7), custom_call_target="tpu_custom_call" | custom-call | flops 2750000128 | bytes 8750000 | tf_op jit(solution)/shard_map/pack/pallas_call | solution.py:730
  4.8 3.0 %collective-permute-start.1 = (bf16[240,384]{1,0:T(8,128)(2,1)}, bf16[240,384]{1,0:T(8,128)(2,1)}, u32[]{:S(2)}, u32[]{:S(2)}) collective-permute-start(bf16[240,384]{1,0:T(8,128)(2,1)} %bundle.1.refs_0_), channel_id=1, source_target_pairs={{0,2},{1,3},{2,0},{3,1},{4,6},{5,7},{6,4},{7,5},{8,10},{9,11},{10,... | collective-permute-start | bytes 552968 | tf_op jit(solution)/shard_map/ppermute | solution.py:812
  8.0 2.7 %pack.5 = (bf16[8,32,1764]{2,1,0:T(8,128)(2,1)}, bf16[8,32,1764]{2,1,0:T(8,128)(2,1)}) custom-call(s32[1]{0:T(128)} %bitcast.me_ref, bf16[32,32,1764]{2,1,0:T(8,128)(2,1)} %maps_ref.7, bf16[4,32,1764]{2,1,0:T(8,128)(2,1)} %get-tuple-element.86.refs_4_.refs_0_), custom_call_target="tpu_custom_call" | custom-call | flops 2750000128 | bytes 8750000 | tf_op jit(solution)/shard_map/pack/pallas_call | solution.py:730
  15.2 2.3 %pack.7 = (bf16[2,32,1764]{2,1,0:T(8,128)(2,1)}, bf16[2,32,1764]{2,1,0:T(8,128)(2,1)}) custom-call(s32[1]{0:T(128)} %bitcast.me_ref, bf16[32,32,1764]{2,1,0:T(8,128)(2,1)} %maps_ref.7, bf16[240,384]{1,0:T(8,128)(2,1)} %collective-permute-done.1.refs_2_.refs_0_), custom_call_target="tpu_custom_call" | custom-call | flops 2750000128 | bytes 8750000 | tf_op jit(solution)/shard_map/pack/pallas_call | solution.py:730
  19.5 2.4 %unbundle.1 = (bf16[384,384]{1,0:T(8,128)(2,1)}, bf16[384,384]{1,0:T(8,128)(2,1)}, bf16[384,384]{1,0:T(8,128)(2,1)}, bf16[384,384]{1,0:T(8,128)(2,1)}, f32[2,128,100]{2,1,0:T(8,128)}, /*index=5*/f32[8,128]{1,0:T(8,128)}) custom-call(s32[1]{0:T(128)} %bitcast.me_ref, s32[1]{0:T(128)} %bitcast.2.task_ref, f32[2,100]{1,0:T(2,128)} %context_ref.1, ...), custom_call_target="tpu_custom_call" | custom-call | flops 2200000000 | bytes 7000000 | tf_op jit(solution)/shard_map/unbundle/pallas_call | solution.py:875
  21.9 11.4 %collective-permute-done.4.refs_0_.refs_2_ = bf16[4,32,1764]{2,1,0:T(8,128)(2,1)} collective-permute-done((bf16[4,32,1764]{2,1,0:T(8,128)(2,1)}, bf16[4,32,1764]{2,1,0:T(8,128)(2,1)}, u32[]{:S(2)}, u32[]{:S(2)}) %collective-permute-start.4) | collective-permute-done | bytes 451616 | tf_op jit(solution)/shard_map/ppermute | solution.py:812
  33.2 2.3 %pack.6 = (bf16[2,32,1764]{2,1,0:T(8,128)(2,1)}, bf16[2,32,1764]{2,1,0:T(8,128)(2,1)}) custom-call(s32[1]{0:T(128)} %bitcast.me_ref, bf16[32,32,1764]{2,1,0:T(8,128)(2,1)} %maps_ref.7, bf16[4,32,1764]{2,1,0:T(8,128)(2,1)} %collective-permute-done.4.refs_0_.refs_2_), custom_call_target="tpu_custom_call" | custom-call | flops 2750000128 | bytes 8750000 | tf_op jit(solution)/shard_map/pack/pallas_call | solution.py:730
  38.6 8.0 %first_conv.3 = (f32[8,128,1792]{2,1,0:T(8,128)}, bf16[8,128,1792]{2,1,0:T(8,128)(2,1)}, f32[128,128]{1,0:T(8,128)}) custom-call(s32[1]{0:T(128)} %bitcast.me_ref, f32[8]{0:T(128)} %compare_convert_fusion.live_ref, f32[8,128]{1,0:T(8,128)} %pad.4.told_ref, bf16[384,384]{1,0:T(8,128)(2,1)} %get-tuple-element.87.weights_ref, ...), custom_call_target="tpu_custom_call" | custom-call | flops 10119999488 | bytes 32200000 | tf_op jit(solution)/shard_map/first_conv/pallas_call | solution.py:904
  46.7 4.8 %first_conv.4 = (f32[8,128,1792]{2,1,0:T(8,128)}, bf16[8,128,1792]{2,1,0:T(8,128)(2,1)}, f32[128,128]{1,0:T(8,128)}) custom-call(s32[1]{0:T(128)} %bitcast.me_ref, f32[8]{0:T(128)} %compare_convert_fusion.live_ref, f32[8,128]{1,0:T(8,128)} %pad.4.told_ref, ...), custom_call_target="tpu_custom_call", output_to_operand_aliasing={{0}: (9, {}), {1}: (10, {})} | custom-call | flops 5059999744 | bytes 16099999 | tf_op jit(solution)/shard_map/first_conv/pallas_call | solution.py:904
  52.1 4.8 %first_conv.5 = (f32[8,128,1792]{2,1,0:T(8,128)}, bf16[8,128,1792]{2,1,0:T(8,128)(2,1)}, f32[32,4,128]{2,1,0:T(4,128)}) custom-call(s32[1]{0:T(128)} %bitcast.me_ref, f32[8]{0:T(128)} %compare_convert_fusion.live_ref, f32[8,128]{1,0:T(8,128)} %pad.4.told_ref, ...), custom_call_target="tpu_custom_call", output_to_operand_aliasing={{0}: (9, {}), {1}: (10, {})} | custom-call | flops 5059999744 | bytes 16099999 | tf_op jit(solution)/shard_map/first_conv/pallas_call | solution.py:904
  56.9 6.3 %all-to-all-start = ((f32[32,4,128]{2,1,0:T(4,128)}), f32[32,4,128]{2,1,0:T(4,128)S(1)}, u32[]{:S(2)}, u32[]{:S(2)}) async-start(f32[32,4,128]{2,1,0:T(4,128)} %get-tuple-element.101), calls=%async_computation | async-start | bytes 131072 | tf_op jit(solution)/shard_map/all_to_all | solution.py:815
  63.1 7.2 %all-to-all-done.heard_ref.heard_two_ref = f32[32,4,128]{2,1,0:T(4,128)S(1)} async-done(((f32[32,4,128]{2,1,0:T(4,128)}), f32[32,4,128]{2,1,0:T(4,128)S(1)}, u32[]{:S(2)}, u32[]{:S(2)}) %all-to-all-start) | async-done | bytes 65568 | tf_op jit(solution)/shard_map/all_to_all | solution.py:815
  71.0 14.0 %middle.1 = (bf16[8,32,441]{2,1,0:T(8,128)(2,1)}, bf16[8,32,441]{2,1,0:T(8,128)(2,1)}, bf16[8,32,441]{2,1,0:T(8,128)(2,1)}, bf16[8,32,441]{2,1,0:T(8,128)(2,1)},...) custom-call(s32[1]{0:T(128)} %bitcast.me_ref, ...), custom_call_target="tpu_custom_call" | custom-call | flops 17600000000 | bytes 56000000 | tf_op jit(solution)/shard_map/middle/pallas_call | solution.py:936
  85.0 2.6 %all-to-all-start.1 = ((f32[32,4,128]{2,1,0:T(4,128)}), f32[32,4,128]{2,1,0:T(4,128)S(1)}, u32[]{:S(2)}, u32[]{:S(2)}) async-start(f32[32,4,128]{2,1,0:T(4,128)} %get-tuple-element.107.own_ref), calls=%async_computation.1 | async-start | bytes 131072 | tf_op jit(solution)/shard_map/all_to_all | solution.py:815
  95.6 6.0 %top.1 = (bf16[8,32,100]{2,1,0:T(8,128)(2,1)}, bf16[8,32,100]{2,1,0:T(8,128)(2,1)}, bf16[8,32,100]{2,1,0:T(8,128)(2,1)}, bf16[8,32,100]{2,1,0:T(8,128)(2,1)}, f3...) custom-call(s32[1]{0:T(128)} %bitcast.me_ref, ...), custom_call_target="tpu_custom_call" | custom-call | flops 7040000000 | bytes 22400000 | tf_op jit(solution)/shard_map/top/pallas_call | solution.py:979
  101.7 4.1 %all-to-all-start.2 = ((f32[32,4,128]{2,1,0:T(4,128)}), f32[32,4,128]{2,1,0:T(4,128)S(1)}, u32[]{:S(2)}, u32[]{:S(2)}) async-start(f32[32,4,128]{2,1,0:T(4,128)} %get-tuple-element.116), calls=%async_computation.2 | async-start | bytes 131072 | tf_op jit(solution)/shard_map/all_to_all | solution.py:815
  107.9 5.3 %all-to-all-done.2.heard_ref.heard_top_ref = f32[32,4,128]{2,1,0:T(4,128)S(1)} async-done(((f32[32,4,128]{2,1,0:T(4,128)}), f32[32,4,128]{2,1,0:T(4,128)S(1)}, u32[]{:S(2)}, u32[]{:S(2)}) %all-to-all-start.2) | async-done | bytes 65568 | tf_op jit(solution)/shard_map/all_to_all | solution.py:815
  113.9 15.9 %back.1 = (bf16[8,128,1792]{2,1,0:T(8,128)(2,1)}, bf16[8,128,1792]{2,1,0:T(8,128)(2,1)}, f32[32,4,128]{2,1,0:T(4,128)}, bf16[4,2,3,32,384]{4,3,2,1,0:T(8,128)(2,1)}) custom-call(f32[8]{0:T(128)} %compare_convert_fusion.live_ref, f32[32,4,128]{2,1,0:T(4,128)} %copy-done.8, f32[8,128]{1,0:T(8,128)} %get-tuple-element.117.norm_three_ref, ...), custom_call_target="tpu_custom_call" | custom-call | flops 17600000000 | bytes 56000000 | tf_op jit(solution)/shard_map/back/pallas_call | solution.py:1033
  129.8 2.8 %all-to-all-start.3 = ((f32[32,4,128]{2,1,0:T(4,128)}), f32[32,4,128]{2,1,0:T(4,128)S(1)}, u32[]{:S(2)}, u32[]{:S(2)}) async-start(f32[32,4,128]{2,1,0:T(4,128)} %get-tuple-element.123), calls=%async_computation.3 | async-start | bytes 131072 | tf_op jit(solution)/shard_map/all_to_all | solution.py:815
  134.1 3.2 %collective-permute-done.15.refs_7_.refs_2_ = bf16[8,32,100]{2,1,0:T(8,128)(2,1)S(1)} collective-permute-done((bf16[8,32,100]{2,1,0:T(8,128)(2,1)}, bf16[8,32,100]{2,1,0:T(8,128)(2,1)S(1)}, u32[]{:S(2)}, u32[]{:S(2)}) %collective-permute-start.15) | collective-permute-done | bytes 51232 | tf_op jit(solution)/shard_map/ppermute | solution.py:812
  140.4 6.7 %last.4 = (bf16[8,32,1764]{2,1,0:T(8,128)(2,1)}, bf16[8,32,1764]{2,1,0:T(8,128)(2,1)}, bf16[2,32,1764]{2,1,0:T(8,128)(2,1)}, bf16[2,32,1764]{2,1,0:T(8,128)(2,1)}, f32[384,384]{1,0:T(8,128)}) custom-call(s32[1]{0:T(128)} %bitcast.me_ref, f32[8]{0:T(128)} %compare_convert_fusion.live_ref, f32[32,4,128]{2,1,0:T(4,128)} %copy-done.9, ...), custom_call_target="tpu_custom_call" | custom-call | flops 5500000256 | bytes 17500000 | tf_op jit(solution)/shard_map/last/pallas_call | solution.py:1124
  149.0 6.9 %last.5 = (bf16[8,32,1764]{2,1,0:T(8,128)(2,1)}, bf16[8,32,1764]{2,1,0:T(8,128)(2,1)}, bf16[2,32,1764]{2,1,0:T(8,128)(2,1)}, bf16[2,32,1764]{2,1,0:T(8,128)(2,1)}, f32[384,384]{1,0:T(8,128)}) custom-call(s32[1]{0:T(128)} %bitcast.me_ref, f32[8]{0:T(128)} %compare_convert_fusion.live_ref, ...), custom_call_target="tpu_custom_call", output_to_operand_aliasing={{0}: (10, {}), {1}: (11, {})} | custom-call | flops 5500000256 | bytes 17500000 | tf_op jit(solution)/shard_map/last/pallas_call | solution.py:1124
  158.6 6.9 %last.6 = (bf16[8,32,1764]{2,1,0:T(8,128)(2,1)}, bf16[8,32,1764]{2,1,0:T(8,128)(2,1)}, bf16[2,32,1764]{2,1,0:T(8,128)(2,1)}, bf16[2,32,1764]{2,1,0:T(8,128)(2,1)}, f32[384,384]{1,0:T(8,128)}) custom-call(s32[1]{0:T(128)} %bitcast.me_ref, f32[8]{0:T(128)} %compare_convert_fusion.live_ref, ...), custom_call_target="tpu_custom_call", output_to_operand_aliasing={{0}: (11, {}), {1}: (12, {})} | custom-call | flops 5500000256 | bytes 17500000 | tf_op jit(solution)/shard_map/last/pallas_call | solution.py:1124
  168.1 6.8 %last.7 = (bf16[8,32,1764]{2,1,0:T(8,128)(2,1)}, bf16[8,32,1764]{2,1,0:T(8,128)(2,1)}, bf16[2,32,1764]{2,1,0:T(8,128)(2,1)}, bf16[2,32,1764]{2,1,0:T(8,128)(2,1)}, bf16[4,2,3,32,384]{4,3,2,1,0:T(8,128)(2,1)}) custom-call(s32[1]{0:T(128)} %bitcast.me_ref, ...), custom_call_target="tpu_custom_call", output_to_operand_aliasing={{0}: (14, {}), {1}: (15, {}), {4}: (13, {})} | custom-call | flops 5500000256 | bytes 17500000 | tf_op jit(solution)/shard_map/last/pallas_call | solution.py:1124
  174.8 5.8 %all-to-all-start.4 = ((bf16[32,24,384]{2,1,0:T(8,128)(2,1)}), bf16[32,24,384]{2,1,0:T(8,128)(2,1)}, u32[]{:S(2)}, u32[]{:S(2)}) async-start(bf16[32,24,384]{2,1,0:T(8,128)(2,1)} %bitcast.41), calls=%async_computation.4 | async-start | bytes 1179648 | tf_op jit(solution)/shard_map/all_to_all | solution.py:1176
  180.6 2.5 %finish.1 = (f32[2,32,100]{2,1,0:T(8,128)}, f32[2,32]{1,0:T(2,128)}, f32[2,100]{1,0:T(2,128)}, f32[8,32]{1,0:T(8,128)}, f32[1,128]{1,0:T(1,128)}) custom-call(s32[1]{0:T(128)} %bitcast.17.here_ref, s32[1]{0:T(128)} %bitcast.me_ref, f32[32,4,128]{2,1,0:T(4,128)} %copy-done.7, f32[32,4,128]{2,1,0:T(4,128)} %copy-done.8, f32[32,4,128]{2,1,0:T(4,128)} %copy-done.9, ...), custom_call_target="tpu_custom_call" | custom-call | flops 2200000000 | bytes 7000000 | tf_op jit(solution)/shard_map/finish/pallas_call | solution.py:1188
  189.7 2.4 %unpack.8.refs_1_ = f32[32,32,1764]{2,1,0:T(8,128)} custom-call(s32[1]{0:T(128)} %bitcast.me_ref, bf16[8,32,1764]{2,1,0:T(8,128)(2,1)} %get-tuple-element.141.refs_4_.refs_6_.refs_0_, bf16[2,32,1764]{2,1,0:T(8,128)(2,1)} %copy-done.2, bf16[2,32,1764]{2,1,0:T(8,128)(2,1)} %copy-done, bf16[2,32,1764]{2,1,0:T(8,128)(2,1)} %copy-done.1), custom_call_target="tpu_custom_call" | custom-call | flops 2200000000 | bytes 7000000 | tf_op jit(solution)/shard_map/unpack/pallas_call | solution.py:770
  192.1 3.3 %collective-permute-done.22.refs_5_.refs_7_.refs_2_ = bf16[2,32,1764]{2,1,0:T(8,128)(2,1)S(1)} collective-permute-done((bf16[2,32,1764]{2,1,0:T(8,128)(2,1)}, bf16[2,32,1764]{2,1,0:T(8,128)(2,1)S(1)}, u32[]{:S(2)}, u32[]{:S(2)}) %collective-permute-start.22) | collective-permute-done | bytes 225824 | tf_op jit(solution)/shard_map/ppermute | solution.py:812
  201.9 6.0 %all-to-all-start.5 = ((f32[8,24,384]{2,1,0:T(8,128)}), f32[8,24,384]{2,1,0:T(8,128)S(1)}, u32[]{:S(2)}, u32[]{:S(2)}) async-start(f32[8,24,384]{2,1,0:T(8,128)} %strips.1), calls=%async_computation.5 | async-start | bytes 589824 | tf_op jit(solution)/shard_map/all_to_all | solution.py:1184
  207.9 2.4 %unpack.9.refs_4_ = f32[32,32,1764]{2,1,0:T(8,128)} custom-call(s32[1]{0:T(128)} %bitcast.me_ref, bf16[8,32,1764]{2,1,0:T(8,128)(2,1)} %collective-permute-done.27.refs_0_, f32[32,32,1764]{2,1,0:T(8,128)} %unpack.8.refs_1_), custom_call_target="tpu_custom_call", output_to_operand_aliasing={{}: (2, {})} | custom-call | flops 2200000000 | bytes 7000000 | tf_op jit(solution)/shard_map/unpack/pallas_call | solution.py:770
  210.3 2.5 %unpack.10.refs_4_ = f32[32,32,1764]{2,1,0:T(8,128)} custom-call(s32[1]{0:T(128)} %bitcast.me_ref, bf16[2,32,1764]{2,1,0:T(8,128)(2,1)} %copy-done.4, bf16[2,32,1764]{2,1,0:T(8,128)(2,1)} %copy-done.1, bf16[2,32,1764]{2,1,0:T(8,128)(2,1)} %copy-done.2, bf16[2,32,1764]{2,1,0:T(8,128)(2,1)} %collective-permute-done.26.refs_3_, ...), custom_call_target="tpu_custom_call", output_to_operand_aliasing={{}: (5, {})} | custom-call | flops 2200000000 | bytes 7000000 | tf_op jit(solution)/shard_map/unpack/pallas_call | solution.py:770
  213.4 2.4 %unpack.11 = f32[32,32,1764]{2,1,0:T(8,128)} custom-call(s32[1]{0:T(128)} %bitcast.me_ref, bf16[2,32,1764]{2,1,0:T(8,128)(2,1)} %collective-permute-done.21.refs_2_.refs_0_, bf16[2,32,1764]{2,1,0:T(8,128)(2,1)} %copy-done, bf16[2,32,1764]{2,1,0:T(8,128)(2,1)} %copy-done.5, bf16[2,32,1764]{2,1,0:T(8,128)(2,1)} %copy-done.6, ...), custom_call_target="tpu_custom_call", output_to_operand_aliasing={{}: (5, {})} | custom-call | flops 2200000000 | bytes 7000000 | tf_op jit(solution)/shard_map/unpack/pallas_call | solution.py:770
  (123 shorter events, 52.4 us)
Async XLA Ops:
  4.8 10.2 %collective-permute-start.1 = (bf16[240,384]{1,0:T(8,128)(2,1)}, bf16[240,384]{1,0:T(8,128)(2,1)}, u32[]{:S(2)}, u32[]{:S(2)}) collective-permute-start(bf16[240,384]{1,0:T(8,128)(2,1)} %bundle.1.refs_0_), channel_id=1, source_target_pairs={{0,2},{1,3},{2,0},{3,1},{4,6},{5,7},{6,4},{7,5},{8,10},{9,11},{10,... | collective-permute-start | bytes 552968 | tf_op jit(solution)/shard_map/ppermute | solution.py:812
  7.8 9.7 %collective-permute-start = (bf16[240,384]{1,0:T(8,128)(2,1)}, bf16[240,384]{1,0:T(8,128)(2,1)}, u32[]{:S(2)}, u32[]{:S(2)}) collective-permute-start(bf16[240,384]{1,0:T(8,128)(2,1)} %bundle.1.refs_0_), channel_id=1, source_target_pairs={{0,1},{1,0},{2,3},{3,2},{4,5},{5,4},{6,7},{7,6},{8,9},{9,8},{10,11... | collective-permute-start | bytes 552968 | tf_op jit(solution)/shard_map/ppermute | solution.py:812
  7.8 27.7 %collective-permute-start.9 = (bf16[4,32,1764]{2,1,0:T(8,128)(2,1)}, bf16[4,32,1764]{2,1,0:T(8,128)(2,1)}, u32[]{:S(2)}, u32[]{:S(2)}) collective-permute-start(bf16[4,32,1764]{2,1,0:T(8,128)(2,1)} %get-tuple-element.86.refs_4_.refs_0_), channel_id=1, source_target_pairs={{0,3},{1,2},{2,1},{3,0},{4,7},{5,6},{6,5},{7,4},{8,11},{9,10},{10,... | collective-permute-start | bytes 1354760 | tf_op jit(solution)/shard_map/ppermute | solution.py:812
  10.7 27.0 %collective-permute-start.3 = (bf16[8,32,1764]{2,1,0:T(8,128)(2,1)}, bf16[8,32,1764]{2,1,0:T(8,128)(2,1)S(1)}, u32[]{:S(2)}, u32[]{:S(2)}) collective-permute-start(bf16[8,32,1764]{2,1,0:T(8,128)(2,1)} %get-tuple-element.89), channel_id=1, source_target_pairs={{0,1},{1,0},{2,3},{3,2},{4,5},{5,4},{6,7},{7,6},{8,9},{9,8},{10,11... | collective-permute-start | bytes 2709512 | tf_op jit(solution)/shard_map/ppermute | solution.py:812
  11.0 22.2 %collective-permute-start.4 = (bf16[4,32,1764]{2,1,0:T(8,128)(2,1)}, bf16[4,32,1764]{2,1,0:T(8,128)(2,1)}, u32[]{:S(2)}, u32[]{:S(2)}) collective-permute-start(bf16[4,32,1764]{2,1,0:T(8,128)(2,1)} %get-tuple-element.90), channel_id=1, source_target_pairs={{0,2},{1,3},{2,0},{3,1},{4,6},{5,7},{6,4},{7,5},{8,10},{9,11},{10,... | collective-permute-start | bytes 1354760 | tf_op jit(solution)/shard_map/ppermute | solution.py:812
  15.0 3.1 %collective-permute-start.2 = (bf16[240,384]{1,0:T(8,128)(2,1)}, bf16[240,384]{1,0:T(8,128)(2,1)}, u32[]{:S(2)}, u32[]{:S(2)}) collective-permute-start(bf16[240,384]{1,0:T(8,128)(2,1)} %collective-permute-done.1.refs_2_.refs_0_), channel_id=1, source_target_pairs={{0,1},{1,0},{2,3},{3,2},{4,5},{5,4},{6,7},{7,6},{8,9},{9,8},{10,11... | collective-permute-start | bytes 552968 | tf_op jit(solution)/shard_map/ppermute | solution.py:812
  17.5 29.1 %collective-permute-start.8 = (bf16[2,32,1764]{2,1,0:T(8,128)(2,1)}, bf16[2,32,1764]{2,1,0:T(8,128)(2,1)}, u32[]{:S(2)}, u32[]{:S(2)}) collective-permute-start(bf16[2,32,1764]{2,1,0:T(8,128)(2,1)} %get-tuple-element.94.refs_4_), channel_id=1, source_target_pairs={{0,3},{1,2},{2,1},{3,0},{4,7},{5,6},{6,5},{7,4},{8,11},{9,10},{10,... | collective-permute-start | bytes 677384 | tf_op jit(solution)/shard_map/ppermute | solution.py:812
  18.1 28.6 %collective-permute-start.7 = (bf16[2,32,1764]{2,1,0:T(8,128)(2,1)}, bf16[2,32,1764]{2,1,0:T(8,128)(2,1)}, u32[]{:S(2)}, u32[]{:S(2)}) collective-permute-start(bf16[2,32,1764]{2,1,0:T(8,128)(2,1)} %get-tuple-element.93), channel_id=1, source_target_pairs={{0,2},{1,3},{2,0},{3,1},{4,6},{5,7},{6,4},{7,5},{8,10},{9,11},{10,... | collective-permute-start | bytes 677384 | tf_op jit(solution)/shard_map/ppermute | solution.py:812
  35.5 15.9 %collective-permute-start.6 = (bf16[2,32,1764]{2,1,0:T(8,128)(2,1)}, bf16[2,32,1764]{2,1,0:T(8,128)(2,1)}, u32[]{:S(2)}, u32[]{:S(2)}) collective-permute-start(bf16[2,32,1764]{2,1,0:T(8,128)(2,1)} %get-tuple-element.92.refs_7_), channel_id=1, source_target_pairs={{0,3},{1,2},{2,1},{3,0},{4,7},{5,6},{6,5},{7,4},{8,11},{9,10},{10,... | collective-permute-start | bytes 677384 | tf_op jit(solution)/shard_map/ppermute | solution.py:812
  35.5 16.6 %collective-permute-start.5 = (bf16[2,32,1764]{2,1,0:T(8,128)(2,1)}, bf16[2,32,1764]{2,1,0:T(8,128)(2,1)}, u32[]{:S(2)}, u32[]{:S(2)}) collective-permute-start(bf16[2,32,1764]{2,1,0:T(8,128)(2,1)} %get-tuple-element.91), channel_id=1, source_target_pairs={{0,2},{1,3},{2,0},{3,1},{4,6},{5,7},{6,4},{7,5},{8,10},{9,11},{10,... | collective-permute-start | bytes 677384 | tf_op jit(solution)/shard_map/ppermute | solution.py:812
  56.9 13.5 %all-to-all-start = ((f32[32,4,128]{2,1,0:T(4,128)}), f32[32,4,128]{2,1,0:T(4,128)S(1)}, u32[]{:S(2)}, u32[]{:S(2)}) async-start(f32[32,4,128]{2,1,0:T(4,128)} %get-tuple-element.101), calls=%async_computation | async-start | bytes 131072 | tf_op jit(solution)/shard_map/all_to_all | solution.py:815
  85.0 10.0 %all-to-all-start.1 = ((f32[32,4,128]{2,1,0:T(4,128)}), f32[32,4,128]{2,1,0:T(4,128)S(1)}, u32[]{:S(2)}, u32[]{:S(2)}) async-start(f32[32,4,128]{2,1,0:T(4,128)} %get-tuple-element.107.own_ref), calls=%async_computation.1 | async-start | bytes 131072 | tf_op jit(solution)/shard_map/all_to_all | solution.py:815
  87.9 4.8 %collective-permute-start.13 = (bf16[8,32,100]{2,1,0:T(8,128)(2,1)S(1)}, bf16[8,32,100]{2,1,0:T(8,128)(2,1)S(1)}, u32[]{:S(2)}, u32[]{:S(2)}) collective-permute-start(bf16[8,32,100]{2,1,0:T(8,128)(2,1)S(1)} %bitcast.44), channel_id=1, source_target_pairs={{0,2},{1,3},{2,0},{3,1},{4,6},{5,7},{6,4},{7,5},{8,10},{9,11},{10,... | collective-permute-start | bytes 153608 | tf_op jit(solution)/shard_map/ppermute | solution.py:812
  89.7 4.5 %collective-permute-start.14 = (bf16[8,32,100]{2,1,0:T(8,128)(2,1)S(1)}, bf16[8,32,100]{2,1,0:T(8,128)(2,1)S(1)}, u32[]{:S(2)}, u32[]{:S(2)}) collective-permute-start(bf16[8,32,100]{2,1,0:T(8,128)(2,1)S(1)} %bitcast.45), channel_id=1, source_target_pairs={{0,3},{1,2},{2,1},{3,0},{4,7},{5,6},{6,5},{7,4},{8,11},{9,10},{10,... | collective-permute-start | bytes 153608 | tf_op jit(solution)/shard_map/ppermute | solution.py:812
  101.7 11.6 %all-to-all-start.2 = ((f32[32,4,128]{2,1,0:T(4,128)}), f32[32,4,128]{2,1,0:T(4,128)S(1)}, u32[]{:S(2)}, u32[]{:S(2)}) async-start(f32[32,4,128]{2,1,0:T(4,128)} %get-tuple-element.116), calls=%async_computation.2 | async-start | bytes 131072 | tf_op jit(solution)/shard_map/all_to_all | solution.py:815
  105.7 33.3 %collective-permute-start.10 = (bf16[8,32,441]{2,1,0:T(8,128)(2,1)}, bf16[8,32,441]{2,1,0:T(8,128)(2,1)S(1)}, u32[]{:S(2)}, u32[]{:S(2)}) collective-permute-start(bf16[8,32,441]{2,1,0:T(8,128)(2,1)} %get-tuple-element.105), channel_id=1, source_target_pairs={{0,2},{1,3},{2,0},{3,1},{4,6},{5,7},{6,4},{7,5},{8,10},{9,11},{10,... | collective-permute-start | bytes 677384 | tf_op jit(solution)/shard_map/ppermute | solution.py:812
  107.6 31.4 %collective-permute-start.11 = (bf16[8,32,441]{2,1,0:T(8,128)(2,1)}, bf16[8,32,441]{2,1,0:T(8,128)(2,1)S(1)}, u32[]{:S(2)}, u32[]{:S(2)}) collective-permute-start(bf16[8,32,441]{2,1,0:T(8,128)(2,1)} %get-tuple-element.106), channel_id=1, source_target_pairs={{0,3},{1,2},{2,1},{3,0},{4,7},{5,6},{6,5},{7,4},{8,11},{9,10},{10,... | collective-permute-start | bytes 677384 | tf_op jit(solution)/shard_map/ppermute | solution.py:812
  107.6 31.5 %collective-permute-start.17 = (bf16[8,32,441]{2,1,0:T(8,128)(2,1)}, bf16[8,32,441]{2,1,0:T(8,128)(2,1)S(1)}, u32[]{:S(2)}, u32[]{:S(2)}) collective-permute-start(bf16[8,32,441]{2,1,0:T(8,128)(2,1)} %get-tuple-element.113), channel_id=1, source_target_pairs={{0,1},{1,0},{2,3},{3,2},{4,5},{5,4},{6,7},{7,6},{8,9},{9,8},{10,11... | collective-permute-start | bytes 677384 | tf_op jit(solution)/shard_map/ppermute | solution.py:812
  129.8 10.0 %all-to-all-start.3 = ((f32[32,4,128]{2,1,0:T(4,128)}), f32[32,4,128]{2,1,0:T(4,128)S(1)}, u32[]{:S(2)}, u32[]{:S(2)}) async-start(f32[32,4,128]{2,1,0:T(4,128)} %get-tuple-element.123), calls=%async_computation.3 | async-start | bytes 131072 | tf_op jit(solution)/shard_map/all_to_all | solution.py:815
  132.6 4.7 %collective-permute-start.15 = (bf16[8,32,100]{2,1,0:T(8,128)(2,1)}, bf16[8,32,100]{2,1,0:T(8,128)(2,1)S(1)}, u32[]{:S(2)}, u32[]{:S(2)}) collective-permute-start(bf16[8,32,100]{2,1,0:T(8,128)(2,1)} %get-tuple-element.110), channel_id=1, source_target_pairs={{0,2},{1,3},{2,0},{3,1},{4,6},{5,7},{6,4},{7,5},{8,10},{9,11},{10,... | collective-permute-start | bytes 153608 | tf_op jit(solution)/shard_map/ppermute | solution.py:812
  134.1 4.9 %collective-permute-start.16 = (bf16[8,32,100]{2,1,0:T(8,128)(2,1)}, bf16[8,32,100]{2,1,0:T(8,128)(2,1)S(1)}, u32[]{:S(2)}, u32[]{:S(2)}) collective-permute-start(bf16[8,32,100]{2,1,0:T(8,128)(2,1)} %get-tuple-element.111), channel_id=1, source_target_pairs={{0,3},{1,2},{2,1},{3,0},{4,7},{5,6},{6,5},{7,4},{8,11},{9,10},{10,... | collective-permute-start | bytes 153608 | tf_op jit(solution)/shard_map/ppermute | solution.py:812
  147.1 10.8 %collective-permute-start.19 = (bf16[2,32,1764]{2,1,0:T(8,128)(2,1)}, bf16[2,32,1764]{2,1,0:T(8,128)(2,1)S(1)}, u32[]{:S(2)}, u32[]{:S(2)}) collective-permute-start(bf16[2,32,1764]{2,1,0:T(8,128)(2,1)} %get-tuple-element.132), channel_id=1, source_target_pairs={{0,2},{1,3},{2,0},{3,1},{4,6},{5,7},{6,4},{7,5},{8,10},{9,11},{10,... | collective-permute-start | bytes 677384 | tf_op jit(solution)/shard_map/ppermute | solution.py:812
  155.9 11.5 %collective-permute-start.20 = (bf16[2,32,1764]{2,1,0:T(8,128)(2,1)}, bf16[2,32,1764]{2,1,0:T(8,128)(2,1)S(1)}, u32[]{:S(2)}, u32[]{:S(2)}) collective-permute-start(bf16[2,32,1764]{2,1,0:T(8,128)(2,1)} %get-tuple-element.136), channel_id=1, source_target_pairs={{0,2},{1,3},{2,0},{3,1},{4,6},{5,7},{6,4},{7,5},{8,10},{9,11},{10,... | collective-permute-start | bytes 677384 | tf_op jit(solution)/shard_map/ppermute | solution.py:812
  156.2 11.3 %collective-permute-start.21 = (bf16[2,32,1764]{2,1,0:T(8,128)(2,1)S(1)}, bf16[2,32,1764]{2,1,0:T(8,128)(2,1)}, u32[]{:S(2)}, u32[]{:S(2)}) collective-permute-start(bf16[2,32,1764]{2,1,0:T(8,128)(2,1)S(1)} %copy-done.15), channel_id=1, source_target_pairs={{0,3},{1,2},{2,1},{3,0},{4,7},{5,6},{6,5},{7,4},{8,11},{9,10},{10,... | collective-permute-start | bytes 677384 | tf_op jit(solution)/shard_map/ppermute | solution.py:812
  157.2 30.6 %collective-permute-start.24 = (bf16[2,32,1764]{2,1,0:T(8,128)(2,1)}, bf16[2,32,1764]{2,1,0:T(8,128)(2,1)S(1)}, u32[]{:S(2)}, u32[]{:S(2)}) collective-permute-start(bf16[2,32,1764]{2,1,0:T(8,128)(2,1)} %get-tuple-element.148), channel_id=1, source_target_pairs={{0,3},{1,2},{2,1},{3,0},{4,7},{5,6},{6,5},{7,4},{8,11},{9,10},{10,... | collective-permute-start | bytes 677384 | tf_op jit(solution)/shard_map/ppermute | solution.py:812
  165.5 23.5 %collective-permute-start.23 = (bf16[2,32,1764]{2,1,0:T(8,128)(2,1)}, bf16[2,32,1764]{2,1,0:T(8,128)(2,1)S(1)}, u32[]{:S(2)}, u32[]{:S(2)}) collective-permute-start(bf16[2,32,1764]{2,1,0:T(8,128)(2,1)} %get-tuple-element.143), channel_id=1, source_target_pairs={{0,2},{1,3},{2,0},{3,1},{4,6},{5,7},{6,4},{7,5},{8,10},{9,11},{10,... | collective-permute-start | bytes 677384 | tf_op jit(solution)/shard_map/ppermute | solution.py:812
  174.8 25.2 %all-to-all-start.4 = ((bf16[32,24,384]{2,1,0:T(8,128)(2,1)}), bf16[32,24,384]{2,1,0:T(8,128)(2,1)}, u32[]{:S(2)}, u32[]{:S(2)}) async-start(bf16[32,24,384]{2,1,0:T(8,128)(2,1)} %bitcast.41), calls=%async_computation.4 | async-start | bytes 1179648 | tf_op jit(solution)/shard_map/all_to_all | solution.py:1176
  184.5 23.4 %collective-permute-start.27 = (bf16[8,32,1764]{2,1,0:T(8,128)(2,1)}, bf16[8,32,1764]{2,1,0:T(8,128)(2,1)}, u32[]{:S(2)}, u32[]{:S(2)}) collective-permute-start(bf16[8,32,1764]{2,1,0:T(8,128)(2,1)} %get-tuple-element.151), channel_id=1, source_target_pairs={{0,1},{1,0},{2,3},{3,2},{4,5},{5,4},{6,7},{7,6},{8,9},{9,8},{10,11... | collective-permute-start | bytes 2709512 | tf_op jit(solution)/shard_map/ppermute | solution.py:812
  184.7 10.7 %collective-permute-start.22 = (bf16[2,32,1764]{2,1,0:T(8,128)(2,1)}, bf16[2,32,1764]{2,1,0:T(8,128)(2,1)S(1)}, u32[]{:S(2)}, u32[]{:S(2)}) collective-permute-start(bf16[2,32,1764]{2,1,0:T(8,128)(2,1)} %get-tuple-element.142), channel_id=1, source_target_pairs={{0,3},{1,2},{2,1},{3,0},{4,7},{5,6},{6,5},{7,4},{8,11},{9,10},{10,... | collective-permute-start | bytes 677384 | tf_op jit(solution)/shard_map/ppermute | solution.py:812
  187.5 22.8 %collective-permute-start.26 = (bf16[2,32,1764]{2,1,0:T(8,128)(2,1)}, bf16[2,32,1764]{2,1,0:T(8,128)(2,1)}, u32[]{:S(2)}, u32[]{:S(2)}) collective-permute-start(bf16[2,32,1764]{2,1,0:T(8,128)(2,1)} %get-tuple-element.150), channel_id=1, source_target_pairs={{0,2},{1,3},{2,0},{3,1},{4,6},{5,7},{6,4},{7,5},{8,10},{9,11},{10,... | collective-permute-start | bytes 677384 | tf_op jit(solution)/shard_map/ppermute | solution.py:812
  187.8 24.9 %collective-permute-start.25 = (bf16[2,32,1764]{2,1,0:T(8,128)(2,1)}, bf16[2,32,1764]{2,1,0:T(8,128)(2,1)S(1)}, u32[]{:S(2)}, u32[]{:S(2)}) collective-permute-start(bf16[2,32,1764]{2,1,0:T(8,128)(2,1)} %get-tuple-element.149), channel_id=1, source_target_pairs={{0,3},{1,2},{2,1},{3,0},{4,7},{5,6},{6,5},{7,4},{8,11},{9,10},{10,... | collective-permute-start | bytes 677384 | tf_op jit(solution)/shard_map/ppermute | solution.py:812
  201.9 15.8 %all-to-all-start.5 = ((f32[8,24,384]{2,1,0:T(8,128)}), f32[8,24,384]{2,1,0:T(8,128)S(1)}, u32[]{:S(2)}, u32[]{:S(2)}) async-start(f32[8,24,384]{2,1,0:T(8,128)} %strips.1), calls=%async_computation.5 | async-start | bytes 589824 | tf_op jit(solution)/shard_map/all_to_all | solution.py:1184
  (26 other events, 67.1 us)

commit v3 on v2

--- a/solution.py
+++ b/solution.py
@@ -547,11 +547,10 @@
     return norm_back_columns(norm_ref, row(vectors_ref, 0), sums[0:1], sums[1:2])
 
 
-def last_kernel(
+def last_conv_kernel(
     partners,
     near,
     first,
-    final,
     steps,
     me_ref,
     live_ref,
@@ -561,27 +560,22 @@
     weights_ref,
     grad_ref,
     away_ref,
-    maps_ref,
     *refs,
 ):
     far = partners - near
-    before_ref, (filter_ref, product, columns, output, upright, stack) = refs[0], refs[-6:]
-    piece_refs = refs[-6 - near - far * len(steps) : -6]
+    piece_refs, (columns, output, upright) = refs[-3 - near - far * len(steps) : -3], refs[-3:]
     step = pl.program_id(0)
     count = grad_ref.shape[0]
 
     @pl.when(step == 0)
     def _():
         columns[...] = last_columns(heard_ref, norm_ref, vectors_ref)
-        product[...] = before_ref[...] if first else jnp.zeros_like(product)
 
     for image in range(count):
         live = live_ref[first + step * count + image]
         error = norm_back(live, columns, grad_ref[image], away_ref[image], CELLS_TWO)
         stack_upright(cut(error, WIDE), MAP, upright.at[image])
         write(output.at[image], [block.astype(BF16) for block in conv_behind(weights_ref, upright.at[image], MAP)])
-        stack_sideways(cut(maps_ref[image], WIDE), MAP, stack.at[image])
-        product[...] += across_cells(upright.at[image], stack.at[image])
     rows = C // partners
     start = 0
     for place, length in enumerate(steps):
@@ -595,15 +589,30 @@
 
         start += length
 
+
+def last_filter_kernel(live_ref, heard_ref, norm_ref, vectors_ref, grad_ref, away_ref, maps_ref, *refs):
+    filter_ref, product, columns, stack, upright = refs[-5:]
+    step = pl.program_id(0)
+    count = grad_ref.shape[0]
+
+    @pl.when(step == 0)
+    def _():
+        columns[...] = last_columns(heard_ref, norm_ref, vectors_ref)
+        product[...] = jnp.zeros_like(product)
+
+    for image in range(count):
+        error = norm_back(live_ref[step * count + image], columns, grad_ref[image], away_ref[image], CELLS_TWO)
+        stack_upright(cut(error, WIDE), MAP, upright.at[image])
+        stack_sideways(cut(maps_ref[image], WIDE), MAP, stack.at[image])
+        product[...] += across_cells(upright.at[image], stack.at[image])
+
     @pl.when(step == pl.num_programs(0) - 1)
     def _():
-        if final:
-            split_filter(product, filter_ref)
-        else:
-            filter_ref[...] = product[...]
-
-
-def strips_kernel(heard_ref, out_ref):
+        split_filter(product, filter_ref)
+
+
+def strips_kernel(heard_ref, *refs):
+    out_ref = refs[-1]
     out_ref[...] = jnp.broadcast_to(jnp.sum(heard_ref[...].astype(F32), axis=0)[None], out_ref.shape)
 
 
@@ -631,7 +640,7 @@
     film_ref,
     *refs,
 ):
-    film_w_ref, film_b_ref, context_ref, sums_ref, levels_ref, product = refs[-6:]
+    film_w_ref, film_b_ref, context_ref, *sum_refs, levels_ref, product = refs[-9:]
     devices = heard_two_ref.shape[0]
     tasks = devices // group
     contexts = context_ref.shape[0]
@@ -661,7 +670,8 @@
 
     back = jnp.sum(heard_back_ref[...], axis=0)
     top = jnp.sum(heard_top_ref[...], axis=0)
-    sums_ref[...] = own_lanes(row_tile([back[1:2], back[0:1], top[3:4], top[2:3]]))
+    for sum_ref, sums in zip(sum_refs, (back[1:2], back[0:1], top[3:4], top[2:3])):
+        sum_ref[...] = own_lanes(sums)[0]
 
     live = norm_two_ref[3:4, 0:1] * (1.0 / CELLS_TWO)
     lanes = lane_ids(C)
@@ -688,7 +698,7 @@
     level = jnp.zeros((1, C), F32)
     for place, value in enumerate(known):
         level = jnp.where(lanes == place, value, level)
-    levels_ref[...] = jnp.sqrt(level)
+    levels_ref[...] = jnp.sqrt(level)[0, : levels_ref.shape[0]]
 
 
 def pool_matrix(side, width, out_width):
@@ -749,8 +759,7 @@
 
 def unpack(arrays, me, images_each, dtype, place, outs=(), earlier=()):
     partners = len(arrays[0])
-    span = max(8, images_each) if dtype == F32 else 16
-    group = span // images_each
+    group = CAP // images_each
     halves = 2
     given, specs, counts, shapes, out_specs = [], [], [], [], []
     for pieces in arrays:
@@ -762,7 +771,7 @@
             specs.append(pl.BlockSpec((piece.shape[0], rows // halves, cells), lambda n, me_ref: (0, n, 0)))
         shapes.append(jax.ShapeDtypeStruct((rows, partners * images_each, cells), dtype))
         out_specs.append(
-            pl.BlockSpec((rows // halves, span, cells), lambda n, me_ref: (n, (me_ref[0] // group) ^ place, 0))
+            pl.BlockSpec((rows // halves, CAP, cells), lambda n, me_ref: (n, (me_ref[0] // group) ^ place, 0))
         )
     aliases = {1 + len(given) + k: k for k in range(len(outs))}
     given += [*outs, *earlier]
@@ -801,7 +810,7 @@
     rows, slots = images.shape[:2]
     images_each = slots // partners
     group = CAP // images_each
-    one = 1
+    one = min(images_each, 2)
     pair, some = min(images_each, 2), min(images_each, 4)
     position = lax.axis_index("tensor")
     me = jnp.reshape(position, (1,)).astype(jnp.int32)
@@ -817,7 +826,8 @@
     near = 2
     half, quarter = images_each // 2, images_each // 4
     sizes_in = (half, quarter, quarter) if quarter >= pair else (half, half)
-    calls_out = ((pair,),) * (images_each // pair)
+    half = images_each // 2
+    calls_out = ((pair,) * (half // pair), (half,))
     starts_in = [sum(sizes_in[:part]) for part in range(len(sizes_in))]
     counts_of = [(images_each,) if partner < near else sizes_in for partner in range(partners)]
     far = [partner for partner in reversed(range(partners)) if partner >= near]
@@ -864,7 +874,7 @@
         bit //= 2
 
     sent_in = {
-        part: send_in((part,), False, (bundles[partners // 2] if part == 1 else maps[far[-1]][0],))
+        part: send_in((part,), False, (maps[far[0]][0],))
         for part in range(1, len(sizes_in))
     }
 
@@ -1090,110 +1100,115 @@
 
     returned = [[] for partner in range(partners)]
     waits = [pieces[0] for pieces in (*block_two, *out_pieces)]
+    common = [heard_back, norm_two, vectors]
+    common_specs = [whole(devices, SENT, C), whole(8, C), whole(8, C)]
     kept = []
-    product = vectors
     first = 0
-    for part, sizes in enumerate(calls_out):
+    for sizes in calls_out:
         count = sum(sizes)
-        final = part == len(calls_out) - 1
-        if part == 2:
-            waits = waits + [returned[near][0]]
-        if part == 3:
-            waits = waits + [returned[near][1], *(returned[partner][0] for partner in far)]
-        if final:
-            waits = waits + [filter_sums]
-        size = one
-        steps = [some // size for some in sizes]
-        first_steps = [sum(steps[:place]) for place in range(len(steps))]
-        out_specs = [each(rows, CELLS_TWO, first=first // size, count=size)] * near
+        steps = [some // one for some in sizes]
+        out_specs = [each(rows, CELLS_TWO, first=first // one, count=one)] * near
         out_shape = [jax.ShapeDtypeStruct((images_each, rows, CELLS_TWO), BF16)] * near
-        for start, length in zip(first_steps, steps):
+        for place, length in enumerate(steps):
+            start = sum(steps[:place])
             out_specs += [
                 pl.BlockSpec(
-                    (size, rows, CELLS_TWO),
+                    (one, rows, CELLS_TWO),
                     lambda n, start=start, length=length: (jnp.clip(n - start, 0, length - 1), 0, 0),
                 )
             ] * len(far)
-            out_shape += [jax.ShapeDtypeStruct((length * size, rows, CELLS_TWO), BF16)] * len(far)
-        out_specs.append(filter_spec(0) if final else whole(3 * C, 3 * C))
-        out_shape.append(filter_shape if final else jax.ShapeDtypeStruct((3 * C, 3 * C), F32))
-        inputs = [me, live, heard_back, norm_two, vectors, behind_two, grad_two, away_two, whole_maps, product]
-        aliases = {len(inputs) + len(waits) + k: k for k in range(len(kept))}
-        if final:
-            aliases[len(inputs) + len(waits) - 1] = len(out_shape) - 1
-        *pieces, product = pl.pallas_call(
-            functools.partial(last_kernel, partners, near, first, final, steps),
-            grid=(count // size,),
+            out_shape += [jax.ShapeDtypeStruct((length * one, rows, CELLS_TWO), BF16)] * len(far)
+        inputs = [me, live, *common, behind_two, grad_two, away_two]
+        pieces = pl.pallas_call(
+            functools.partial(last_conv_kernel, partners, near, first, steps),
+            grid=(count // one,),
             in_specs=[
                 smem(),
                 smem(),
-                whole(devices, SENT, C),
-                whole(8, C),
-                whole(8, C),
+                *common_specs,
                 whole(3 * C, 3 * C),
-                *[each(C, LANES_TWO, first=first // size, count=size)] * 3,
-                whole(*product.shape),
+                *[each(C, LANES_TWO, first=first // one, count=one)] * 2,
                 *anywhere(len(waits) + len(kept)),
             ],
             out_specs=out_specs,
             out_shape=out_shape,
             scratch_shapes=[
-                pltpu.VMEM((3 * C, 3 * C), F32),
                 pltpu.VMEM((C, C), F32),
-                pltpu.VMEM((size, C, LANES_TWO), BF16),
-                pltpu.VMEM((size, 3 * C, LANES_TWO), BF16),
-                pltpu.VMEM((size, 3 * C, LANES_TWO), BF16),
+                pltpu.VMEM((one, C, LANES_TWO), BF16),
+                pltpu.VMEM((one, 3 * C, LANES_TWO), BF16),
             ],
-            input_output_aliases=aliases,
+            input_output_aliases={len(inputs) + len(waits) + k: k for k in range(len(kept))},
             compiler_params=kernel_params(),
-            name="last",
-            cost_estimate=lasting(2.5 * count),
+            name="last_conv",
+            cost_estimate=lasting(1.5 * count),
         )(*inputs, *waits, *kept)
         kept, waits, first = pieces[:near], [], first + count
         for place in range(len(sizes)):
             for partner in reversed(far):
                 returned[partner].append(swap(pieces[near + place * len(far) + partner - near], partner))
+        if first < images_each:
+            product = pl.pallas_call(
+                last_filter_kernel,
+                grid=(images_each // pair,),
+                in_specs=[
+                    smem(),
+                    *common_specs,
+                    *[each(C, LANES_TWO, count=pair)] * 3,
+                    *anywhere(2),
+                ],
+                out_specs=filter_spec(0),
+                out_shape=filter_shape,
+                scratch_shapes=[
+                    pltpu.VMEM((3 * C, 3 * C), F32),
+                    pltpu.VMEM((C, C), F32),
+                    pltpu.VMEM((pair, 3 * C, LANES_TWO), BF16),
+                    pltpu.VMEM((pair, 3 * C, LANES_TWO), BF16),
+                ],
+                input_output_aliases={7: 0},
+                compiler_params=kernel_params(),
+                name="last_filter",
+                cost_estimate=lasting(1.2 * images_each),
+            )(live, *common, grad_two, away_two, whole_maps, filter_sums, kept[0])
+            waits = [product, *(piece for partner in far[:-1] for piece in returned[partner]), returned[near][0]]
     for partner in range(near):
         returned[partner].append(swap(kept[partner], partner))
 
-    ahead = (returned[near][-2], *(returned[partner][-3:][0] for partner in far))
-    spans = partners * images_each // max(8, images_each)
-    near_spans = max(1, near * images_each // 8)
-    grad_images = ()
-    for place in [*range(near_spans), *range(near_spans, spans)]:
-        grad_images = unpack(
-            [returned], me, images_each, F32, place, grad_images, () if grad_images else ahead
-        )
-    (grad_images,) = grad_images
-
+    arrivals = [returned[partner][place] for place in range(len(returned[near])) for partner in reversed(far)]
+    count_first = len(far) * len(calls_out[0])
     blocks = ()
     for place in range(partners // group):
-        waits = [kept[0], *(returned[partner][-2] for partner in far)]
-        blocks = unpack([block_two, out_pieces], me, images_each, BF16, place, blocks, waits)
+        blocks = unpack([block_two, out_pieces], me, images_each, BF16, place, blocks, [kept[0]])
     block_two, block_three = blocks
 
     strip = 6 * rows // columns
     heard = lax.all_to_all(product.reshape(devices, strip, 3 * C), ("tensor", "dp"), 0, 0)
     strips = pl.pallas_call(
         strips_kernel,
+        in_specs=[pl.BlockSpec(memory_space=pltpu.VMEM), *anywhere(1)],
         out_shape=jax.ShapeDtypeStruct((columns, strip, 3 * C), F32),
         compiler_params=kernel_params(0),
         name="strips",
         cost_estimate=lasting(1.5),
-    )(heard)
+    )(heard, kept[0])
     strips = lax.all_to_all(strips, "dp", 0, 0).reshape(2, 3, rows, 3, C)
     grad_filters = jnp.transpose(strips, (0, 2, 4, 1, 3))
 
+    grad_images = ()
+    for place in range(partners // group):
+        waits = () if grad_images else (arrivals[count_first],)
+        grad_images = unpack([returned], me, images_each, F32, place, grad_images, waits)
+    (grad_images,) = grad_images
+
     contexts = context.shape[0]
-    grad_film_w, grad_film_b, grad_context, norm_sums, levels = pl.pallas_call(
+    grad_film_w, grad_film_b, grad_context, *norm_sums, levels = pl.pallas_call(
         functools.partial(finish_kernel, partners, group),
         in_specs=[smem(), smem(), *[pl.BlockSpec(memory_space=pltpu.VMEM)] * 7, *anywhere(1)],
         out_shape=[
             jax.ShapeDtypeStruct((2, rows, entries), F32),
             jax.ShapeDtypeStruct((2, rows), F32),
             jax.ShapeDtypeStruct((contexts, entries), F32),
-            jax.ShapeDtypeStruct((8, rows), F32),
-            jax.ShapeDtypeStruct((1, C), F32),
+            *[jax.ShapeDtypeStruct((rows,), F32)] * 4,
+            jax.ShapeDtypeStruct((9,), F32),
         ],
         scratch_shapes=[pltpu.VMEM((C, C), F32)],
         compiler_params=kernel_params(0),
@@ -1224,7 +1239,7 @@
         jnp.transpose(grad_film_w, (2, 0, 1)),
         grad_film_b,
         grad_context,
-        levels[0, :9],
+        levels,
     )
 
 

time: 220 us -> 209 us (0.950)
  Pallas kernels: 113 us -> 107 us
  starting transfers between devices: 51.8 us -> 45.8 us
  waiting for transfers between devices: 39.9 us -> 44.1 us
  local copies, waits for them, and re-layouts: 12.8 us -> 9.13 us
    ppermute x28 -> x26, waiting for transfers between devices: 24 us -> 28.3 us  [swap(): lax.ppermute(value, 'tensor', [(i, i ^ partner) for i in range(partners)])]
    pallas_call x5 -> x4, Pallas kernels: 29.1 us -> 26.1 us  [the longest x2 13.8 us: local(): pl.pallas_call(functools.partial(last_conv_kernel, partners, near, first,...]
    pallas_call x6 -> x4, Pallas kernels: 13.6 us -> 10.7 us  [unpack(): pl.pallas_call(functools.partial(unpack_kernel, counts), grid_spec=pltpu....]
    all_to_all x1, starting transfers between devices: 5.98 us -> 3.42 us  [local(): strips = lax.all_to_all(strips, 'dp', 0, 0).reshape(2, 3, rows, 3, C)]
    squeeze x2 -> x0, local copies, waits for them, and re-layouts: 2.53 us -> none  [the longest x1 1.36 us: local(): norm_sums[3]]
    all_to_all x1, waiting for transfers between devices: 0.01 us -> 2.27 us  [local(): lax.all_to_all(product.reshape(devices, strip, 3 * C), ('tensor', 'dp'),...]
    ppermute x28 -> x26, starting transfers between devices: 24.3 us -> 22.1 us  [swap(): lax.ppermute(value, 'tensor', [(i, i ^ partner) for i in range(partners)])]
    unnamed x54 -> x50, local copies, waits for them, and re-layouts: 8.84 us -> 7.7 us
  transfers between devices with their start and end apart: 34 -> 32, of which waited for: 13 -> 15; matrix products, arithmetic and copies ran while one was open for 3% -> 1% of each run, Pallas kernels for 35% -> 34%
where the time goes in v3:
time: 209 us; the launch traced here: 208 us
  Pallas kernels  107 us (51%)
  starting transfers between devices  45.8 us (22%)
  waiting for transfers between devices  44.1 us (21%)
  local copies, waits for them, and re-layouts  9.13 us (4%)
    ppermute x26, waiting for transfers between devices, swap(): lax.ppermute(value, 'tensor', [(i, i ^ partner) for i in range(partners)])  28.3 us
    ppermute x26, starting transfers between devices, swap(): lax.ppermute(value, 'tensor', [(i, i ^ partner) for i in range(partners)])  22.1 us
    pallas_call x3, Pallas kernels, local(): pl.pallas_call(functools.partial(first_conv_kernel, partners, first, fina...  17.6 us
    pallas_call x1, Pallas kernels, local(): pl.pallas_call(back_kernel, grid=(images_each // pair,), in_specs=[smem()...  15.9 us
    all_to_all x4, starting transfers between devices, share(): return lax.all_to_all(copies, ('dp', 'tensor'), 0, 0)  15.7 us
    pallas_call x1, Pallas kernels, local(): pl.pallas_call(functools.partial(middle_kernel, partners), grid=(images_e...  14 us
    pallas_call x2, Pallas kernels, local(): pl.pallas_call(functools.partial(last_conv_kernel, partners, near, first,...  13.8 us
    all_to_all x4, waiting for transfers between devices, share(): return lax.all_to_all(copies, ('dp', 'tensor'), 0, 0)  13.5 us
  transfers between devices with their start and end apart: 32, of which 15 were waited for; matrix products, arithmetic and copies ran while one was open for 1% of the time, Pallas kernels for 34%

profile of v3, /device:TPU:0, one launch (start us, length us, event | category | flops | bytes accessed | tf_op | source)
XLA Modules:
  0.0 207.8 jit_solution(13346630596204563814)
XLA Ops:
  0.6 2.5 %pack.4 = (bf16[4,32,1764]{2,1,0:T(8,128)(2,1)}, bf16[4,32,1764]{2,1,0:T(8,128)(2,1)}) custom-call(s32[1]{0:T(128)} %bitcast.me_ref, bf16[32,32,1764]{2,1,0:T(8,128)(2,1)} %maps_ref.7), custom_call_target="tpu_custom_call" | custom-call | flops 2750000128 | bytes 8750000 | tf_op jit(solution)/shard_map/pack/pallas_call | solution.py:740
  4.8 3.0 %collective-permute-start.1 = (bf16[240,384]{1,0:T(8,128)(2,1)}, bf16[240,384]{1,0:T(8,128)(2,1)}, u32[]{:S(2)}, u32[]{:S(2)}) collective-permute-start(bf16[240,384]{1,0:T(8,128)(2,1)} %bundle.1.refs_0_), channel_id=1, source_target_pairs={{0,2},{1,3},{2,0},{3,1},{4,6},{5,7},{6,4},{7,5},{8,10},{9,11},{10,... | collective-permute-start | bytes 552968 | tf_op jit(solution)/shard_map/ppermute | solution.py:821
  8.0 2.7 %pack.5 = (bf16[8,32,1764]{2,1,0:T(8,128)(2,1)}, bf16[8,32,1764]{2,1,0:T(8,128)(2,1)}) custom-call(s32[1]{0:T(128)} %bitcast.me_ref, bf16[32,32,1764]{2,1,0:T(8,128)(2,1)} %maps_ref.7, bf16[4,32,1764]{2,1,0:T(8,128)(2,1)} %get-tuple-element.79.refs_4_.refs_0_), custom_call_target="tpu_custom_call" | custom-call | flops 2750000128 | bytes 8750000 | tf_op jit(solution)/shard_map/pack/pallas_call | solution.py:740
  15.9 2.4 %unbundle.1 = (bf16[384,384]{1,0:T(8,128)(2,1)}, bf16[384,384]{1,0:T(8,128)(2,1)}, bf16[384,384]{1,0:T(8,128)(2,1)}, bf16[384,384]{1,0:T(8,128)(2,1)}, f32[2,128,100]{2,1,0:T(8,128)}, /*index=5*/f32[8,128]{1,0:T(8,128)}) custom-call(s32[1]{0:T(128)} %bitcast.me_ref, s32[1]{0:T(128)} %bitcast.2.task_ref, f32[2,100]{1,0:T(2,128)} %context_ref.1, ...), custom_call_target="tpu_custom_call" | custom-call | flops 2200000000 | bytes 7000000 | tf_op jit(solution)/shard_map/unbundle/pallas_call | solution.py:885
  18.3 4.7 %collective-permute-done.4.refs_0_.refs_3_ = bf16[4,32,1764]{2,1,0:T(8,128)(2,1)} collective-permute-done((bf16[4,32,1764]{2,1,0:T(8,128)(2,1)}, bf16[4,32,1764]{2,1,0:T(8,128)(2,1)}, u32[]{:S(2)}, u32[]{:S(2)}) %collective-permute-start.4) | collective-permute-done | bytes 451616 | tf_op jit(solution)/shard_map/ppermute | solution.py:821
  23.0 2.3 %pack.7 = (bf16[2,32,1764]{2,1,0:T(8,128)(2,1)}, bf16[2,32,1764]{2,1,0:T(8,128)(2,1)}) custom-call(s32[1]{0:T(128)} %bitcast.me_ref, bf16[32,32,1764]{2,1,0:T(8,128)(2,1)} %maps_ref.7, bf16[4,32,1764]{2,1,0:T(8,128)(2,1)} %collective-permute-done.4.refs_0_.refs_3_), custom_call_target="tpu_custom_call" | custom-call | flops 2750000128 | bytes 8750000 | tf_op jit(solution)/shard_map/pack/pallas_call | solution.py:740
  27.2 2.3 %pack.6 = (bf16[2,32,1764]{2,1,0:T(8,128)(2,1)}, bf16[2,32,1764]{2,1,0:T(8,128)(2,1)}) custom-call(s32[1]{0:T(128)} %bitcast.me_ref, bf16[32,32,1764]{2,1,0:T(8,128)(2,1)} %maps_ref.7, bf16[4,32,1764]{2,1,0:T(8,128)(2,1)} %collective-permute-done.4.refs_0_.refs_3_), custom_call_target="tpu_custom_call" | custom-call | flops 2750000128 | bytes 8750000 | tf_op jit(solution)/shard_map/pack/pallas_call | solution.py:740
  29.5 3.7 %collective-permute-done.9.refs_2_ = bf16[4,32,1764]{2,1,0:T(8,128)(2,1)} collective-permute-done((bf16[4,32,1764]{2,1,0:T(8,128)(2,1)}, bf16[4,32,1764]{2,1,0:T(8,128)(2,1)}, u32[]{:S(2)}, u32[]{:S(2)}) %collective-permute-start.9) | collective-permute-done | bytes 451616 | tf_op jit(solution)/shard_map/ppermute | solution.py:821
  36.3 8.0 %first_conv.3 = (f32[8,128,1792]{2,1,0:T(8,128)}, bf16[8,128,1792]{2,1,0:T(8,128)(2,1)}, f32[128,128]{1,0:T(8,128)}) custom-call(s32[1]{0:T(128)} %bitcast.me_ref, f32[8]{0:T(128)} %compare_convert_fusion.live_ref, f32[8,128]{1,0:T(8,128)} %pad.4.told_ref, bf16[384,384]{1,0:T(8,128)(2,1)} %get-tuple-element.80.weights_ref, ...), custom_call_target="tpu_custom_call" | custom-call | flops 10119999488 | bytes 32200000 | tf_op jit(solution)/shard_map/first_conv/pallas_call | solution.py:914
  44.3 4.8 %first_conv.4 = (f32[8,128,1792]{2,1,0:T(8,128)}, bf16[8,128,1792]{2,1,0:T(8,128)(2,1)}, f32[128,128]{1,0:T(8,128)}) custom-call(s32[1]{0:T(128)} %bitcast.me_ref, f32[8]{0:T(128)} %compare_convert_fusion.live_ref, f32[8,128]{1,0:T(8,128)} %pad.4.told_ref, ...), custom_call_target="tpu_custom_call", output_to_operand_aliasing={{0}: (9, {}), {1}: (10, {})} | custom-call | flops 5059999744 | bytes 16099999 | tf_op jit(solution)/shard_map/first_conv/pallas_call | solution.py:914
  49.1 2.9 %collective-permute-done.5.refs_2_ = bf16[2,32,1764]{2,1,0:T(8,128)(2,1)} collective-permute-done((bf16[2,32,1764]{2,1,0:T(8,128)(2,1)}, bf16[2,32,1764]{2,1,0:T(8,128)(2,1)}, u32[]{:S(2)}, u32[]{:S(2)}) %collective-permute-start.5) | collective-permute-done | bytes 225824 | tf_op jit(solution)/shard_map/ppermute | solution.py:821
  52.1 4.8 %first_conv.5 = (f32[8,128,1792]{2,1,0:T(8,128)}, bf16[8,128,1792]{2,1,0:T(8,128)(2,1)}, f32[32,4,128]{2,1,0:T(4,128)}) custom-call(s32[1]{0:T(128)} %bitcast.me_ref, f32[8]{0:T(128)} %compare_convert_fusion.live_ref, f32[8,128]{1,0:T(8,128)} %pad.4.told_ref, ...), custom_call_target="tpu_custom_call", output_to_operand_aliasing={{0}: (9, {}), {1}: (10, {})} | custom-call | flops 5059999744 | bytes 16099999 | tf_op jit(solution)/shard_map/first_conv/pallas_call | solution.py:914
  56.9 6.2 %all-to-all-start = ((f32[32,4,128]{2,1,0:T(4,128)}), f32[32,4,128]{2,1,0:T(4,128)S(1)}, u32[]{:S(2)}, u32[]{:S(2)}) async-start(f32[32,4,128]{2,1,0:T(4,128)} %get-tuple-element.94), calls=%async_computation | async-start | bytes 131072 | tf_op jit(solution)/shard_map/all_to_all | solution.py:824
  63.1 7.2 %all-to-all-done.heard_ref.heard_two_ref = f32[32,4,128]{2,1,0:T(4,128)S(1)} async-done(((f32[32,4,128]{2,1,0:T(4,128)}), f32[32,4,128]{2,1,0:T(4,128)S(1)}, u32[]{:S(2)}, u32[]{:S(2)}) %all-to-all-start) | async-done | bytes 65568 | tf_op jit(solution)/shard_map/all_to_all | solution.py:824
  71.0 14.0 %middle.1 = (bf16[8,32,441]{2,1,0:T(8,128)(2,1)}, bf16[8,32,441]{2,1,0:T(8,128)(2,1)}, bf16[8,32,441]{2,1,0:T(8,128)(2,1)}, bf16[8,32,441]{2,1,0:T(8,128)(2,1)},...) custom-call(s32[1]{0:T(128)} %bitcast.me_ref, ...), custom_call_target="tpu_custom_call" | custom-call | flops 17600000000 | bytes 56000000 | tf_op jit(solution)/shard_map/middle/pallas_call | solution.py:946
  85.0 2.6 %all-to-all-start.1 = ((f32[32,4,128]{2,1,0:T(4,128)}), f32[32,4,128]{2,1,0:T(4,128)S(1)}, u32[]{:S(2)}, u32[]{:S(2)}) async-start(f32[32,4,128]{2,1,0:T(4,128)} %get-tuple-element.100.own_ref), calls=%async_computation.1 | async-start | bytes 131072 | tf_op jit(solution)/shard_map/all_to_all | solution.py:824
  95.6 6.1 %top.1 = (bf16[8,32,100]{2,1,0:T(8,128)(2,1)}, bf16[8,32,100]{2,1,0:T(8,128)(2,1)}, bf16[8,32,100]{2,1,0:T(8,128)(2,1)}, bf16[8,32,100]{2,1,0:T(8,128)(2,1)}, f3...) custom-call(s32[1]{0:T(128)} %bitcast.me_ref, ...), custom_call_target="tpu_custom_call" | custom-call | flops 7040000000 | bytes 22400000 | tf_op jit(solution)/shard_map/top/pallas_call | solution.py:989
  101.7 4.1 %all-to-all-start.2 = ((f32[32,4,128]{2,1,0:T(4,128)}), f32[32,4,128]{2,1,0:T(4,128)S(1)}, u32[]{:S(2)}, u32[]{:S(2)}) async-start(f32[32,4,128]{2,1,0:T(4,128)} %get-tuple-element.109), calls=%async_computation.2 | async-start | bytes 131072 | tf_op jit(solution)/shard_map/all_to_all | solution.py:824
  107.9 5.3 %all-to-all-done.2.heard_ref.heard_top_ref = f32[32,4,128]{2,1,0:T(4,128)S(1)} async-done(((f32[32,4,128]{2,1,0:T(4,128)}), f32[32,4,128]{2,1,0:T(4,128)S(1)}, u32[]{:S(2)}, u32[]{:S(2)}) %all-to-all-start.2) | async-done | bytes 65568 | tf_op jit(solution)/shard_map/all_to_all | solution.py:824
  113.9 15.9 %back.1 = (bf16[8,128,1792]{2,1,0:T(8,128)(2,1)}, bf16[8,128,1792]{2,1,0:T(8,128)(2,1)}, f32[32,4,128]{2,1,0:T(4,128)}, bf16[4,2,3,32,384]{4,3,2,1,0:T(8,128)(2,1)}) custom-call(f32[8]{0:T(128)} %compare_convert_fusion.live_ref, f32[32,4,128]{2,1,0:T(4,128)} %copy-done.7, f32[8,128]{1,0:T(8,128)} %get-tuple-element.110.norm_three_ref, ...), custom_call_target="tpu_custom_call" | custom-call | flops 17600000000 | bytes 56000000 | tf_op jit(solution)/shard_map/back/pallas_call | solution.py:1043
  129.8 2.8 %all-to-all-start.3 = ((f32[32,4,128]{2,1,0:T(4,128)}), f32[32,4,128]{2,1,0:T(4,128)S(1)}, u32[]{:S(2)}, u32[]{:S(2)}) async-start(f32[32,4,128]{2,1,0:T(4,128)} %get-tuple-element.116), calls=%async_computation.3 | async-start | bytes 131072 | tf_op jit(solution)/shard_map/all_to_all | solution.py:824
  134.1 3.2 %collective-permute-done.15.refs_6_.refs_2_ = bf16[8,32,100]{2,1,0:T(8,128)(2,1)S(1)} collective-permute-done((bf16[8,32,100]{2,1,0:T(8,128)(2,1)}, bf16[8,32,100]{2,1,0:T(8,128)(2,1)S(1)}, u32[]{:S(2)}, u32[]{:S(2)}) %collective-permute-start.15) | collective-permute-done | bytes 51232 | tf_op jit(solution)/shard_map/ppermute | solution.py:821
  140.5 7.0 %last_conv.2 = (bf16[8,32,1764]{2,1,0:T(8,128)(2,1)}, bf16[8,32,1764]{2,1,0:T(8,128)(2,1)}, bf16[2,32,1764]{2,1,0:T(8,128)(2,1)}, bf16[2,32,1764]{2,1,0:T(8,128)...) custom-call(s32[1]{0:T(128)} %bitcast.me_ref, f32[8]{0:T(128)} %compare_convert_fusion.live_ref, ...), custom_call_target="tpu_custom_call" | custom-call | flops 6600000000 | bytes 21000000 | tf_op jit(solution)/shard_map/last_conv/pallas_call | solution.py:1122
  151.3 10.4 %last_filter.1.refs_0_ = bf16[4,2,3,32,384]{4,3,2,1,0:T(8,128)(2,1)} custom-call(f32[8]{0:T(128)} %compare_convert_fusion.live_ref, f32[32,4,128]{2,1,0:T(4,128)} %copy-done.8, f32[8,128]{1,0:T(8,128)} %get-tuple-element.111.norm_two_ref.norm_ref, f32[8,128]{1,0:T(8,128)} %get-tuple-element.95.vectors_ref, ...), custom_call_target="tpu_custom_call", output_to_operand_aliasing={{}: (7, {})} | custom-call | flops 10560000000 | bytes 33600000 | tf_op jit(solution)/shard_map/last_filter/pallas_call | solution.py:1150
  161.6 4.6 %all-to-all-start.4 = ((bf16[32,24,384]{2,1,0:T(8,128)(2,1)}), bf16[32,24,384]{2,1,0:T(8,128)(2,1)}, u32[]{:S(2)}, u32[]{:S(2)}) async-start(bf16[32,24,384]{2,1,0:T(8,128)(2,1)} %bitcast.31), calls=%async_computation.4 | async-start | bytes 1179648 | tf_op jit(solution)/shard_map/all_to_all | solution.py:1184
  167.1 6.8 %last_conv.3 = (bf16[8,32,1764]{2,1,0:T(8,128)(2,1)}, bf16[8,32,1764]{2,1,0:T(8,128)(2,1)}, bf16[4,32,1764]{2,1,0:T(8,128)(2,1)}, bf16[4,32,1764]{2,1,0:T(8,128)(2,1)}) custom-call(s32[1]{0:T(128)} %bitcast.me_ref, f32[8]{0:T(128)} %compare_convert_fusion.live_ref, f32[32,4,128]{2,1,0:T(4,128)} %copy-done.8, ...), custom_call_target="tpu_custom_call", output_to_operand_aliasing={{0}: (12, {}), {1}: (13, {})} | custom-call | flops 6600000000 | bytes 21000000 | tf_op jit(solution)/shard_map/last_conv/pallas_call | solution.py:1122
  179.2 2.5 %finish.1 = (f32[2,32,100]{2,1,0:T(8,128)}, f32[2,32]{1,0:T(2,128)}, f32[2,100]{1,0:T(2,128)}, f32[32]{0:T(128)}, f32[32]{0:T(128)}, /*index=5*/f32[32]{0:T(128)}, f32[32]{0:T(128)}, f32[9]{0:T(128)}) custom-call(s32[1]{0:T(128)} %bitcast.17.here_ref, s32[1]{0:T(128)} %bitcast.me_ref, f32[32,4,128]{2,1,0:T(4,128)} %copy-done.6, f32[32,4,128]{2,1,0:T(4,128)} %copy-done.7, ...), custom_call_target="tpu_custom_call" | custom-call | flops 2200000000 | bytes 7000000 | tf_op jit(solution)/shard_map/finish/pallas_call | solution.py:1203
  181.7 2.3 %all-to-all-done.4.heard_ref = bf16[32,24,384]{2,1,0:T(8,128)(2,1)} async-done(((bf16[32,24,384]{2,1,0:T(8,128)(2,1)}), bf16[32,24,384]{2,1,0:T(8,128)(2,1)}, u32[]{:S(2)}, u32[]{:S(2)}) %all-to-all-start.4) | async-done | bytes 589856 | tf_op jit(solution)/shard_map/all_to_all | solution.py:1184
  185.9 3.4 %all-to-all-start.5 = ((f32[8,24,384]{2,1,0:T(8,128)}), f32[8,24,384]{2,1,0:T(8,128)S(1)}, u32[]{:S(2)}, u32[]{:S(2)}) async-start(f32[8,24,384]{2,1,0:T(8,128)} %strips.1), calls=%async_computation.5 | async-start | bytes 589824 | tf_op jit(solution)/shard_map/all_to_all | solution.py:1193
  194.2 3.3 %unpack.6.refs_6_ = f32[32,32,1764]{2,1,0:T(8,128)} custom-call(s32[1]{0:T(128)} %bitcast.me_ref, bf16[8,32,1764]{2,1,0:T(8,128)(2,1)} %get-tuple-element.127.refs_4_.refs_6_.refs_0_, bf16[8,32,1764]{2,1,0:T(8,128)(2,1)} %collective-permute-done.25.refs_1_, bf16[4,32,1764]{2,1,0:T(8,128)(2,1)} %copy-done), custom_call_target="tpu_custom_call" | custom-call | flops 2200000000 | bytes 7000000 | tf_op jit(solution)/shard_map/unpack/pallas_call | solution.py:779
  197.5 5.3 %collective-permute-done.24.refs_5_ = bf16[4,32,1764]{2,1,0:T(8,128)(2,1)} collective-permute-done((bf16[4,32,1764]{2,1,0:T(8,128)(2,1)}, bf16[4,32,1764]{2,1,0:T(8,128)(2,1)}, u32[]{:S(2)}, u32[]{:S(2)}) %collective-permute-start.24) | collective-permute-done | bytes 451616 | tf_op jit(solution)/shard_map/ppermute | solution.py:821
  202.8 3.4 %unpack.7 = f32[32,32,1764]{2,1,0:T(8,128)} custom-call(s32[1]{0:T(128)} %bitcast.me_ref, bf16[2,32,1764]{2,1,0:T(8,128)(2,1)} %copy-done.4, bf16[2,32,1764]{2,1,0:T(8,128)(2,1)} %copy-done.5, bf16[4,32,1764]{2,1,0:T(8,128)(2,1)} %copy-done, bf16[2,32,1764]{2,1,0:T(8,128)(2,1)} %copy-done.2, ...), custom_call_target="tpu_custom_call", output_to_operand_aliasing={{}: (7, {})} | custom-call | flops 2200000000 | bytes 7000000 | tf_op jit(solution)/shard_map/unpack/pallas_call | solution.py:779
  (110 shorter events, 46.4 us)
Async XLA Ops:
  4.8 8.8 %collective-permute-start.1 = (bf16[240,384]{1,0:T(8,128)(2,1)}, bf16[240,384]{1,0:T(8,128)(2,1)}, u32[]{:S(2)}, u32[]{:S(2)}) collective-permute-start(bf16[240,384]{1,0:T(8,128)(2,1)} %bundle.1.refs_0_), channel_id=1, source_target_pairs={{0,2},{1,3},{2,0},{3,1},{4,6},{5,7},{6,4},{7,5},{8,10},{9,11},{10,... | collective-permute-start | bytes 552968 | tf_op jit(solution)/shard_map/ppermute | solution.py:821
  7.8 8.1 %collective-permute-start = (bf16[240,384]{1,0:T(8,128)(2,1)}, bf16[240,384]{1,0:T(8,128)(2,1)}, u32[]{:S(2)}, u32[]{:S(2)}) collective-permute-start(bf16[240,384]{1,0:T(8,128)(2,1)} %bundle.1.refs_0_), channel_id=1, source_target_pairs={{0,1},{1,0},{2,3},{3,2},{4,5},{5,4},{6,7},{7,6},{8,9},{9,8},{10,11... | collective-permute-start | bytes 552968 | tf_op jit(solution)/shard_map/ppermute | solution.py:821
  7.8 15.2 %collective-permute-start.4 = (bf16[4,32,1764]{2,1,0:T(8,128)(2,1)}, bf16[4,32,1764]{2,1,0:T(8,128)(2,1)}, u32[]{:S(2)}, u32[]{:S(2)}) collective-permute-start(bf16[4,32,1764]{2,1,0:T(8,128)(2,1)} %get-tuple-element.79.refs_4_.refs_0_), channel_id=1, source_target_pairs={{0,3},{1,2},{2,1},{3,0},{4,7},{5,6},{6,5},{7,4},{8,11},{9,10},{10,... | collective-permute-start | bytes 1354760 | tf_op jit(solution)/shard_map/ppermute | solution.py:821
  10.7 24.6 %collective-permute-start.3 = (bf16[8,32,1764]{2,1,0:T(8,128)(2,1)}, bf16[8,32,1764]{2,1,0:T(8,128)(2,1)S(1)}, u32[]{:S(2)}, u32[]{:S(2)}) collective-permute-start(bf16[8,32,1764]{2,1,0:T(8,128)(2,1)} %get-tuple-element.82), channel_id=1, source_target_pairs={{0,1},{1,0},{2,3},{3,2},{4,5},{5,4},{6,7},{7,6},{8,9},{9,8},{10,11... | collective-permute-start | bytes 2709512 | tf_op jit(solution)/shard_map/ppermute | solution.py:821
  11.0 22.2 %collective-permute-start.9 = (bf16[4,32,1764]{2,1,0:T(8,128)(2,1)}, bf16[4,32,1764]{2,1,0:T(8,128)(2,1)}, u32[]{:S(2)}, u32[]{:S(2)}) collective-permute-start(bf16[4,32,1764]{2,1,0:T(8,128)(2,1)} %get-tuple-element.87), channel_id=1, source_target_pairs={{0,2},{1,3},{2,0},{3,1},{4,6},{5,7},{6,4},{7,5},{8,10},{9,11},{10,... | collective-permute-start | bytes 1354760 | tf_op jit(solution)/shard_map/ppermute | solution.py:821
  13.6 2.4 %collective-permute-start.2 = (bf16[240,384]{1,0:T(8,128)(2,1)}, bf16[240,384]{1,0:T(8,128)(2,1)}, u32[]{:S(2)}, u32[]{:S(2)}) collective-permute-start(bf16[240,384]{1,0:T(8,128)(2,1)} %collective-permute-done.1.refs_2_), channel_id=1, source_target_pairs={{0,1},{1,0},{2,3},{3,2},{4,5},{5,4},{6,7},{7,6},{8,9},{9,8},{10,11... | collective-permute-start | bytes 552968 | tf_op jit(solution)/shard_map/ppermute | solution.py:821
  25.2 19.1 %collective-permute-start.8 = (bf16[2,32,1764]{2,1,0:T(8,128)(2,1)}, bf16[2,32,1764]{2,1,0:T(8,128)(2,1)}, u32[]{:S(2)}, u32[]{:S(2)}) collective-permute-start(bf16[2,32,1764]{2,1,0:T(8,128)(2,1)} %get-tuple-element.86.refs_4_), channel_id=1, source_target_pairs={{0,3},{1,2},{2,1},{3,0},{4,7},{5,6},{6,5},{7,4},{8,11},{9,10},{10,... | collective-permute-start | bytes 677384 | tf_op jit(solution)/shard_map/ppermute | solution.py:821
  27.2 17.2 %collective-permute-start.7 = (bf16[2,32,1764]{2,1,0:T(8,128)(2,1)}, bf16[2,32,1764]{2,1,0:T(8,128)(2,1)}, u32[]{:S(2)}, u32[]{:S(2)}) collective-permute-start(bf16[2,32,1764]{2,1,0:T(8,128)(2,1)} %get-tuple-element.85), channel_id=1, source_target_pairs={{0,2},{1,3},{2,0},{3,1},{4,6},{5,7},{6,4},{7,5},{8,10},{9,11},{10,... | collective-permute-start | bytes 677384 | tf_op jit(solution)/shard_map/ppermute | solution.py:821
  29.5 19.7 %collective-permute-start.6 = (bf16[2,32,1764]{2,1,0:T(8,128)(2,1)}, bf16[2,32,1764]{2,1,0:T(8,128)(2,1)}, u32[]{:S(2)}, u32[]{:S(2)}) collective-permute-start(bf16[2,32,1764]{2,1,0:T(8,128)(2,1)} %get-tuple-element.84.refs_7_), channel_id=1, source_target_pairs={{0,3},{1,2},{2,1},{3,0},{4,7},{5,6},{6,5},{7,4},{8,11},{9,10},{10,... | collective-permute-start | bytes 677384 | tf_op jit(solution)/shard_map/ppermute | solution.py:821
  33.2 18.8 %collective-permute-start.5 = (bf16[2,32,1764]{2,1,0:T(8,128)(2,1)}, bf16[2,32,1764]{2,1,0:T(8,128)(2,1)}, u32[]{:S(2)}, u32[]{:S(2)}) collective-permute-start(bf16[2,32,1764]{2,1,0:T(8,128)(2,1)} %get-tuple-element.83), channel_id=1, source_target_pairs={{0,2},{1,3},{2,0},{3,1},{4,6},{5,7},{6,4},{7,5},{8,10},{9,11},{10,... | collective-permute-start | bytes 677384 | tf_op jit(solution)/shard_map/ppermute | solution.py:821
  56.9 13.5 %all-to-all-start = ((f32[32,4,128]{2,1,0:T(4,128)}), f32[32,4,128]{2,1,0:T(4,128)S(1)}, u32[]{:S(2)}, u32[]{:S(2)}) async-start(f32[32,4,128]{2,1,0:T(4,128)} %get-tuple-element.94), calls=%async_computation | async-start | bytes 131072 | tf_op jit(solution)/shard_map/all_to_all | solution.py:824
  85.0 10.0 %all-to-all-start.1 = ((f32[32,4,128]{2,1,0:T(4,128)}), f32[32,4,128]{2,1,0:T(4,128)S(1)}, u32[]{:S(2)}, u32[]{:S(2)}) async-start(f32[32,4,128]{2,1,0:T(4,128)} %get-tuple-element.100.own_ref), calls=%async_computation.1 | async-start | bytes 131072 | tf_op jit(solution)/shard_map/all_to_all | solution.py:824
  87.7 2.7 %collective-permute-start.12 = (bf16[8,32,100]{2,1,0:T(8,128)(2,1)S(1)}, bf16[8,32,100]{2,1,0:T(8,128)(2,1)S(1)}, u32[]{:S(2)}, u32[]{:S(2)}) collective-permute-start(bf16[8,32,100]{2,1,0:T(8,128)(2,1)S(1)} %bitcast.33), channel_id=1, source_target_pairs={{0,1},{1,0},{2,3},{3,2},{4,5},{5,4},{6,7},{7,6},{8,9},{9,8},{10,11... | collective-permute-start | bytes 153608 | tf_op jit(solution)/shard_map/ppermute | solution.py:821
  87.8 4.8 %collective-permute-start.13 = (bf16[8,32,100]{2,1,0:T(8,128)(2,1)S(1)}, bf16[8,32,100]{2,1,0:T(8,128)(2,1)S(1)}, u32[]{:S(2)}, u32[]{:S(2)}) collective-permute-start(bf16[8,32,100]{2,1,0:T(8,128)(2,1)S(1)} %bitcast.34), channel_id=1, source_target_pairs={{0,2},{1,3},{2,0},{3,1},{4,6},{5,7},{6,4},{7,5},{8,10},{9,11},{10,... | collective-permute-start | bytes 153608 | tf_op jit(solution)/shard_map/ppermute | solution.py:821
  89.6 4.5 %collective-permute-start.14 = (bf16[8,32,100]{2,1,0:T(8,128)(2,1)S(1)}, bf16[8,32,100]{2,1,0:T(8,128)(2,1)S(1)}, u32[]{:S(2)}, u32[]{:S(2)}) collective-permute-start(bf16[8,32,100]{2,1,0:T(8,128)(2,1)S(1)} %bitcast.35), channel_id=1, source_target_pairs={{0,3},{1,2},{2,1},{3,0},{4,7},{5,6},{6,5},{7,4},{8,11},{9,10},{10,... | collective-permute-start | bytes 153608 | tf_op jit(solution)/shard_map/ppermute | solution.py:821
  101.7 11.6 %all-to-all-start.2 = ((f32[32,4,128]{2,1,0:T(4,128)}), f32[32,4,128]{2,1,0:T(4,128)S(1)}, u32[]{:S(2)}, u32[]{:S(2)}) async-start(f32[32,4,128]{2,1,0:T(4,128)} %get-tuple-element.109), calls=%async_computation.2 | async-start | bytes 131072 | tf_op jit(solution)/shard_map/all_to_all | solution.py:824
  105.7 33.2 %collective-permute-start.10 = (bf16[8,32,441]{2,1,0:T(8,128)(2,1)}, bf16[8,32,441]{2,1,0:T(8,128)(2,1)S(1)}, u32[]{:S(2)}, u32[]{:S(2)}) collective-permute-start(bf16[8,32,441]{2,1,0:T(8,128)(2,1)} %get-tuple-element.98), channel_id=1, source_target_pairs={{0,2},{1,3},{2,0},{3,1},{4,6},{5,7},{6,4},{7,5},{8,10},{9,11},{10,... | collective-permute-start | bytes 677384 | tf_op jit(solution)/shard_map/ppermute | solution.py:821
  107.6 31.4 %collective-permute-start.11 = (bf16[8,32,441]{2,1,0:T(8,128)(2,1)}, bf16[8,32,441]{2,1,0:T(8,128)(2,1)S(1)}, u32[]{:S(2)}, u32[]{:S(2)}) collective-permute-start(bf16[8,32,441]{2,1,0:T(8,128)(2,1)} %get-tuple-element.99), channel_id=1, source_target_pairs={{0,3},{1,2},{2,1},{3,0},{4,7},{5,6},{6,5},{7,4},{8,11},{9,10},{10,... | collective-permute-start | bytes 677384 | tf_op jit(solution)/shard_map/ppermute | solution.py:821
  107.6 32.0 %collective-permute-start.17 = (bf16[8,32,441]{2,1,0:T(8,128)(2,1)}, bf16[8,32,441]{2,1,0:T(8,128)(2,1)S(1)}, u32[]{:S(2)}, u32[]{:S(2)}) collective-permute-start(bf16[8,32,441]{2,1,0:T(8,128)(2,1)} %get-tuple-element.106), channel_id=1, source_target_pairs={{0,1},{1,0},{2,3},{3,2},{4,5},{5,4},{6,7},{7,6},{8,9},{9,8},{10,11... | collective-permute-start | bytes 677384 | tf_op jit(solution)/shard_map/ppermute | solution.py:821
  129.8 10.0 %all-to-all-start.3 = ((f32[32,4,128]{2,1,0:T(4,128)}), f32[32,4,128]{2,1,0:T(4,128)S(1)}, u32[]{:S(2)}, u32[]{:S(2)}) async-start(f32[32,4,128]{2,1,0:T(4,128)} %get-tuple-element.116), calls=%async_computation.3 | async-start | bytes 131072 | tf_op jit(solution)/shard_map/all_to_all | solution.py:824
  132.6 4.7 %collective-permute-start.15 = (bf16[8,32,100]{2,1,0:T(8,128)(2,1)}, bf16[8,32,100]{2,1,0:T(8,128)(2,1)S(1)}, u32[]{:S(2)}, u32[]{:S(2)}) collective-permute-start(bf16[8,32,100]{2,1,0:T(8,128)(2,1)} %get-tuple-element.103), channel_id=1, source_target_pairs={{0,2},{1,3},{2,0},{3,1},{4,6},{5,7},{6,4},{7,5},{8,10},{9,11},{10,... | collective-permute-start | bytes 153608 | tf_op jit(solution)/shard_map/ppermute | solution.py:821
  134.1 4.9 %collective-permute-start.16 = (bf16[8,32,100]{2,1,0:T(8,128)(2,1)}, bf16[8,32,100]{2,1,0:T(8,128)(2,1)S(1)}, u32[]{:S(2)}, u32[]{:S(2)}) collective-permute-start(bf16[8,32,100]{2,1,0:T(8,128)(2,1)} %get-tuple-element.104), channel_id=1, source_target_pairs={{0,3},{1,2},{2,1},{3,0},{4,7},{5,6},{6,5},{7,4},{8,11},{9,10},{10,... | collective-permute-start | bytes 153608 | tf_op jit(solution)/shard_map/ppermute | solution.py:821
  137.3 1.7 collective-permute-start.18
  147.4 18.8 %collective-permute-start.19 = (bf16[2,32,1764]{2,1,0:T(8,128)(2,1)}, bf16[2,32,1764]{2,1,0:T(8,128)(2,1)S(1)}, u32[]{:S(2)}, u32[]{:S(2)}) collective-permute-start(bf16[2,32,1764]{2,1,0:T(8,128)(2,1)} %get-tuple-element.123), channel_id=1, source_target_pairs={{0,3},{1,2},{2,1},{3,0},{4,7},{5,6},{6,5},{7,4},{8,11},{9,10},{10,... | collective-permute-start | bytes 677384 | tf_op jit(solution)/shard_map/ppermute | solution.py:821
  149.3 17.0 %collective-permute-start.20 = (bf16[2,32,1764]{2,1,0:T(8,128)(2,1)}, bf16[2,32,1764]{2,1,0:T(8,128)(2,1)S(1)}, u32[]{:S(2)}, u32[]{:S(2)}) collective-permute-start(bf16[2,32,1764]{2,1,0:T(8,128)(2,1)} %get-tuple-element.124), channel_id=1, source_target_pairs={{0,3},{1,2},{2,1},{3,0},{4,7},{5,6},{6,5},{7,4},{8,11},{9,10},{10,... | collective-permute-start | bytes 677384 | tf_op jit(solution)/shard_map/ppermute | solution.py:821
  149.3 16.9 %collective-permute-start.21 = (bf16[2,32,1764]{2,1,0:T(8,128)(2,1)}, bf16[2,32,1764]{2,1,0:T(8,128)(2,1)S(1)}, u32[]{:S(2)}, u32[]{:S(2)}) collective-permute-start(bf16[2,32,1764]{2,1,0:T(8,128)(2,1)} %get-tuple-element.125), channel_id=1, source_target_pairs={{0,2},{1,3},{2,0},{3,1},{4,6},{5,7},{6,4},{7,5},{8,10},{9,11},{10,... | collective-permute-start | bytes 677384 | tf_op jit(solution)/shard_map/ppermute | solution.py:821
  161.6 22.3 %all-to-all-start.4 = ((bf16[32,24,384]{2,1,0:T(8,128)(2,1)}), bf16[32,24,384]{2,1,0:T(8,128)(2,1)}, u32[]{:S(2)}, u32[]{:S(2)}) async-start(bf16[32,24,384]{2,1,0:T(8,128)(2,1)} %bitcast.31), calls=%async_computation.4 | async-start | bytes 1179648 | tf_op jit(solution)/shard_map/all_to_all | solution.py:1184
  173.9 19.5 %collective-permute-start.25 = (bf16[8,32,1764]{2,1,0:T(8,128)(2,1)}, bf16[8,32,1764]{2,1,0:T(8,128)(2,1)}, u32[]{:S(2)}, u32[]{:S(2)}) collective-permute-start(bf16[8,32,1764]{2,1,0:T(8,128)(2,1)} %get-tuple-element.135), channel_id=1, source_target_pairs={{0,1},{1,0},{2,3},{3,2},{4,5},{5,4},{6,7},{7,6},{8,9},{9,8},{10,11... | collective-permute-start | bytes 2709512 | tf_op jit(solution)/shard_map/ppermute | solution.py:821
  174.1 23.4 %collective-permute-start.22 = (bf16[2,32,1764]{2,1,0:T(8,128)(2,1)}, bf16[2,32,1764]{2,1,0:T(8,128)(2,1)S(1)}, u32[]{:S(2)}, u32[]{:S(2)}) collective-permute-start(bf16[2,32,1764]{2,1,0:T(8,128)(2,1)} %get-tuple-element.132), channel_id=1, source_target_pairs={{0,2},{1,3},{2,0},{3,1},{4,6},{5,7},{6,4},{7,5},{8,10},{9,11},{10,... | collective-permute-start | bytes 677384 | tf_op jit(solution)/shard_map/ppermute | solution.py:821
  175.8 17.6 %collective-permute-start.23 = (bf16[4,32,1764]{2,1,0:T(8,128)(2,1)}, bf16[4,32,1764]{2,1,0:T(8,128)(2,1)S(1)}, u32[]{:S(2)}, u32[]{:S(2)}) collective-permute-start(bf16[4,32,1764]{2,1,0:T(8,128)(2,1)} %get-tuple-element.133), channel_id=1, source_target_pairs={{0,2},{1,3},{2,0},{3,1},{4,6},{5,7},{6,4},{7,5},{8,10},{9,11},{10,... | collective-permute-start | bytes 1354760 | tf_op jit(solution)/shard_map/ppermute | solution.py:821
  176.2 26.6 %collective-permute-start.24 = (bf16[4,32,1764]{2,1,0:T(8,128)(2,1)}, bf16[4,32,1764]{2,1,0:T(8,128)(2,1)}, u32[]{:S(2)}, u32[]{:S(2)}) collective-permute-start(bf16[4,32,1764]{2,1,0:T(8,128)(2,1)} %get-tuple-element.134), channel_id=1, source_target_pairs={{0,3},{1,2},{2,1},{3,0},{4,7},{5,6},{6,5},{7,4},{8,11},{9,10},{10,... | collective-permute-start | bytes 1354760 | tf_op jit(solution)/shard_map/ppermute | solution.py:821
  185.9 20.4 %all-to-all-start.5 = ((f32[8,24,384]{2,1,0:T(8,128)}), f32[8,24,384]{2,1,0:T(8,128)S(1)}, u32[]{:S(2)}, u32[]{:S(2)}) async-start(f32[8,24,384]{2,1,0:T(8,128)} %strips.1), calls=%async_computation.5 | async-start | bytes 589824 | tf_op jit(solution)/shard_map/all_to_all | solution.py:1193
  (22 other events, 60.4 us)

commit v4 on v3

--- a/solution.py
+++ b/solution.py
@@ -360,16 +360,25 @@
 
     merged = [column(state, k) for k in range(3)]
     active_squares, hidden_squares = column(state, 3), column(state, 4)
-    for image in range(count):
-        live = live_ref[step * count + image]
+    lives = [live_ref[step * count + image] for image in range(count)]
+
+    def activate(image):
         pre = (conv_ref[image] - column(columns, 0)) * column(columns, 1) + column(columns, 2)
         active = pre * gelu_gate(pre)
         counted = trim(active, 0, CELLS_TWO)
-        active_squares = active_squares + live * lane_sum(counted * counted)
-        split = halves(active)
+        return halves(active), lives[image] * lane_sum(counted * counted)
+
+    def pool(split):
         (left,) = dot_halves(split[:, :1152], pool_a_ref)
         (right,) = dot_halves(split[:, 896:], pool_b_ref)
-        hidden = live * jnp.concatenate([left, right], axis=1)
+        return jnp.concatenate([left, right], axis=1)
+
+    split, squares = activate(0)
+    for image in range(count):
+        hidden = lives[image] * pool(split)
+        active_squares = active_squares + squares
+        if image + 1 < count:
+            split, squares = activate(image + 1)
         hidden_squares = hidden_squares + lane_sum(hidden * hidden)
         hidden_low = hidden.astype(BF16)
         hidden_ref[image] = hidden_low
@@ -378,7 +387,7 @@
         conv = conv_ahead(weights_ref, stack.at[image], HALF)
         write(conv_three_ref.at[image], conv)
         mean, spread = moments(conv, CELLS_THREE)
-        merged = merge_moments(merged, live, mean, spread, CELLS_THREE)
+        merged = merge_moments(merged, lives[image], mean, spread, CELLS_THREE)
     state[...] = column_tile([*merged, active_squares, hidden_squares])
 
     @pl.when(step == pl.num_programs(0) - 1)
@@ -483,11 +492,10 @@
     unpool_b_ref,
     grad_ref,
     conv_three_ref,
-    hidden_ref,
     conv_two_ref,
     *refs,
 ):
-    out_ref, away_ref, sums_ref, filter_ref, columns_three, columns_two, totals, product, stack, upright = refs[-10:]
+    out_ref, away_ref, error_ref, sums_ref, columns_three, columns_two, totals, upright = refs[-8:]
     step = pl.program_id(0)
     count = conv_two_ref.shape[0]
 
@@ -499,14 +507,13 @@
             row_tile([row(norm_two_ref, 0), row(vectors_ref, 0) * row(norm_two_ref, 1), row(vectors_ref, 1)])
         )
         totals[...] = jnp.zeros_like(totals)
-        product[...] = jnp.zeros_like(product)
 
     grad_sum, product_sum = column(totals, 0), column(totals, 1)
     for image in range(count):
         away = conv_three_ref[image] - column(columns_three, 0)
         error = norm_back(live_ref[step * count + image], columns_three, grad_ref[image], away, CELLS_THREE)
+        error_ref[image] = error
         stack_upright(cut(error, WIDE), HALF, upright.at[image])
-        stack_sideways(cut(hidden_ref[image], WIDE), HALF, stack.at[image])
     split = jnp.concatenate(
         [
             halves(jnp.concatenate(conv_behind(weights_ref, upright.at[image], HALF), axis=1))
@@ -524,12 +531,10 @@
         away_ref[image] = away.astype(BF16)
         grad_sum = grad_sum + lane_sum(grad_pre)
         product_sum = product_sum + lane_sum(grad_pre * away)
-    product[...] += sum(across_cells(upright.at[image], stack.at[image]) for image in range(count))
     totals[...] = column_tile([grad_sum, product_sum])
 
     @pl.when(step == pl.num_programs(0) - 1)
     def _():
-        split_filter(product, filter_ref)
         turned = totals[...].T
         normed_sum = turned[1:2] * row(norm_two_ref, 1)
         spread_rows(row_tile([turned[0:1], normed_sum, levels_ref[0:1, :]], SENT), sums_ref)
@@ -540,6 +545,25 @@
     for tap in range(3):
         for owner in range(partners):
             filter_ref[owner, tap] = product[tap * C + owner * rows : tap * C + (owner + 1) * rows].astype(BF16)
+
+
+def filter_three_kernel(error_ref, hidden_ref, *refs):
+    filter_ref, product, stack, upright = refs[-4:]
+    step = pl.program_id(0)
+    count = error_ref.shape[0]
+
+    @pl.when(step == 0)
+    def _():
+        product[...] = jnp.zeros_like(product)
+
+    for image in range(count):
+        stack_upright(cut(error_ref[image], WIDE), HALF, upright.at[image])
+        stack_sideways(cut(hidden_ref[image], WIDE), HALF, stack.at[image])
+        product[...] += across_cells(upright.at[image], stack.at[image])
+
+    @pl.when(step == pl.num_programs(0) - 1)
+    def _():
+        split_filter(product, filter_ref)
 
 
 def last_columns(heard_ref, norm_ref, vectors_ref):
@@ -1040,7 +1064,7 @@
     def filter_spec(block):
         return pl.BlockSpec((partners, None, 3, rows, 3 * C), lambda n: (0, block, 0, 0, 0))
 
-    grad_two, away_two, sums_two, filter_sums = pl.pallas_call(
+    grad_two, away_two, error_three, sums_two = pl.pallas_call(
         back_kernel,
         grid=(images_each // pair,),
         in_specs=[
@@ -1055,27 +1079,24 @@
             whole(384, 896),
             each(C, LANES_THREE, count=pair),
             each(C, LANES_THREE, count=pair),
-            each(C, LANES_THREE, count=pair),
             each(C, LANES_TWO, count=pair),
         ],
         out_specs=[
             each(C, LANES_TWO, count=pair),
             each(C, LANES_TWO, count=pair),
+            each(C, LANES_THREE, count=pair),
             whole(devices, SENT, C),
-            filter_spec(1),
         ],
         out_shape=[
             jax.ShapeDtypeStruct((images_each, C, LANES_TWO), BF16),
             jax.ShapeDtypeStruct((images_each, C, LANES_TWO), BF16),
+            jax.ShapeDtypeStruct((images_each, C, LANES_THREE), BF16),
             jax.ShapeDtypeStruct((devices, SENT, C), F32),
-            filter_shape,
         ],
         scratch_shapes=[
             pltpu.VMEM((C, C), F32),
             pltpu.VMEM((C, C), F32),
             pltpu.VMEM((C, C), F32),
-            pltpu.VMEM((3 * C, 3 * C), F32),
-            pltpu.VMEM((pair, 3 * C, LANES_THREE), BF16),
             pltpu.VMEM((pair, 3 * C, LANES_THREE), BF16),
         ],
         compiler_params=kernel_params(),
@@ -1093,13 +1114,28 @@
         jnp.asarray(pool[896:, 128:].T, BF16),
         grad_three,
         conv_three,
-        hidden,
         conv_two,
     )
     heard_back = share(sums_two)
 
+    filter_sums = pl.pallas_call(
+        filter_three_kernel,
+        grid=(images_each // some,),
+        in_specs=[*[each(C, LANES_THREE, count=some)] * 2, *anywhere(1)],
+        out_specs=filter_spec(1),
+        out_shape=filter_shape,
+        scratch_shapes=[
+            pltpu.VMEM((3 * C, 3 * C), F32),
+            pltpu.VMEM((some, 3 * C, LANES_THREE), BF16),
+            pltpu.VMEM((some, 3 * C, LANES_THREE), BF16),
+        ],
+        compiler_params=kernel_params(),
+        name="filter_three",
+        cost_estimate=lasting(5.0),
+    )(error_three, hidden, sums_two)
+
     returned = [[] for partner in range(partners)]
-    waits = [pieces[0] for pieces in (*block_two, *out_pieces)]
+    waits = [filter_sums, *(pieces[0] for pieces in (*block_two, *out_pieces))]
     common = [heard_back, norm_two, vectors]
     common_specs = [whole(devices, SENT, C), whole(8, C), whole(8, C)]
     kept = []
@@ -1190,12 +1226,12 @@
         name="strips",
         cost_estimate=lasting(1.5),
     )(heard, kept[0])
-    strips = lax.all_to_all(strips, "dp", 0, 0).reshape(2, 3, rows, 3, C)
-    grad_filters = jnp.transpose(strips, (0, 2, 4, 1, 3))
+    strips = lax.all_to_all(strips, "dp", 0, 0)
+    grad_filters = jnp.transpose(strips.reshape(2, 3, rows, 3, C), (0, 2, 4, 1, 3))
 
     grad_images = ()
     for place in range(partners // group):
-        waits = () if grad_images else (arrivals[count_first],)
+        waits = (strips,) if grad_images else (returned[near][1],)
         grad_images = unpack([returned], me, images_each, F32, place, grad_images, waits)
     (grad_images,) = grad_images
 

time: 209 us -> 203 us (0.971)
  starting transfers between devices: 45.8 us -> 42.1 us
  waiting for transfers between devices: 44.1 us -> 40.5 us
    ppermute x26, waiting for transfers between devices: 28.3 us -> 21.2 us  [swap(): lax.ppermute(value, 'tensor', [(i, i ^ partner) for i in range(partners)])]
    pallas_call x0 -> x1, Pallas kernels: none -> 4.18 us  [local(): pl.pallas_call(filter_three_kernel, grid=(images_each // some,), in_specs...]
    ppermute x26, starting transfers between devices: 22.1 us -> 19.4 us  [swap(): lax.ppermute(value, 'tensor', [(i, i ^ partner) for i in range(partners)])]
  transfers between devices with their start and end apart: 32 -> 32, of which waited for: 15 -> 17; matrix products, arithmetic and copies ran while one was open for 1% -> 2% of each run, Pallas kernels for 34% -> 35%
where the time goes in v4:
time: 203 us; the launch traced here: 202 us
  Pallas kernels  109 us (54%)
  starting transfers between devices  42.1 us (21%)
  waiting for transfers between devices  40.5 us (20%)
  local copies, waits for them, and re-layouts  8.28 us (4%)
    ppermute x26, waiting for transfers between devices, swap(): lax.ppermute(value, 'tensor', [(i, i ^ partner) for i in range(partners)])  21.2 us
    ppermute x26, starting transfers between devices, swap(): lax.ppermute(value, 'tensor', [(i, i ^ partner) for i in range(partners)])  19.4 us
    pallas_call x3, Pallas kernels, local(): pl.pallas_call(functools.partial(first_conv_kernel, partners, first, fina...  17.6 us
    all_to_all x4, starting transfers between devices, share(): return lax.all_to_all(copies, ('dp', 'tensor'), 0, 0)  15.9 us
    pallas_call x1, Pallas kernels, local(): pl.pallas_call(back_kernel, grid=(images_each // pair,), in_specs=[smem()...  14.6 us
    all_to_all x4, waiting for transfers between devices, share(): return lax.all_to_all(copies, ('dp', 'tensor'), 0, 0)  14.4 us
    pallas_call x2, Pallas kernels, local(): pl.pallas_call(functools.partial(last_conv_kernel, partners, near, first,...  13.8 us
    pallas_call x1, Pallas kernels, local(): pl.pallas_call(functools.partial(middle_kernel, partners), grid=(images_e...  13.8 us
  transfers between devices with their start and end apart: 32, of which 17 were waited for; matrix products, arithmetic and copies ran while one was open for 2% of the time, Pallas kernels for 35%

profile of v4, /device:TPU:0, one launch (start us, length us, event | category | flops | bytes accessed | tf_op | source)
XLA Modules:
  0.0 202.4 jit_solution(8406036930422735784)
XLA Ops:
  0.6 2.5 %pack.4 = (bf16[4,32,1764]{2,1,0:T(8,128)(2,1)}, bf16[4,32,1764]{2,1,0:T(8,128)(2,1)}) custom-call(s32[1]{0:T(128)} %bitcast.me_ref, bf16[32,32,1764]{2,1,0:T(8,128)(2,1)} %maps_ref.7), custom_call_target="tpu_custom_call" | custom-call | flops 2750000128 | bytes 8750000 | tf_op jit(solution)/shard_map/pack/pallas_call | solution.py:764
  4.8 3.0 %collective-permute-start.1 = (bf16[240,384]{1,0:T(8,128)(2,1)}, bf16[240,384]{1,0:T(8,128)(2,1)}, u32[]{:S(2)}, u32[]{:S(2)}) collective-permute-start(bf16[240,384]{1,0:T(8,128)(2,1)} %bundle.1.refs_0_), channel_id=1, source_target_pairs={{0,2},{1,3},{2,0},{3,1},{4,6},{5,7},{6,4},{7,5},{8,10},{9,11},{10,... | collective-permute-start | bytes 552968 | tf_op jit(solution)/shard_map/ppermute | solution.py:845
  9.9 2.7 %pack.5 = (bf16[8,32,1764]{2,1,0:T(8,128)(2,1)}, bf16[8,32,1764]{2,1,0:T(8,128)(2,1)}) custom-call(s32[1]{0:T(128)} %bitcast.me_ref, bf16[32,32,1764]{2,1,0:T(8,128)(2,1)} %maps_ref.7, bf16[4,32,1764]{2,1,0:T(8,128)(2,1)} %get-tuple-element.79.refs_4_.refs_0_), custom_call_target="tpu_custom_call" | custom-call | flops 2750000128 | bytes 8750000 | tf_op jit(solution)/shard_map/pack/pallas_call | solution.py:764
  15.7 2.4 %unbundle.1 = (bf16[384,384]{1,0:T(8,128)(2,1)}, bf16[384,384]{1,0:T(8,128)(2,1)}, bf16[384,384]{1,0:T(8,128)(2,1)}, bf16[384,384]{1,0:T(8,128)(2,1)}, f32[2,128,100]{2,1,0:T(8,128)}, /*index=5*/f32[8,128]{1,0:T(8,128)}) custom-call(s32[1]{0:T(128)} %bitcast.me_ref, s32[1]{0:T(128)} %bitcast.2.task_ref, f32[2,100]{1,0:T(2,128)} %context_ref.1, ...), custom_call_target="tpu_custom_call" | custom-call | flops 2200000000 | bytes 7000000 | tf_op jit(solution)/shard_map/unbundle/pallas_call | solution.py:909
  18.1 4.9 %collective-permute-done.4.refs_0_.refs_3_ = bf16[4,32,1764]{2,1,0:T(8,128)(2,1)} collective-permute-done((bf16[4,32,1764]{2,1,0:T(8,128)(2,1)}, bf16[4,32,1764]{2,1,0:T(8,128)(2,1)}, u32[]{:S(2)}, u32[]{:S(2)}) %collective-permute-start.4) | collective-permute-done | bytes 451616 | tf_op jit(solution)/shard_map/ppermute | solution.py:845
  23.0 2.3 %pack.7 = (bf16[2,32,1764]{2,1,0:T(8,128)(2,1)}, bf16[2,32,1764]{2,1,0:T(8,128)(2,1)}) custom-call(s32[1]{0:T(128)} %bitcast.me_ref, bf16[32,32,1764]{2,1,0:T(8,128)(2,1)} %maps_ref.7, bf16[4,32,1764]{2,1,0:T(8,128)(2,1)} %collective-permute-done.4.refs_0_.refs_3_), custom_call_target="tpu_custom_call" | custom-call | flops 2750000128 | bytes 8750000 | tf_op jit(solution)/shard_map/pack/pallas_call | solution.py:764
  27.2 2.3 %pack.6 = (bf16[2,32,1764]{2,1,0:T(8,128)(2,1)}, bf16[2,32,1764]{2,1,0:T(8,128)(2,1)}) custom-call(s32[1]{0:T(128)} %bitcast.me_ref, bf16[32,32,1764]{2,1,0:T(8,128)(2,1)} %maps_ref.7, bf16[4,32,1764]{2,1,0:T(8,128)(2,1)} %collective-permute-done.4.refs_0_.refs_3_), custom_call_target="tpu_custom_call" | custom-call | flops 2750000128 | bytes 8750000 | tf_op jit(solution)/shard_map/pack/pallas_call | solution.py:764
  34.2 8.0 %first_conv.3 = (f32[8,128,1792]{2,1,0:T(8,128)}, bf16[8,128,1792]{2,1,0:T(8,128)(2,1)}, f32[128,128]{1,0:T(8,128)}) custom-call(s32[1]{0:T(128)} %bitcast.me_ref, f32[8]{0:T(128)} %compare_convert_fusion.live_ref, f32[8,128]{1,0:T(8,128)} %pad.4.told_ref, bf16[384,384]{1,0:T(8,128)(2,1)} %get-tuple-element.80.weights_ref, ...), custom_call_target="tpu_custom_call" | custom-call | flops 10119999488 | bytes 32200000 | tf_op jit(solution)/shard_map/first_conv/pallas_call | solution.py:938
  42.6 4.8 %first_conv.4 = (f32[8,128,1792]{2,1,0:T(8,128)}, bf16[8,128,1792]{2,1,0:T(8,128)(2,1)}, f32[128,128]{1,0:T(8,128)}) custom-call(s32[1]{0:T(128)} %bitcast.me_ref, f32[8]{0:T(128)} %compare_convert_fusion.live_ref, f32[8,128]{1,0:T(8,128)} %pad.4.told_ref, ...), custom_call_target="tpu_custom_call", output_to_operand_aliasing={{0}: (9, {}), {1}: (10, {})} | custom-call | flops 5059999744 | bytes 16099999 | tf_op jit(solution)/shard_map/first_conv/pallas_call | solution.py:938
  48.0 3.4 %collective-permute-done.6.refs_3_ = bf16[2,32,1764]{2,1,0:T(8,128)(2,1)} collective-permute-done((bf16[2,32,1764]{2,1,0:T(8,128)(2,1)}, bf16[2,32,1764]{2,1,0:T(8,128)(2,1)}, u32[]{:S(2)}, u32[]{:S(2)}) %collective-permute-start.6) | collective-permute-done | bytes 225824 | tf_op jit(solution)/shard_map/ppermute | solution.py:845
  51.3 4.8 %first_conv.5 = (f32[8,128,1792]{2,1,0:T(8,128)}, bf16[8,128,1792]{2,1,0:T(8,128)(2,1)}, f32[32,4,128]{2,1,0:T(4,128)}) custom-call(s32[1]{0:T(128)} %bitcast.me_ref, f32[8]{0:T(128)} %compare_convert_fusion.live_ref, f32[8,128]{1,0:T(8,128)} %pad.4.told_ref, ...), custom_call_target="tpu_custom_call", output_to_operand_aliasing={{0}: (9, {}), {1}: (10, {})} | custom-call | flops 5059999744 | bytes 16099999 | tf_op jit(solution)/shard_map/first_conv/pallas_call | solution.py:938
  56.1 6.4 %all-to-all-start = ((f32[32,4,128]{2,1,0:T(4,128)}), f32[32,4,128]{2,1,0:T(4,128)S(1)}, u32[]{:S(2)}, u32[]{:S(2)}) async-start(f32[32,4,128]{2,1,0:T(4,128)} %get-tuple-element.94), calls=%async_computation | async-start | bytes 131072 | tf_op jit(solution)/shard_map/all_to_all | solution.py:848
  62.6 7.2 %all-to-all-done.heard_ref.heard_two_ref = f32[32,4,128]{2,1,0:T(4,128)S(1)} async-done(((f32[32,4,128]{2,1,0:T(4,128)}), f32[32,4,128]{2,1,0:T(4,128)S(1)}, u32[]{:S(2)}, u32[]{:S(2)}) %all-to-all-start) | async-done | bytes 65568 | tf_op jit(solution)/shard_map/all_to_all | solution.py:848
  70.4 13.8 %middle.1 = (bf16[8,32,441]{2,1,0:T(8,128)(2,1)}, bf16[8,32,441]{2,1,0:T(8,128)(2,1)}, bf16[8,32,441]{2,1,0:T(8,128)(2,1)}, bf16[8,32,441]{2,1,0:T(8,128)(2,1)},...) custom-call(s32[1]{0:T(128)} %bitcast.me_ref, ...), custom_call_target="tpu_custom_call" | custom-call | flops 17600000000 | bytes 56000000 | tf_op jit(solution)/shard_map/middle/pallas_call | solution.py:970
  84.2 2.6 %all-to-all-start.1 = ((f32[32,4,128]{2,1,0:T(4,128)}), f32[32,4,128]{2,1,0:T(4,128)S(1)}, u32[]{:S(2)}, u32[]{:S(2)}) async-start(f32[32,4,128]{2,1,0:T(4,128)} %get-tuple-element.100.own_ref), calls=%async_computation.1 | async-start | bytes 131072 | tf_op jit(solution)/shard_map/all_to_all | solution.py:848
  94.8 6.1 %top.1 = (bf16[8,32,100]{2,1,0:T(8,128)(2,1)}, bf16[8,32,100]{2,1,0:T(8,128)(2,1)}, bf16[8,32,100]{2,1,0:T(8,128)(2,1)}, bf16[8,32,100]{2,1,0:T(8,128)(2,1)}, f3...) custom-call(s32[1]{0:T(128)} %bitcast.me_ref, ...), custom_call_target="tpu_custom_call" | custom-call | flops 7040000000 | bytes 22400000 | tf_op jit(solution)/shard_map/top/pallas_call | solution.py:1013
  100.9 4.1 %all-to-all-start.2 = ((f32[32,4,128]{2,1,0:T(4,128)}), f32[32,4,128]{2,1,0:T(4,128)S(1)}, u32[]{:S(2)}, u32[]{:S(2)}) async-start(f32[32,4,128]{2,1,0:T(4,128)} %get-tuple-element.109), calls=%async_computation.2 | async-start | bytes 131072 | tf_op jit(solution)/shard_map/all_to_all | solution.py:848
  108.9 3.5 %all-to-all-done.2.heard_ref.heard_top_ref = f32[32,4,128]{2,1,0:T(4,128)S(1)} async-done(((f32[32,4,128]{2,1,0:T(4,128)}), f32[32,4,128]{2,1,0:T(4,128)S(1)}, u32[]{:S(2)}, u32[]{:S(2)}) %all-to-all-start.2) | async-done | bytes 65568 | tf_op jit(solution)/shard_map/all_to_all | solution.py:848
  113.1 14.6 %back.1 = (bf16[8,128,1792]{2,1,0:T(8,128)(2,1)}, bf16[8,128,1792]{2,1,0:T(8,128)(2,1)}, bf16[8,128,512]{2,1,0:T(8,128)(2,1)}, f32[32,4,128]{2,1,0:T(4,128)}) custom-call(f32[8]{0:T(128)} %compare_convert_fusion.live_ref, f32[32,4,128]{2,1,0:T(4,128)} %copy-done.8, f32[8,128]{1,0:T(8,128)} %get-tuple-element.110.norm_three_ref, ...), custom_call_target="tpu_custom_call" | custom-call | flops 17600000000 | bytes 56000000 | tf_op jit(solution)/shard_map/back/pallas_call | solution.py:1067
  127.7 2.8 %all-to-all-start.3 = ((f32[32,4,128]{2,1,0:T(4,128)}), f32[32,4,128]{2,1,0:T(4,128)S(1)}, u32[]{:S(2)}, u32[]{:S(2)}) async-start(f32[32,4,128]{2,1,0:T(4,128)} %get-tuple-element.115.refs_0_), calls=%async_computation.3 | async-start | bytes 131072 | tf_op jit(solution)/shard_map/all_to_all | solution.py:848
  130.6 4.2 %filter_three.1.refs_0_ = bf16[4,2,3,32,384]{4,3,2,1,0:T(8,128)(2,1)} custom-call(bf16[8,128,512]{2,1,0:T(8,128)(2,1)} %get-tuple-element.120.error_ref, bf16[8,128,512]{2,1,0:T(8,128)(2,1)} %get-tuple-element.121.hidden_ref, f32[32,4,128]{2,1,0:T(4,128)} %get-tuple-element.115.refs_0_), custom_call_target="tpu_custom_call" | custom-call | flops 5500000256 | bytes 17500000 | tf_op jit(solution)/shard_map/filter_three/pallas_call | solution.py:1121
  134.8 2.8 %all-to-all-done.3.heard_ref.heard_back_ref = f32[32,4,128]{2,1,0:T(4,128)S(1)} async-done(((f32[32,4,128]{2,1,0:T(4,128)}), f32[32,4,128]{2,1,0:T(4,128)S(1)}, u32[]{:S(2)}, u32[]{:S(2)}) %all-to-all-start.3) | async-done | bytes 65568 | tf_op jit(solution)/shard_map/all_to_all | solution.py:848
  138.3 7.0 %last_conv.2 = (bf16[8,32,1764]{2,1,0:T(8,128)(2,1)}, bf16[8,32,1764]{2,1,0:T(8,128)(2,1)}, bf16[2,32,1764]{2,1,0:T(8,128)(2,1)}, bf16[2,32,1764]{2,1,0:T(8,128)...) custom-call(s32[1]{0:T(128)} %bitcast.me_ref, f32[8]{0:T(128)} %compare_convert_fusion.live_ref, ...), custom_call_target="tpu_custom_call" | custom-call | flops 6600000000 | bytes 21000000 | tf_op jit(solution)/shard_map/last_conv/pallas_call | solution.py:1158
  147.5 10.4 %last_filter.1.refs_0_ = bf16[4,2,3,32,384]{4,3,2,1,0:T(8,128)(2,1)} custom-call(f32[8]{0:T(128)} %compare_convert_fusion.live_ref, f32[32,4,128]{2,1,0:T(4,128)} %copy-done.9, f32[8,128]{1,0:T(8,128)} %get-tuple-element.111.norm_two_ref.norm_ref, f32[8,128]{1,0:T(8,128)} %get-tuple-element.95.vectors_ref, ...), custom_call_target="tpu_custom_call", output_to_operand_aliasing={{}: (7, {})} | custom-call | flops 10560000000 | bytes 33600000 | tf_op jit(solution)/shard_map/last_filter/pallas_call | solution.py:1186
  157.9 3.4 %all-to-all-start.4 = ((bf16[32,24,384]{2,1,0:T(8,128)(2,1)}), bf16[32,24,384]{2,1,0:T(8,128)(2,1)}, u32[]{:S(2)}, u32[]{:S(2)}) async-start(bf16[32,24,384]{2,1,0:T(8,128)(2,1)} %bitcast.31), calls=%async_computation.4 | async-start | bytes 1179648 | tf_op jit(solution)/shard_map/all_to_all | solution.py:1220
  164.0 6.8 %last_conv.3 = (bf16[8,32,1764]{2,1,0:T(8,128)(2,1)}, bf16[8,32,1764]{2,1,0:T(8,128)(2,1)}, bf16[4,32,1764]{2,1,0:T(8,128)(2,1)}, bf16[4,32,1764]{2,1,0:T(8,128)(2,1)}) custom-call(s32[1]{0:T(128)} %bitcast.me_ref, f32[8]{0:T(128)} %compare_convert_fusion.live_ref, f32[32,4,128]{2,1,0:T(4,128)} %copy-done.9, ...), custom_call_target="tpu_custom_call", output_to_operand_aliasing={{0}: (12, {}), {1}: (13, {})} | custom-call | flops 6600000000 | bytes 21000000 | tf_op jit(solution)/shard_map/last_conv/pallas_call | solution.py:1158
  174.9 4.1 %all-to-all-done.4.heard_ref = bf16[32,24,384]{2,1,0:T(8,128)(2,1)} async-done(((bf16[32,24,384]{2,1,0:T(8,128)(2,1)}), bf16[32,24,384]{2,1,0:T(8,128)(2,1)}, u32[]{:S(2)}, u32[]{:S(2)}) %all-to-all-start.4) | async-done | bytes 589856 | tf_op jit(solution)/shard_map/all_to_all | solution.py:1220
  180.9 3.4 %all-to-all-start.5 = ((f32[8,24,384]{2,1,0:T(8,128)}), f32[8,24,384]{2,1,0:T(8,128)S(1)}, u32[]{:S(2)}, u32[]{:S(2)}) async-start(f32[8,24,384]{2,1,0:T(8,128)} %strips.1), calls=%async_computation.5 | async-start | bytes 589824 | tf_op jit(solution)/shard_map/all_to_all | solution.py:1229
  184.4 2.5 %finish.1 = (f32[2,32,100]{2,1,0:T(8,128)}, f32[2,32]{1,0:T(2,128)}, f32[2,100]{1,0:T(2,128)}, f32[32]{0:T(128)}, f32[32]{0:T(128)}, /*index=5*/f32[32]{0:T(128)}, f32[32]{0:T(128)}, f32[9]{0:T(128)}) custom-call(s32[1]{0:T(128)} %bitcast.17.here_ref, s32[1]{0:T(128)} %bitcast.me_ref, f32[32,4,128]{2,1,0:T(4,128)} %copy-done.7, f32[32,4,128]{2,1,0:T(4,128)} %copy-done.8, ...), custom_call_target="tpu_custom_call" | custom-call | flops 2200000000 | bytes 7000000 | tf_op jit(solution)/shard_map/finish/pallas_call | solution.py:1239
  189.6 3.3 %unpack.6.refs_6_ = f32[32,32,1764]{2,1,0:T(8,128)} custom-call(s32[1]{0:T(128)} %bitcast.me_ref, bf16[8,32,1764]{2,1,0:T(8,128)(2,1)} %get-tuple-element.127.refs_4_.refs_6_.refs_0_, bf16[8,32,1764]{2,1,0:T(8,128)(2,1)} %collective-permute-done.25.refs_1_, bf16[2,32,1764]{2,1,0:T(8,128)(2,1)} %copy-done.1), custom_call_target="tpu_custom_call" | custom-call | flops 2200000000 | bytes 7000000 | tf_op jit(solution)/shard_map/unpack/pallas_call | solution.py:803
  195.3 3.7 %collective-permute-done.24.refs_5_ = bf16[4,32,1764]{2,1,0:T(8,128)(2,1)} collective-permute-done((bf16[4,32,1764]{2,1,0:T(8,128)(2,1)}, bf16[4,32,1764]{2,1,0:T(8,128)(2,1)}, u32[]{:S(2)}, u32[]{:S(2)}) %collective-permute-start.24) | collective-permute-done | bytes 451616 | tf_op jit(solution)/shard_map/ppermute | solution.py:845
  199.0 3.4 %unpack.7 = f32[32,32,1764]{2,1,0:T(8,128)} custom-call(s32[1]{0:T(128)} %bitcast.me_ref, bf16[2,32,1764]{2,1,0:T(8,128)(2,1)} %copy-done.6, bf16[2,32,1764]{2,1,0:T(8,128)(2,1)} %copy-done.1, bf16[4,32,1764]{2,1,0:T(8,128)(2,1)} %copy-done.2, bf16[2,32,1764]{2,1,0:T(8,128)(2,1)} %copy-done.4, ...), custom_call_target="tpu_custom_call", output_to_operand_aliasing={{}: (7, {})} | custom-call | flops 2200000000 | bytes 7000000 | tf_op jit(solution)/shard_map/unpack/pallas_call | solution.py:803
  (111 shorter events, 44.3 us)
Async XLA Ops:
  4.8 8.8 %collective-permute-start.1 = (bf16[240,384]{1,0:T(8,128)(2,1)}, bf16[240,384]{1,0:T(8,128)(2,1)}, u32[]{:S(2)}, u32[]{:S(2)}) collective-permute-start(bf16[240,384]{1,0:T(8,128)(2,1)} %bundle.1.refs_0_), channel_id=1, source_target_pairs={{0,2},{1,3},{2,0},{3,1},{4,6},{5,7},{6,4},{7,5},{8,10},{9,11},{10,... | collective-permute-start | bytes 552968 | tf_op jit(solution)/shard_map/ppermute | solution.py:845
  7.8 7.7 %collective-permute-start = (bf16[240,384]{1,0:T(8,128)(2,1)}, bf16[240,384]{1,0:T(8,128)(2,1)}, u32[]{:S(2)}, u32[]{:S(2)}) collective-permute-start(bf16[240,384]{1,0:T(8,128)(2,1)} %bundle.1.refs_0_), channel_id=1, source_target_pairs={{0,1},{1,0},{2,3},{3,2},{4,5},{5,4},{6,7},{7,6},{8,9},{9,8},{10,11... | collective-permute-start | bytes 552968 | tf_op jit(solution)/shard_map/ppermute | solution.py:845
  7.8 15.2 %collective-permute-start.4 = (bf16[4,32,1764]{2,1,0:T(8,128)(2,1)}, bf16[4,32,1764]{2,1,0:T(8,128)(2,1)}, u32[]{:S(2)}, u32[]{:S(2)}) collective-permute-start(bf16[4,32,1764]{2,1,0:T(8,128)(2,1)} %get-tuple-element.79.refs_4_.refs_0_), channel_id=1, source_target_pairs={{0,3},{1,2},{2,1},{3,0},{4,7},{5,6},{6,5},{7,4},{8,11},{9,10},{10,... | collective-permute-start | bytes 1354760 | tf_op jit(solution)/shard_map/ppermute | solution.py:845
  7.9 25.3 %collective-permute-start.9 = (bf16[4,32,1764]{2,1,0:T(8,128)(2,1)}, bf16[4,32,1764]{2,1,0:T(8,128)(2,1)}, u32[]{:S(2)}, u32[]{:S(2)}) collective-permute-start(bf16[4,32,1764]{2,1,0:T(8,128)(2,1)} %get-tuple-element.87), channel_id=1, source_target_pairs={{0,2},{1,3},{2,0},{3,1},{4,6},{5,7},{6,4},{7,5},{8,10},{9,11},{10,... | collective-permute-start | bytes 1354760 | tf_op jit(solution)/shard_map/ppermute | solution.py:845
  12.6 20.6 %collective-permute-start.3 = (bf16[8,32,1764]{2,1,0:T(8,128)(2,1)}, bf16[8,32,1764]{2,1,0:T(8,128)(2,1)S(1)}, u32[]{:S(2)}, u32[]{:S(2)}) collective-permute-start(bf16[8,32,1764]{2,1,0:T(8,128)(2,1)} %get-tuple-element.82), channel_id=1, source_target_pairs={{0,1},{1,0},{2,3},{3,2},{4,5},{5,4},{6,7},{7,6},{8,9},{9,8},{10,11... | collective-permute-start | bytes 2709512 | tf_op jit(solution)/shard_map/ppermute | solution.py:845
  13.6 2.1 %collective-permute-start.2 = (bf16[240,384]{1,0:T(8,128)(2,1)}, bf16[240,384]{1,0:T(8,128)(2,1)}, u32[]{:S(2)}, u32[]{:S(2)}) collective-permute-start(bf16[240,384]{1,0:T(8,128)(2,1)} %collective-permute-done.1.refs_2_), channel_id=1, source_target_pairs={{0,1},{1,0},{2,3},{3,2},{4,5},{5,4},{6,7},{7,6},{8,9},{9,8},{10,11... | collective-permute-start | bytes 552968 | tf_op jit(solution)/shard_map/ppermute | solution.py:845
  25.2 17.0 %collective-permute-start.7 = (bf16[2,32,1764]{2,1,0:T(8,128)(2,1)}, bf16[2,32,1764]{2,1,0:T(8,128)(2,1)}, u32[]{:S(2)}, u32[]{:S(2)}) collective-permute-start(bf16[2,32,1764]{2,1,0:T(8,128)(2,1)} %get-tuple-element.85), channel_id=1, source_target_pairs={{0,2},{1,3},{2,0},{3,1},{4,6},{5,7},{6,4},{7,5},{8,10},{9,11},{10,... | collective-permute-start | bytes 677384 | tf_op jit(solution)/shard_map/ppermute | solution.py:845
  25.4 17.2 %collective-permute-start.8 = (bf16[2,32,1764]{2,1,0:T(8,128)(2,1)}, bf16[2,32,1764]{2,1,0:T(8,128)(2,1)}, u32[]{:S(2)}, u32[]{:S(2)}) collective-permute-start(bf16[2,32,1764]{2,1,0:T(8,128)(2,1)} %get-tuple-element.86.refs_4_), channel_id=1, source_target_pairs={{0,3},{1,2},{2,1},{3,0},{4,7},{5,6},{6,5},{7,4},{8,11},{9,10},{10,... | collective-permute-start | bytes 677384 | tf_op jit(solution)/shard_map/ppermute | solution.py:845
  29.5 18.5 %collective-permute-start.5 = (bf16[2,32,1764]{2,1,0:T(8,128)(2,1)}, bf16[2,32,1764]{2,1,0:T(8,128)(2,1)}, u32[]{:S(2)}, u32[]{:S(2)}) collective-permute-start(bf16[2,32,1764]{2,1,0:T(8,128)(2,1)} %get-tuple-element.83), channel_id=1, source_target_pairs={{0,2},{1,3},{2,0},{3,1},{4,6},{5,7},{6,4},{7,5},{8,10},{9,11},{10,... | collective-permute-start | bytes 677384 | tf_op jit(solution)/shard_map/ppermute | solution.py:845
  33.2 18.1 %collective-permute-start.6 = (bf16[2,32,1764]{2,1,0:T(8,128)(2,1)}, bf16[2,32,1764]{2,1,0:T(8,128)(2,1)}, u32[]{:S(2)}, u32[]{:S(2)}) collective-permute-start(bf16[2,32,1764]{2,1,0:T(8,128)(2,1)} %get-tuple-element.84.refs_7_), channel_id=1, source_target_pairs={{0,3},{1,2},{2,1},{3,0},{4,7},{5,6},{6,5},{7,4},{8,11},{9,10},{10,... | collective-permute-start | bytes 677384 | tf_op jit(solution)/shard_map/ppermute | solution.py:845
  56.1 13.7 %all-to-all-start = ((f32[32,4,128]{2,1,0:T(4,128)}), f32[32,4,128]{2,1,0:T(4,128)S(1)}, u32[]{:S(2)}, u32[]{:S(2)}) async-start(f32[32,4,128]{2,1,0:T(4,128)} %get-tuple-element.94), calls=%async_computation | async-start | bytes 131072 | tf_op jit(solution)/shard_map/all_to_all | solution.py:848
  84.2 10.0 %all-to-all-start.1 = ((f32[32,4,128]{2,1,0:T(4,128)}), f32[32,4,128]{2,1,0:T(4,128)S(1)}, u32[]{:S(2)}, u32[]{:S(2)}) async-start(f32[32,4,128]{2,1,0:T(4,128)} %get-tuple-element.100.own_ref), calls=%async_computation.1 | async-start | bytes 131072 | tf_op jit(solution)/shard_map/all_to_all | solution.py:848
  86.9 2.7 %collective-permute-start.12 = (bf16[8,32,100]{2,1,0:T(8,128)(2,1)S(1)}, bf16[8,32,100]{2,1,0:T(8,128)(2,1)S(1)}, u32[]{:S(2)}, u32[]{:S(2)}) collective-permute-start(bf16[8,32,100]{2,1,0:T(8,128)(2,1)S(1)} %bitcast.33), channel_id=1, source_target_pairs={{0,1},{1,0},{2,3},{3,2},{4,5},{5,4},{6,7},{7,6},{8,9},{9,8},{10,11... | collective-permute-start | bytes 153608 | tf_op jit(solution)/shard_map/ppermute | solution.py:845
  87.1 4.8 %collective-permute-start.13 = (bf16[8,32,100]{2,1,0:T(8,128)(2,1)S(1)}, bf16[8,32,100]{2,1,0:T(8,128)(2,1)S(1)}, u32[]{:S(2)}, u32[]{:S(2)}) collective-permute-start(bf16[8,32,100]{2,1,0:T(8,128)(2,1)S(1)} %bitcast.34), channel_id=1, source_target_pairs={{0,2},{1,3},{2,0},{3,1},{4,6},{5,7},{6,4},{7,5},{8,10},{9,11},{10,... | collective-permute-start | bytes 153608 | tf_op jit(solution)/shard_map/ppermute | solution.py:845
  88.8 4.5 %collective-permute-start.14 = (bf16[8,32,100]{2,1,0:T(8,128)(2,1)S(1)}, bf16[8,32,100]{2,1,0:T(8,128)(2,1)S(1)}, u32[]{:S(2)}, u32[]{:S(2)}) collective-permute-start(bf16[8,32,100]{2,1,0:T(8,128)(2,1)S(1)} %bitcast.35), channel_id=1, source_target_pairs={{0,3},{1,2},{2,1},{3,0},{4,7},{5,6},{6,5},{7,4},{8,11},{9,10},{10,... | collective-permute-start | bytes 153608 | tf_op jit(solution)/shard_map/ppermute | solution.py:845
  100.9 11.6 %all-to-all-start.2 = ((f32[32,4,128]{2,1,0:T(4,128)}), f32[32,4,128]{2,1,0:T(4,128)S(1)}, u32[]{:S(2)}, u32[]{:S(2)}) async-start(f32[32,4,128]{2,1,0:T(4,128)} %get-tuple-element.109), calls=%async_computation.2 | async-start | bytes 131072 | tf_op jit(solution)/shard_map/all_to_all | solution.py:848
  105.0 29.8 %collective-permute-start.10 = (bf16[8,32,441]{2,1,0:T(8,128)(2,1)}, bf16[8,32,441]{2,1,0:T(8,128)(2,1)S(1)}, u32[]{:S(2)}, u32[]{:S(2)}) collective-permute-start(bf16[8,32,441]{2,1,0:T(8,128)(2,1)} %get-tuple-element.98), channel_id=1, source_target_pairs={{0,2},{1,3},{2,0},{3,1},{4,6},{5,7},{6,4},{7,5},{8,10},{9,11},{10,... | collective-permute-start | bytes 677384 | tf_op jit(solution)/shard_map/ppermute | solution.py:845
  106.8 28.0 %collective-permute-start.11 = (bf16[8,32,441]{2,1,0:T(8,128)(2,1)}, bf16[8,32,441]{2,1,0:T(8,128)(2,1)S(1)}, u32[]{:S(2)}, u32[]{:S(2)}) collective-permute-start(bf16[8,32,441]{2,1,0:T(8,128)(2,1)} %get-tuple-element.99), channel_id=1, source_target_pairs={{0,3},{1,2},{2,1},{3,0},{4,7},{5,6},{6,5},{7,4},{8,11},{9,10},{10,... | collective-permute-start | bytes 677384 | tf_op jit(solution)/shard_map/ppermute | solution.py:845
  106.8 28.0 %collective-permute-start.17 = (bf16[8,32,441]{2,1,0:T(8,128)(2,1)}, bf16[8,32,441]{2,1,0:T(8,128)(2,1)S(1)}, u32[]{:S(2)}, u32[]{:S(2)}) collective-permute-start(bf16[8,32,441]{2,1,0:T(8,128)(2,1)} %get-tuple-element.106), channel_id=1, source_target_pairs={{0,1},{1,0},{2,3},{3,2},{4,5},{5,4},{6,7},{7,6},{8,9},{9,8},{10,11... | collective-permute-start | bytes 677384 | tf_op jit(solution)/shard_map/ppermute | solution.py:845
  107.2 23.3 %collective-permute-start.15 = (bf16[8,32,100]{2,1,0:T(8,128)(2,1)}, bf16[8,32,100]{2,1,0:T(8,128)(2,1)S(1)}, u32[]{:S(2)}, u32[]{:S(2)}) collective-permute-start(bf16[8,32,100]{2,1,0:T(8,128)(2,1)} %get-tuple-element.103), channel_id=1, source_target_pairs={{0,2},{1,3},{2,0},{3,1},{4,6},{5,7},{6,4},{7,5},{8,10},{9,11},{10,... | collective-permute-start | bytes 153608 | tf_op jit(solution)/shard_map/ppermute | solution.py:845
  108.9 25.8 %collective-permute-start.16 = (bf16[8,32,100]{2,1,0:T(8,128)(2,1)}, bf16[8,32,100]{2,1,0:T(8,128)(2,1)S(1)}, u32[]{:S(2)}, u32[]{:S(2)}) collective-permute-start(bf16[8,32,100]{2,1,0:T(8,128)(2,1)} %get-tuple-element.104), channel_id=1, source_target_pairs={{0,3},{1,2},{2,1},{3,0},{4,7},{5,6},{6,5},{7,4},{8,11},{9,10},{10,... | collective-permute-start | bytes 153608 | tf_op jit(solution)/shard_map/ppermute | solution.py:845
  127.7 10.0 %all-to-all-start.3 = ((f32[32,4,128]{2,1,0:T(4,128)}), f32[32,4,128]{2,1,0:T(4,128)S(1)}, u32[]{:S(2)}, u32[]{:S(2)}) async-start(f32[32,4,128]{2,1,0:T(4,128)} %get-tuple-element.115.refs_0_), calls=%async_computation.3 | async-start | bytes 131072 | tf_op jit(solution)/shard_map/all_to_all | solution.py:848
  130.5 4.3 %collective-permute-start.18 = (bf16[8,32,100]{2,1,0:T(8,128)(2,1)}, bf16[8,32,100]{2,1,0:T(8,128)(2,1)}, u32[]{:S(2)}, u32[]{:S(2)}) collective-permute-start(bf16[8,32,100]{2,1,0:T(8,128)(2,1)} %get-tuple-element.108), channel_id=1, source_target_pairs={{0,1},{1,0},{2,3},{3,2},{4,5},{5,4},{6,7},{7,6},{8,9},{9,8},{10,11... | collective-permute-start | bytes 153608 | tf_op jit(solution)/shard_map/ppermute | solution.py:845
  145.3 16.0 %collective-permute-start.19 = (bf16[2,32,1764]{2,1,0:T(8,128)(2,1)}, bf16[2,32,1764]{2,1,0:T(8,128)(2,1)S(1)}, u32[]{:S(2)}, u32[]{:S(2)}) collective-permute-start(bf16[2,32,1764]{2,1,0:T(8,128)(2,1)} %get-tuple-element.123), channel_id=1, source_target_pairs={{0,3},{1,2},{2,1},{3,0},{4,7},{5,6},{6,5},{7,4},{8,11},{9,10},{10,... | collective-permute-start | bytes 677384 | tf_op jit(solution)/shard_map/ppermute | solution.py:845
  145.5 15.9 %collective-permute-start.20 = (bf16[2,32,1764]{2,1,0:T(8,128)(2,1)}, bf16[2,32,1764]{2,1,0:T(8,128)(2,1)S(1)}, u32[]{:S(2)}, u32[]{:S(2)}) collective-permute-start(bf16[2,32,1764]{2,1,0:T(8,128)(2,1)} %get-tuple-element.124), channel_id=1, source_target_pairs={{0,3},{1,2},{2,1},{3,0},{4,7},{5,6},{6,5},{7,4},{8,11},{9,10},{10,... | collective-permute-start | bytes 677384 | tf_op jit(solution)/shard_map/ppermute | solution.py:845
  147.1 16.2 %collective-permute-start.21 = (bf16[2,32,1764]{2,1,0:T(8,128)(2,1)}, bf16[2,32,1764]{2,1,0:T(8,128)(2,1)S(1)}, u32[]{:S(2)}, u32[]{:S(2)}) collective-permute-start(bf16[2,32,1764]{2,1,0:T(8,128)(2,1)} %get-tuple-element.125), channel_id=1, source_target_pairs={{0,2},{1,3},{2,0},{3,1},{4,6},{5,7},{6,4},{7,5},{8,10},{9,11},{10,... | collective-permute-start | bytes 677384 | tf_op jit(solution)/shard_map/ppermute | solution.py:845
  157.9 21.1 %all-to-all-start.4 = ((bf16[32,24,384]{2,1,0:T(8,128)(2,1)}), bf16[32,24,384]{2,1,0:T(8,128)(2,1)}, u32[]{:S(2)}, u32[]{:S(2)}) async-start(bf16[32,24,384]{2,1,0:T(8,128)(2,1)} %bitcast.31), calls=%async_computation.4 | async-start | bytes 1179648 | tf_op jit(solution)/shard_map/all_to_all | solution.py:1220
  170.8 18.1 %collective-permute-start.25 = (bf16[8,32,1764]{2,1,0:T(8,128)(2,1)}, bf16[8,32,1764]{2,1,0:T(8,128)(2,1)}, u32[]{:S(2)}, u32[]{:S(2)}) collective-permute-start(bf16[8,32,1764]{2,1,0:T(8,128)(2,1)} %get-tuple-element.135), channel_id=1, source_target_pairs={{0,1},{1,0},{2,3},{3,2},{4,5},{5,4},{6,7},{7,6},{8,9},{9,8},{10,11... | collective-permute-start | bytes 2709512 | tf_op jit(solution)/shard_map/ppermute | solution.py:845
  170.8 18.1 %collective-permute-start.22 = (bf16[2,32,1764]{2,1,0:T(8,128)(2,1)}, bf16[2,32,1764]{2,1,0:T(8,128)(2,1)S(1)}, u32[]{:S(2)}, u32[]{:S(2)}) collective-permute-start(bf16[2,32,1764]{2,1,0:T(8,128)(2,1)} %get-tuple-element.132), channel_id=1, source_target_pairs={{0,2},{1,3},{2,0},{3,1},{4,6},{5,7},{6,4},{7,5},{8,10},{9,11},{10,... | collective-permute-start | bytes 677384 | tf_op jit(solution)/shard_map/ppermute | solution.py:845
  171.3 23.9 %collective-permute-start.23 = (bf16[4,32,1764]{2,1,0:T(8,128)(2,1)}, bf16[4,32,1764]{2,1,0:T(8,128)(2,1)S(1)}, u32[]{:S(2)}, u32[]{:S(2)}) collective-permute-start(bf16[4,32,1764]{2,1,0:T(8,128)(2,1)} %get-tuple-element.133), channel_id=1, source_target_pairs={{0,2},{1,3},{2,0},{3,1},{4,6},{5,7},{6,4},{7,5},{8,10},{9,11},{10,... | collective-permute-start | bytes 1354760 | tf_op jit(solution)/shard_map/ppermute | solution.py:845
  172.9 26.1 %collective-permute-start.24 = (bf16[4,32,1764]{2,1,0:T(8,128)(2,1)}, bf16[4,32,1764]{2,1,0:T(8,128)(2,1)}, u32[]{:S(2)}, u32[]{:S(2)}) collective-permute-start(bf16[4,32,1764]{2,1,0:T(8,128)(2,1)} %get-tuple-element.134), channel_id=1, source_target_pairs={{0,3},{1,2},{2,1},{3,0},{4,7},{5,6},{6,5},{7,4},{8,11},{9,10},{10,... | collective-permute-start | bytes 1354760 | tf_op jit(solution)/shard_map/ppermute | solution.py:845
  180.9 12.8 %all-to-all-start.5 = ((f32[8,24,384]{2,1,0:T(8,128)}), f32[8,24,384]{2,1,0:T(8,128)S(1)}, u32[]{:S(2)}, u32[]{:S(2)}) async-start(f32[8,24,384]{2,1,0:T(8,128)} %strips.1), calls=%async_computation.5 | async-start | bytes 589824 | tf_op jit(solution)/shard_map/all_to_all | solution.py:1229
  (22 other events, 68.2 us)

commit v5 on v4

--- a/solution.py
+++ b/solution.py
@@ -508,7 +508,7 @@
         )
         totals[...] = jnp.zeros_like(totals)
 
-    grad_sum, product_sum = column(totals, 0), column(totals, 1)
+    grad_tile = product_tile = jnp.zeros((C, C), F32)
     for image in range(count):
         away = conv_three_ref[image] - column(columns_three, 0)
         error = norm_back(live_ref[step * count + image], columns_three, grad_ref[image], away, CELLS_THREE)
@@ -521,16 +521,21 @@
         ],
         axis=0,
     )
-    left = dot_halves(split[:, :256], unpool_a_ref)
-    right = dot_halves(split[:, 128:], unpool_b_ref)
     for image in range(count):
-        away = conv_two_ref[image] - column(columns_two, 0)
-        pre = away * column(columns_two, 1) + column(columns_two, 2)
-        grad_pre = jnp.concatenate([left[image], right[image]], axis=1) * gelu_slope(pre, gelu_gate(pre))
-        out_ref[image] = grad_pre.astype(BF16)
-        away_ref[image] = away.astype(BF16)
-        grad_sum = grad_sum + lane_sum(grad_pre)
-        product_sum = product_sum + lane_sum(grad_pre * away)
+        both = split[2 * C * image : 2 * C * (image + 1)]
+        for first, (half, unpool_ref) in enumerate(((both[:, :256], unpool_a_ref), (both[:, 128:], unpool_b_ref))):
+            for start, stop in ((0, 384), (384, 640), (640, 896)):
+                (spread,) = dot_halves(half, unpool_ref.at[:, start:stop])
+                cells = slice(first * 896 + start, first * 896 + stop)
+                away = conv_two_ref[image, :, cells] - column(columns_two, 0)
+                away_ref[image, :, cells] = away.astype(BF16)
+                pre = away * column(columns_two, 1) + column(columns_two, 2)
+                grad_pre = spread * gelu_slope(pre, gelu_gate(pre))
+                out_ref[image, :, cells] = grad_pre.astype(BF16)
+                grad_tile = grad_tile + sum(cut(grad_pre, 128))
+                product_tile = product_tile + sum(cut(grad_pre * away, 128))
+    grad_sum = column(totals, 0) + lane_sum(grad_tile)
+    product_sum = column(totals, 1) + lane_sum(product_tile)
     totals[...] = column_tile([grad_sum, product_sum])
 
     @pl.when(step == pl.num_programs(0) - 1)
@@ -851,7 +856,7 @@
     half, quarter = images_each // 2, images_each // 4
     sizes_in = (half, quarter, quarter) if quarter >= pair else (half, half)
     half = images_each // 2
-    calls_out = ((pair,) * (half // pair), (half,))
+    calls_out = (*[(pair,)] * (half // pair), (half,))
     starts_in = [sum(sizes_in[:part]) for part in range(len(sizes_in))]
     counts_of = [(images_each,) if partner < near else sizes_in for partner in range(partners)]
     far = [partner for partner in reversed(range(partners)) if partner >= near]
@@ -1182,7 +1187,7 @@
         for place in range(len(sizes)):
             for partner in reversed(far):
                 returned[partner].append(swap(pieces[near + place * len(far) + partner - near], partner))
-        if first < images_each:
+        if first == half:
             product = pl.pallas_call(
                 last_filter_kernel,
                 grid=(images_each // pair,),
@@ -1205,35 +1210,14 @@
                 name="last_filter",
                 cost_estimate=lasting(1.2 * images_each),
             )(live, *common, grad_two, away_two, whole_maps, filter_sums, kept[0])
-            waits = [product, *(piece for partner in far[:-1] for piece in returned[partner]), returned[near][0]]
+            waits = [product, *(piece for partner in far for piece in returned[partner])]
     for partner in range(near):
         returned[partner].append(swap(kept[partner], partner))
 
-    arrivals = [returned[partner][place] for place in range(len(returned[near])) for partner in reversed(far)]
-    count_first = len(far) * len(calls_out[0])
     blocks = ()
     for place in range(partners // group):
         blocks = unpack([block_two, out_pieces], me, images_each, BF16, place, blocks, [kept[0]])
     block_two, block_three = blocks
-
-    strip = 6 * rows // columns
-    heard = lax.all_to_all(product.reshape(devices, strip, 3 * C), ("tensor", "dp"), 0, 0)
-    strips = pl.pallas_call(
-        strips_kernel,
-        in_specs=[pl.BlockSpec(memory_space=pltpu.VMEM), *anywhere(1)],
-        out_shape=jax.ShapeDtypeStruct((columns, strip, 3 * C), F32),
-        compiler_params=kernel_params(0),
-        name="strips",
-        cost_estimate=lasting(1.5),
-    )(heard, kept[0])
-    strips = lax.all_to_all(strips, "dp", 0, 0)
-    grad_filters = jnp.transpose(strips.reshape(2, 3, rows, 3, C), (0, 2, 4, 1, 3))
-
-    grad_images = ()
-    for place in range(partners // group):
-        waits = (strips,) if grad_images else (returned[near][1],)
-        grad_images = unpack([returned], me, images_each, F32, place, grad_images, waits)
-    (grad_images,) = grad_images
 
     contexts = context.shape[0]
     grad_film_w, grad_film_b, grad_context, *norm_sums, levels = pl.pallas_call(
@@ -1262,6 +1246,26 @@
         film,
         kept[0],
     )
+
+    strip = 6 * rows // columns
+    heard = lax.all_to_all(product.reshape(devices, strip, 3 * C), ("tensor", "dp"), 0, 0)
+    strips = pl.pallas_call(
+        strips_kernel,
+        in_specs=[pl.BlockSpec(memory_space=pltpu.VMEM), *anywhere(2)],
+        out_shape=jax.ShapeDtypeStruct((columns, strip, 3 * C), F32),
+        compiler_params=kernel_params(0),
+        name="strips",
+        cost_estimate=lasting(1.5),
+    )(heard, block_two, norm_sums[0])
+    strips = lax.all_to_all(strips, "dp", 0, 0)
+    grad_filters = jnp.transpose(strips.reshape(2, 3, rows, 3, C), (0, 2, 4, 1, 3))
+
+    grad_images = ()
+    for place in range(partners // group):
+        waits = () if grad_images else (kept[0],)
+        grad_images = unpack([returned], me, images_each, F32, place, grad_images, waits)
+    (grad_images,) = grad_images
+
     return (
         block_two,
         block_three,

time: 203 us -> 202 us (level)
  waiting for transfers between devices: 40.5 us -> 36.1 us
    all_to_all x1, waiting for transfers between devices: 4.15 us -> 1.23 us  [local(): lax.all_to_all(product.reshape(devices, strip, 3 * C), ('tensor', 'dp'),...]
    pallas_call x2 -> x3, Pallas kernels: 13.8 us -> 16.2 us  [local(): pl.pallas_call(functools.partial(last_conv_kernel, partners, near, first,...]
    unnamed x50 -> x42, local copies, waits for them, and re-layouts: 6.84 us -> 6.32 us
  transfers between devices with their start and end apart: 32 -> 32, of which waited for: 17 -> 16; matrix products, arithmetic and copies ran while one was open for 2% -> 2% of each run, Pallas kernels for 35% -> 39%
where the time goes in v5:
time: 202 us; the launch traced here: 201 us
  Pallas kernels  111 us (55%)
  starting transfers between devices  43.5 us (22%)
  waiting for transfers between devices  36.1 us (18%)
  local copies, waits for them, and re-layouts  7.76 us (4%)
    ppermute x26, waiting for transfers between devices, swap(): lax.ppermute(value, 'tensor', [(i, i ^ partner) for i in range(partners)])  20.5 us
    ppermute x26, starting transfers between devices, swap(): lax.ppermute(value, 'tensor', [(i, i ^ partner) for i in range(partners)])  20.5 us
    pallas_call x3, Pallas kernels, local(): pl.pallas_call(functools.partial(first_conv_kernel, partners, first, fina...  17.6 us
    pallas_call x3, Pallas kernels, local(): pl.pallas_call(functools.partial(last_conv_kernel, partners, near, first,...  16.2 us
    all_to_all x4, starting transfers between devices, share(): return lax.all_to_all(copies, ('dp', 'tensor'), 0, 0)  15.9 us
    pallas_call x1, Pallas kernels, local(): pl.pallas_call(back_kernel, grid=(images_each // pair,), in_specs=[smem()...  14.4 us
    all_to_all x4, waiting for transfers between devices, share(): return lax.all_to_all(copies, ('dp', 'tensor'), 0, 0)  14.4 us
    pallas_call x1, Pallas kernels, local(): pl.pallas_call(functools.partial(middle_kernel, partners), grid=(images_e...  13.8 us
  transfers between devices with their start and end apart: 32, of which 16 were waited for; matrix products, arithmetic and copies ran while one was open for 2% of the time, Pallas kernels for 39%

profile of v5, /device:TPU:0, one launch (start us, length us, event | category | flops | bytes accessed | tf_op | source)
XLA Modules:
  0.0 201.0 jit_solution(18120485097941727059)
XLA Ops:
  0.6 2.4 %pack.4 = (bf16[4,32,1764]{2,1,0:T(8,128)(2,1)}, bf16[4,32,1764]{2,1,0:T(8,128)(2,1)}) custom-call(s32[1]{0:T(128)} %bitcast.me_ref, bf16[32,32,1764]{2,1,0:T(8,128)(2,1)} %maps_ref.7), custom_call_target="tpu_custom_call" | custom-call | flops 2750000128 | bytes 8750000 | tf_op jit(solution)/shard_map/pack/pallas_call | solution.py:769
  4.8 3.0 %collective-permute-start.1 = (bf16[240,384]{1,0:T(8,128)(2,1)}, bf16[240,384]{1,0:T(8,128)(2,1)}, u32[]{:S(2)}, u32[]{:S(2)}) collective-permute-start(bf16[240,384]{1,0:T(8,128)(2,1)} %bundle.1.refs_0_), channel_id=1, source_target_pairs={{0,2},{1,3},{2,0},{3,1},{4,6},{5,7},{6,4},{7,5},{8,10},{9,11},{10,... | collective-permute-start | bytes 552968 | tf_op jit(solution)/shard_map/ppermute | solution.py:850
  9.9 2.7 %pack.5 = (bf16[8,32,1764]{2,1,0:T(8,128)(2,1)}, bf16[8,32,1764]{2,1,0:T(8,128)(2,1)}) custom-call(s32[1]{0:T(128)} %bitcast.me_ref, bf16[32,32,1764]{2,1,0:T(8,128)(2,1)} %maps_ref.7, bf16[4,32,1764]{2,1,0:T(8,128)(2,1)} %get-tuple-element.81.refs_4_.refs_0_), custom_call_target="tpu_custom_call" | custom-call | flops 2750000128 | bytes 8750000 | tf_op jit(solution)/shard_map/pack/pallas_call | solution.py:769
  15.7 2.4 %unbundle.1 = (bf16[384,384]{1,0:T(8,128)(2,1)}, bf16[384,384]{1,0:T(8,128)(2,1)}, bf16[384,384]{1,0:T(8,128)(2,1)}, bf16[384,384]{1,0:T(8,128)(2,1)}, f32[2,128,100]{2,1,0:T(8,128)}, /*index=5*/f32[8,128]{1,0:T(8,128)}) custom-call(s32[1]{0:T(128)} %bitcast.me_ref, s32[1]{0:T(128)} %bitcast.2.task_ref, f32[2,100]{1,0:T(2,128)} %context_ref.1, ...), custom_call_target="tpu_custom_call" | custom-call | flops 2200000000 | bytes 7000000 | tf_op jit(solution)/shard_map/unbundle/pallas_call | solution.py:914
  18.0 4.9 %collective-permute-done.4.refs_0_.refs_3_ = bf16[4,32,1764]{2,1,0:T(8,128)(2,1)} collective-permute-done((bf16[4,32,1764]{2,1,0:T(8,128)(2,1)}, bf16[4,32,1764]{2,1,0:T(8,128)(2,1)}, u32[]{:S(2)}, u32[]{:S(2)}) %collective-permute-start.4) | collective-permute-done | bytes 451616 | tf_op jit(solution)/shard_map/ppermute | solution.py:850
  22.9 2.3 %pack.7 = (bf16[2,32,1764]{2,1,0:T(8,128)(2,1)}, bf16[2,32,1764]{2,1,0:T(8,128)(2,1)}) custom-call(s32[1]{0:T(128)} %bitcast.me_ref, bf16[32,32,1764]{2,1,0:T(8,128)(2,1)} %maps_ref.7, bf16[4,32,1764]{2,1,0:T(8,128)(2,1)} %collective-permute-done.4.refs_0_.refs_3_), custom_call_target="tpu_custom_call" | custom-call | flops 2750000128 | bytes 8750000 | tf_op jit(solution)/shard_map/pack/pallas_call | solution.py:769
  27.2 2.3 %pack.6 = (bf16[2,32,1764]{2,1,0:T(8,128)(2,1)}, bf16[2,32,1764]{2,1,0:T(8,128)(2,1)}) custom-call(s32[1]{0:T(128)} %bitcast.me_ref, bf16[32,32,1764]{2,1,0:T(8,128)(2,1)} %maps_ref.7, bf16[4,32,1764]{2,1,0:T(8,128)(2,1)} %collective-permute-done.4.refs_0_.refs_3_), custom_call_target="tpu_custom_call" | custom-call | flops 2750000128 | bytes 8750000 | tf_op jit(solution)/shard_map/pack/pallas_call | solution.py:769
  34.2 8.0 %first_conv.3 = (f32[8,128,1792]{2,1,0:T(8,128)}, bf16[8,128,1792]{2,1,0:T(8,128)(2,1)}, f32[128,128]{1,0:T(8,128)}) custom-call(s32[1]{0:T(128)} %bitcast.me_ref, f32[8]{0:T(128)} %compare_convert_fusion.live_ref, f32[8,128]{1,0:T(8,128)} %pad.4.told_ref, bf16[384,384]{1,0:T(8,128)(2,1)} %get-tuple-element.82.weights_ref, ...), custom_call_target="tpu_custom_call" | custom-call | flops 10119999488 | bytes 32200000 | tf_op jit(solution)/shard_map/first_conv/pallas_call | solution.py:943
  42.6 4.8 %first_conv.4 = (f32[8,128,1792]{2,1,0:T(8,128)}, bf16[8,128,1792]{2,1,0:T(8,128)(2,1)}, f32[128,128]{1,0:T(8,128)}) custom-call(s32[1]{0:T(128)} %bitcast.me_ref, f32[8]{0:T(128)} %compare_convert_fusion.live_ref, f32[8,128]{1,0:T(8,128)} %pad.4.told_ref, ...), custom_call_target="tpu_custom_call", output_to_operand_aliasing={{0}: (9, {}), {1}: (10, {})} | custom-call | flops 5059999744 | bytes 16099999 | tf_op jit(solution)/shard_map/first_conv/pallas_call | solution.py:943
  47.9 3.4 %collective-permute-done.6.refs_3_ = bf16[2,32,1764]{2,1,0:T(8,128)(2,1)} collective-permute-done((bf16[2,32,1764]{2,1,0:T(8,128)(2,1)}, bf16[2,32,1764]{2,1,0:T(8,128)(2,1)}, u32[]{:S(2)}, u32[]{:S(2)}) %collective-permute-start.6) | collective-permute-done | bytes 225824 | tf_op jit(solution)/shard_map/ppermute | solution.py:850
  51.3 4.8 %first_conv.5 = (f32[8,128,1792]{2,1,0:T(8,128)}, bf16[8,128,1792]{2,1,0:T(8,128)(2,1)}, f32[32,4,128]{2,1,0:T(4,128)}) custom-call(s32[1]{0:T(128)} %bitcast.me_ref, f32[8]{0:T(128)} %compare_convert_fusion.live_ref, f32[8,128]{1,0:T(8,128)} %pad.4.told_ref, ...), custom_call_target="tpu_custom_call", output_to_operand_aliasing={{0}: (9, {}), {1}: (10, {})} | custom-call | flops 5059999744 | bytes 16099999 | tf_op jit(solution)/shard_map/first_conv/pallas_call | solution.py:943
  56.1 6.4 %all-to-all-start = ((f32[32,4,128]{2,1,0:T(4,128)}), f32[32,4,128]{2,1,0:T(4,128)S(1)}, u32[]{:S(2)}, u32[]{:S(2)}) async-start(f32[32,4,128]{2,1,0:T(4,128)} %get-tuple-element.96), calls=%async_computation | async-start | bytes 131072 | tf_op jit(solution)/shard_map/all_to_all | solution.py:853
  62.5 7.2 %all-to-all-done.heard_ref.heard_two_ref = f32[32,4,128]{2,1,0:T(4,128)S(1)} async-done(((f32[32,4,128]{2,1,0:T(4,128)}), f32[32,4,128]{2,1,0:T(4,128)S(1)}, u32[]{:S(2)}, u32[]{:S(2)}) %all-to-all-start) | async-done | bytes 65568 | tf_op jit(solution)/shard_map/all_to_all | solution.py:853
  70.4 13.8 %middle.1 = (bf16[8,32,441]{2,1,0:T(8,128)(2,1)}, bf16[8,32,441]{2,1,0:T(8,128)(2,1)}, bf16[8,32,441]{2,1,0:T(8,128)(2,1)}, bf16[8,32,441]{2,1,0:T(8,128)(2,1)},...) custom-call(s32[1]{0:T(128)} %bitcast.me_ref, ...), custom_call_target="tpu_custom_call" | custom-call | flops 17600000000 | bytes 56000000 | tf_op jit(solution)/shard_map/middle/pallas_call | solution.py:975
  84.1 2.6 %all-to-all-start.1 = ((f32[32,4,128]{2,1,0:T(4,128)}), f32[32,4,128]{2,1,0:T(4,128)S(1)}, u32[]{:S(2)}, u32[]{:S(2)}) async-start(f32[32,4,128]{2,1,0:T(4,128)} %get-tuple-element.102.own_ref), calls=%async_computation.1 | async-start | bytes 131072 | tf_op jit(solution)/shard_map/all_to_all | solution.py:853
  94.8 6.0 %top.1 = (bf16[8,32,100]{2,1,0:T(8,128)(2,1)}, bf16[8,32,100]{2,1,0:T(8,128)(2,1)}, bf16[8,32,100]{2,1,0:T(8,128)(2,1)}, bf16[8,32,100]{2,1,0:T(8,128)(2,1)}, f3...) custom-call(s32[1]{0:T(128)} %bitcast.me_ref, ...), custom_call_target="tpu_custom_call" | custom-call | flops 7040000000 | bytes 22400000 | tf_op jit(solution)/shard_map/top/pallas_call | solution.py:1018
  100.8 4.1 %all-to-all-start.2 = ((f32[32,4,128]{2,1,0:T(4,128)}), f32[32,4,128]{2,1,0:T(4,128)S(1)}, u32[]{:S(2)}, u32[]{:S(2)}) async-start(f32[32,4,128]{2,1,0:T(4,128)} %get-tuple-element.111), calls=%async_computation.2 | async-start | bytes 131072 | tf_op jit(solution)/shard_map/all_to_all | solution.py:853
  108.9 3.5 %all-to-all-done.2.heard_ref.heard_top_ref = f32[32,4,128]{2,1,0:T(4,128)S(1)} async-done(((f32[32,4,128]{2,1,0:T(4,128)}), f32[32,4,128]{2,1,0:T(4,128)S(1)}, u32[]{:S(2)}, u32[]{:S(2)}) %all-to-all-start.2) | async-done | bytes 65568 | tf_op jit(solution)/shard_map/all_to_all | solution.py:853
  113.0 14.4 %back.1 = (bf16[8,128,1792]{2,1,0:T(8,128)(2,1)}, bf16[8,128,1792]{2,1,0:T(8,128)(2,1)}, bf16[8,128,512]{2,1,0:T(8,128)(2,1)}, f32[32,4,128]{2,1,0:T(4,128)}) custom-call(f32[8]{0:T(128)} %compare_convert_fusion.live_ref, f32[32,4,128]{2,1,0:T(4,128)} %copy-done.4, f32[8,128]{1,0:T(8,128)} %get-tuple-element.112.norm_three_ref, ...), custom_call_target="tpu_custom_call" | custom-call | flops 17600000000 | bytes 56000000 | tf_op jit(solution)/shard_map/back/pallas_call | solution.py:1072
  127.4 2.8 %all-to-all-start.3 = ((f32[32,4,128]{2,1,0:T(4,128)}), f32[32,4,128]{2,1,0:T(4,128)S(1)}, u32[]{:S(2)}, u32[]{:S(2)}) async-start(f32[32,4,128]{2,1,0:T(4,128)} %get-tuple-element.117.refs_0_), calls=%async_computation.3 | async-start | bytes 131072 | tf_op jit(solution)/shard_map/all_to_all | solution.py:853
  130.3 4.2 %filter_three.1.refs_0_ = bf16[4,2,3,32,384]{4,3,2,1,0:T(8,128)(2,1)} custom-call(bf16[8,128,512]{2,1,0:T(8,128)(2,1)} %get-tuple-element.122.error_ref, bf16[8,128,512]{2,1,0:T(8,128)(2,1)} %get-tuple-element.123.hidden_ref, f32[32,4,128]{2,1,0:T(4,128)} %get-tuple-element.117.refs_0_), custom_call_target="tpu_custom_call" | custom-call | flops 5500000256 | bytes 17500000 | tf_op jit(solution)/shard_map/filter_three/pallas_call | solution.py:1126
  134.6 2.8 %all-to-all-done.3.heard_ref.heard_back_ref = f32[32,4,128]{2,1,0:T(4,128)S(1)} async-done(((f32[32,4,128]{2,1,0:T(4,128)}), f32[32,4,128]{2,1,0:T(4,128)S(1)}, u32[]{:S(2)}, u32[]{:S(2)}) %all-to-all-start.3) | async-done | bytes 65568 | tf_op jit(solution)/shard_map/all_to_all | solution.py:853
  138.0 4.6 %last_conv.3 = (bf16[8,32,1764]{2,1,0:T(8,128)(2,1)}, bf16[8,32,1764]{2,1,0:T(8,128)(2,1)}, bf16[2,32,1764]{2,1,0:T(8,128)(2,1)}, bf16[2,32,1764]{2,1,0:T(8,128)(2,1)}) custom-call(s32[1]{0:T(128)} %bitcast.me_ref, f32[8]{0:T(128)} %compare_convert_fusion.live_ref, f32[32,4,128]{2,1,0:T(4,128)} %copy-done.5, ...), custom_call_target="tpu_custom_call" | custom-call | flops 3300000000 | bytes 10500000 | tf_op jit(solution)/shard_map/last_conv/pallas_call | solution.py:1163
  144.4 4.7 %last_conv.4 = (bf16[8,32,1764]{2,1,0:T(8,128)(2,1)}, bf16[8,32,1764]{2,1,0:T(8,128)(2,1)}, bf16[2,32,1764]{2,1,0:T(8,128)(2,1)}, bf16[2,32,1764]{2,1,0:T(8,128)(2,1)}) custom-call(s32[1]{0:T(128)} %bitcast.me_ref, f32[8]{0:T(128)} %compare_convert_fusion.live_ref, f32[32,4,128]{2,1,0:T(4,128)} %copy-done.5, ...), custom_call_target="tpu_custom_call", output_to_operand_aliasing={{0}: (8, {}), {1}: (9, {})} | custom-call | flops 3300000000 | bytes 10500000 | tf_op jit(solution)/shard_map/last_conv/pallas_call | solution.py:1163
  150.9 10.4 %last_filter.1.refs_0_ = bf16[4,2,3,32,384]{4,3,2,1,0:T(8,128)(2,1)} custom-call(f32[8]{0:T(128)} %compare_convert_fusion.live_ref, f32[32,4,128]{2,1,0:T(4,128)} %copy-done.5, f32[8,128]{1,0:T(8,128)} %get-tuple-element.113.norm_two_ref.norm_ref, f32[8,128]{1,0:T(8,128)} %get-tuple-element.97.vectors_ref, ...), custom_call_target="tpu_custom_call", output_to_operand_aliasing={{}: (7, {})} | custom-call | flops 10560000000 | bytes 33600000 | tf_op jit(solution)/shard_map/last_filter/pallas_call | solution.py:1191
  161.3 3.1 %all-to-all-start.4 = ((bf16[32,24,384]{2,1,0:T(8,128)(2,1)}), bf16[32,24,384]{2,1,0:T(8,128)(2,1)S(1)}, u32[]{:S(2)}, u32[]{:S(2)}) async-start(bf16[32,24,384]{2,1,0:T(8,128)(2,1)} %bitcast.31), calls=%async_computation.4 | async-start | bytes 1179648 | tf_op jit(solution)/shard_map/all_to_all | solution.py:1251
  165.7 6.9 %last_conv.5 = (bf16[8,32,1764]{2,1,0:T(8,128)(2,1)}, bf16[8,32,1764]{2,1,0:T(8,128)(2,1)}, bf16[4,32,1764]{2,1,0:T(8,128)(2,1)}, bf16[4,32,1764]{2,1,0:T(8,128)(2,1)}) custom-call(s32[1]{0:T(128)} %bitcast.me_ref, f32[8]{0:T(128)} %compare_convert_fusion.live_ref, f32[32,4,128]{2,1,0:T(4,128)} %copy-done.5, ...), custom_call_target="tpu_custom_call", output_to_operand_aliasing={{0}: (13, {}), {1}: (14, {})} | custom-call | flops 6600000000 | bytes 21000000 | tf_op jit(solution)/shard_map/last_conv/pallas_call | solution.py:1163
  176.4 2.5 %finish.1 = (f32[2,32,100]{2,1,0:T(8,128)}, f32[2,32]{1,0:T(2,128)}, f32[2,100]{1,0:T(2,128)}, f32[32]{0:T(128)}, f32[32]{0:T(128)}, /*index=5*/f32[32]{0:T(128)}, f32[32]{0:T(128)}, f32[9]{0:T(128)}) custom-call(s32[1]{0:T(128)} %bitcast.15.here_ref, s32[1]{0:T(128)} %bitcast.me_ref, f32[32,4,128]{2,1,0:T(4,128)} %copy-done.3, f32[32,4,128]{2,1,0:T(4,128)} %copy-done.4, ...), custom_call_target="tpu_custom_call" | custom-call | flops 2200000000 | bytes 7000000 | tf_op jit(solution)/shard_map/finish/pallas_call | solution.py:1223
  184.9 4.0 %all-to-all-start.5 = ((f32[8,24,384]{2,1,0:T(8,128)}), f32[8,24,384]{2,1,0:T(8,128)S(1)}, u32[]{:S(2)}, u32[]{:S(2)}) async-start(f32[8,24,384]{2,1,0:T(8,128)} %strips.1), calls=%async_computation.5 | async-start | bytes 589824 | tf_op jit(solution)/shard_map/all_to_all | solution.py:1260
  188.9 3.3 %unpack.6.refs_6_ = f32[32,32,1764]{2,1,0:T(8,128)} custom-call(s32[1]{0:T(128)} %bitcast.me_ref, bf16[8,32,1764]{2,1,0:T(8,128)(2,1)} %get-tuple-element.132.refs_4_.refs_6_.refs_0_.refs_2_, bf16[8,32,1764]{2,1,0:T(8,128)(2,1)} %collective-permute-done.25.refs_1_, bf16[8,32,1764]{2,1,0:T(8,128)(2,1)} %get-tuple-element.132.refs_4_.refs_6_.refs_0_.refs_2_), custom_call_target="tpu_custom_call" | custom-call | flops 2200000000 | bytes 7000000 | tf_op jit(solution)/shard_map/unpack/pallas_call | solution.py:808
  192.2 3.8 %collective-permute-done.24.refs_5_ = bf16[4,32,1764]{2,1,0:T(8,128)(2,1)} collective-permute-done((bf16[4,32,1764]{2,1,0:T(8,128)(2,1)}, bf16[4,32,1764]{2,1,0:T(8,128)(2,1)}, u32[]{:S(2)}, u32[]{:S(2)}) %collective-permute-start.24) | collective-permute-done | bytes 451616 | tf_op jit(solution)/shard_map/ppermute | solution.py:850
  196.0 3.4 %unpack.7 = f32[32,32,1764]{2,1,0:T(8,128)} custom-call(s32[1]{0:T(128)} %bitcast.me_ref, bf16[2,32,1764]{2,1,0:T(8,128)(2,1)} %collective-permute-done.21.refs_3_.refs_0_, bf16[2,32,1764]{2,1,0:T(8,128)(2,1)} %collective-permute-done.22.refs_4_.refs_1_, bf16[4,32,1764]{2,1,0:T(8,128)(2,1)} %collective-permute-done.23.refs_2_, ...), custom_call_target="tpu_custom_call", output_to_operand_aliasing={{}: (7, {})} | custom-call | flops 2200000000 | bytes 7000000 | tf_op jit(solution)/shard_map/unpack/pallas_call | solution.py:808
  (104 shorter events, 44.5 us)
Async XLA Ops:
  4.8 8.8 %collective-permute-start.1 = (bf16[240,384]{1,0:T(8,128)(2,1)}, bf16[240,384]{1,0:T(8,128)(2,1)}, u32[]{:S(2)}, u32[]{:S(2)}) collective-permute-start(bf16[240,384]{1,0:T(8,128)(2,1)} %bundle.1.refs_0_), channel_id=1, source_target_pairs={{0,2},{1,3},{2,0},{3,1},{4,6},{5,7},{6,4},{7,5},{8,10},{9,11},{10,... | collective-permute-start | bytes 552968 | tf_op jit(solution)/shard_map/ppermute | solution.py:850
  7.7 7.7 %collective-permute-start = (bf16[240,384]{1,0:T(8,128)(2,1)}, bf16[240,384]{1,0:T(8,128)(2,1)}, u32[]{:S(2)}, u32[]{:S(2)}) collective-permute-start(bf16[240,384]{1,0:T(8,128)(2,1)} %bundle.1.refs_0_), channel_id=1, source_target_pairs={{0,1},{1,0},{2,3},{3,2},{4,5},{5,4},{6,7},{7,6},{8,9},{9,8},{10,11... | collective-permute-start | bytes 552968 | tf_op jit(solution)/shard_map/ppermute | solution.py:850
  7.7 15.2 %collective-permute-start.4 = (bf16[4,32,1764]{2,1,0:T(8,128)(2,1)}, bf16[4,32,1764]{2,1,0:T(8,128)(2,1)}, u32[]{:S(2)}, u32[]{:S(2)}) collective-permute-start(bf16[4,32,1764]{2,1,0:T(8,128)(2,1)} %get-tuple-element.81.refs_4_.refs_0_), channel_id=1, source_target_pairs={{0,3},{1,2},{2,1},{3,0},{4,7},{5,6},{6,5},{7,4},{8,11},{9,10},{10,... | collective-permute-start | bytes 1354760 | tf_op jit(solution)/shard_map/ppermute | solution.py:850
  7.9 25.3 %collective-permute-start.9 = (bf16[4,32,1764]{2,1,0:T(8,128)(2,1)}, bf16[4,32,1764]{2,1,0:T(8,128)(2,1)}, u32[]{:S(2)}, u32[]{:S(2)}) collective-permute-start(bf16[4,32,1764]{2,1,0:T(8,128)(2,1)} %get-tuple-element.89), channel_id=1, source_target_pairs={{0,2},{1,3},{2,0},{3,1},{4,6},{5,7},{6,4},{7,5},{8,10},{9,11},{10,... | collective-permute-start | bytes 1354760 | tf_op jit(solution)/shard_map/ppermute | solution.py:850
  12.6 20.6 %collective-permute-start.3 = (bf16[8,32,1764]{2,1,0:T(8,128)(2,1)}, bf16[8,32,1764]{2,1,0:T(8,128)(2,1)S(1)}, u32[]{:S(2)}, u32[]{:S(2)}) collective-permute-start(bf16[8,32,1764]{2,1,0:T(8,128)(2,1)} %get-tuple-element.84), channel_id=1, source_target_pairs={{0,1},{1,0},{2,3},{3,2},{4,5},{5,4},{6,7},{7,6},{8,9},{9,8},{10,11... | collective-permute-start | bytes 2709512 | tf_op jit(solution)/shard_map/ppermute | solution.py:850
  13.5 2.1 %collective-permute-start.2 = (bf16[240,384]{1,0:T(8,128)(2,1)}, bf16[240,384]{1,0:T(8,128)(2,1)}, u32[]{:S(2)}, u32[]{:S(2)}) collective-permute-start(bf16[240,384]{1,0:T(8,128)(2,1)} %collective-permute-done.1.refs_2_), channel_id=1, source_target_pairs={{0,1},{1,0},{2,3},{3,2},{4,5},{5,4},{6,7},{7,6},{8,9},{9,8},{10,11... | collective-permute-start | bytes 552968 | tf_op jit(solution)/shard_map/ppermute | solution.py:850
  25.2 17.0 %collective-permute-start.7 = (bf16[2,32,1764]{2,1,0:T(8,128)(2,1)}, bf16[2,32,1764]{2,1,0:T(8,128)(2,1)}, u32[]{:S(2)}, u32[]{:S(2)}) collective-permute-start(bf16[2,32,1764]{2,1,0:T(8,128)(2,1)} %get-tuple-element.87), channel_id=1, source_target_pairs={{0,2},{1,3},{2,0},{3,1},{4,6},{5,7},{6,4},{7,5},{8,10},{9,11},{10,... | collective-permute-start | bytes 677384 | tf_op jit(solution)/shard_map/ppermute | solution.py:850
  25.4 17.2 %collective-permute-start.8 = (bf16[2,32,1764]{2,1,0:T(8,128)(2,1)}, bf16[2,32,1764]{2,1,0:T(8,128)(2,1)}, u32[]{:S(2)}, u32[]{:S(2)}) collective-permute-start(bf16[2,32,1764]{2,1,0:T(8,128)(2,1)} %get-tuple-element.88.refs_4_), channel_id=1, source_target_pairs={{0,3},{1,2},{2,1},{3,0},{4,7},{5,6},{6,5},{7,4},{8,11},{9,10},{10,... | collective-permute-start | bytes 677384 | tf_op jit(solution)/shard_map/ppermute | solution.py:850
  29.5 18.5 %collective-permute-start.5 = (bf16[2,32,1764]{2,1,0:T(8,128)(2,1)}, bf16[2,32,1764]{2,1,0:T(8,128)(2,1)}, u32[]{:S(2)}, u32[]{:S(2)}) collective-permute-start(bf16[2,32,1764]{2,1,0:T(8,128)(2,1)} %get-tuple-element.85), channel_id=1, source_target_pairs={{0,2},{1,3},{2,0},{3,1},{4,6},{5,7},{6,4},{7,5},{8,10},{9,11},{10,... | collective-permute-start | bytes 677384 | tf_op jit(solution)/shard_map/ppermute | solution.py:850
  33.2 18.1 %collective-permute-start.6 = (bf16[2,32,1764]{2,1,0:T(8,128)(2,1)}, bf16[2,32,1764]{2,1,0:T(8,128)(2,1)}, u32[]{:S(2)}, u32[]{:S(2)}) collective-permute-start(bf16[2,32,1764]{2,1,0:T(8,128)(2,1)} %get-tuple-element.86.refs_7_), channel_id=1, source_target_pairs={{0,3},{1,2},{2,1},{3,0},{4,7},{5,6},{6,5},{7,4},{8,11},{9,10},{10,... | collective-permute-start | bytes 677384 | tf_op jit(solution)/shard_map/ppermute | solution.py:850
  56.1 13.7 %all-to-all-start = ((f32[32,4,128]{2,1,0:T(4,128)}), f32[32,4,128]{2,1,0:T(4,128)S(1)}, u32[]{:S(2)}, u32[]{:S(2)}) async-start(f32[32,4,128]{2,1,0:T(4,128)} %get-tuple-element.96), calls=%async_computation | async-start | bytes 131072 | tf_op jit(solution)/shard_map/all_to_all | solution.py:853
  84.1 10.0 %all-to-all-start.1 = ((f32[32,4,128]{2,1,0:T(4,128)}), f32[32,4,128]{2,1,0:T(4,128)S(1)}, u32[]{:S(2)}, u32[]{:S(2)}) async-start(f32[32,4,128]{2,1,0:T(4,128)} %get-tuple-element.102.own_ref), calls=%async_computation.1 | async-start | bytes 131072 | tf_op jit(solution)/shard_map/all_to_all | solution.py:853
  86.8 2.7 %collective-permute-start.12 = (bf16[8,32,100]{2,1,0:T(8,128)(2,1)S(1)}, bf16[8,32,100]{2,1,0:T(8,128)(2,1)S(1)}, u32[]{:S(2)}, u32[]{:S(2)}) collective-permute-start(bf16[8,32,100]{2,1,0:T(8,128)(2,1)S(1)} %bitcast.33), channel_id=1, source_target_pairs={{0,1},{1,0},{2,3},{3,2},{4,5},{5,4},{6,7},{7,6},{8,9},{9,8},{10,11... | collective-permute-start | bytes 153608 | tf_op jit(solution)/shard_map/ppermute | solution.py:850
  87.0 4.8 %collective-permute-start.13 = (bf16[8,32,100]{2,1,0:T(8,128)(2,1)S(1)}, bf16[8,32,100]{2,1,0:T(8,128)(2,1)S(1)}, u32[]{:S(2)}, u32[]{:S(2)}) collective-permute-start(bf16[8,32,100]{2,1,0:T(8,128)(2,1)S(1)} %bitcast.34), channel_id=1, source_target_pairs={{0,2},{1,3},{2,0},{3,1},{4,6},{5,7},{6,4},{7,5},{8,10},{9,11},{10,... | collective-permute-start | bytes 153608 | tf_op jit(solution)/shard_map/ppermute | solution.py:850
  88.8 4.5 %collective-permute-start.14 = (bf16[8,32,100]{2,1,0:T(8,128)(2,1)S(1)}, bf16[8,32,100]{2,1,0:T(8,128)(2,1)S(1)}, u32[]{:S(2)}, u32[]{:S(2)}) collective-permute-start(bf16[8,32,100]{2,1,0:T(8,128)(2,1)S(1)} %bitcast.35), channel_id=1, source_target_pairs={{0,3},{1,2},{2,1},{3,0},{4,7},{5,6},{6,5},{7,4},{8,11},{9,10},{10,... | collective-permute-start | bytes 153608 | tf_op jit(solution)/shard_map/ppermute | solution.py:850
  100.8 11.6 %all-to-all-start.2 = ((f32[32,4,128]{2,1,0:T(4,128)}), f32[32,4,128]{2,1,0:T(4,128)S(1)}, u32[]{:S(2)}, u32[]{:S(2)}) async-start(f32[32,4,128]{2,1,0:T(4,128)} %get-tuple-element.111), calls=%async_computation.2 | async-start | bytes 131072 | tf_op jit(solution)/shard_map/all_to_all | solution.py:853
  104.9 29.6 %collective-permute-start.10 = (bf16[8,32,441]{2,1,0:T(8,128)(2,1)}, bf16[8,32,441]{2,1,0:T(8,128)(2,1)S(1)}, u32[]{:S(2)}, u32[]{:S(2)}) collective-permute-start(bf16[8,32,441]{2,1,0:T(8,128)(2,1)} %get-tuple-element.100), channel_id=1, source_target_pairs={{0,2},{1,3},{2,0},{3,1},{4,6},{5,7},{6,4},{7,5},{8,10},{9,11},{10,... | collective-permute-start | bytes 677384 | tf_op jit(solution)/shard_map/ppermute | solution.py:850
  106.7 27.8 %collective-permute-start.11 = (bf16[8,32,441]{2,1,0:T(8,128)(2,1)}, bf16[8,32,441]{2,1,0:T(8,128)(2,1)S(1)}, u32[]{:S(2)}, u32[]{:S(2)}) collective-permute-start(bf16[8,32,441]{2,1,0:T(8,128)(2,1)} %get-tuple-element.101), channel_id=1, source_target_pairs={{0,3},{1,2},{2,1},{3,0},{4,7},{5,6},{6,5},{7,4},{8,11},{9,10},{10,... | collective-permute-start | bytes 677384 | tf_op jit(solution)/shard_map/ppermute | solution.py:850
  106.7 27.9 %collective-permute-start.17 = (bf16[8,32,441]{2,1,0:T(8,128)(2,1)}, bf16[8,32,441]{2,1,0:T(8,128)(2,1)S(1)}, u32[]{:S(2)}, u32[]{:S(2)}) collective-permute-start(bf16[8,32,441]{2,1,0:T(8,128)(2,1)} %get-tuple-element.108), channel_id=1, source_target_pairs={{0,1},{1,0},{2,3},{3,2},{4,5},{5,4},{6,7},{7,6},{8,9},{9,8},{10,11... | collective-permute-start | bytes 677384 | tf_op jit(solution)/shard_map/ppermute | solution.py:850
  107.1 23.2 %collective-permute-start.15 = (bf16[8,32,100]{2,1,0:T(8,128)(2,1)}, bf16[8,32,100]{2,1,0:T(8,128)(2,1)S(1)}, u32[]{:S(2)}, u32[]{:S(2)}) collective-permute-start(bf16[8,32,100]{2,1,0:T(8,128)(2,1)} %get-tuple-element.105), channel_id=1, source_target_pairs={{0,2},{1,3},{2,0},{3,1},{4,6},{5,7},{6,4},{7,5},{8,10},{9,11},{10,... | collective-permute-start | bytes 153608 | tf_op jit(solution)/shard_map/ppermute | solution.py:850
  108.9 25.7 %collective-permute-start.16 = (bf16[8,32,100]{2,1,0:T(8,128)(2,1)}, bf16[8,32,100]{2,1,0:T(8,128)(2,1)S(1)}, u32[]{:S(2)}, u32[]{:S(2)}) collective-permute-start(bf16[8,32,100]{2,1,0:T(8,128)(2,1)} %get-tuple-element.106), channel_id=1, source_target_pairs={{0,3},{1,2},{2,1},{3,0},{4,7},{5,6},{6,5},{7,4},{8,11},{9,10},{10,... | collective-permute-start | bytes 153608 | tf_op jit(solution)/shard_map/ppermute | solution.py:850
  127.4 10.0 %all-to-all-start.3 = ((f32[32,4,128]{2,1,0:T(4,128)}), f32[32,4,128]{2,1,0:T(4,128)S(1)}, u32[]{:S(2)}, u32[]{:S(2)}) async-start(f32[32,4,128]{2,1,0:T(4,128)} %get-tuple-element.117.refs_0_), calls=%async_computation.3 | async-start | bytes 131072 | tf_op jit(solution)/shard_map/all_to_all | solution.py:853
  130.3 4.3 %collective-permute-start.18 = (bf16[8,32,100]{2,1,0:T(8,128)(2,1)}, bf16[8,32,100]{2,1,0:T(8,128)(2,1)}, u32[]{:S(2)}, u32[]{:S(2)}) collective-permute-start(bf16[8,32,100]{2,1,0:T(8,128)(2,1)} %get-tuple-element.110), channel_id=1, source_target_pairs={{0,1},{1,0},{2,3},{3,2},{4,5},{5,4},{6,7},{7,6},{8,9},{9,8},{10,11... | collective-permute-start | bytes 153608 | tf_op jit(solution)/shard_map/ppermute | solution.py:850
  142.7 21.7 %collective-permute-start.19 = (bf16[2,32,1764]{2,1,0:T(8,128)(2,1)}, bf16[2,32,1764]{2,1,0:T(8,128)(2,1)S(1)}, u32[]{:S(2)}, u32[]{:S(2)}) collective-permute-start(bf16[2,32,1764]{2,1,0:T(8,128)(2,1)} %get-tuple-element.127), channel_id=1, source_target_pairs={{0,3},{1,2},{2,1},{3,0},{4,7},{5,6},{6,5},{7,4},{8,11},{9,10},{10,... | collective-permute-start | bytes 677384 | tf_op jit(solution)/shard_map/ppermute | solution.py:850
  142.8 21.6 %collective-permute-start.21 = (bf16[2,32,1764]{2,1,0:T(8,128)(2,1)}, bf16[2,32,1764]{2,1,0:T(8,128)(2,1)}, u32[]{:S(2)}, u32[]{:S(2)}) collective-permute-start(bf16[2,32,1764]{2,1,0:T(8,128)(2,1)} %get-tuple-element.129), channel_id=1, source_target_pairs={{0,2},{1,3},{2,0},{3,1},{4,6},{5,7},{6,4},{7,5},{8,10},{9,11},{10,... | collective-permute-start | bytes 677384 | tf_op jit(solution)/shard_map/ppermute | solution.py:850
  149.1 15.3 %collective-permute-start.20 = (bf16[2,32,1764]{2,1,0:T(8,128)(2,1)}, bf16[2,32,1764]{2,1,0:T(8,128)(2,1)}, u32[]{:S(2)}, u32[]{:S(2)}) collective-permute-start(bf16[2,32,1764]{2,1,0:T(8,128)(2,1)} %get-tuple-element.128), channel_id=1, source_target_pairs={{0,3},{1,2},{2,1},{3,0},{4,7},{5,6},{6,5},{7,4},{8,11},{9,10},{10,... | collective-permute-start | bytes 677384 | tf_op jit(solution)/shard_map/ppermute | solution.py:850
  149.3 16.4 %collective-permute-start.22 = (bf16[2,32,1764]{2,1,0:T(8,128)(2,1)}, bf16[2,32,1764]{2,1,0:T(8,128)(2,1)}, u32[]{:S(2)}, u32[]{:S(2)}) collective-permute-start(bf16[2,32,1764]{2,1,0:T(8,128)(2,1)} %get-tuple-element.130), channel_id=1, source_target_pairs={{0,2},{1,3},{2,0},{3,1},{4,6},{5,7},{6,4},{7,5},{8,10},{9,11},{10,... | collective-permute-start | bytes 677384 | tf_op jit(solution)/shard_map/ppermute | solution.py:850
  161.3 20.9 %all-to-all-start.4 = ((bf16[32,24,384]{2,1,0:T(8,128)(2,1)}), bf16[32,24,384]{2,1,0:T(8,128)(2,1)S(1)}, u32[]{:S(2)}, u32[]{:S(2)}) async-start(bf16[32,24,384]{2,1,0:T(8,128)(2,1)} %bitcast.31), calls=%async_computation.4 | async-start | bytes 1179648 | tf_op jit(solution)/shard_map/all_to_all | solution.py:1251
  172.5 16.3 %collective-permute-start.25 = (bf16[8,32,1764]{2,1,0:T(8,128)(2,1)}, bf16[8,32,1764]{2,1,0:T(8,128)(2,1)}, u32[]{:S(2)}, u32[]{:S(2)}) collective-permute-start(bf16[8,32,1764]{2,1,0:T(8,128)(2,1)} %get-tuple-element.139), channel_id=1, source_target_pairs={{0,1},{1,0},{2,3},{3,2},{4,5},{5,4},{6,7},{7,6},{8,9},{9,8},{10,11... | collective-permute-start | bytes 2709512 | tf_op jit(solution)/shard_map/ppermute | solution.py:850
  172.6 19.6 %collective-permute-start.23 = (bf16[4,32,1764]{2,1,0:T(8,128)(2,1)}, bf16[4,32,1764]{2,1,0:T(8,128)(2,1)}, u32[]{:S(2)}, u32[]{:S(2)}) collective-permute-start(bf16[4,32,1764]{2,1,0:T(8,128)(2,1)} %get-tuple-element.137), channel_id=1, source_target_pairs={{0,2},{1,3},{2,0},{3,1},{4,6},{5,7},{6,4},{7,5},{8,10},{9,11},{10,... | collective-permute-start | bytes 1354760 | tf_op jit(solution)/shard_map/ppermute | solution.py:850
  173.9 22.1 %collective-permute-start.24 = (bf16[4,32,1764]{2,1,0:T(8,128)(2,1)}, bf16[4,32,1764]{2,1,0:T(8,128)(2,1)}, u32[]{:S(2)}, u32[]{:S(2)}) collective-permute-start(bf16[4,32,1764]{2,1,0:T(8,128)(2,1)} %get-tuple-element.138), channel_id=1, source_target_pairs={{0,3},{1,2},{2,1},{3,0},{4,7},{5,6},{6,5},{7,4},{8,11},{9,10},{10,... | collective-permute-start | bytes 1354760 | tf_op jit(solution)/shard_map/ppermute | solution.py:850
  184.9 14.5 %all-to-all-start.5 = ((f32[8,24,384]{2,1,0:T(8,128)}), f32[8,24,384]{2,1,0:T(8,128)S(1)}, u32[]{:S(2)}, u32[]{:S(2)}) async-start(f32[8,24,384]{2,1,0:T(8,128)} %strips.1), calls=%async_computation.5 | async-start | bytes 589824 | tf_op jit(solution)/shard_map/all_to_all | solution.py:1260
  (18 other events, 56.1 us)

commit v6 on v5

--- a/solution.py
+++ b/solution.py
@@ -495,7 +495,7 @@
     conv_two_ref,
     *refs,
 ):
-    out_ref, away_ref, error_ref, sums_ref, columns_three, columns_two, totals, upright = refs[-8:]
+    out_ref, error_ref, sums_ref, columns_three, columns_two, totals, upright = refs[-7:]
     step = pl.program_id(0)
     count = conv_two_ref.shape[0]
 
@@ -528,10 +528,9 @@
                 (spread,) = dot_halves(half, unpool_ref.at[:, start:stop])
                 cells = slice(first * 896 + start, first * 896 + stop)
                 away = conv_two_ref[image, :, cells] - column(columns_two, 0)
-                away_ref[image, :, cells] = away.astype(BF16)
                 pre = away * column(columns_two, 1) + column(columns_two, 2)
                 grad_pre = spread * gelu_slope(pre, gelu_gate(pre))
-                out_ref[image, :, cells] = grad_pre.astype(BF16)
+                out_ref[image, :, cells] = grad_pre
                 grad_tile = grad_tile + sum(cut(grad_pre, 128))
                 product_tile = product_tile + sum(cut(grad_pre * away, 128))
     grad_sum = column(totals, 0) + lane_sum(grad_tile)
@@ -549,7 +548,7 @@
     partners, _, rows, _ = filter_ref.shape
     for tap in range(3):
         for owner in range(partners):
-            filter_ref[owner, tap] = product[tap * C + owner * rows : tap * C + (owner + 1) * rows].astype(BF16)
+            filter_ref[owner, tap] = product[tap * C + owner * rows : tap * C + (owner + 1) * rows]
 
 
 def filter_three_kernel(error_ref, hidden_ref, *refs):
@@ -588,7 +587,7 @@
     vectors_ref,
     weights_ref,
     grad_ref,
-    away_ref,
+    conv_ref,
     *refs,
 ):
     far = partners - near
@@ -602,7 +601,8 @@
 
     for image in range(count):
         live = live_ref[first + step * count + image]
-        error = norm_back(live, columns, grad_ref[image], away_ref[image], CELLS_TWO)
+        away = conv_ref[image] - column(columns, 0)
+        error = norm_back(live, columns, grad_ref[image], away, CELLS_TWO)
         stack_upright(cut(error, WIDE), MAP, upright.at[image])
         write(output.at[image], [block.astype(BF16) for block in conv_behind(weights_ref, upright.at[image], MAP)])
     rows = C // partners
@@ -619,7 +619,7 @@
         start += length
 
 
-def last_filter_kernel(live_ref, heard_ref, norm_ref, vectors_ref, grad_ref, away_ref, maps_ref, *refs):
+def last_filter_kernel(live_ref, heard_ref, norm_ref, vectors_ref, grad_ref, conv_ref, maps_ref, *refs):
     filter_ref, product, columns, stack, upright = refs[-5:]
     step = pl.program_id(0)
     count = grad_ref.shape[0]
@@ -630,7 +630,8 @@
         product[...] = jnp.zeros_like(product)
 
     for image in range(count):
-        error = norm_back(live_ref[step * count + image], columns, grad_ref[image], away_ref[image], CELLS_TWO)
+        away = conv_ref[image] - column(columns, 0)
+        error = norm_back(live_ref[step * count + image], columns, grad_ref[image], away, CELLS_TWO)
         stack_upright(cut(error, WIDE), MAP, upright.at[image])
         stack_sideways(cut(maps_ref[image], WIDE), MAP, stack.at[image])
         product[...] += across_cells(upright.at[image], stack.at[image])
@@ -1064,12 +1065,12 @@
     block_two = [[swap(block_pieces[k], k)] for k in range(partners)]
     out_pieces = [[swap(out_pieces[k], k)] for k in range(partners)]
 
-    filter_shape = jax.ShapeDtypeStruct((partners, 2, 3, rows, 3 * C), BF16)
+    filter_shape = jax.ShapeDtypeStruct((partners, 2, 3, rows, 3 * C), F32)
 
     def filter_spec(block):
         return pl.BlockSpec((partners, None, 3, rows, 3 * C), lambda n: (0, block, 0, 0, 0))
 
-    grad_two, away_two, error_three, sums_two = pl.pallas_call(
+    grad_two, error_three, sums_two = pl.pallas_call(
         back_kernel,
         grid=(images_each // pair,),
         in_specs=[
@@ -1088,13 +1089,11 @@
         ],
         out_specs=[
             each(C, LANES_TWO, count=pair),
-            each(C, LANES_TWO, count=pair),
             each(C, LANES_THREE, count=pair),
             whole(devices, SENT, C),
         ],
         out_shape=[
-            jax.ShapeDtypeStruct((images_each, C, LANES_TWO), BF16),
-            jax.ShapeDtypeStruct((images_each, C, LANES_TWO), BF16),
+            jax.ShapeDtypeStruct((images_each, C, LANES_TWO), F32),
             jax.ShapeDtypeStruct((images_each, C, LANES_THREE), BF16),
             jax.ShapeDtypeStruct((devices, SENT, C), F32),
         ],
@@ -1159,7 +1158,7 @@
                 )
             ] * len(far)
             out_shape += [jax.ShapeDtypeStruct((length * one, rows, CELLS_TWO), BF16)] * len(far)
-        inputs = [me, live, *common, behind_two, grad_two, away_two]
+        inputs = [me, live, *common, behind_two, grad_two, conv_two]
         pieces = pl.pallas_call(
             functools.partial(last_conv_kernel, partners, near, first, steps),
             grid=(count // one,),
@@ -1209,7 +1208,7 @@
                 compiler_params=kernel_params(),
                 name="last_filter",
                 cost_estimate=lasting(1.2 * images_each),
-            )(live, *common, grad_two, away_two, whole_maps, filter_sums, kept[0])
+            )(live, *common, grad_two, conv_two, whole_maps, filter_sums, kept[0])
             waits = [product, *(piece for partner in far for piece in returned[partner])]
     for partner in range(near):
         returned[partner].append(swap(kept[partner], partner))

time: 202 us -> 236 us (1.17)
  waiting for transfers between devices: 36.1 us -> 64.8 us
  Pallas kernels: 111 us -> 115 us
    ppermute x26, waiting for transfers between devices: 20.5 us -> 50.6 us  [swap(): lax.ppermute(value, 'tensor', [(i, i ^ partner) for i in range(partners)])]
    unnamed x42 -> x48, local copies, waits for them, and re-layouts: 6.32 us -> 6.17 us
  transfers between devices with their start and end apart: 32 -> 32, of which waited for: 16 -> 18; matrix products, arithmetic and copies ran while one was open for 2% -> 1% of each run, Pallas kernels for 39% -> 27%
where the time goes in v6:
time: 236 us; the launch traced here: 235 us
  Pallas kernels  115 us (49%)
  waiting for transfers between devices  64.8 us (27%)
  starting transfers between devices  45.2 us (19%)
  local copies, waits for them, and re-layouts  7.61 us (3%)
    ppermute x26, waiting for transfers between devices, swap(): lax.ppermute(value, 'tensor', [(i, i ^ partner) for i in range(partners)])  50.6 us
    ppermute x26, starting transfers between devices, swap(): lax.ppermute(value, 'tensor', [(i, i ^ partner) for i in range(partners)])  20.6 us
    pallas_call x3, Pallas kernels, local(): pl.pallas_call(functools.partial(last_conv_kernel, partners, near, first,...  18.1 us
    pallas_call x3, Pallas kernels, local(): pl.pallas_call(functools.partial(first_conv_kernel, partners, first, fina...  17.6 us
    all_to_all x4, starting transfers between devices, share(): return lax.all_to_all(copies, ('dp', 'tensor'), 0, 0)  15.8 us
    all_to_all x4, waiting for transfers between devices, share(): return lax.all_to_all(copies, ('dp', 'tensor'), 0, 0)  14.2 us
    pallas_call x1, Pallas kernels, local(): pl.pallas_call(back_kernel, grid=(images_each // pair,), in_specs=[smem()...  14.1 us
    pallas_call x1, Pallas kernels, local(): pl.pallas_call(functools.partial(middle_kernel, partners), grid=(images_e...  13.8 us
  transfers between devices with their start and end apart: 32, of which 18 were waited for; matrix products, arithmetic and copies ran while one was open for 1% of the time, Pallas kernels for 27%

profile of v6, /device:TPU:0, one launch (start us, length us, event | category | flops | bytes accessed | tf_op | source)
XLA Modules:
  0.0 234.8 jit_solution(1342486733715553077)
XLA Ops:
  4.8 3.0 %collective-permute-start.1 = (bf16[240,384]{1,0:T(8,128)(2,1)}, bf16[240,384]{1,0:T(8,128)(2,1)}, u32[]{:S(2)}, u32[]{:S(2)}) collective-permute-start(bf16[240,384]{1,0:T(8,128)(2,1)} %bundle.1.refs_0_), channel_id=1, source_target_pairs={{0,2},{1,3},{2,0},{3,1},{4,6},{5,7},{6,4},{7,5},{8,10},{9,11},{10,... | collective-permute-start | bytes 552968 | tf_op jit(solution)/shard_map/ppermute | solution.py:851
  9.9 2.7 %pack.5 = (bf16[8,32,1764]{2,1,0:T(8,128)(2,1)}, bf16[8,32,1764]{2,1,0:T(8,128)(2,1)}) custom-call(s32[1]{0:T(128)} %bitcast.me_ref, bf16[32,32,1764]{2,1,0:T(8,128)(2,1)} %maps_ref.7, bf16[4,32,1764]{2,1,0:T(8,128)(2,1)} %get-tuple-element.80.refs_4_.refs_0_), custom_call_target="tpu_custom_call" | custom-call | flops 2750000128 | bytes 8750000 | tf_op jit(solution)/shard_map/pack/pallas_call | solution.py:770
  18.1 4.9 %collective-permute-done.4.refs_0_.refs_3_ = bf16[4,32,1764]{2,1,0:T(8,128)(2,1)} collective-permute-done((bf16[4,32,1764]{2,1,0:T(8,128)(2,1)}, bf16[4,32,1764]{2,1,0:T(8,128)(2,1)}, u32[]{:S(2)}, u32[]{:S(2)}) %collective-permute-start.4) | collective-permute-done | bytes 451616 | tf_op jit(solution)/shard_map/ppermute | solution.py:851
  34.2 8.0 %first_conv.3 = (f32[8,128,1792]{2,1,0:T(8,128)}, bf16[8,128,1792]{2,1,0:T(8,128)(2,1)}, f32[128,128]{1,0:T(8,128)}) custom-call(s32[1]{0:T(128)} %bitcast.me_ref, f32[8]{0:T(128)} %compare_convert_fusion.live_ref, f32[8,128]{1,0:T(8,128)} %pad.4.told_ref, bf16[384,384]{1,0:T(8,128)(2,1)} %get-tuple-element.81.weights_ref, ...), custom_call_target="tpu_custom_call" | custom-call | flops 10119999488 | bytes 32200000 | tf_op jit(solution)/shard_map/first_conv/pallas_call | solution.py:944
  42.6 4.8 %first_conv.4 = (f32[8,128,1792]{2,1,0:T(8,128)}, bf16[8,128,1792]{2,1,0:T(8,128)(2,1)}, f32[128,128]{1,0:T(8,128)}) custom-call(s32[1]{0:T(128)} %bitcast.me_ref, f32[8]{0:T(128)} %compare_convert_fusion.live_ref, f32[8,128]{1,0:T(8,128)} %pad.4.told_ref, ...), custom_call_target="tpu_custom_call", output_to_operand_aliasing={{0}: (9, {}), {1}: (10, {})} | custom-call | flops 5059999744 | bytes 16099999 | tf_op jit(solution)/shard_map/first_conv/pallas_call | solution.py:944
  48.0 3.4 %collective-permute-done.6.refs_3_ = bf16[2,32,1764]{2,1,0:T(8,128)(2,1)} collective-permute-done((bf16[2,32,1764]{2,1,0:T(8,128)(2,1)}, bf16[2,32,1764]{2,1,0:T(8,128)(2,1)}, u32[]{:S(2)}, u32[]{:S(2)}) %collective-permute-start.6) | collective-permute-done | bytes 225824 | tf_op jit(solution)/shard_map/ppermute | solution.py:851
  51.3 4.8 %first_conv.5 = (f32[8,128,1792]{2,1,0:T(8,128)}, bf16[8,128,1792]{2,1,0:T(8,128)(2,1)}, f32[32,4,128]{2,1,0:T(4,128)}) custom-call(s32[1]{0:T(128)} %bitcast.me_ref, f32[8]{0:T(128)} %compare_convert_fusion.live_ref, f32[8,128]{1,0:T(8,128)} %pad.4.told_ref, ...), custom_call_target="tpu_custom_call", output_to_operand_aliasing={{0}: (9, {}), {1}: (10, {})} | custom-call | flops 5059999744 | bytes 16099999 | tf_op jit(solution)/shard_map/first_conv/pallas_call | solution.py:944
  56.1 6.4 %all-to-all-start = ((f32[32,4,128]{2,1,0:T(4,128)}), f32[32,4,128]{2,1,0:T(4,128)S(1)}, u32[]{:S(2)}, u32[]{:S(2)}) async-start(f32[32,4,128]{2,1,0:T(4,128)} %get-tuple-element.95), calls=%async_computation | async-start | bytes 131072 | tf_op jit(solution)/shard_map/all_to_all | solution.py:854
  62.6 7.2 %all-to-all-done.heard_ref.heard_two_ref = f32[32,4,128]{2,1,0:T(4,128)S(1)} async-done(((f32[32,4,128]{2,1,0:T(4,128)}), f32[32,4,128]{2,1,0:T(4,128)S(1)}, u32[]{:S(2)}, u32[]{:S(2)}) %all-to-all-start) | async-done | bytes 65568 | tf_op jit(solution)/shard_map/all_to_all | solution.py:854
  70.4 13.8 %middle.1 = (bf16[8,32,441]{2,1,0:T(8,128)(2,1)}, bf16[8,32,441]{2,1,0:T(8,128)(2,1)}, bf16[8,32,441]{2,1,0:T(8,128)(2,1)}, bf16[8,32,441]{2,1,0:T(8,128)(2,1)},...) custom-call(s32[1]{0:T(128)} %bitcast.me_ref, ...), custom_call_target="tpu_custom_call" | custom-call | flops 17600000000 | bytes 56000000 | tf_op jit(solution)/shard_map/middle/pallas_call | solution.py:976
  84.2 2.6 %all-to-all-start.1 = ((f32[32,4,128]{2,1,0:T(4,128)}), f32[32,4,128]{2,1,0:T(4,128)S(1)}, u32[]{:S(2)}, u32[]{:S(2)}) async-start(f32[32,4,128]{2,1,0:T(4,128)} %get-tuple-element.101.own_ref), calls=%async_computation.1 | async-start | bytes 131072 | tf_op jit(solution)/shard_map/all_to_all | solution.py:854
  94.8 6.0 %top.1 = (bf16[8,32,100]{2,1,0:T(8,128)(2,1)}, bf16[8,32,100]{2,1,0:T(8,128)(2,1)}, bf16[8,32,100]{2,1,0:T(8,128)(2,1)}, bf16[8,32,100]{2,1,0:T(8,128)(2,1)}, f3...) custom-call(s32[1]{0:T(128)} %bitcast.me_ref, ...), custom_call_target="tpu_custom_call" | custom-call | flops 7040000000 | bytes 22400000 | tf_op jit(solution)/shard_map/top/pallas_call | solution.py:1019
  100.8 4.1 %all-to-all-start.2 = ((f32[32,4,128]{2,1,0:T(4,128)}), f32[32,4,128]{2,1,0:T(4,128)S(1)}, u32[]{:S(2)}, u32[]{:S(2)}) async-start(f32[32,4,128]{2,1,0:T(4,128)} %get-tuple-element.110), calls=%async_computation.2 | async-start | bytes 131072 | tf_op jit(solution)/shard_map/all_to_all | solution.py:854
  108.9 3.5 %all-to-all-done.2.heard_ref.heard_top_ref = f32[32,4,128]{2,1,0:T(4,128)S(1)} async-done(((f32[32,4,128]{2,1,0:T(4,128)}), f32[32,4,128]{2,1,0:T(4,128)S(1)}, u32[]{:S(2)}, u32[]{:S(2)}) %all-to-all-start.2) | async-done | bytes 65568 | tf_op jit(solution)/shard_map/all_to_all | solution.py:854
  113.0 14.1 %back.1 = (f32[8,128,1792]{2,1,0:T(8,128)}, bf16[8,128,512]{2,1,0:T(8,128)(2,1)}, f32[32,4,128]{2,1,0:T(4,128)}) custom-call(f32[8]{0:T(128)} %compare_convert_fusion.live_ref, f32[32,4,128]{2,1,0:T(4,128)} %copy-done.13, f32[8,128]{1,0:T(8,128)} %get-tuple-element.111.norm_three_ref, f32[8,128]{1,0:T(8,128)} %get-tuple-element.112.norm_two_ref.norm_ref, ...), custom_call_target="tpu_custom_call" | custom-call | flops 17600000000 | bytes 56000000 | tf_op jit(solution)/shard_map/back/pallas_call | solution.py:1073
  127.1 2.7 %all-to-all-start.3 = ((f32[32,4,128]{2,1,0:T(4,128)}), f32[32,4,128]{2,1,0:T(4,128)S(1)}, u32[]{:S(2)}, u32[]{:S(2)}) async-start(f32[32,4,128]{2,1,0:T(4,128)} %get-tuple-element.116.refs_0_), calls=%async_computation.3 | async-start | bytes 131072 | tf_op jit(solution)/shard_map/all_to_all | solution.py:854
  130.0 4.3 %filter_three.1.refs_0_ = f32[4,2,3,32,384]{4,3,2,1,0:T(8,128)} custom-call(bf16[8,128,512]{2,1,0:T(8,128)(2,1)} %get-tuple-element.120.error_ref, bf16[8,128,512]{2,1,0:T(8,128)(2,1)} %get-tuple-element.121.hidden_ref, f32[32,4,128]{2,1,0:T(4,128)} %get-tuple-element.116.refs_0_), custom_call_target="tpu_custom_call" | custom-call | flops 5500000256 | bytes 17500000 | tf_op jit(solution)/shard_map/filter_three/pallas_call | solution.py:1125
  134.4 2.7 %all-to-all-done.3.heard_ref.heard_back_ref = f32[32,4,128]{2,1,0:T(4,128)S(1)} async-done(((f32[32,4,128]{2,1,0:T(4,128)}), f32[32,4,128]{2,1,0:T(4,128)S(1)}, u32[]{:S(2)}, u32[]{:S(2)}) %all-to-all-start.3) | async-done | bytes 65568 | tf_op jit(solution)/shard_map/all_to_all | solution.py:854
  137.7 5.3 %last_conv.3 = (bf16[8,32,1764]{2,1,0:T(8,128)(2,1)}, bf16[8,32,1764]{2,1,0:T(8,128)(2,1)}, bf16[2,32,1764]{2,1,0:T(8,128)(2,1)}, bf16[2,32,1764]{2,1,0:T(8,128)(2,1)}) custom-call(s32[1]{0:T(128)} %bitcast.me_ref, f32[8]{0:T(128)} %compare_convert_fusion.live_ref, f32[32,4,128]{2,1,0:T(4,128)} %copy-done, ...), custom_call_target="tpu_custom_call" | custom-call | flops 3300000000 | bytes 10500000 | tf_op jit(solution)/shard_map/last_conv/pallas_call | solution.py:1162
  143.0 5.3 %last_conv.4 = (bf16[8,32,1764]{2,1,0:T(8,128)(2,1)}, bf16[8,32,1764]{2,1,0:T(8,128)(2,1)}, bf16[2,32,1764]{2,1,0:T(8,128)(2,1)}, bf16[2,32,1764]{2,1,0:T(8,128)(2,1)}) custom-call(s32[1]{0:T(128)} %bitcast.me_ref, f32[8]{0:T(128)} %compare_convert_fusion.live_ref, f32[32,4,128]{2,1,0:T(4,128)} %copy-done, ...), custom_call_target="tpu_custom_call", output_to_operand_aliasing={{0}: (8, {}), {1}: (9, {})} | custom-call | flops 3300000000 | bytes 10500000 | tf_op jit(solution)/shard_map/last_conv/pallas_call | solution.py:1162
  148.3 12.0 %last_filter.1.refs_0_ = f32[4,2,3,32,384]{4,3,2,1,0:T(8,128)} custom-call(f32[8]{0:T(128)} %compare_convert_fusion.live_ref, f32[32,4,128]{2,1,0:T(4,128)} %copy-done, f32[8,128]{1,0:T(8,128)} %get-tuple-element.112.norm_two_ref.norm_ref, f32[8,128]{1,0:T(8,128)} %get-tuple-element.96.vectors_ref, ...), custom_call_target="tpu_custom_call", output_to_operand_aliasing={{}: (7, {})} | custom-call | flops 10560000000 | bytes 33600000 | tf_op jit(solution)/shard_map/last_filter/pallas_call | solution.py:1190
  160.3 3.5 %all-to-all-start.4 = ((f32[32,24,384]{2,1,0:T(8,128)}), f32[32,24,384]{2,1,0:T(8,128)}, u32[]{:S(2)}, u32[]{:S(2)}) async-start(f32[32,24,384]{2,1,0:T(8,128)} %bitcast.30), calls=%async_computation.4 | async-start | bytes 2359296 | tf_op jit(solution)/shard_map/all_to_all | solution.py:1250
  167.4 15.3 %collective-permute-done.19.refs_1_.refs_3_ = bf16[2,32,1764]{2,1,0:T(8,128)(2,1)S(1)} collective-permute-done((bf16[2,32,1764]{2,1,0:T(8,128)(2,1)}, bf16[2,32,1764]{2,1,0:T(8,128)(2,1)S(1)}, u32[]{:S(2)}, u32[]{:S(2)}) %collective-permute-start.19) | collective-permute-done | bytes 225824 | tf_op jit(solution)/shard_map/ppermute | solution.py:851
  182.7 6.4 %collective-permute-done.21.refs_3_.refs_0_ = bf16[2,32,1764]{2,1,0:T(8,128)(2,1)S(1)} collective-permute-done((bf16[2,32,1764]{2,1,0:T(8,128)(2,1)}, bf16[2,32,1764]{2,1,0:T(8,128)(2,1)S(1)}, u32[]{:S(2)}, u32[]{:S(2)}) %collective-permute-start.21) | collective-permute-done | bytes 225824 | tf_op jit(solution)/shard_map/ppermute | solution.py:851
  189.1 4.3 %collective-permute-done.20.refs_2_.refs_4_ = bf16[2,32,1764]{2,1,0:T(8,128)(2,1)S(1)} collective-permute-done((bf16[2,32,1764]{2,1,0:T(8,128)(2,1)}, bf16[2,32,1764]{2,1,0:T(8,128)(2,1)S(1)}, u32[]{:S(2)}, u32[]{:S(2)}) %collective-permute-start.20) | collective-permute-done | bytes 225824 | tf_op jit(solution)/shard_map/ppermute | solution.py:851
  193.3 5.6 %collective-permute-done.22.refs_4_.refs_1_ = bf16[2,32,1764]{2,1,0:T(8,128)(2,1)S(1)} collective-permute-done((bf16[2,32,1764]{2,1,0:T(8,128)(2,1)}, bf16[2,32,1764]{2,1,0:T(8,128)(2,1)S(1)}, u32[]{:S(2)}, u32[]{:S(2)}) %collective-permute-start.22) | collective-permute-done | bytes 225824 | tf_op jit(solution)/shard_map/ppermute | solution.py:851
  199.6 7.5 %last_conv.5 = (bf16[8,32,1764]{2,1,0:T(8,128)(2,1)}, bf16[8,32,1764]{2,1,0:T(8,128)(2,1)}, bf16[4,32,1764]{2,1,0:T(8,128)(2,1)}, bf16[4,32,1764]{2,1,0:T(8,128)(2,1)}) custom-call(s32[1]{0:T(128)} %bitcast.me_ref, f32[8]{0:T(128)} %compare_convert_fusion.live_ref, f32[32,4,128]{2,1,0:T(4,128)} %copy-done, ...), custom_call_target="tpu_custom_call", output_to_operand_aliasing={{0}: (13, {}), {1}: (14, {})} | custom-call | flops 6600000000 | bytes 21000000 | tf_op jit(solution)/shard_map/last_conv/pallas_call | solution.py:1162
  211.0 2.5 %finish.1 = (f32[2,32,100]{2,1,0:T(8,128)}, f32[2,32]{1,0:T(2,128)}, f32[2,100]{1,0:T(2,128)}, f32[32]{0:T(128)}, f32[32]{0:T(128)}, /*index=5*/f32[32]{0:T(128)}, f32[32]{0:T(128)}, f32[9]{0:T(128)}) custom-call(s32[1]{0:T(128)} %bitcast.15.here_ref, s32[1]{0:T(128)} %bitcast.me_ref, f32[32,4,128]{2,1,0:T(4,128)} %copy-done.12, f32[32,4,128]{2,1,0:T(4,128)} %copy-done.13, ...), custom_call_target="tpu_custom_call" | custom-call | flops 2200000000 | bytes 7000000 | tf_op jit(solution)/shard_map/finish/pallas_call | solution.py:1222
  217.6 5.4 %all-to-all-start.5 = ((f32[8,24,384]{2,1,0:T(8,128)}), f32[8,24,384]{2,1,0:T(8,128)S(1)}, u32[]{:S(2)}, u32[]{:S(2)}) async-start(f32[8,24,384]{2,1,0:T(8,128)} %strips.1), calls=%async_computation.5 | async-start | bytes 589824 | tf_op jit(solution)/shard_map/all_to_all | solution.py:1259
  223.0 3.3 %unpack.6.refs_6_ = f32[32,32,1764]{2,1,0:T(8,128)} custom-call(s32[1]{0:T(128)} %bitcast.me_ref, bf16[8,32,1764]{2,1,0:T(8,128)(2,1)} %get-tuple-element.130.refs_4_.refs_6_.refs_0_.refs_2_, bf16[8,32,1764]{2,1,0:T(8,128)(2,1)} %collective-permute-done.25.refs_1_, bf16[8,32,1764]{2,1,0:T(8,128)(2,1)} %get-tuple-element.130.refs_4_.refs_6_.refs_0_.refs_2_), custom_call_target="tpu_custom_call" | custom-call | flops 2200000000 | bytes 7000000 | tf_op jit(solution)/shard_map/unpack/pallas_call | solution.py:809
  226.3 3.5 %collective-permute-done.24.refs_5_ = bf16[4,32,1764]{2,1,0:T(8,128)(2,1)} collective-permute-done((bf16[4,32,1764]{2,1,0:T(8,128)(2,1)}, bf16[4,32,1764]{2,1,0:T(8,128)(2,1)}, u32[]{:S(2)}, u32[]{:S(2)}) %collective-permute-start.24) | collective-permute-done | bytes 451616 | tf_op jit(solution)/shard_map/ppermute | solution.py:851
  229.8 3.4 %unpack.7 = f32[32,32,1764]{2,1,0:T(8,128)} custom-call(s32[1]{0:T(128)} %bitcast.me_ref, bf16[2,32,1764]{2,1,0:T(8,128)(2,1)} %copy-done.7, bf16[2,32,1764]{2,1,0:T(8,128)(2,1)} %copy-done.9, bf16[4,32,1764]{2,1,0:T(8,128)(2,1)} %copy-done.1, bf16[2,32,1764]{2,1,0:T(8,128)(2,1)} %copy-done.6, ...), custom_call_target="tpu_custom_call", output_to_operand_aliasing={{}: (7, {})} | custom-call | flops 2200000000 | bytes 7000000 | tf_op jit(solution)/shard_map/unpack/pallas_call | solution.py:809
  (110 shorter events, 51.6 us)
Async XLA Ops:
  4.8 8.8 %collective-permute-start.1 = (bf16[240,384]{1,0:T(8,128)(2,1)}, bf16[240,384]{1,0:T(8,128)(2,1)}, u32[]{:S(2)}, u32[]{:S(2)}) collective-permute-start(bf16[240,384]{1,0:T(8,128)(2,1)} %bundle.1.refs_0_), channel_id=1, source_target_pairs={{0,2},{1,3},{2,0},{3,1},{4,6},{5,7},{6,4},{7,5},{8,10},{9,11},{10,... | collective-permute-start | bytes 552968 | tf_op jit(solution)/shard_map/ppermute | solution.py:851
  7.8 7.7 %collective-permute-start = (bf16[240,384]{1,0:T(8,128)(2,1)}, bf16[240,384]{1,0:T(8,128)(2,1)}, u32[]{:S(2)}, u32[]{:S(2)}) collective-permute-start(bf16[240,384]{1,0:T(8,128)(2,1)} %bundle.1.refs_0_), channel_id=1, source_target_pairs={{0,1},{1,0},{2,3},{3,2},{4,5},{5,4},{6,7},{7,6},{8,9},{9,8},{10,11... | collective-permute-start | bytes 552968 | tf_op jit(solution)/shard_map/ppermute | solution.py:851
  7.8 15.2 %collective-permute-start.4 = (bf16[4,32,1764]{2,1,0:T(8,128)(2,1)}, bf16[4,32,1764]{2,1,0:T(8,128)(2,1)}, u32[]{:S(2)}, u32[]{:S(2)}) collective-permute-start(bf16[4,32,1764]{2,1,0:T(8,128)(2,1)} %get-tuple-element.80.refs_4_.refs_0_), channel_id=1, source_target_pairs={{0,3},{1,2},{2,1},{3,0},{4,7},{5,6},{6,5},{7,4},{8,11},{9,10},{10,... | collective-permute-start | bytes 1354760 | tf_op jit(solution)/shard_map/ppermute | solution.py:851
  7.9 25.3 %collective-permute-start.9 = (bf16[4,32,1764]{2,1,0:T(8,128)(2,1)}, bf16[4,32,1764]{2,1,0:T(8,128)(2,1)}, u32[]{:S(2)}, u32[]{:S(2)}) collective-permute-start(bf16[4,32,1764]{2,1,0:T(8,128)(2,1)} %get-tuple-element.88), channel_id=1, source_target_pairs={{0,2},{1,3},{2,0},{3,1},{4,6},{5,7},{6,4},{7,5},{8,10},{9,11},{10,... | collective-permute-start | bytes 1354760 | tf_op jit(solution)/shard_map/ppermute | solution.py:851
  12.6 20.6 %collective-permute-start.3 = (bf16[8,32,1764]{2,1,0:T(8,128)(2,1)}, bf16[8,32,1764]{2,1,0:T(8,128)(2,1)S(1)}, u32[]{:S(2)}, u32[]{:S(2)}) collective-permute-start(bf16[8,32,1764]{2,1,0:T(8,128)(2,1)} %get-tuple-element.83), channel_id=1, source_target_pairs={{0,1},{1,0},{2,3},{3,2},{4,5},{5,4},{6,7},{7,6},{8,9},{9,8},{10,11... | collective-permute-start | bytes 2709512 | tf_op jit(solution)/shard_map/ppermute | solution.py:851
  13.6 2.1 collective-permute-start.2
  25.2 17.0 %collective-permute-start.7 = (bf16[2,32,1764]{2,1,0:T(8,128)(2,1)}, bf16[2,32,1764]{2,1,0:T(8,128)(2,1)}, u32[]{:S(2)}, u32[]{:S(2)}) collective-permute-start(bf16[2,32,1764]{2,1,0:T(8,128)(2,1)} %get-tuple-element.86), channel_id=1, source_target_pairs={{0,2},{1,3},{2,0},{3,1},{4,6},{5,7},{6,4},{7,5},{8,10},{9,11},{10,... | collective-permute-start | bytes 677384 | tf_op jit(solution)/shard_map/ppermute | solution.py:851
  25.4 17.2 %collective-permute-start.8 = (bf16[2,32,1764]{2,1,0:T(8,128)(2,1)}, bf16[2,32,1764]{2,1,0:T(8,128)(2,1)}, u32[]{:S(2)}, u32[]{:S(2)}) collective-permute-start(bf16[2,32,1764]{2,1,0:T(8,128)(2,1)} %get-tuple-element.87.refs_4_), channel_id=1, source_target_pairs={{0,3},{1,2},{2,1},{3,0},{4,7},{5,6},{6,5},{7,4},{8,11},{9,10},{10,... | collective-permute-start | bytes 677384 | tf_op jit(solution)/shard_map/ppermute | solution.py:851
  29.5 18.5 %collective-permute-start.5 = (bf16[2,32,1764]{2,1,0:T(8,128)(2,1)}, bf16[2,32,1764]{2,1,0:T(8,128)(2,1)}, u32[]{:S(2)}, u32[]{:S(2)}) collective-permute-start(bf16[2,32,1764]{2,1,0:T(8,128)(2,1)} %get-tuple-element.84), channel_id=1, source_target_pairs={{0,2},{1,3},{2,0},{3,1},{4,6},{5,7},{6,4},{7,5},{8,10},{9,11},{10,... | collective-permute-start | bytes 677384 | tf_op jit(solution)/shard_map/ppermute | solution.py:851
  33.2 18.1 %collective-permute-start.6 = (bf16[2,32,1764]{2,1,0:T(8,128)(2,1)}, bf16[2,32,1764]{2,1,0:T(8,128)(2,1)}, u32[]{:S(2)}, u32[]{:S(2)}) collective-permute-start(bf16[2,32,1764]{2,1,0:T(8,128)(2,1)} %get-tuple-element.85.refs_7_), channel_id=1, source_target_pairs={{0,3},{1,2},{2,1},{3,0},{4,7},{5,6},{6,5},{7,4},{8,11},{9,10},{10,... | collective-permute-start | bytes 677384 | tf_op jit(solution)/shard_map/ppermute | solution.py:851
  56.1 13.7 %all-to-all-start = ((f32[32,4,128]{2,1,0:T(4,128)}), f32[32,4,128]{2,1,0:T(4,128)S(1)}, u32[]{:S(2)}, u32[]{:S(2)}) async-start(f32[32,4,128]{2,1,0:T(4,128)} %get-tuple-element.95), calls=%async_computation | async-start | bytes 131072 | tf_op jit(solution)/shard_map/all_to_all | solution.py:854
  84.2 10.0 %all-to-all-start.1 = ((f32[32,4,128]{2,1,0:T(4,128)}), f32[32,4,128]{2,1,0:T(4,128)S(1)}, u32[]{:S(2)}, u32[]{:S(2)}) async-start(f32[32,4,128]{2,1,0:T(4,128)} %get-tuple-element.101.own_ref), calls=%async_computation.1 | async-start | bytes 131072 | tf_op jit(solution)/shard_map/all_to_all | solution.py:854
  86.9 2.8 %collective-permute-start.12 = (bf16[8,32,100]{2,1,0:T(8,128)(2,1)S(1)}, bf16[8,32,100]{2,1,0:T(8,128)(2,1)S(1)}, u32[]{:S(2)}, u32[]{:S(2)}) collective-permute-start(bf16[8,32,100]{2,1,0:T(8,128)(2,1)S(1)} %bitcast.33), channel_id=1, source_target_pairs={{0,1},{1,0},{2,3},{3,2},{4,5},{5,4},{6,7},{7,6},{8,9},{9,8},{10,11... | collective-permute-start | bytes 153608 | tf_op jit(solution)/shard_map/ppermute | solution.py:851
  87.1 4.8 %collective-permute-start.13 = (bf16[8,32,100]{2,1,0:T(8,128)(2,1)S(1)}, bf16[8,32,100]{2,1,0:T(8,128)(2,1)S(1)}, u32[]{:S(2)}, u32[]{:S(2)}) collective-permute-start(bf16[8,32,100]{2,1,0:T(8,128)(2,1)S(1)} %bitcast.34), channel_id=1, source_target_pairs={{0,2},{1,3},{2,0},{3,1},{4,6},{5,7},{6,4},{7,5},{8,10},{9,11},{10,... | collective-permute-start | bytes 153608 | tf_op jit(solution)/shard_map/ppermute | solution.py:851
  88.8 4.5 %collective-permute-start.14 = (bf16[8,32,100]{2,1,0:T(8,128)(2,1)S(1)}, bf16[8,32,100]{2,1,0:T(8,128)(2,1)S(1)}, u32[]{:S(2)}, u32[]{:S(2)}) collective-permute-start(bf16[8,32,100]{2,1,0:T(8,128)(2,1)S(1)} %bitcast.35), channel_id=1, source_target_pairs={{0,3},{1,2},{2,1},{3,0},{4,7},{5,6},{6,5},{7,4},{8,11},{9,10},{10,... | collective-permute-start | bytes 153608 | tf_op jit(solution)/shard_map/ppermute | solution.py:851
  100.8 11.6 %all-to-all-start.2 = ((f32[32,4,128]{2,1,0:T(4,128)}), f32[32,4,128]{2,1,0:T(4,128)S(1)}, u32[]{:S(2)}, u32[]{:S(2)}) async-start(f32[32,4,128]{2,1,0:T(4,128)} %get-tuple-element.110), calls=%async_computation.2 | async-start | bytes 131072 | tf_op jit(solution)/shard_map/all_to_all | solution.py:854
  104.9 29.4 %collective-permute-start.10 = (bf16[8,32,441]{2,1,0:T(8,128)(2,1)}, bf16[8,32,441]{2,1,0:T(8,128)(2,1)S(1)}, u32[]{:S(2)}, u32[]{:S(2)}) collective-permute-start(bf16[8,32,441]{2,1,0:T(8,128)(2,1)} %get-tuple-element.99), channel_id=1, source_target_pairs={{0,2},{1,3},{2,0},{3,1},{4,6},{5,7},{6,4},{7,5},{8,10},{9,11},{10,... | collective-permute-start | bytes 677384 | tf_op jit(solution)/shard_map/ppermute | solution.py:851
  106.8 27.6 %collective-permute-start.11 = (bf16[8,32,441]{2,1,0:T(8,128)(2,1)}, bf16[8,32,441]{2,1,0:T(8,128)(2,1)S(1)}, u32[]{:S(2)}, u32[]{:S(2)}) collective-permute-start(bf16[8,32,441]{2,1,0:T(8,128)(2,1)} %get-tuple-element.100), channel_id=1, source_target_pairs={{0,3},{1,2},{2,1},{3,0},{4,7},{5,6},{6,5},{7,4},{8,11},{9,10},{10,... | collective-permute-start | bytes 677384 | tf_op jit(solution)/shard_map/ppermute | solution.py:851
  106.8 27.6 %collective-permute-start.17 = (bf16[8,32,441]{2,1,0:T(8,128)(2,1)}, bf16[8,32,441]{2,1,0:T(8,128)(2,1)S(1)}, u32[]{:S(2)}, u32[]{:S(2)}) collective-permute-start(bf16[8,32,441]{2,1,0:T(8,128)(2,1)} %get-tuple-element.107), channel_id=1, source_target_pairs={{0,1},{1,0},{2,3},{3,2},{4,5},{5,4},{6,7},{7,6},{8,9},{9,8},{10,11... | collective-permute-start | bytes 677384 | tf_op jit(solution)/shard_map/ppermute | solution.py:851
  107.1 22.8 %collective-permute-start.15 = (bf16[8,32,100]{2,1,0:T(8,128)(2,1)}, bf16[8,32,100]{2,1,0:T(8,128)(2,1)S(1)}, u32[]{:S(2)}, u32[]{:S(2)}) collective-permute-start(bf16[8,32,100]{2,1,0:T(8,128)(2,1)} %get-tuple-element.104), channel_id=1, source_target_pairs={{0,2},{1,3},{2,0},{3,1},{4,6},{5,7},{6,4},{7,5},{8,10},{9,11},{10,... | collective-permute-start | bytes 153608 | tf_op jit(solution)/shard_map/ppermute | solution.py:851
  108.9 25.4 %collective-permute-start.16 = (bf16[8,32,100]{2,1,0:T(8,128)(2,1)}, bf16[8,32,100]{2,1,0:T(8,128)(2,1)S(1)}, u32[]{:S(2)}, u32[]{:S(2)}) collective-permute-start(bf16[8,32,100]{2,1,0:T(8,128)(2,1)} %get-tuple-element.105), channel_id=1, source_target_pairs={{0,3},{1,2},{2,1},{3,0},{4,7},{5,6},{6,5},{7,4},{8,11},{9,10},{10,... | collective-permute-start | bytes 153608 | tf_op jit(solution)/shard_map/ppermute | solution.py:851
  127.1 9.9 %all-to-all-start.3 = ((f32[32,4,128]{2,1,0:T(4,128)}), f32[32,4,128]{2,1,0:T(4,128)S(1)}, u32[]{:S(2)}, u32[]{:S(2)}) async-start(f32[32,4,128]{2,1,0:T(4,128)} %get-tuple-element.116.refs_0_), calls=%async_computation.3 | async-start | bytes 131072 | tf_op jit(solution)/shard_map/all_to_all | solution.py:854
  129.9 4.4 %collective-permute-start.18 = (bf16[8,32,100]{2,1,0:T(8,128)(2,1)}, bf16[8,32,100]{2,1,0:T(8,128)(2,1)}, u32[]{:S(2)}, u32[]{:S(2)}) collective-permute-start(bf16[8,32,100]{2,1,0:T(8,128)(2,1)} %get-tuple-element.109), channel_id=1, source_target_pairs={{0,1},{1,0},{2,3},{3,2},{4,5},{5,4},{6,7},{7,6},{8,9},{9,8},{10,11... | collective-permute-start | bytes 153608 | tf_op jit(solution)/shard_map/ppermute | solution.py:851
  160.3 55.2 %all-to-all-start.4 = ((f32[32,24,384]{2,1,0:T(8,128)}), f32[32,24,384]{2,1,0:T(8,128)}, u32[]{:S(2)}, u32[]{:S(2)}) async-start(f32[32,24,384]{2,1,0:T(8,128)} %bitcast.30), calls=%async_computation.4 | async-start | bytes 2359296 | tf_op jit(solution)/shard_map/all_to_all | solution.py:1250
  163.8 18.9 %collective-permute-start.19 = (bf16[2,32,1764]{2,1,0:T(8,128)(2,1)}, bf16[2,32,1764]{2,1,0:T(8,128)(2,1)S(1)}, u32[]{:S(2)}, u32[]{:S(2)}) collective-permute-start(bf16[2,32,1764]{2,1,0:T(8,128)(2,1)} %get-tuple-element.125), channel_id=1, source_target_pairs={{0,3},{1,2},{2,1},{3,0},{4,7},{5,6},{6,5},{7,4},{8,11},{9,10},{10,... | collective-permute-start | bytes 677384 | tf_op jit(solution)/shard_map/ppermute | solution.py:851
  165.3 23.8 %collective-permute-start.21 = (bf16[2,32,1764]{2,1,0:T(8,128)(2,1)}, bf16[2,32,1764]{2,1,0:T(8,128)(2,1)S(1)}, u32[]{:S(2)}, u32[]{:S(2)}) collective-permute-start(bf16[2,32,1764]{2,1,0:T(8,128)(2,1)} %get-tuple-element.127), channel_id=1, source_target_pairs={{0,2},{1,3},{2,0},{3,1},{4,6},{5,7},{6,4},{7,5},{8,10},{9,11},{10,... | collective-permute-start | bytes 677384 | tf_op jit(solution)/shard_map/ppermute | solution.py:851
  165.7 27.7 %collective-permute-start.20 = (bf16[2,32,1764]{2,1,0:T(8,128)(2,1)}, bf16[2,32,1764]{2,1,0:T(8,128)(2,1)S(1)}, u32[]{:S(2)}, u32[]{:S(2)}) collective-permute-start(bf16[2,32,1764]{2,1,0:T(8,128)(2,1)} %get-tuple-element.126), channel_id=1, source_target_pairs={{0,3},{1,2},{2,1},{3,0},{4,7},{5,6},{6,5},{7,4},{8,11},{9,10},{10,... | collective-permute-start | bytes 677384 | tf_op jit(solution)/shard_map/ppermute | solution.py:851
  167.0 31.9 %collective-permute-start.22 = (bf16[2,32,1764]{2,1,0:T(8,128)(2,1)}, bf16[2,32,1764]{2,1,0:T(8,128)(2,1)S(1)}, u32[]{:S(2)}, u32[]{:S(2)}) collective-permute-start(bf16[2,32,1764]{2,1,0:T(8,128)(2,1)} %get-tuple-element.128), channel_id=1, source_target_pairs={{0,2},{1,3},{2,0},{3,1},{4,6},{5,7},{6,4},{7,5},{8,10},{9,11},{10,... | collective-permute-start | bytes 677384 | tf_op jit(solution)/shard_map/ppermute | solution.py:851
  207.1 15.8 %collective-permute-start.25 = (bf16[8,32,1764]{2,1,0:T(8,128)(2,1)}, bf16[8,32,1764]{2,1,0:T(8,128)(2,1)}, u32[]{:S(2)}, u32[]{:S(2)}) collective-permute-start(bf16[8,32,1764]{2,1,0:T(8,128)(2,1)} %get-tuple-element.137), channel_id=1, source_target_pairs={{0,1},{1,0},{2,3},{3,2},{4,5},{5,4},{6,7},{7,6},{8,9},{9,8},{10,11... | collective-permute-start | bytes 2709512 | tf_op jit(solution)/shard_map/ppermute | solution.py:851
  207.2 19.1 %collective-permute-start.23 = (bf16[4,32,1764]{2,1,0:T(8,128)(2,1)}, bf16[4,32,1764]{2,1,0:T(8,128)(2,1)S(1)}, u32[]{:S(2)}, u32[]{:S(2)}) collective-permute-start(bf16[4,32,1764]{2,1,0:T(8,128)(2,1)} %get-tuple-element.135), channel_id=1, source_target_pairs={{0,2},{1,3},{2,0},{3,1},{4,6},{5,7},{6,4},{7,5},{8,10},{9,11},{10,... | collective-permute-start | bytes 1354760 | tf_op jit(solution)/shard_map/ppermute | solution.py:851
  207.6 22.2 %collective-permute-start.24 = (bf16[4,32,1764]{2,1,0:T(8,128)(2,1)}, bf16[4,32,1764]{2,1,0:T(8,128)(2,1)}, u32[]{:S(2)}, u32[]{:S(2)}) collective-permute-start(bf16[4,32,1764]{2,1,0:T(8,128)(2,1)} %get-tuple-element.136), channel_id=1, source_target_pairs={{0,3},{1,2},{2,1},{3,0},{4,7},{5,6},{6,5},{7,4},{8,11},{9,10},{10,... | collective-permute-start | bytes 1354760 | tf_op jit(solution)/shard_map/ppermute | solution.py:851
  217.6 15.6 %all-to-all-start.5 = ((f32[8,24,384]{2,1,0:T(8,128)}), f32[8,24,384]{2,1,0:T(8,128)S(1)}, u32[]{:S(2)}, u32[]{:S(2)}) async-start(f32[8,24,384]{2,1,0:T(8,128)} %strips.1), calls=%async_computation.5 | async-start | bytes 589824 | tf_op jit(solution)/shard_map/all_to_all | solution.py:1259
  (21 other events, 89.5 us)

commit v7 on v6

--- a/solution.py
+++ b/solution.py
@@ -620,7 +620,7 @@
 
 
 def last_filter_kernel(live_ref, heard_ref, norm_ref, vectors_ref, grad_ref, conv_ref, maps_ref, *refs):
-    filter_ref, product, columns, stack, upright = refs[-5:]
+    product, columns, stack, upright = refs[-4:]
     step = pl.program_id(0)
     count = grad_ref.shape[0]
 
@@ -636,9 +636,9 @@
         stack_sideways(cut(maps_ref[image], WIDE), MAP, stack.at[image])
         product[...] += across_cells(upright.at[image], stack.at[image])
 
-    @pl.when(step == pl.num_programs(0) - 1)
-    def _():
-        split_filter(product, filter_ref)
+
+def split_kernel(product_ref, *refs):
+    split_filter(product_ref, refs[-1])
 
 
 def strips_kernel(heard_ref, *refs):
@@ -1194,22 +1194,32 @@
                     smem(),
                     *common_specs,
                     *[each(C, LANES_TWO, count=pair)] * 3,
-                    *anywhere(2),
+                    *anywhere(1),
                 ],
-                out_specs=filter_spec(0),
-                out_shape=filter_shape,
+                out_specs=whole(3 * C, 3 * C),
+                out_shape=jax.ShapeDtypeStruct((3 * C, 3 * C), F32),
                 scratch_shapes=[
-                    pltpu.VMEM((3 * C, 3 * C), F32),
                     pltpu.VMEM((C, C), F32),
                     pltpu.VMEM((pair, 3 * C, LANES_TWO), BF16),
                     pltpu.VMEM((pair, 3 * C, LANES_TWO), BF16),
                 ],
-                input_output_aliases={7: 0},
                 compiler_params=kernel_params(),
                 name="last_filter",
                 cost_estimate=lasting(1.2 * images_each),
-            )(live, *common, grad_two, conv_two, whole_maps, filter_sums, kept[0])
-            waits = [product, *(piece for partner in far for piece in returned[partner])]
+            )(live, *common, grad_two, conv_two, whole_maps, kept[0])
+            waits = [piece for partner in far for piece in returned[partner]]
+            product = pl.pallas_call(
+                split_kernel,
+                grid=(1,),
+                in_specs=[whole(3 * C, 3 * C), *anywhere(1 + len(waits))],
+                out_specs=filter_spec(0),
+                out_shape=filter_shape,
+                input_output_aliases={1: 0},
+                compiler_params=kernel_params(),
+                name="split",
+                cost_estimate=lasting(1.5),
+            )(product, filter_sums, *waits)
+            waits = [product, *waits]
     for partner in range(near):
         returned[partner].append(swap(kept[partner], partner))
 

time: 236 us -> 220 us (0.932)
  waiting for transfers between devices: 64.8 us -> 48.3 us
    ppermute x26, waiting for transfers between devices: 50.6 us -> 17.6 us  [swap(): lax.ppermute(value, 'tensor', [(i, i ^ partner) for i in range(partners)])]
    all_to_all x1, waiting for transfers between devices: 0.01 us -> 14.4 us  [local(): lax.all_to_all(product.reshape(devices, strip, 3 * C), ('tensor', 'dp'),...]
  transfers between devices with their start and end apart: 32 -> 32, of which waited for: 18 -> 16; matrix products, arithmetic and copies ran while one was open for 1% -> 1% of each run, Pallas kernels for 27% -> 37%
where the time goes in v7:
time: 220 us; the launch traced here: 219 us
  Pallas kernels  117 us (53%)
  waiting for transfers between devices  48.3 us (22%)
  starting transfers between devices  43.2 us (20%)
  local copies, waits for them, and re-layouts  8.39 us (4%)
    ppermute x26, starting transfers between devices, swap(): lax.ppermute(value, 'tensor', [(i, i ^ partner) for i in range(partners)])  20.5 us
    pallas_call x3, Pallas kernels, local(): pl.pallas_call(functools.partial(last_conv_kernel, partners, near, first,...  18.2 us
    pallas_call x3, Pallas kernels, local(): pl.pallas_call(functools.partial(first_conv_kernel, partners, first, fina...  17.6 us
    ppermute x26, waiting for transfers between devices, swap(): lax.ppermute(value, 'tensor', [(i, i ^ partner) for i in range(partners)])  17.6 us
    all_to_all x4, starting transfers between devices, share(): return lax.all_to_all(copies, ('dp', 'tensor'), 0, 0)  15.8 us
    all_to_all x1, waiting for transfers between devices, local(): lax.all_to_all(product.reshape(devices, strip, 3 * C), ('tensor', 'dp'),...  14.4 us
    all_to_all x4, waiting for transfers between devices, share(): return lax.all_to_all(copies, ('dp', 'tensor'), 0, 0)  14.2 us
    pallas_call x1, Pallas kernels, local(): pl.pallas_call(back_kernel, grid=(images_each // pair,), in_specs=[smem()...  14.1 us
  transfers between devices with their start and end apart: 32, of which 16 were waited for; matrix products, arithmetic and copies ran while one was open for 1% of the time, Pallas kernels for 37%

profile of v7, /device:TPU:0, one launch (start us, length us, event | category | flops | bytes accessed | tf_op | source)
XLA Modules:
  0.0 219.0 jit_solution(1352661245760560413)
XLA Ops:
  0.6 2.5 %pack.4 = (bf16[4,32,1764]{2,1,0:T(8,128)(2,1)}, bf16[4,32,1764]{2,1,0:T(8,128)(2,1)}) custom-call(s32[1]{0:T(128)} %bitcast.me_ref, bf16[32,32,1764]{2,1,0:T(8,128)(2,1)} %maps_ref.7), custom_call_target="tpu_custom_call" | custom-call | flops 2750000128 | bytes 8750000 | tf_op jit(solution)/shard_map/pack/pallas_call | solution.py:770
  4.8 3.0 %collective-permute-start.1 = (bf16[240,384]{1,0:T(8,128)(2,1)}, bf16[240,384]{1,0:T(8,128)(2,1)}, u32[]{:S(2)}, u32[]{:S(2)}) collective-permute-start(bf16[240,384]{1,0:T(8,128)(2,1)} %bundle.1.refs_0_), channel_id=1, source_target_pairs={{0,2},{1,3},{2,0},{3,1},{4,6},{5,7},{6,4},{7,5},{8,10},{9,11},{10,... | collective-permute-start | bytes 552968 | tf_op jit(solution)/shard_map/ppermute | solution.py:851
  9.9 2.7 %pack.5 = (bf16[8,32,1764]{2,1,0:T(8,128)(2,1)}, bf16[8,32,1764]{2,1,0:T(8,128)(2,1)}) custom-call(s32[1]{0:T(128)} %bitcast.me_ref, bf16[32,32,1764]{2,1,0:T(8,128)(2,1)} %maps_ref.7, bf16[4,32,1764]{2,1,0:T(8,128)(2,1)} %get-tuple-element.80.refs_4_.refs_0_), custom_call_target="tpu_custom_call" | custom-call | flops 2750000128 | bytes 8750000 | tf_op jit(solution)/shard_map/pack/pallas_call | solution.py:770
  15.7 2.4 %unbundle.1 = (bf16[384,384]{1,0:T(8,128)(2,1)}, bf16[384,384]{1,0:T(8,128)(2,1)}, bf16[384,384]{1,0:T(8,128)(2,1)}, bf16[384,384]{1,0:T(8,128)(2,1)}, f32[2,128,100]{2,1,0:T(8,128)}, /*index=5*/f32[8,128]{1,0:T(8,128)}) custom-call(s32[1]{0:T(128)} %bitcast.me_ref, s32[1]{0:T(128)} %bitcast.2.task_ref, f32[2,100]{1,0:T(2,128)} %context_ref.1, ...), custom_call_target="tpu_custom_call" | custom-call | flops 2200000000 | bytes 7000000 | tf_op jit(solution)/shard_map/unbundle/pallas_call | solution.py:915
  18.1 4.9 %collective-permute-done.4.refs_0_.refs_3_ = bf16[4,32,1764]{2,1,0:T(8,128)(2,1)} collective-permute-done((bf16[4,32,1764]{2,1,0:T(8,128)(2,1)}, bf16[4,32,1764]{2,1,0:T(8,128)(2,1)}, u32[]{:S(2)}, u32[]{:S(2)}) %collective-permute-start.4) | collective-permute-done | bytes 451616 | tf_op jit(solution)/shard_map/ppermute | solution.py:851
  23.0 2.3 %pack.7 = (bf16[2,32,1764]{2,1,0:T(8,128)(2,1)}, bf16[2,32,1764]{2,1,0:T(8,128)(2,1)}) custom-call(s32[1]{0:T(128)} %bitcast.me_ref, bf16[32,32,1764]{2,1,0:T(8,128)(2,1)} %maps_ref.7, bf16[4,32,1764]{2,1,0:T(8,128)(2,1)} %collective-permute-done.4.refs_0_.refs_3_), custom_call_target="tpu_custom_call" | custom-call | flops 2750000128 | bytes 8750000 | tf_op jit(solution)/shard_map/pack/pallas_call | solution.py:770
  27.2 2.3 %pack.6 = (bf16[2,32,1764]{2,1,0:T(8,128)(2,1)}, bf16[2,32,1764]{2,1,0:T(8,128)(2,1)}) custom-call(s32[1]{0:T(128)} %bitcast.me_ref, bf16[32,32,1764]{2,1,0:T(8,128)(2,1)} %maps_ref.7, bf16[4,32,1764]{2,1,0:T(8,128)(2,1)} %collective-permute-done.4.refs_0_.refs_3_), custom_call_target="tpu_custom_call" | custom-call | flops 2750000128 | bytes 8750000 | tf_op jit(solution)/shard_map/pack/pallas_call | solution.py:770
  34.2 8.0 %first_conv.3 = (f32[8,128,1792]{2,1,0:T(8,128)}, bf16[8,128,1792]{2,1,0:T(8,128)(2,1)}, f32[128,128]{1,0:T(8,128)}) custom-call(s32[1]{0:T(128)} %bitcast.me_ref, f32[8]{0:T(128)} %compare_convert_fusion.live_ref, f32[8,128]{1,0:T(8,128)} %pad.4.told_ref, bf16[384,384]{1,0:T(8,128)(2,1)} %get-tuple-element.81.weights_ref, ...), custom_call_target="tpu_custom_call" | custom-call | flops 10119999488 | bytes 32200000 | tf_op jit(solution)/shard_map/first_conv/pallas_call | solution.py:944
  42.6 4.8 %first_conv.4 = (f32[8,128,1792]{2,1,0:T(8,128)}, bf16[8,128,1792]{2,1,0:T(8,128)(2,1)}, f32[128,128]{1,0:T(8,128)}) custom-call(s32[1]{0:T(128)} %bitcast.me_ref, f32[8]{0:T(128)} %compare_convert_fusion.live_ref, f32[8,128]{1,0:T(8,128)} %pad.4.told_ref, ...), custom_call_target="tpu_custom_call", output_to_operand_aliasing={{0}: (9, {}), {1}: (10, {})} | custom-call | flops 5059999744 | bytes 16099999 | tf_op jit(solution)/shard_map/first_conv/pallas_call | solution.py:944
  48.0 3.4 %collective-permute-done.6.refs_3_ = bf16[2,32,1764]{2,1,0:T(8,128)(2,1)} collective-permute-done((bf16[2,32,1764]{2,1,0:T(8,128)(2,1)}, bf16[2,32,1764]{2,1,0:T(8,128)(2,1)}, u32[]{:S(2)}, u32[]{:S(2)}) %collective-permute-start.6) | collective-permute-done | bytes 225824 | tf_op jit(solution)/shard_map/ppermute | solution.py:851
  51.3 4.8 %first_conv.5 = (f32[8,128,1792]{2,1,0:T(8,128)}, bf16[8,128,1792]{2,1,0:T(8,128)(2,1)}, f32[32,4,128]{2,1,0:T(4,128)}) custom-call(s32[1]{0:T(128)} %bitcast.me_ref, f32[8]{0:T(128)} %compare_convert_fusion.live_ref, f32[8,128]{1,0:T(8,128)} %pad.4.told_ref, ...), custom_call_target="tpu_custom_call", output_to_operand_aliasing={{0}: (9, {}), {1}: (10, {})} | custom-call | flops 5059999744 | bytes 16099999 | tf_op jit(solution)/shard_map/first_conv/pallas_call | solution.py:944
  56.1 6.4 %all-to-all-start = ((f32[32,4,128]{2,1,0:T(4,128)}), f32[32,4,128]{2,1,0:T(4,128)S(1)}, u32[]{:S(2)}, u32[]{:S(2)}) async-start(f32[32,4,128]{2,1,0:T(4,128)} %get-tuple-element.95), calls=%async_computation | async-start | bytes 131072 | tf_op jit(solution)/shard_map/all_to_all | solution.py:854
  62.6 7.2 %all-to-all-done.heard_ref.heard_two_ref = f32[32,4,128]{2,1,0:T(4,128)S(1)} async-done(((f32[32,4,128]{2,1,0:T(4,128)}), f32[32,4,128]{2,1,0:T(4,128)S(1)}, u32[]{:S(2)}, u32[]{:S(2)}) %all-to-all-start) | async-done | bytes 65568 | tf_op jit(solution)/shard_map/all_to_all | solution.py:854
  70.4 13.8 %middle.1 = (bf16[8,32,441]{2,1,0:T(8,128)(2,1)}, bf16[8,32,441]{2,1,0:T(8,128)(2,1)}, bf16[8,32,441]{2,1,0:T(8,128)(2,1)}, bf16[8,32,441]{2,1,0:T(8,128)(2,1)},...) custom-call(s32[1]{0:T(128)} %bitcast.me_ref, ...), custom_call_target="tpu_custom_call" | custom-call | flops 17600000000 | bytes 56000000 | tf_op jit(solution)/shard_map/middle/pallas_call | solution.py:976
  84.2 2.6 %all-to-all-start.1 = ((f32[32,4,128]{2,1,0:T(4,128)}), f32[32,4,128]{2,1,0:T(4,128)S(1)}, u32[]{:S(2)}, u32[]{:S(2)}) async-start(f32[32,4,128]{2,1,0:T(4,128)} %get-tuple-element.101.own_ref), calls=%async_computation.1 | async-start | bytes 131072 | tf_op jit(solution)/shard_map/all_to_all | solution.py:854
  94.8 6.0 %top.1 = (bf16[8,32,100]{2,1,0:T(8,128)(2,1)}, bf16[8,32,100]{2,1,0:T(8,128)(2,1)}, bf16[8,32,100]{2,1,0:T(8,128)(2,1)}, bf16[8,32,100]{2,1,0:T(8,128)(2,1)}, f3...) custom-call(s32[1]{0:T(128)} %bitcast.me_ref, ...), custom_call_target="tpu_custom_call" | custom-call | flops 7040000000 | bytes 22400000 | tf_op jit(solution)/shard_map/top/pallas_call | solution.py:1019
  100.8 4.1 %all-to-all-start.2 = ((f32[32,4,128]{2,1,0:T(4,128)}), f32[32,4,128]{2,1,0:T(4,128)S(1)}, u32[]{:S(2)}, u32[]{:S(2)}) async-start(f32[32,4,128]{2,1,0:T(4,128)} %get-tuple-element.110), calls=%async_computation.2 | async-start | bytes 131072 | tf_op jit(solution)/shard_map/all_to_all | solution.py:854
  108.9 3.5 %all-to-all-done.2.heard_ref.heard_top_ref = f32[32,4,128]{2,1,0:T(4,128)S(1)} async-done(((f32[32,4,128]{2,1,0:T(4,128)}), f32[32,4,128]{2,1,0:T(4,128)S(1)}, u32[]{:S(2)}, u32[]{:S(2)}) %all-to-all-start.2) | async-done | bytes 65568 | tf_op jit(solution)/shard_map/all_to_all | solution.py:854
  113.0 14.1 %back.1 = (f32[8,128,1792]{2,1,0:T(8,128)}, bf16[8,128,512]{2,1,0:T(8,128)(2,1)}, f32[32,4,128]{2,1,0:T(4,128)}) custom-call(f32[8]{0:T(128)} %compare_convert_fusion.live_ref, f32[32,4,128]{2,1,0:T(4,128)} %copy-done.13, f32[8,128]{1,0:T(8,128)} %get-tuple-element.111.norm_three_ref, f32[8,128]{1,0:T(8,128)} %get-tuple-element.112.norm_two_ref.norm_ref, ...), custom_call_target="tpu_custom_call" | custom-call | flops 17600000000 | bytes 56000000 | tf_op jit(solution)/shard_map/back/pallas_call | solution.py:1073
  127.1 2.7 %all-to-all-start.3 = ((f32[32,4,128]{2,1,0:T(4,128)}), f32[32,4,128]{2,1,0:T(4,128)S(1)}, u32[]{:S(2)}, u32[]{:S(2)}) async-start(f32[32,4,128]{2,1,0:T(4,128)} %get-tuple-element.116.refs_0_), calls=%async_computation.3 | async-start | bytes 131072 | tf_op jit(solution)/shard_map/all_to_all | solution.py:854
  130.0 4.3 %filter_three.1.refs_0_ = f32[4,2,3,32,384]{4,3,2,1,0:T(8,128)} custom-call(bf16[8,128,512]{2,1,0:T(8,128)(2,1)} %get-tuple-element.120.error_ref, bf16[8,128,512]{2,1,0:T(8,128)(2,1)} %get-tuple-element.121.hidden_ref, f32[32,4,128]{2,1,0:T(4,128)} %get-tuple-element.116.refs_0_), custom_call_target="tpu_custom_call" | custom-call | flops 5500000256 | bytes 17500000 | tf_op jit(solution)/shard_map/filter_three/pallas_call | solution.py:1125
  134.4 2.7 %all-to-all-done.3.heard_ref.heard_back_ref = f32[32,4,128]{2,1,0:T(4,128)S(1)} async-done(((f32[32,4,128]{2,1,0:T(4,128)}), f32[32,4,128]{2,1,0:T(4,128)S(1)}, u32[]{:S(2)}, u32[]{:S(2)}) %all-to-all-start.3) | async-done | bytes 65568 | tf_op jit(solution)/shard_map/all_to_all | solution.py:854
  137.7 5.3 %last_conv.3 = (bf16[8,32,1764]{2,1,0:T(8,128)(2,1)}, bf16[8,32,1764]{2,1,0:T(8,128)(2,1)}, bf16[2,32,1764]{2,1,0:T(8,128)(2,1)}, bf16[2,32,1764]{2,1,0:T(8,128)(2,1)}) custom-call(s32[1]{0:T(128)} %bitcast.me_ref, f32[8]{0:T(128)} %compare_convert_fusion.live_ref, f32[32,4,128]{2,1,0:T(4,128)} %copy-done, ...), custom_call_target="tpu_custom_call" | custom-call | flops 3300000000 | bytes 10500000 | tf_op jit(solution)/shard_map/last_conv/pallas_call | solution.py:1162
  144.8 5.3 %last_conv.4 = (bf16[8,32,1764]{2,1,0:T(8,128)(2,1)}, bf16[8,32,1764]{2,1,0:T(8,128)(2,1)}, bf16[2,32,1764]{2,1,0:T(8,128)(2,1)}, bf16[2,32,1764]{2,1,0:T(8,128)(2,1)}) custom-call(s32[1]{0:T(128)} %bitcast.me_ref, f32[8]{0:T(128)} %compare_convert_fusion.live_ref, f32[32,4,128]{2,1,0:T(4,128)} %copy-done, ...), custom_call_target="tpu_custom_call", output_to_operand_aliasing={{0}: (8, {}), {1}: (9, {})} | custom-call | flops 3300000000 | bytes 10500000 | tf_op jit(solution)/shard_map/last_conv/pallas_call | solution.py:1162
  151.8 11.9 %last_filter.1.product_ref = f32[384,384]{1,0:T(8,128)} custom-call(f32[8]{0:T(128)} %compare_convert_fusion.live_ref, f32[32,4,128]{2,1,0:T(4,128)} %copy-done, f32[8,128]{1,0:T(8,128)} %get-tuple-element.112.norm_two_ref.norm_ref, f32[8,128]{1,0:T(8,128)} %get-tuple-element.96.vectors_ref, f32[8,128,1792]{2,1,0:T(8,128)} %get-tuple-element.118.grad_ref, ...), custom_call_target="tpu_custom_call" | custom-call | flops 10560000000 | bytes 33600000 | tf_op jit(solution)/shard_map/last_filter/pallas_call | solution.py:1190
  168.5 3.4 %all-to-all-start.4 = ((f32[32,24,384]{2,1,0:T(8,128)}), f32[32,24,384]{2,1,0:T(8,128)}, u32[]{:S(2)}, u32[]{:S(2)}) async-start(f32[32,24,384]{2,1,0:T(8,128)} %bitcast.30), calls=%async_computation.4 | async-start | bytes 2359296 | tf_op jit(solution)/shard_map/all_to_all | solution.py:1260
  172.0 7.5 %last_conv.5 = (bf16[8,32,1764]{2,1,0:T(8,128)(2,1)}, bf16[8,32,1764]{2,1,0:T(8,128)(2,1)}, bf16[4,32,1764]{2,1,0:T(8,128)(2,1)}, bf16[4,32,1764]{2,1,0:T(8,128)(2,1)}) custom-call(s32[1]{0:T(128)} %bitcast.me_ref, f32[8]{0:T(128)} %compare_convert_fusion.live_ref, f32[32,4,128]{2,1,0:T(4,128)} %copy-done, ...), custom_call_target="tpu_custom_call", output_to_operand_aliasing={{0}: (13, {}), {1}: (14, {})} | custom-call | flops 6600000000 | bytes 21000000 | tf_op jit(solution)/shard_map/last_conv/pallas_call | solution.py:1162
  183.4 2.5 %finish.1 = (f32[2,32,100]{2,1,0:T(8,128)}, f32[2,32]{1,0:T(2,128)}, f32[2,100]{1,0:T(2,128)}, f32[32]{0:T(128)}, f32[32]{0:T(128)}, /*index=5*/f32[32]{0:T(128)}, f32[32]{0:T(128)}, f32[9]{0:T(128)}) custom-call(s32[1]{0:T(128)} %bitcast.15.here_ref, s32[1]{0:T(128)} %bitcast.me_ref, f32[32,4,128]{2,1,0:T(4,128)} %copy-done.12, f32[32,4,128]{2,1,0:T(4,128)} %copy-done.13, ...), custom_call_target="tpu_custom_call" | custom-call | flops 2200000000 | bytes 7000000 | tf_op jit(solution)/shard_map/finish/pallas_call | solution.py:1232
  187.9 14.4 %all-to-all-done.4.heard_ref = f32[32,24,384]{2,1,0:T(8,128)} async-done(((f32[32,24,384]{2,1,0:T(8,128)}), f32[32,24,384]{2,1,0:T(8,128)}, u32[]{:S(2)}, u32[]{:S(2)}) %all-to-all-start.4) | async-done | bytes 1179680 | tf_op jit(solution)/shard_map/all_to_all | solution.py:1260
  204.4 3.4 %all-to-all-start.5 = ((f32[8,24,384]{2,1,0:T(8,128)}), f32[8,24,384]{2,1,0:T(8,128)S(1)}, u32[]{:S(2)}, u32[]{:S(2)}) async-start(f32[8,24,384]{2,1,0:T(8,128)} %strips.1), calls=%async_computation.5 | async-start | bytes 589824 | tf_op jit(solution)/shard_map/all_to_all | solution.py:1269
  207.8 3.3 %unpack.6.refs_6_ = f32[32,32,1764]{2,1,0:T(8,128)} custom-call(s32[1]{0:T(128)} %bitcast.me_ref, bf16[8,32,1764]{2,1,0:T(8,128)(2,1)} %get-tuple-element.130.refs_4_.refs_6_.refs_0_.refs_2_, bf16[8,32,1764]{2,1,0:T(8,128)(2,1)} %collective-permute-done.25.refs_1_, bf16[8,32,1764]{2,1,0:T(8,128)(2,1)} %get-tuple-element.130.refs_4_.refs_6_.refs_0_.refs_2_), custom_call_target="tpu_custom_call" | custom-call | flops 2200000000 | bytes 7000000 | tf_op jit(solution)/shard_map/unpack/pallas_call | solution.py:809
  212.0 3.4 %unpack.7 = f32[32,32,1764]{2,1,0:T(8,128)} custom-call(s32[1]{0:T(128)} %bitcast.me_ref, bf16[2,32,1764]{2,1,0:T(8,128)(2,1)} %copy-done.7, bf16[2,32,1764]{2,1,0:T(8,128)(2,1)} %copy-done.9, bf16[4,32,1764]{2,1,0:T(8,128)(2,1)} %copy-done.1, bf16[2,32,1764]{2,1,0:T(8,128)(2,1)} %copy-done.6, ...), custom_call_target="tpu_custom_call", output_to_operand_aliasing={{}: (7, {})} | custom-call | flops 2200000000 | bytes 7000000 | tf_op jit(solution)/shard_map/unpack/pallas_call | solution.py:809
  (111 shorter events, 49.0 us)
Async XLA Ops:
  4.8 8.8 %collective-permute-start.1 = (bf16[240,384]{1,0:T(8,128)(2,1)}, bf16[240,384]{1,0:T(8,128)(2,1)}, u32[]{:S(2)}, u32[]{:S(2)}) collective-permute-start(bf16[240,384]{1,0:T(8,128)(2,1)} %bundle.1.refs_0_), channel_id=1, source_target_pairs={{0,2},{1,3},{2,0},{3,1},{4,6},{5,7},{6,4},{7,5},{8,10},{9,11},{10,... | collective-permute-start | bytes 552968 | tf_op jit(solution)/shard_map/ppermute | solution.py:851
  7.8 7.7 %collective-permute-start = (bf16[240,384]{1,0:T(8,128)(2,1)}, bf16[240,384]{1,0:T(8,128)(2,1)}, u32[]{:S(2)}, u32[]{:S(2)}) collective-permute-start(bf16[240,384]{1,0:T(8,128)(2,1)} %bundle.1.refs_0_), channel_id=1, source_target_pairs={{0,1},{1,0},{2,3},{3,2},{4,5},{5,4},{6,7},{7,6},{8,9},{9,8},{10,11... | collective-permute-start | bytes 552968 | tf_op jit(solution)/shard_map/ppermute | solution.py:851
  7.8 15.2 %collective-permute-start.4 = (bf16[4,32,1764]{2,1,0:T(8,128)(2,1)}, bf16[4,32,1764]{2,1,0:T(8,128)(2,1)}, u32[]{:S(2)}, u32[]{:S(2)}) collective-permute-start(bf16[4,32,1764]{2,1,0:T(8,128)(2,1)} %get-tuple-element.80.refs_4_.refs_0_), channel_id=1, source_target_pairs={{0,3},{1,2},{2,1},{3,0},{4,7},{5,6},{6,5},{7,4},{8,11},{9,10},{10,... | collective-permute-start | bytes 1354760 | tf_op jit(solution)/shard_map/ppermute | solution.py:851
  7.9 25.3 %collective-permute-start.9 = (bf16[4,32,1764]{2,1,0:T(8,128)(2,1)}, bf16[4,32,1764]{2,1,0:T(8,128)(2,1)}, u32[]{:S(2)}, u32[]{:S(2)}) collective-permute-start(bf16[4,32,1764]{2,1,0:T(8,128)(2,1)} %get-tuple-element.88), channel_id=1, source_target_pairs={{0,2},{1,3},{2,0},{3,1},{4,6},{5,7},{6,4},{7,5},{8,10},{9,11},{10,... | collective-permute-start | bytes 1354760 | tf_op jit(solution)/shard_map/ppermute | solution.py:851
  12.6 20.6 %collective-permute-start.3 = (bf16[8,32,1764]{2,1,0:T(8,128)(2,1)}, bf16[8,32,1764]{2,1,0:T(8,128)(2,1)S(1)}, u32[]{:S(2)}, u32[]{:S(2)}) collective-permute-start(bf16[8,32,1764]{2,1,0:T(8,128)(2,1)} %get-tuple-element.83), channel_id=1, source_target_pairs={{0,1},{1,0},{2,3},{3,2},{4,5},{5,4},{6,7},{7,6},{8,9},{9,8},{10,11... | collective-permute-start | bytes 2709512 | tf_op jit(solution)/shard_map/ppermute | solution.py:851
  13.6 2.1 collective-permute-start.2
  25.2 17.0 %collective-permute-start.7 = (bf16[2,32,1764]{2,1,0:T(8,128)(2,1)}, bf16[2,32,1764]{2,1,0:T(8,128)(2,1)}, u32[]{:S(2)}, u32[]{:S(2)}) collective-permute-start(bf16[2,32,1764]{2,1,0:T(8,128)(2,1)} %get-tuple-element.86), channel_id=1, source_target_pairs={{0,2},{1,3},{2,0},{3,1},{4,6},{5,7},{6,4},{7,5},{8,10},{9,11},{10,... | collective-permute-start | bytes 677384 | tf_op jit(solution)/shard_map/ppermute | solution.py:851
  25.4 17.2 %collective-permute-start.8 = (bf16[2,32,1764]{2,1,0:T(8,128)(2,1)}, bf16[2,32,1764]{2,1,0:T(8,128)(2,1)}, u32[]{:S(2)}, u32[]{:S(2)}) collective-permute-start(bf16[2,32,1764]{2,1,0:T(8,128)(2,1)} %get-tuple-element.87.refs_4_), channel_id=1, source_target_pairs={{0,3},{1,2},{2,1},{3,0},{4,7},{5,6},{6,5},{7,4},{8,11},{9,10},{10,... | collective-permute-start | bytes 677384 | tf_op jit(solution)/shard_map/ppermute | solution.py:851
  29.5 18.5 %collective-permute-start.5 = (bf16[2,32,1764]{2,1,0:T(8,128)(2,1)}, bf16[2,32,1764]{2,1,0:T(8,128)(2,1)}, u32[]{:S(2)}, u32[]{:S(2)}) collective-permute-start(bf16[2,32,1764]{2,1,0:T(8,128)(2,1)} %get-tuple-element.84), channel_id=1, source_target_pairs={{0,2},{1,3},{2,0},{3,1},{4,6},{5,7},{6,4},{7,5},{8,10},{9,11},{10,... | collective-permute-start | bytes 677384 | tf_op jit(solution)/shard_map/ppermute | solution.py:851
  33.2 18.1 %collective-permute-start.6 = (bf16[2,32,1764]{2,1,0:T(8,128)(2,1)}, bf16[2,32,1764]{2,1,0:T(8,128)(2,1)}, u32[]{:S(2)}, u32[]{:S(2)}) collective-permute-start(bf16[2,32,1764]{2,1,0:T(8,128)(2,1)} %get-tuple-element.85.refs_7_), channel_id=1, source_target_pairs={{0,3},{1,2},{2,1},{3,0},{4,7},{5,6},{6,5},{7,4},{8,11},{9,10},{10,... | collective-permute-start | bytes 677384 | tf_op jit(solution)/shard_map/ppermute | solution.py:851
  56.1 13.7 %all-to-all-start = ((f32[32,4,128]{2,1,0:T(4,128)}), f32[32,4,128]{2,1,0:T(4,128)S(1)}, u32[]{:S(2)}, u32[]{:S(2)}) async-start(f32[32,4,128]{2,1,0:T(4,128)} %get-tuple-element.95), calls=%async_computation | async-start | bytes 131072 | tf_op jit(solution)/shard_map/all_to_all | solution.py:854
  84.2 10.0 %all-to-all-start.1 = ((f32[32,4,128]{2,1,0:T(4,128)}), f32[32,4,128]{2,1,0:T(4,128)S(1)}, u32[]{:S(2)}, u32[]{:S(2)}) async-start(f32[32,4,128]{2,1,0:T(4,128)} %get-tuple-element.101.own_ref), calls=%async_computation.1 | async-start | bytes 131072 | tf_op jit(solution)/shard_map/all_to_all | solution.py:854
  86.9 2.8 %collective-permute-start.12 = (bf16[8,32,100]{2,1,0:T(8,128)(2,1)S(1)}, bf16[8,32,100]{2,1,0:T(8,128)(2,1)S(1)}, u32[]{:S(2)}, u32[]{:S(2)}) collective-permute-start(bf16[8,32,100]{2,1,0:T(8,128)(2,1)S(1)} %bitcast.33), channel_id=1, source_target_pairs={{0,1},{1,0},{2,3},{3,2},{4,5},{5,4},{6,7},{7,6},{8,9},{9,8},{10,11... | collective-permute-start | bytes 153608 | tf_op jit(solution)/shard_map/ppermute | solution.py:851
  87.1 4.8 %collective-permute-start.13 = (bf16[8,32,100]{2,1,0:T(8,128)(2,1)S(1)}, bf16[8,32,100]{2,1,0:T(8,128)(2,1)S(1)}, u32[]{:S(2)}, u32[]{:S(2)}) collective-permute-start(bf16[8,32,100]{2,1,0:T(8,128)(2,1)S(1)} %bitcast.34), channel_id=1, source_target_pairs={{0,2},{1,3},{2,0},{3,1},{4,6},{5,7},{6,4},{7,5},{8,10},{9,11},{10,... | collective-permute-start | bytes 153608 | tf_op jit(solution)/shard_map/ppermute | solution.py:851
  88.8 4.5 %collective-permute-start.14 = (bf16[8,32,100]{2,1,0:T(8,128)(2,1)S(1)}, bf16[8,32,100]{2,1,0:T(8,128)(2,1)S(1)}, u32[]{:S(2)}, u32[]{:S(2)}) collective-permute-start(bf16[8,32,100]{2,1,0:T(8,128)(2,1)S(1)} %bitcast.35), channel_id=1, source_target_pairs={{0,3},{1,2},{2,1},{3,0},{4,7},{5,6},{6,5},{7,4},{8,11},{9,10},{10,... | collective-permute-start | bytes 153608 | tf_op jit(solution)/shard_map/ppermute | solution.py:851
  100.8 11.6 %all-to-all-start.2 = ((f32[32,4,128]{2,1,0:T(4,128)}), f32[32,4,128]{2,1,0:T(4,128)S(1)}, u32[]{:S(2)}, u32[]{:S(2)}) async-start(f32[32,4,128]{2,1,0:T(4,128)} %get-tuple-element.110), calls=%async_computation.2 | async-start | bytes 131072 | tf_op jit(solution)/shard_map/all_to_all | solution.py:854
  104.9 29.4 %collective-permute-start.10 = (bf16[8,32,441]{2,1,0:T(8,128)(2,1)}, bf16[8,32,441]{2,1,0:T(8,128)(2,1)S(1)}, u32[]{:S(2)}, u32[]{:S(2)}) collective-permute-start(bf16[8,32,441]{2,1,0:T(8,128)(2,1)} %get-tuple-element.99), channel_id=1, source_target_pairs={{0,2},{1,3},{2,0},{3,1},{4,6},{5,7},{6,4},{7,5},{8,10},{9,11},{10,... | collective-permute-start | bytes 677384 | tf_op jit(solution)/shard_map/ppermute | solution.py:851
  106.8 27.6 %collective-permute-start.11 = (bf16[8,32,441]{2,1,0:T(8,128)(2,1)}, bf16[8,32,441]{2,1,0:T(8,128)(2,1)S(1)}, u32[]{:S(2)}, u32[]{:S(2)}) collective-permute-start(bf16[8,32,441]{2,1,0:T(8,128)(2,1)} %get-tuple-element.100), channel_id=1, source_target_pairs={{0,3},{1,2},{2,1},{3,0},{4,7},{5,6},{6,5},{7,4},{8,11},{9,10},{10,... | collective-permute-start | bytes 677384 | tf_op jit(solution)/shard_map/ppermute | solution.py:851
  106.8 27.6 %collective-permute-start.17 = (bf16[8,32,441]{2,1,0:T(8,128)(2,1)}, bf16[8,32,441]{2,1,0:T(8,128)(2,1)S(1)}, u32[]{:S(2)}, u32[]{:S(2)}) collective-permute-start(bf16[8,32,441]{2,1,0:T(8,128)(2,1)} %get-tuple-element.107), channel_id=1, source_target_pairs={{0,1},{1,0},{2,3},{3,2},{4,5},{5,4},{6,7},{7,6},{8,9},{9,8},{10,11... | collective-permute-start | bytes 677384 | tf_op jit(solution)/shard_map/ppermute | solution.py:851
  107.1 22.8 %collective-permute-start.15 = (bf16[8,32,100]{2,1,0:T(8,128)(2,1)}, bf16[8,32,100]{2,1,0:T(8,128)(2,1)S(1)}, u32[]{:S(2)}, u32[]{:S(2)}) collective-permute-start(bf16[8,32,100]{2,1,0:T(8,128)(2,1)} %get-tuple-element.104), channel_id=1, source_target_pairs={{0,2},{1,3},{2,0},{3,1},{4,6},{5,7},{6,4},{7,5},{8,10},{9,11},{10,... | collective-permute-start | bytes 153608 | tf_op jit(solution)/shard_map/ppermute | solution.py:851
  108.9 25.4 %collective-permute-start.16 = (bf16[8,32,100]{2,1,0:T(8,128)(2,1)}, bf16[8,32,100]{2,1,0:T(8,128)(2,1)S(1)}, u32[]{:S(2)}, u32[]{:S(2)}) collective-permute-start(bf16[8,32,100]{2,1,0:T(8,128)(2,1)} %get-tuple-element.105), channel_id=1, source_target_pairs={{0,3},{1,2},{2,1},{3,0},{4,7},{5,6},{6,5},{7,4},{8,11},{9,10},{10,... | collective-permute-start | bytes 153608 | tf_op jit(solution)/shard_map/ppermute | solution.py:851
  127.1 9.9 %all-to-all-start.3 = ((f32[32,4,128]{2,1,0:T(4,128)}), f32[32,4,128]{2,1,0:T(4,128)S(1)}, u32[]{:S(2)}, u32[]{:S(2)}) async-start(f32[32,4,128]{2,1,0:T(4,128)} %get-tuple-element.116.refs_0_), calls=%async_computation.3 | async-start | bytes 131072 | tf_op jit(solution)/shard_map/all_to_all | solution.py:854
  129.9 4.4 %collective-permute-start.18 = (bf16[8,32,100]{2,1,0:T(8,128)(2,1)}, bf16[8,32,100]{2,1,0:T(8,128)(2,1)}, u32[]{:S(2)}, u32[]{:S(2)}) collective-permute-start(bf16[8,32,100]{2,1,0:T(8,128)(2,1)} %get-tuple-element.109), channel_id=1, source_target_pairs={{0,1},{1,0},{2,3},{3,2},{4,5},{5,4},{6,7},{7,6},{8,9},{9,8},{10,11... | collective-permute-start | bytes 153608 | tf_op jit(solution)/shard_map/ppermute | solution.py:851
  143.0 20.7 %collective-permute-start.19 = (bf16[2,32,1764]{2,1,0:T(8,128)(2,1)}, bf16[2,32,1764]{2,1,0:T(8,128)(2,1)S(1)}, u32[]{:S(2)}, u32[]{:S(2)}) collective-permute-start(bf16[2,32,1764]{2,1,0:T(8,128)(2,1)} %get-tuple-element.125), channel_id=1, source_target_pairs={{0,3},{1,2},{2,1},{3,0},{4,7},{5,6},{6,5},{7,4},{8,11},{9,10},{10,... | collective-permute-start | bytes 677384 | tf_op jit(solution)/shard_map/ppermute | solution.py:851
  143.2 20.6 %collective-permute-start.21 = (bf16[2,32,1764]{2,1,0:T(8,128)(2,1)}, bf16[2,32,1764]{2,1,0:T(8,128)(2,1)S(1)}, u32[]{:S(2)}, u32[]{:S(2)}) collective-permute-start(bf16[2,32,1764]{2,1,0:T(8,128)(2,1)} %get-tuple-element.127), channel_id=1, source_target_pairs={{0,2},{1,3},{2,0},{3,1},{4,6},{5,7},{6,4},{7,5},{8,10},{9,11},{10,... | collective-permute-start | bytes 677384 | tf_op jit(solution)/shard_map/ppermute | solution.py:851
  150.1 13.7 %collective-permute-start.20 = (bf16[2,32,1764]{2,1,0:T(8,128)(2,1)}, bf16[2,32,1764]{2,1,0:T(8,128)(2,1)S(1)}, u32[]{:S(2)}, u32[]{:S(2)}) collective-permute-start(bf16[2,32,1764]{2,1,0:T(8,128)(2,1)} %get-tuple-element.126), channel_id=1, source_target_pairs={{0,3},{1,2},{2,1},{3,0},{4,7},{5,6},{6,5},{7,4},{8,11},{9,10},{10,... | collective-permute-start | bytes 677384 | tf_op jit(solution)/shard_map/ppermute | solution.py:851
  150.2 15.6 %collective-permute-start.22 = (bf16[2,32,1764]{2,1,0:T(8,128)(2,1)}, bf16[2,32,1764]{2,1,0:T(8,128)(2,1)S(1)}, u32[]{:S(2)}, u32[]{:S(2)}) collective-permute-start(bf16[2,32,1764]{2,1,0:T(8,128)(2,1)} %get-tuple-element.128), channel_id=1, source_target_pairs={{0,2},{1,3},{2,0},{3,1},{4,6},{5,7},{6,4},{7,5},{8,10},{9,11},{10,... | collective-permute-start | bytes 677384 | tf_op jit(solution)/shard_map/ppermute | solution.py:851
  168.5 33.8 %all-to-all-start.4 = ((f32[32,24,384]{2,1,0:T(8,128)}), f32[32,24,384]{2,1,0:T(8,128)}, u32[]{:S(2)}, u32[]{:S(2)}) async-start(f32[32,24,384]{2,1,0:T(8,128)} %bitcast.30), calls=%async_computation.4 | async-start | bytes 2359296 | tf_op jit(solution)/shard_map/all_to_all | solution.py:1260
  179.5 28.3 %collective-permute-start.25 = (bf16[8,32,1764]{2,1,0:T(8,128)(2,1)}, bf16[8,32,1764]{2,1,0:T(8,128)(2,1)}, u32[]{:S(2)}, u32[]{:S(2)}) collective-permute-start(bf16[8,32,1764]{2,1,0:T(8,128)(2,1)} %get-tuple-element.137), channel_id=1, source_target_pairs={{0,1},{1,0},{2,3},{3,2},{4,5},{5,4},{6,7},{7,6},{8,9},{9,8},{10,11... | collective-permute-start | bytes 2709512 | tf_op jit(solution)/shard_map/ppermute | solution.py:851
  179.7 31.4 %collective-permute-start.23 = (bf16[4,32,1764]{2,1,0:T(8,128)(2,1)}, bf16[4,32,1764]{2,1,0:T(8,128)(2,1)S(1)}, u32[]{:S(2)}, u32[]{:S(2)}) collective-permute-start(bf16[4,32,1764]{2,1,0:T(8,128)(2,1)} %get-tuple-element.135), channel_id=1, source_target_pairs={{0,2},{1,3},{2,0},{3,1},{4,6},{5,7},{6,4},{7,5},{8,10},{9,11},{10,... | collective-permute-start | bytes 1354760 | tf_op jit(solution)/shard_map/ppermute | solution.py:851
  181.4 29.8 %collective-permute-start.24 = (bf16[4,32,1764]{2,1,0:T(8,128)(2,1)}, bf16[4,32,1764]{2,1,0:T(8,128)(2,1)}, u32[]{:S(2)}, u32[]{:S(2)}) collective-permute-start(bf16[4,32,1764]{2,1,0:T(8,128)(2,1)} %get-tuple-element.136), channel_id=1, source_target_pairs={{0,3},{1,2},{2,1},{3,0},{4,7},{5,6},{6,5},{7,4},{8,11},{9,10},{10,... | collective-permute-start | bytes 1354760 | tf_op jit(solution)/shard_map/ppermute | solution.py:851
  204.4 13.0 %all-to-all-start.5 = ((f32[8,24,384]{2,1,0:T(8,128)}), f32[8,24,384]{2,1,0:T(8,128)S(1)}, u32[]{:S(2)}, u32[]{:S(2)}) async-start(f32[8,24,384]{2,1,0:T(8,128)} %strips.1), calls=%async_computation.5 | async-start | bytes 589824 | tf_op jit(solution)/shard_map/all_to_all | solution.py:1269
  (21 other events, 61.3 us)

commit v8 on v7

--- a/solution.py
+++ b/solution.py
@@ -1211,14 +1211,14 @@
             product = pl.pallas_call(
                 split_kernel,
                 grid=(1,),
-                in_specs=[whole(3 * C, 3 * C), *anywhere(1 + len(waits))],
+                in_specs=[whole(3 * C, 3 * C), *anywhere(len(waits))],
                 out_specs=filter_spec(0),
                 out_shape=filter_shape,
                 input_output_aliases={1: 0},
                 compiler_params=kernel_params(),
                 name="split",
                 cost_estimate=lasting(1.5),
-            )(product, filter_sums, *waits)
+            )(product, filter_sums, *waits[:-1])
             waits = [product, *waits]
     for partner in range(near):
         returned[partner].append(swap(kept[partner], partner))

time: 220 us -> 226 us (1.027)
  waiting for transfers between devices: 48.3 us -> 52.6 us
    ppermute x26, waiting for transfers between devices: 17.6 us -> 38.3 us  [swap(): lax.ppermute(value, 'tensor', [(i, i ^ partner) for i in range(partners)])]
    all_to_all x1, waiting for transfers between devices: 14.4 us -> 0.01 us  [local(): lax.all_to_all(product.reshape(devices, strip, 3 * C), ('tensor', 'dp'),...]
    unnamed x48 -> x50, local copies, waits for them, and re-layouts: 6.95 us -> 7.62 us
  transfers between devices with their start and end apart: 32 -> 32, of which waited for: 16 -> 15; matrix products, arithmetic and copies ran while one was open for 1% -> 1% of each run, Pallas kernels for 37% -> 36%
where the time goes in v8:
time: 226 us; the launch traced here: 225 us
  Pallas kernels  117 us (52%)
  waiting for transfers between devices  52.6 us (23%)
  starting transfers between devices  43.7 us (19%)
  local copies, waits for them, and re-layouts  9.06 us (4%)
    ppermute x26, waiting for transfers between devices, swap(): lax.ppermute(value, 'tensor', [(i, i ^ partner) for i in range(partners)])  38.3 us
    ppermute x26, starting transfers between devices, swap(): lax.ppermute(value, 'tensor', [(i, i ^ partner) for i in range(partners)])  20.7 us
    pallas_call x3, Pallas kernels, local(): pl.pallas_call(functools.partial(last_conv_kernel, partners, near, first,...  18.2 us
    pallas_call x3, Pallas kernels, local(): pl.pallas_call(functools.partial(first_conv_kernel, partners, first, fina...  17.6 us
    all_to_all x4, starting transfers between devices, share(): return lax.all_to_all(copies, ('dp', 'tensor'), 0, 0)  15.8 us
    all_to_all x4, waiting for transfers between devices, share(): return lax.all_to_all(copies, ('dp', 'tensor'), 0, 0)  14.2 us
    pallas_call x1, Pallas kernels, local(): pl.pallas_call(back_kernel, grid=(images_each // pair,), in_specs=[smem()...  14.1 us
    pallas_call x1, Pallas kernels, local(): pl.pallas_call(functools.partial(middle_kernel, partners), grid=(images_e...  13.8 us
  transfers between devices with their start and end apart: 32, of which 15 were waited for; matrix products, arithmetic and copies ran while one was open for 1% of the time, Pallas kernels for 36%

profile of v8, /device:TPU:0, one launch (start us, length us, event | category | flops | bytes accessed | tf_op | source)
XLA Modules:
  0.0 224.5 jit_solution(14893416107902801263)
XLA Ops:
  0.6 2.5 %pack.4 = (bf16[4,32,1764]{2,1,0:T(8,128)(2,1)}, bf16[4,32,1764]{2,1,0:T(8,128)(2,1)}) custom-call(s32[1]{0:T(128)} %bitcast.me_ref, bf16[32,32,1764]{2,1,0:T(8,128)(2,1)} %maps_ref.7), custom_call_target="tpu_custom_call" | custom-call | flops 2750000128 | bytes 8750000 | tf_op jit(solution)/shard_map/pack/pallas_call | solution.py:770
  4.8 3.0 %collective-permute-start.1 = (bf16[240,384]{1,0:T(8,128)(2,1)}, bf16[240,384]{1,0:T(8,128)(2,1)}, u32[]{:S(2)}, u32[]{:S(2)}) collective-permute-start(bf16[240,384]{1,0:T(8,128)(2,1)} %bundle.1.refs_0_), channel_id=1, source_target_pairs={{0,2},{1,3},{2,0},{3,1},{4,6},{5,7},{6,4},{7,5},{8,10},{9,11},{10,... | collective-permute-start | bytes 552968 | tf_op jit(solution)/shard_map/ppermute | solution.py:851
  9.9 2.7 %pack.5 = (bf16[8,32,1764]{2,1,0:T(8,128)(2,1)}, bf16[8,32,1764]{2,1,0:T(8,128)(2,1)}) custom-call(s32[1]{0:T(128)} %bitcast.me_ref, bf16[32,32,1764]{2,1,0:T(8,128)(2,1)} %maps_ref.7, bf16[4,32,1764]{2,1,0:T(8,128)(2,1)} %get-tuple-element.80.refs_4_.refs_0_), custom_call_target="tpu_custom_call" | custom-call | flops 2750000128 | bytes 8750000 | tf_op jit(solution)/shard_map/pack/pallas_call | solution.py:770
  15.7 2.4 %unbundle.1 = (bf16[384,384]{1,0:T(8,128)(2,1)}, bf16[384,384]{1,0:T(8,128)(2,1)}, bf16[384,384]{1,0:T(8,128)(2,1)}, bf16[384,384]{1,0:T(8,128)(2,1)}, f32[2,128,100]{2,1,0:T(8,128)}, /*index=5*/f32[8,128]{1,0:T(8,128)}) custom-call(s32[1]{0:T(128)} %bitcast.me_ref, s32[1]{0:T(128)} %bitcast.2.task_ref, f32[2,100]{1,0:T(2,128)} %context_ref.1, ...), custom_call_target="tpu_custom_call" | custom-call | flops 2200000000 | bytes 7000000 | tf_op jit(solution)/shard_map/unbundle/pallas_call | solution.py:915
  18.1 4.9 %collective-permute-done.4.refs_0_.refs_3_ = bf16[4,32,1764]{2,1,0:T(8,128)(2,1)} collective-permute-done((bf16[4,32,1764]{2,1,0:T(8,128)(2,1)}, bf16[4,32,1764]{2,1,0:T(8,128)(2,1)}, u32[]{:S(2)}, u32[]{:S(2)}) %collective-permute-start.4) | collective-permute-done | bytes 451616 | tf_op jit(solution)/shard_map/ppermute | solution.py:851
  23.0 2.3 %pack.7 = (bf16[2,32,1764]{2,1,0:T(8,128)(2,1)}, bf16[2,32,1764]{2,1,0:T(8,128)(2,1)}) custom-call(s32[1]{0:T(128)} %bitcast.me_ref, bf16[32,32,1764]{2,1,0:T(8,128)(2,1)} %maps_ref.7, bf16[4,32,1764]{2,1,0:T(8,128)(2,1)} %collective-permute-done.4.refs_0_.refs_3_), custom_call_target="tpu_custom_call" | custom-call | flops 2750000128 | bytes 8750000 | tf_op jit(solution)/shard_map/pack/pallas_call | solution.py:770
  34.2 8.1 %first_conv.3 = (f32[8,128,1792]{2,1,0:T(8,128)}, bf16[8,128,1792]{2,1,0:T(8,128)(2,1)}, f32[128,128]{1,0:T(8,128)}) custom-call(s32[1]{0:T(128)} %bitcast.me_ref, f32[8]{0:T(128)} %compare_convert_fusion.live_ref, f32[8,128]{1,0:T(8,128)} %pad.4.told_ref, bf16[384,384]{1,0:T(8,128)(2,1)} %get-tuple-element.81.weights_ref, ...), custom_call_target="tpu_custom_call" | custom-call | flops 10119999488 | bytes 32200000 | tf_op jit(solution)/shard_map/first_conv/pallas_call | solution.py:944
  42.6 4.8 %first_conv.4 = (f32[8,128,1792]{2,1,0:T(8,128)}, bf16[8,128,1792]{2,1,0:T(8,128)(2,1)}, f32[128,128]{1,0:T(8,128)}) custom-call(s32[1]{0:T(128)} %bitcast.me_ref, f32[8]{0:T(128)} %compare_convert_fusion.live_ref, f32[8,128]{1,0:T(8,128)} %pad.4.told_ref, ...), custom_call_target="tpu_custom_call", output_to_operand_aliasing={{0}: (9, {}), {1}: (10, {})} | custom-call | flops 5059999744 | bytes 16099999 | tf_op jit(solution)/shard_map/first_conv/pallas_call | solution.py:944
  48.0 3.4 %collective-permute-done.6.refs_3_ = bf16[2,32,1764]{2,1,0:T(8,128)(2,1)} collective-permute-done((bf16[2,32,1764]{2,1,0:T(8,128)(2,1)}, bf16[2,32,1764]{2,1,0:T(8,128)(2,1)}, u32[]{:S(2)}, u32[]{:S(2)}) %collective-permute-start.6) | collective-permute-done | bytes 225824 | tf_op jit(solution)/shard_map/ppermute | solution.py:851
  51.3 4.8 %first_conv.5 = (f32[8,128,1792]{2,1,0:T(8,128)}, bf16[8,128,1792]{2,1,0:T(8,128)(2,1)}, f32[32,4,128]{2,1,0:T(4,128)}) custom-call(s32[1]{0:T(128)} %bitcast.me_ref, f32[8]{0:T(128)} %compare_convert_fusion.live_ref, f32[8,128]{1,0:T(8,128)} %pad.4.told_ref, ...), custom_call_target="tpu_custom_call", output_to_operand_aliasing={{0}: (9, {}), {1}: (10, {})} | custom-call | flops 5059999744 | bytes 16099999 | tf_op jit(solution)/shard_map/first_conv/pallas_call | solution.py:944
  56.1 6.4 %all-to-all-start = ((f32[32,4,128]{2,1,0:T(4,128)}), f32[32,4,128]{2,1,0:T(4,128)S(1)}, u32[]{:S(2)}, u32[]{:S(2)}) async-start(f32[32,4,128]{2,1,0:T(4,128)} %get-tuple-element.95), calls=%async_computation | async-start | bytes 131072 | tf_op jit(solution)/shard_map/all_to_all | solution.py:854
  62.6 7.2 %all-to-all-done.heard_ref.heard_two_ref = f32[32,4,128]{2,1,0:T(4,128)S(1)} async-done(((f32[32,4,128]{2,1,0:T(4,128)}), f32[32,4,128]{2,1,0:T(4,128)S(1)}, u32[]{:S(2)}, u32[]{:S(2)}) %all-to-all-start) | async-done | bytes 65568 | tf_op jit(solution)/shard_map/all_to_all | solution.py:854
  70.4 13.8 %middle.1 = (bf16[8,32,441]{2,1,0:T(8,128)(2,1)}, bf16[8,32,441]{2,1,0:T(8,128)(2,1)}, bf16[8,32,441]{2,1,0:T(8,128)(2,1)}, bf16[8,32,441]{2,1,0:T(8,128)(2,1)},...) custom-call(s32[1]{0:T(128)} %bitcast.me_ref, ...), custom_call_target="tpu_custom_call" | custom-call | flops 17600000000 | bytes 56000000 | tf_op jit(solution)/shard_map/middle/pallas_call | solution.py:976
  84.2 2.6 %all-to-all-start.1 = ((f32[32,4,128]{2,1,0:T(4,128)}), f32[32,4,128]{2,1,0:T(4,128)S(1)}, u32[]{:S(2)}, u32[]{:S(2)}) async-start(f32[32,4,128]{2,1,0:T(4,128)} %get-tuple-element.101.own_ref), calls=%async_computation.1 | async-start | bytes 131072 | tf_op jit(solution)/shard_map/all_to_all | solution.py:854
  94.8 6.0 %top.1 = (bf16[8,32,100]{2,1,0:T(8,128)(2,1)}, bf16[8,32,100]{2,1,0:T(8,128)(2,1)}, bf16[8,32,100]{2,1,0:T(8,128)(2,1)}, bf16[8,32,100]{2,1,0:T(8,128)(2,1)}, f3...) custom-call(s32[1]{0:T(128)} %bitcast.me_ref, ...), custom_call_target="tpu_custom_call" | custom-call | flops 7040000000 | bytes 22400000 | tf_op jit(solution)/shard_map/top/pallas_call | solution.py:1019
  100.8 4.1 %all-to-all-start.2 = ((f32[32,4,128]{2,1,0:T(4,128)}), f32[32,4,128]{2,1,0:T(4,128)S(1)}, u32[]{:S(2)}, u32[]{:S(2)}) async-start(f32[32,4,128]{2,1,0:T(4,128)} %get-tuple-element.110), calls=%async_computation.2 | async-start | bytes 131072 | tf_op jit(solution)/shard_map/all_to_all | solution.py:854
  108.9 3.5 %all-to-all-done.2.heard_ref.heard_top_ref = f32[32,4,128]{2,1,0:T(4,128)S(1)} async-done(((f32[32,4,128]{2,1,0:T(4,128)}), f32[32,4,128]{2,1,0:T(4,128)S(1)}, u32[]{:S(2)}, u32[]{:S(2)}) %all-to-all-start.2) | async-done | bytes 65568 | tf_op jit(solution)/shard_map/all_to_all | solution.py:854
  113.0 14.1 %back.1 = (f32[8,128,1792]{2,1,0:T(8,128)}, bf16[8,128,512]{2,1,0:T(8,128)(2,1)}, f32[32,4,128]{2,1,0:T(4,128)}) custom-call(f32[8]{0:T(128)} %compare_convert_fusion.live_ref, f32[32,4,128]{2,1,0:T(4,128)} %copy-done.13, f32[8,128]{1,0:T(8,128)} %get-tuple-element.111.norm_three_ref, f32[8,128]{1,0:T(8,128)} %get-tuple-element.112.norm_two_ref.norm_ref, ...), custom_call_target="tpu_custom_call" | custom-call | flops 17600000000 | bytes 56000000 | tf_op jit(solution)/shard_map/back/pallas_call | solution.py:1073
  127.2 2.7 %all-to-all-start.3 = ((f32[32,4,128]{2,1,0:T(4,128)}), f32[32,4,128]{2,1,0:T(4,128)S(1)}, u32[]{:S(2)}, u32[]{:S(2)}) async-start(f32[32,4,128]{2,1,0:T(4,128)} %get-tuple-element.116.refs_0_), calls=%async_computation.3 | async-start | bytes 131072 | tf_op jit(solution)/shard_map/all_to_all | solution.py:854
  130.0 4.3 %filter_three.1.refs_0_ = f32[4,2,3,32,384]{4,3,2,1,0:T(8,128)} custom-call(bf16[8,128,512]{2,1,0:T(8,128)(2,1)} %get-tuple-element.120.error_ref, bf16[8,128,512]{2,1,0:T(8,128)(2,1)} %get-tuple-element.121.hidden_ref, f32[32,4,128]{2,1,0:T(4,128)} %get-tuple-element.116.refs_0_), custom_call_target="tpu_custom_call" | custom-call | flops 5500000256 | bytes 17500000 | tf_op jit(solution)/shard_map/filter_three/pallas_call | solution.py:1125
  134.4 2.7 %all-to-all-done.3.heard_ref.heard_back_ref = f32[32,4,128]{2,1,0:T(4,128)S(1)} async-done(((f32[32,4,128]{2,1,0:T(4,128)}), f32[32,4,128]{2,1,0:T(4,128)S(1)}, u32[]{:S(2)}, u32[]{:S(2)}) %all-to-all-start.3) | async-done | bytes 65568 | tf_op jit(solution)/shard_map/all_to_all | solution.py:854
  137.7 5.3 %last_conv.3 = (bf16[8,32,1764]{2,1,0:T(8,128)(2,1)}, bf16[8,32,1764]{2,1,0:T(8,128)(2,1)}, bf16[2,32,1764]{2,1,0:T(8,128)(2,1)}, bf16[2,32,1764]{2,1,0:T(8,128)(2,1)}) custom-call(s32[1]{0:T(128)} %bitcast.me_ref, f32[8]{0:T(128)} %compare_convert_fusion.live_ref, f32[32,4,128]{2,1,0:T(4,128)} %copy-done, ...), custom_call_target="tpu_custom_call" | custom-call | flops 3300000000 | bytes 10500000 | tf_op jit(solution)/shard_map/last_conv/pallas_call | solution.py:1162
  144.8 5.3 %last_conv.4 = (bf16[8,32,1764]{2,1,0:T(8,128)(2,1)}, bf16[8,32,1764]{2,1,0:T(8,128)(2,1)}, bf16[2,32,1764]{2,1,0:T(8,128)(2,1)}, bf16[2,32,1764]{2,1,0:T(8,128)(2,1)}) custom-call(s32[1]{0:T(128)} %bitcast.me_ref, f32[8]{0:T(128)} %compare_convert_fusion.live_ref, f32[32,4,128]{2,1,0:T(4,128)} %copy-done, ...), custom_call_target="tpu_custom_call", output_to_operand_aliasing={{0}: (8, {}), {1}: (9, {})} | custom-call | flops 3300000000 | bytes 10500000 | tf_op jit(solution)/shard_map/last_conv/pallas_call | solution.py:1162
  150.3 11.9 %last_filter.1.product_ref = f32[384,384]{1,0:T(8,128)} custom-call(f32[8]{0:T(128)} %compare_convert_fusion.live_ref, f32[32,4,128]{2,1,0:T(4,128)} %copy-done, f32[8,128]{1,0:T(8,128)} %get-tuple-element.112.norm_two_ref.norm_ref, f32[8,128]{1,0:T(8,128)} %get-tuple-element.96.vectors_ref, f32[8,128,1792]{2,1,0:T(8,128)} %get-tuple-element.118.grad_ref, ...), custom_call_target="tpu_custom_call" | custom-call | flops 10560000000 | bytes 33600000 | tf_op jit(solution)/shard_map/last_filter/pallas_call | solution.py:1190
  165.7 3.8 %all-to-all-start.4 = ((f32[32,24,384]{2,1,0:T(8,128)}), f32[32,24,384]{2,1,0:T(8,128)}, u32[]{:S(2)}, u32[]{:S(2)}) async-start(f32[32,24,384]{2,1,0:T(8,128)} %bitcast.30), calls=%async_computation.4 | async-start | bytes 2359296 | tf_op jit(solution)/shard_map/all_to_all | solution.py:1260
  171.2 17.5 %collective-permute-done.22.refs_4_.refs_1_ = bf16[2,32,1764]{2,1,0:T(8,128)(2,1)S(1)} collective-permute-done((bf16[2,32,1764]{2,1,0:T(8,128)(2,1)S(1)}, bf16[2,32,1764]{2,1,0:T(8,128)(2,1)S(1)}, u32[]{:S(2)}, u32[]{:S(2)}) %collective-permute-start.22) | collective-permute-done | bytes 225824 | tf_op jit(solution)/shard_map/ppermute | solution.py:851
  189.4 7.5 %last_conv.5 = (bf16[8,32,1764]{2,1,0:T(8,128)(2,1)}, bf16[8,32,1764]{2,1,0:T(8,128)(2,1)}, bf16[4,32,1764]{2,1,0:T(8,128)(2,1)}, bf16[4,32,1764]{2,1,0:T(8,128)(2,1)}) custom-call(s32[1]{0:T(128)} %bitcast.me_ref, f32[8]{0:T(128)} %compare_convert_fusion.live_ref, f32[32,4,128]{2,1,0:T(4,128)} %copy-done, ...), custom_call_target="tpu_custom_call", output_to_operand_aliasing={{0}: (13, {}), {1}: (14, {})} | custom-call | flops 6600000000 | bytes 21000000 | tf_op jit(solution)/shard_map/last_conv/pallas_call | solution.py:1162
  200.8 2.5 %finish.1 = (f32[2,32,100]{2,1,0:T(8,128)}, f32[2,32]{1,0:T(2,128)}, f32[2,100]{1,0:T(2,128)}, f32[32]{0:T(128)}, f32[32]{0:T(128)}, /*index=5*/f32[32]{0:T(128)}, f32[32]{0:T(128)}, f32[9]{0:T(128)}) custom-call(s32[1]{0:T(128)} %bitcast.15.here_ref, s32[1]{0:T(128)} %bitcast.me_ref, f32[32,4,128]{2,1,0:T(4,128)} %copy-done.12, f32[32,4,128]{2,1,0:T(4,128)} %copy-done.13, ...), custom_call_target="tpu_custom_call" | custom-call | flops 2200000000 | bytes 7000000 | tf_op jit(solution)/shard_map/finish/pallas_call | solution.py:1232
  207.3 3.5 %all-to-all-start.5 = ((f32[8,24,384]{2,1,0:T(8,128)}), f32[8,24,384]{2,1,0:T(8,128)S(1)}, u32[]{:S(2)}, u32[]{:S(2)}) async-start(f32[8,24,384]{2,1,0:T(8,128)} %strips.1), calls=%async_computation.5 | async-start | bytes 589824 | tf_op jit(solution)/shard_map/all_to_all | solution.py:1269
  210.9 3.3 %unpack.6.refs_6_ = f32[32,32,1764]{2,1,0:T(8,128)} custom-call(s32[1]{0:T(128)} %bitcast.me_ref, bf16[8,32,1764]{2,1,0:T(8,128)(2,1)} %get-tuple-element.130.refs_4_.refs_6_.refs_0_.refs_2_, bf16[8,32,1764]{2,1,0:T(8,128)(2,1)} %collective-permute-done.25.refs_1_, bf16[8,32,1764]{2,1,0:T(8,128)(2,1)} %get-tuple-element.130.refs_4_.refs_6_.refs_0_.refs_2_), custom_call_target="tpu_custom_call" | custom-call | flops 2200000000 | bytes 7000000 | tf_op jit(solution)/shard_map/unpack/pallas_call | solution.py:809
  214.2 5.4 %collective-permute-done.24.refs_5_ = bf16[4,32,1764]{2,1,0:T(8,128)(2,1)} collective-permute-done((bf16[4,32,1764]{2,1,0:T(8,128)(2,1)}, bf16[4,32,1764]{2,1,0:T(8,128)(2,1)}, u32[]{:S(2)}, u32[]{:S(2)}) %collective-permute-start.24) | collective-permute-done | bytes 451616 | tf_op jit(solution)/shard_map/ppermute | solution.py:851
  219.5 3.4 %unpack.7 = f32[32,32,1764]{2,1,0:T(8,128)} custom-call(s32[1]{0:T(128)} %bitcast.me_ref, bf16[2,32,1764]{2,1,0:T(8,128)(2,1)} %copy-done.7, bf16[2,32,1764]{2,1,0:T(8,128)(2,1)} %copy-done.9, bf16[4,32,1764]{2,1,0:T(8,128)(2,1)} %copy-done.1, bf16[2,32,1764]{2,1,0:T(8,128)(2,1)} %copy-done.6, ...), custom_call_target="tpu_custom_call", output_to_operand_aliasing={{}: (7, {})} | custom-call | flops 2200000000 | bytes 7000000 | tf_op jit(solution)/shard_map/unpack/pallas_call | solution.py:809
  (113 shorter events, 47.9 us)
Async XLA Ops:
  4.8 8.8 %collective-permute-start.1 = (bf16[240,384]{1,0:T(8,128)(2,1)}, bf16[240,384]{1,0:T(8,128)(2,1)}, u32[]{:S(2)}, u32[]{:S(2)}) collective-permute-start(bf16[240,384]{1,0:T(8,128)(2,1)} %bundle.1.refs_0_), channel_id=1, source_target_pairs={{0,2},{1,3},{2,0},{3,1},{4,6},{5,7},{6,4},{7,5},{8,10},{9,11},{10,... | collective-permute-start | bytes 552968 | tf_op jit(solution)/shard_map/ppermute | solution.py:851
  7.8 7.7 %collective-permute-start = (bf16[240,384]{1,0:T(8,128)(2,1)}, bf16[240,384]{1,0:T(8,128)(2,1)}, u32[]{:S(2)}, u32[]{:S(2)}) collective-permute-start(bf16[240,384]{1,0:T(8,128)(2,1)} %bundle.1.refs_0_), channel_id=1, source_target_pairs={{0,1},{1,0},{2,3},{3,2},{4,5},{5,4},{6,7},{7,6},{8,9},{9,8},{10,11... | collective-permute-start | bytes 552968 | tf_op jit(solution)/shard_map/ppermute | solution.py:851
  7.8 15.2 %collective-permute-start.4 = (bf16[4,32,1764]{2,1,0:T(8,128)(2,1)}, bf16[4,32,1764]{2,1,0:T(8,128)(2,1)}, u32[]{:S(2)}, u32[]{:S(2)}) collective-permute-start(bf16[4,32,1764]{2,1,0:T(8,128)(2,1)} %get-tuple-element.80.refs_4_.refs_0_), channel_id=1, source_target_pairs={{0,3},{1,2},{2,1},{3,0},{4,7},{5,6},{6,5},{7,4},{8,11},{9,10},{10,... | collective-permute-start | bytes 1354760 | tf_op jit(solution)/shard_map/ppermute | solution.py:851
  7.9 25.3 %collective-permute-start.9 = (bf16[4,32,1764]{2,1,0:T(8,128)(2,1)}, bf16[4,32,1764]{2,1,0:T(8,128)(2,1)}, u32[]{:S(2)}, u32[]{:S(2)}) collective-permute-start(bf16[4,32,1764]{2,1,0:T(8,128)(2,1)} %get-tuple-element.88), channel_id=1, source_target_pairs={{0,2},{1,3},{2,0},{3,1},{4,6},{5,7},{6,4},{7,5},{8,10},{9,11},{10,... | collective-permute-start | bytes 1354760 | tf_op jit(solution)/shard_map/ppermute | solution.py:851
  12.6 20.6 %collective-permute-start.3 = (bf16[8,32,1764]{2,1,0:T(8,128)(2,1)}, bf16[8,32,1764]{2,1,0:T(8,128)(2,1)S(1)}, u32[]{:S(2)}, u32[]{:S(2)}) collective-permute-start(bf16[8,32,1764]{2,1,0:T(8,128)(2,1)} %get-tuple-element.83), channel_id=1, source_target_pairs={{0,1},{1,0},{2,3},{3,2},{4,5},{5,4},{6,7},{7,6},{8,9},{9,8},{10,11... | collective-permute-start | bytes 2709512 | tf_op jit(solution)/shard_map/ppermute | solution.py:851
  13.6 2.1 collective-permute-start.2
  25.3 17.0 %collective-permute-start.7 = (bf16[2,32,1764]{2,1,0:T(8,128)(2,1)}, bf16[2,32,1764]{2,1,0:T(8,128)(2,1)}, u32[]{:S(2)}, u32[]{:S(2)}) collective-permute-start(bf16[2,32,1764]{2,1,0:T(8,128)(2,1)} %get-tuple-element.86), channel_id=1, source_target_pairs={{0,2},{1,3},{2,0},{3,1},{4,6},{5,7},{6,4},{7,5},{8,10},{9,11},{10,... | collective-permute-start | bytes 677384 | tf_op jit(solution)/shard_map/ppermute | solution.py:851
  25.5 17.2 %collective-permute-start.8 = (bf16[2,32,1764]{2,1,0:T(8,128)(2,1)}, bf16[2,32,1764]{2,1,0:T(8,128)(2,1)}, u32[]{:S(2)}, u32[]{:S(2)}) collective-permute-start(bf16[2,32,1764]{2,1,0:T(8,128)(2,1)} %get-tuple-element.87.refs_4_), channel_id=1, source_target_pairs={{0,3},{1,2},{2,1},{3,0},{4,7},{5,6},{6,5},{7,4},{8,11},{9,10},{10,... | collective-permute-start | bytes 677384 | tf_op jit(solution)/shard_map/ppermute | solution.py:851
  29.5 18.5 %collective-permute-start.5 = (bf16[2,32,1764]{2,1,0:T(8,128)(2,1)}, bf16[2,32,1764]{2,1,0:T(8,128)(2,1)}, u32[]{:S(2)}, u32[]{:S(2)}) collective-permute-start(bf16[2,32,1764]{2,1,0:T(8,128)(2,1)} %get-tuple-element.84), channel_id=1, source_target_pairs={{0,2},{1,3},{2,0},{3,1},{4,6},{5,7},{6,4},{7,5},{8,10},{9,11},{10,... | collective-permute-start | bytes 677384 | tf_op jit(solution)/shard_map/ppermute | solution.py:851
  33.2 18.1 %collective-permute-start.6 = (bf16[2,32,1764]{2,1,0:T(8,128)(2,1)}, bf16[2,32,1764]{2,1,0:T(8,128)(2,1)}, u32[]{:S(2)}, u32[]{:S(2)}) collective-permute-start(bf16[2,32,1764]{2,1,0:T(8,128)(2,1)} %get-tuple-element.85.refs_7_), channel_id=1, source_target_pairs={{0,3},{1,2},{2,1},{3,0},{4,7},{5,6},{6,5},{7,4},{8,11},{9,10},{10,... | collective-permute-start | bytes 677384 | tf_op jit(solution)/shard_map/ppermute | solution.py:851
  56.1 13.7 %all-to-all-start = ((f32[32,4,128]{2,1,0:T(4,128)}), f32[32,4,128]{2,1,0:T(4,128)S(1)}, u32[]{:S(2)}, u32[]{:S(2)}) async-start(f32[32,4,128]{2,1,0:T(4,128)} %get-tuple-element.95), calls=%async_computation | async-start | bytes 131072 | tf_op jit(solution)/shard_map/all_to_all | solution.py:854
  84.2 10.0 %all-to-all-start.1 = ((f32[32,4,128]{2,1,0:T(4,128)}), f32[32,4,128]{2,1,0:T(4,128)S(1)}, u32[]{:S(2)}, u32[]{:S(2)}) async-start(f32[32,4,128]{2,1,0:T(4,128)} %get-tuple-element.101.own_ref), calls=%async_computation.1 | async-start | bytes 131072 | tf_op jit(solution)/shard_map/all_to_all | solution.py:854
  86.9 2.7 %collective-permute-start.12 = (bf16[8,32,100]{2,1,0:T(8,128)(2,1)S(1)}, bf16[8,32,100]{2,1,0:T(8,128)(2,1)S(1)}, u32[]{:S(2)}, u32[]{:S(2)}) collective-permute-start(bf16[8,32,100]{2,1,0:T(8,128)(2,1)S(1)} %bitcast.33), channel_id=1, source_target_pairs={{0,1},{1,0},{2,3},{3,2},{4,5},{5,4},{6,7},{7,6},{8,9},{9,8},{10,11... | collective-permute-start | bytes 153608 | tf_op jit(solution)/shard_map/ppermute | solution.py:851
  87.1 4.8 %collective-permute-start.13 = (bf16[8,32,100]{2,1,0:T(8,128)(2,1)S(1)}, bf16[8,32,100]{2,1,0:T(8,128)(2,1)S(1)}, u32[]{:S(2)}, u32[]{:S(2)}) collective-permute-start(bf16[8,32,100]{2,1,0:T(8,128)(2,1)S(1)} %bitcast.34), channel_id=1, source_target_pairs={{0,2},{1,3},{2,0},{3,1},{4,6},{5,7},{6,4},{7,5},{8,10},{9,11},{10,... | collective-permute-start | bytes 153608 | tf_op jit(solution)/shard_map/ppermute | solution.py:851
  88.8 4.5 %collective-permute-start.14 = (bf16[8,32,100]{2,1,0:T(8,128)(2,1)S(1)}, bf16[8,32,100]{2,1,0:T(8,128)(2,1)S(1)}, u32[]{:S(2)}, u32[]{:S(2)}) collective-permute-start(bf16[8,32,100]{2,1,0:T(8,128)(2,1)S(1)} %bitcast.35), channel_id=1, source_target_pairs={{0,3},{1,2},{2,1},{3,0},{4,7},{5,6},{6,5},{7,4},{8,11},{9,10},{10,... | collective-permute-start | bytes 153608 | tf_op jit(solution)/shard_map/ppermute | solution.py:851
  100.8 11.6 %all-to-all-start.2 = ((f32[32,4,128]{2,1,0:T(4,128)}), f32[32,4,128]{2,1,0:T(4,128)S(1)}, u32[]{:S(2)}, u32[]{:S(2)}) async-start(f32[32,4,128]{2,1,0:T(4,128)} %get-tuple-element.110), calls=%async_computation.2 | async-start | bytes 131072 | tf_op jit(solution)/shard_map/all_to_all | solution.py:854
  104.9 29.4 %collective-permute-start.10 = (bf16[8,32,441]{2,1,0:T(8,128)(2,1)}, bf16[8,32,441]{2,1,0:T(8,128)(2,1)S(1)}, u32[]{:S(2)}, u32[]{:S(2)}) collective-permute-start(bf16[8,32,441]{2,1,0:T(8,128)(2,1)} %get-tuple-element.99), channel_id=1, source_target_pairs={{0,2},{1,3},{2,0},{3,1},{4,6},{5,7},{6,4},{7,5},{8,10},{9,11},{10,... | collective-permute-start | bytes 677384 | tf_op jit(solution)/shard_map/ppermute | solution.py:851
  106.8 27.6 %collective-permute-start.11 = (bf16[8,32,441]{2,1,0:T(8,128)(2,1)}, bf16[8,32,441]{2,1,0:T(8,128)(2,1)S(1)}, u32[]{:S(2)}, u32[]{:S(2)}) collective-permute-start(bf16[8,32,441]{2,1,0:T(8,128)(2,1)} %get-tuple-element.100), channel_id=1, source_target_pairs={{0,3},{1,2},{2,1},{3,0},{4,7},{5,6},{6,5},{7,4},{8,11},{9,10},{10,... | collective-permute-start | bytes 677384 | tf_op jit(solution)/shard_map/ppermute | solution.py:851
  106.8 27.6 %collective-permute-start.17 = (bf16[8,32,441]{2,1,0:T(8,128)(2,1)}, bf16[8,32,441]{2,1,0:T(8,128)(2,1)S(1)}, u32[]{:S(2)}, u32[]{:S(2)}) collective-permute-start(bf16[8,32,441]{2,1,0:T(8,128)(2,1)} %get-tuple-element.107), channel_id=1, source_target_pairs={{0,1},{1,0},{2,3},{3,2},{4,5},{5,4},{6,7},{7,6},{8,9},{9,8},{10,11... | collective-permute-start | bytes 677384 | tf_op jit(solution)/shard_map/ppermute | solution.py:851
  107.1 22.8 %collective-permute-start.15 = (bf16[8,32,100]{2,1,0:T(8,128)(2,1)}, bf16[8,32,100]{2,1,0:T(8,128)(2,1)S(1)}, u32[]{:S(2)}, u32[]{:S(2)}) collective-permute-start(bf16[8,32,100]{2,1,0:T(8,128)(2,1)} %get-tuple-element.104), channel_id=1, source_target_pairs={{0,2},{1,3},{2,0},{3,1},{4,6},{5,7},{6,4},{7,5},{8,10},{9,11},{10,... | collective-permute-start | bytes 153608 | tf_op jit(solution)/shard_map/ppermute | solution.py:851
  108.9 25.4 %collective-permute-start.16 = (bf16[8,32,100]{2,1,0:T(8,128)(2,1)}, bf16[8,32,100]{2,1,0:T(8,128)(2,1)S(1)}, u32[]{:S(2)}, u32[]{:S(2)}) collective-permute-start(bf16[8,32,100]{2,1,0:T(8,128)(2,1)} %get-tuple-element.105), channel_id=1, source_target_pairs={{0,3},{1,2},{2,1},{3,0},{4,7},{5,6},{6,5},{7,4},{8,11},{9,10},{10,... | collective-permute-start | bytes 153608 | tf_op jit(solution)/shard_map/ppermute | solution.py:851
  127.2 9.9 %all-to-all-start.3 = ((f32[32,4,128]{2,1,0:T(4,128)}), f32[32,4,128]{2,1,0:T(4,128)S(1)}, u32[]{:S(2)}, u32[]{:S(2)}) async-start(f32[32,4,128]{2,1,0:T(4,128)} %get-tuple-element.116.refs_0_), calls=%async_computation.3 | async-start | bytes 131072 | tf_op jit(solution)/shard_map/all_to_all | solution.py:854
  130.0 4.4 %collective-permute-start.18 = (bf16[8,32,100]{2,1,0:T(8,128)(2,1)}, bf16[8,32,100]{2,1,0:T(8,128)(2,1)}, u32[]{:S(2)}, u32[]{:S(2)}) collective-permute-start(bf16[8,32,100]{2,1,0:T(8,128)(2,1)} %get-tuple-element.109), channel_id=1, source_target_pairs={{0,1},{1,0},{2,3},{3,2},{4,5},{5,4},{6,7},{7,6},{8,9},{9,8},{10,11... | collective-permute-start | bytes 153608 | tf_op jit(solution)/shard_map/ppermute | solution.py:851
  143.1 19.2 %collective-permute-start.19 = (bf16[2,32,1764]{2,1,0:T(8,128)(2,1)}, bf16[2,32,1764]{2,1,0:T(8,128)(2,1)S(1)}, u32[]{:S(2)}, u32[]{:S(2)}) collective-permute-start(bf16[2,32,1764]{2,1,0:T(8,128)(2,1)} %get-tuple-element.125), channel_id=1, source_target_pairs={{0,3},{1,2},{2,1},{3,0},{4,7},{5,6},{6,5},{7,4},{8,11},{9,10},{10,... | collective-permute-start | bytes 677384 | tf_op jit(solution)/shard_map/ppermute | solution.py:851
  143.2 19.1 %collective-permute-start.21 = (bf16[2,32,1764]{2,1,0:T(8,128)(2,1)}, bf16[2,32,1764]{2,1,0:T(8,128)(2,1)S(1)}, u32[]{:S(2)}, u32[]{:S(2)}) collective-permute-start(bf16[2,32,1764]{2,1,0:T(8,128)(2,1)} %get-tuple-element.127), channel_id=1, source_target_pairs={{0,2},{1,3},{2,0},{3,1},{4,6},{5,7},{6,4},{7,5},{8,10},{9,11},{10,... | collective-permute-start | bytes 677384 | tf_op jit(solution)/shard_map/ppermute | solution.py:851
  150.1 12.1 %collective-permute-start.20 = (bf16[2,32,1764]{2,1,0:T(8,128)(2,1)}, bf16[2,32,1764]{2,1,0:T(8,128)(2,1)S(1)}, u32[]{:S(2)}, u32[]{:S(2)}) collective-permute-start(bf16[2,32,1764]{2,1,0:T(8,128)(2,1)} %get-tuple-element.126), channel_id=1, source_target_pairs={{0,3},{1,2},{2,1},{3,0},{4,7},{5,6},{6,5},{7,4},{8,11},{9,10},{10,... | collective-permute-start | bytes 677384 | tf_op jit(solution)/shard_map/ppermute | solution.py:851
  165.7 39.6 %all-to-all-start.4 = ((f32[32,24,384]{2,1,0:T(8,128)}), f32[32,24,384]{2,1,0:T(8,128)}, u32[]{:S(2)}, u32[]{:S(2)}) async-start(f32[32,24,384]{2,1,0:T(8,128)} %bitcast.30), calls=%async_computation.4 | async-start | bytes 2359296 | tf_op jit(solution)/shard_map/all_to_all | solution.py:1260
  169.4 19.2 %collective-permute-start.22 = (bf16[2,32,1764]{2,1,0:T(8,128)(2,1)S(1)}, bf16[2,32,1764]{2,1,0:T(8,128)(2,1)S(1)}, u32[]{:S(2)}, u32[]{:S(2)}) collective-permute-start(bf16[2,32,1764]{2,1,0:T(8,128)(2,1)S(1)} %copy-done.16), channel_id=1, source_target_pairs={{0,2},{1,3},{2,0},{3,1},{4,6},{5,7},{6,4},{7,5},{8,10},{9,11},{10,... | collective-permute-start | bytes 677384 | tf_op jit(solution)/shard_map/ppermute | solution.py:851
  196.9 14.0 %collective-permute-start.25 = (bf16[8,32,1764]{2,1,0:T(8,128)(2,1)}, bf16[8,32,1764]{2,1,0:T(8,128)(2,1)}, u32[]{:S(2)}, u32[]{:S(2)}) collective-permute-start(bf16[8,32,1764]{2,1,0:T(8,128)(2,1)} %get-tuple-element.137), channel_id=1, source_target_pairs={{0,1},{1,0},{2,3},{3,2},{4,5},{5,4},{6,7},{7,6},{8,9},{9,8},{10,11... | collective-permute-start | bytes 2709512 | tf_op jit(solution)/shard_map/ppermute | solution.py:851
  196.9 17.2 %collective-permute-start.23 = (bf16[4,32,1764]{2,1,0:T(8,128)(2,1)}, bf16[4,32,1764]{2,1,0:T(8,128)(2,1)S(1)}, u32[]{:S(2)}, u32[]{:S(2)}) collective-permute-start(bf16[4,32,1764]{2,1,0:T(8,128)(2,1)} %get-tuple-element.135), channel_id=1, source_target_pairs={{0,2},{1,3},{2,0},{3,1},{4,6},{5,7},{6,4},{7,5},{8,10},{9,11},{10,... | collective-permute-start | bytes 1354760 | tf_op jit(solution)/shard_map/ppermute | solution.py:851
  197.4 22.2 %collective-permute-start.24 = (bf16[4,32,1764]{2,1,0:T(8,128)(2,1)}, bf16[4,32,1764]{2,1,0:T(8,128)(2,1)}, u32[]{:S(2)}, u32[]{:S(2)}) collective-permute-start(bf16[4,32,1764]{2,1,0:T(8,128)(2,1)} %get-tuple-element.136), channel_id=1, source_target_pairs={{0,3},{1,2},{2,1},{3,0},{4,7},{5,6},{6,5},{7,4},{8,11},{9,10},{10,... | collective-permute-start | bytes 1354760 | tf_op jit(solution)/shard_map/ppermute | solution.py:851
  207.3 15.6 %all-to-all-start.5 = ((f32[8,24,384]{2,1,0:T(8,128)}), f32[8,24,384]{2,1,0:T(8,128)S(1)}, u32[]{:S(2)}, u32[]{:S(2)}) async-start(f32[8,24,384]{2,1,0:T(8,128)} %strips.1), calls=%async_computation.5 | async-start | bytes 589824 | tf_op jit(solution)/shard_map/all_to_all | solution.py:1269
  (22 other events, 69.0 us)
